TPU v7x, 32 devices: a whole 2x2x4 slice. The times are simulated.
32 devices in a mesh: dp: 8 (over y, x, core), tensor: 4 (over z).
Axes of the slice: x: 2, y: 2, z: 4, core: 2. Of those that a mesh axis runs over, the one named last changes fastest.
Arguments:
- tokens: bfloat16 [8192, 1024], P(('dp', 'tensor')), may hold values from -6 to 6
- cotangent: bfloat16 [8192, 1024], P(('dp', 'tensor')), may hold values from -6 to 6
- lengths: int32 [24], replicated, may hold values from 1 to 512, as said below
- order: int32 [24], replicated, may hold values from 0 to 23, as said below
- w_qkv: bfloat16 [2, 1024, 3, 1024], P(None, 'dp', None, 'tensor'), may hold values from -0.1875 to 0.1875
- w_out: bfloat16 [2, 1024, 1024], P(None, 'tensor', 'dp'), may hold values from -0.75 to 0.75
- w_up: bfloat16 [2, 1024, 4096], P(None, 'dp', 'tensor'), may hold values from -0.1875 to 0.1875
- w_down: bfloat16 [2, 4096, 1024], P(None, 'tensor', 'dp'), may hold values from -0.09375 to 0.09375
- gains: float32 [2, 2, 1024], P(None, None, ('dp', 'tensor')), may hold values from 0.25 to 1.75
- biases: float32 [2, 6, 1024], P(None, None, ('dp', 'tensor')), may hold values from -3 to 3
- up_bias: float32 [2, 4096], P(None, ('dp', 'tensor')), may hold values from -3 to 3
Outputs:
- mixed: bfloat16 [8192, 1024], P(('dp', 'tensor'))
- tokens_grad: float32 [8192, 1024], P(('dp', 'tensor'))
- grad_qkv: float32 [2, 1024, 3, 1024], P(None, 'dp', None, 'tensor')
- grad_out: float32 [2, 1024, 1024], P(None, 'tensor', 'dp')
- grad_up: float32 [2, 1024, 4096], P(None, 'dp', 'tensor')
- grad_down: float32 [2, 4096, 1024], P(None, 'tensor', 'dp')
- grad_gains: float32 [2, 2, 1024], P(None, None, ('dp', 'tensor'))
- grad_biases: float32 [2, 6, 1024], P(None, None, ('dp', 'tensor'))
- grad_up_bias: float32 [2, 4096], P(None, ('dp', 'tensor'))
Inputs may be any that keep to these rules, and one draw needn't show every extreme that they name: The 3 sequences g * 3 to g * 3 + 2 of each group have lengths summing to at most 1024, and one of them in every group is 512 long. A permutation of the 24 sequences in which order[g * 3 + j], j = 0 .. 2, are the sequences g * 3 to g * 3 + 2, each once.
All inputs are finite; a program needn't handle non-finite values.
Results may differ from a plain program's by a relative error of at most 0.02.
Values may be sent and summed in bfloat16 or wider, within the bound.
No kernel may reach another device: no remote copies, remote signals or barrier semaphores. Data moves between devices by JAX's collectives and lax.ppermute only.
A program may use at most 128 MiB of HBM per device.

v0:
```python
import jax
import jax.numpy as jnp
from jax import lax
from jax.sharding import PartitionSpec as P

D = 1024
HEAD_DIM = 64
FF = 4096
LAYERS = 2
SEQ_GRP = 3


EPS = 1e-05
NEG = -1e30


def layer_norm(field_in, gain_row, shift_row):
    centre = jnp.mean(field_in, axis=-1, keepdims=True)
    centred = field_in - centre
    spread = jnp.mean(centred * centred, axis=-1, keepdims=True)
    return centred * lax.rsqrt(spread + EPS) * gain_row + shift_row


def gelu_exact(field_in):
    return jax.nn.gelu(field_in, approximate=False)


def group_maps(own_len, dealt_local, group_rows):
    slot_range = jnp.arange(SEQ_GRP, dtype=jnp.int32)
    own_end = jnp.cumsum(own_len)
    own_start = own_end - own_len
    pick_table = dealt_local[:, None] == slot_range[None, :]
    dealt_len = jnp.sum(jnp.where(pick_table, own_len[None, :], 0), axis=1)
    dealt_src = jnp.sum(jnp.where(pick_table, own_start[None, :], 0), axis=1)
    dealt_end = jnp.cumsum(dealt_len)
    dealt_begin = dealt_end - dealt_len
    position = jnp.arange(group_rows, dtype=jnp.int32)
    segments = jnp.sum((position[:, None] >= dealt_end[None, :]).astype(jnp.int32), axis=1)
    seg_hit = segments[:, None] == slot_range[None, :]
    source = jnp.sum(
        jnp.where(seg_hit, dealt_src[None, :] - dealt_begin[None, :] + position[:, None], 0), axis=1
    ) + jnp.where(segments == SEQ_GRP, position, 0)
    return (segments, source)


def route_rows(rows_here, anchor, slot_here, local_rows):
    holder = anchor // local_rows
    picked = jnp.take(rows_here, anchor % local_rows, axis=0)
    chosen = jnp.where((holder == slot_here)[:, None], picked, jnp.zeros_like(picked))
    return chosen.reshape(-1, local_rows, rows_here.shape[1])


def gather_rows(local_part):
    return lax.all_gather(local_part, "tensor", axis=0, tiled=True)


def sum_rows(partial_term):
    return lax.psum_scatter(partial_term, "tensor", scatter_dimension=0, tiled=True)


def gather_grads(local_part):
    return lax.all_gather(local_part, "tensor", axis=0, tiled=True)


def sum_grads(partial_term):
    return lax.psum_scatter(partial_term, "tensor", scatter_dimension=0, tiled=True)


def score_block(query_part, segment_part, keys_low, segments, score_scale):
    scores = (
        jnp.einsum("bhd,khd->hbk", query_part, keys_low, preferred_element_type=jnp.float32)
        * score_scale
    )
    same_segment = segment_part[:, None] == segments[None, :]
    return jnp.where(same_segment[None], scores, NEG)


def attend(queries, keys_low, values_low, segments, score_scale):
    group_rows, heads_here, _ = queries.shape
    block_rows = min(512, group_rows)
    block_count = group_rows // block_rows
    query_blocks = queries.reshape(block_count, block_rows, heads_here, HEAD_DIM)
    segment_blocks = segments.reshape(block_count, block_rows)

    def one_block(items_in):
        query_part, segment_part = items_in
        masked = score_block(query_part, segment_part, keys_low, segments, score_scale)
        row_peak = jnp.max(masked, axis=2, keepdims=True)
        exponent = jnp.exp(masked - row_peak)
        row_total = jnp.sum(exponent, axis=2, keepdims=True)
        soft_probs = (exponent / row_total).astype(jnp.bfloat16)
        block_out = jnp.einsum(
            "hbk,khd->bhd", soft_probs, values_low, preferred_element_type=jnp.float32
        )
        return (block_out, row_peak, row_total)

    block_outs, row_peaks, row_totals = lax.map(one_block, (query_blocks, segment_blocks))
    return (block_outs.reshape(group_rows, heads_here * HEAD_DIM), row_peaks, row_totals)


def attend_back(
    queries, keys_low, values_low, segments, row_peaks, row_totals, grad_att, score_scale
):
    group_rows, heads_here, _ = queries.shape
    block_rows = min(512, group_rows)
    block_count = group_rows // block_rows
    query_blocks = queries.reshape(block_count, block_rows, heads_here, HEAD_DIM)
    segment_blocks = segments.reshape(block_count, block_rows)
    grad_blocks = grad_att.reshape(block_count, block_rows, heads_here, HEAD_DIM)

    def one_block(running, items_in):
        key_total, value_total = running
        query_part, segment_part, grad_part, row_peak, row_total = items_in
        masked = score_block(query_part, segment_part, keys_low, segments, score_scale)
        soft_probs = jnp.exp(masked - row_peak) / row_total
        grad_prob = jnp.einsum(
            "bhd,khd->hbk", grad_part, values_low, preferred_element_type=jnp.float32
        )
        grad_score = soft_probs * (
            grad_prob - jnp.sum(soft_probs * grad_prob, axis=2, keepdims=True)
        )
        grad_score_low = grad_score.astype(jnp.bfloat16)
        grad_query = (
            jnp.einsum("hbk,khd->bhd", grad_score_low, keys_low, preferred_element_type=jnp.float32)
            * score_scale
        )
        grad_key = (
            jnp.einsum(
                "hbk,bhd->khd", grad_score_low, query_part, preferred_element_type=jnp.float32
            )
            * score_scale
        )
        grad_value = jnp.einsum(
            "hbk,bhd->khd",
            soft_probs.astype(jnp.bfloat16),
            grad_part,
            preferred_element_type=jnp.float32,
        )
        return ((key_total + grad_key, value_total + grad_value), grad_query)

    zero_block = jnp.zeros((group_rows, heads_here, HEAD_DIM), jnp.float32)
    (grad_keys, grad_values), grad_queries = lax.scan(
        one_block,
        (zero_block, zero_block),
        (query_blocks, segment_blocks, grad_blocks, row_peaks, row_totals),
    )
    return (grad_queries.reshape(group_rows, heads_here * HEAD_DIM), grad_keys, grad_values)


def layer_vectors(gains_all, biases_all, upb_all, layer_index, slot_here, head_width, ff_width):
    bias_rows = biases_all[layer_index]
    query_bias = lax.dynamic_slice_in_dim(bias_rows[0], slot_here * head_width, head_width)
    value_bias = lax.dynamic_slice_in_dim(bias_rows[1], slot_here * head_width, head_width)
    upb_own = lax.dynamic_slice_in_dim(upb_all[layer_index], slot_here * ff_width, ff_width)
    return (
        query_bias,
        value_bias,
        bias_rows[2],
        gains_all[layer_index, 0],
        bias_rows[3],
        upb_own,
        bias_rows[4],
        gains_all[layer_index, 1],
        bias_rows[5],
    )


def forward_layer(hidden, weights_now, vectors, segments, score_scale):
    w_qkv_full, w_out_full, w_up_full, w_down_full = weights_now
    (
        query_bias,
        value_bias,
        out_bias,
        gain_one,
        shift_one,
        upb_own,
        down_bias,
        gain_two,
        shift_two,
    ) = vectors
    head_width = w_qkv_full.shape[2]
    heads_here = head_width // HEAD_DIM
    x_full = gather_rows(hidden.astype(jnp.bfloat16))
    group_rows = x_full.shape[0]
    projected = jnp.dot(
        x_full, w_qkv_full.reshape(D, 3 * head_width), preferred_element_type=jnp.float32
    )
    queries = (
        (projected[:, :head_width] + query_bias)
        .astype(jnp.bfloat16)
        .reshape(group_rows, heads_here, HEAD_DIM)
    )
    keys_low = (
        projected[:, head_width : 2 * head_width]
        .astype(jnp.bfloat16)
        .reshape(group_rows, heads_here, HEAD_DIM)
    )
    values_low = (
        (projected[:, 2 * head_width :] + value_bias)
        .astype(jnp.bfloat16)
        .reshape(group_rows, heads_here, HEAD_DIM)
    )
    attended, row_peaks, row_totals = attend(queries, keys_low, values_low, segments, score_scale)
    attended_low = attended.astype(jnp.bfloat16)
    branch = (
        sum_rows(jnp.dot(attended_low, w_out_full, preferred_element_type=jnp.float32)) + out_bias
    )
    pre_one = hidden + branch
    normed = layer_norm(pre_one, gain_one, shift_one)
    normed_full = gather_rows(normed.astype(jnp.bfloat16))
    hidden_up = jnp.dot(normed_full, w_up_full, preferred_element_type=jnp.float32) + upb_own
    act_low = gelu_exact(hidden_up).astype(jnp.bfloat16)
    second = sum_rows(jnp.dot(act_low, w_down_full, preferred_element_type=jnp.float32)) + down_bias
    pre_two = normed + second
    out_value = layer_norm(pre_two, gain_two, shift_two)
    kept_values = (
        x_full,
        queries,
        keys_low,
        values_low,
        row_peaks,
        row_totals,
        attended_low,
        pre_one,
        normed_full,
        hidden_up,
        act_low,
        pre_two,
    )
    return (out_value, kept_values)


def backward_layer(grad_y, weights_now, vectors, segments, kept_values, score_scale):
    w_qkv_full, w_out_full, w_up_full, w_down_full = weights_now
    (
        query_bias,
        value_bias,
        out_bias,
        gain_one,
        shift_one,
        upb_own,
        down_bias,
        gain_two,
        shift_two,
    ) = vectors
    (
        x_full,
        queries,
        keys_low,
        values_low,
        row_peaks,
        row_totals,
        attended_low,
        pre_one,
        normed_full,
        hidden_up,
        act_low,
        pre_two,
    ) = kept_values
    group_rows, heads_here, _ = queries.shape
    head_width = heads_here * HEAD_DIM
    _, norm_two_back = jax.vjp(layer_norm, pre_two, gain_two, shift_two)
    grad_two, grad_gain_two, grad_shift_two = norm_two_back(grad_y)
    grad_down_bias = jnp.sum(grad_two, axis=0)
    two_full = gather_grads(grad_two.astype(jnp.bfloat16))
    grad_down = jnp.einsum("rf,rd->fd", act_low, two_full, preferred_element_type=jnp.float32)
    grad_act = jnp.einsum("rd,fd->rf", two_full, w_down_full, preferred_element_type=jnp.float32)
    _, gelu_back = jax.vjp(gelu_exact, hidden_up)
    (grad_hidden_up,) = gelu_back(grad_act)
    grad_upb = jnp.sum(grad_hidden_up, axis=0)
    up_low = grad_hidden_up.astype(jnp.bfloat16)
    grad_up = jnp.einsum("rd,rf->df", normed_full, up_low, preferred_element_type=jnp.float32)
    grad_normed = grad_two + sum_grads(
        jnp.einsum("rf,df->rd", up_low, w_up_full, preferred_element_type=jnp.float32)
    )
    _, norm_one_back = jax.vjp(layer_norm, pre_one, gain_one, shift_one)
    grad_one, grad_gain_one, grad_shift_one = norm_one_back(grad_normed)
    grad_out_bias = jnp.sum(grad_one, axis=0)
    one_full = gather_grads(grad_one.astype(jnp.bfloat16))
    grad_out = jnp.einsum("rc,rd->cd", attended_low, one_full, preferred_element_type=jnp.float32)
    grad_att = jnp.einsum(
        "rd,cd->rc", one_full, w_out_full, preferred_element_type=jnp.float32
    ).astype(jnp.bfloat16)
    grad_queries, grad_keys, grad_values = attend_back(
        queries,
        keys_low,
        values_low,
        segments,
        row_peaks,
        row_totals,
        grad_att.reshape(group_rows, heads_here, HEAD_DIM),
        score_scale,
    )
    grad_keys = grad_keys.reshape(group_rows, head_width)
    grad_values = grad_values.reshape(group_rows, head_width)
    grad_query_bias = jnp.sum(grad_queries, axis=0)
    grad_value_bias = jnp.sum(grad_values, axis=0)
    proj_low = jnp.stack([grad_queries, grad_keys, grad_values], axis=1).astype(jnp.bfloat16)
    grad_qkv = jnp.einsum("rd,rjc->djc", x_full, proj_low, preferred_element_type=jnp.float32)
    grad_x = grad_one + sum_grads(
        jnp.einsum("rjc,djc->rd", proj_low, w_qkv_full, preferred_element_type=jnp.float32)
    )
    small_terms = (
        grad_query_bias,
        grad_value_bias,
        grad_out_bias,
        grad_gain_one,
        grad_shift_one,
        grad_upb,
        grad_down_bias,
        grad_gain_two,
        grad_shift_two,
    )
    return (grad_x, (grad_qkv, grad_out, grad_up, grad_down), small_terms)


def body(tokens, cotangent, lengths, order, w_qkv, w_out, w_up, w_down, gains, biases, up_bias):
    local_rows = tokens.shape[0]
    tensor_count = lax.axis_size("tensor")
    group_rows = local_rows * tensor_count
    head_width = D // tensor_count
    ff_width = FF // tensor_count
    score_scale = HEAD_DIM ** (-0.5)
    slot_here = lax.axis_index("tensor")
    group_here = lax.axis_index("dp")
    seq_base = group_here * SEQ_GRP
    own_len = lax.dynamic_slice_in_dim(lengths, seq_base, SEQ_GRP)
    dealt_local = lax.dynamic_slice_in_dim(order, seq_base, SEQ_GRP) - seq_base
    segments, source = group_maps(own_len, dealt_local, group_rows)
    segment_own = lax.dynamic_slice_in_dim(segments, slot_here * local_rows, local_rows)
    valid_rows = (segment_own < SEQ_GRP).astype(jnp.float32)[:, None]
    gains_all, biases_all, upb_all = (
        lax.all_gather(gains, ("dp", "tensor"), axis=2, tiled=True),
        lax.all_gather(biases, ("dp", "tensor"), axis=2, tiled=True),
        lax.all_gather(up_bias, ("dp", "tensor"), axis=1, tiled=True),
    )
    token_send = route_rows(tokens, source, slot_here, local_rows)
    cot_send = route_rows(cotangent, source, slot_here, local_rows)
    token_recv, cot_recv = (
        lax.all_to_all(token_send, "tensor", split_axis=0, concat_axis=0, tiled=True),
        lax.all_to_all(cot_send, "tensor", split_axis=0, concat_axis=0, tiled=True),
    )
    hidden = jnp.sum(token_recv.astype(jnp.float32), axis=0)
    cot_own = jnp.sum(cot_recv.astype(jnp.float32), axis=0)
    weights_kept = []
    states_kept = []
    vectors_kept = []
    for layer_index in range(LAYERS):
        weights_now = (
            lax.all_gather(w_qkv[layer_index], "dp", axis=0, tiled=True),
            lax.all_gather(w_out[layer_index], "dp", axis=1, tiled=True),
            lax.all_gather(w_up[layer_index], "dp", axis=0, tiled=True),
            lax.all_gather(w_down[layer_index], "dp", axis=1, tiled=True),
        )
        vectors = layer_vectors(
            gains_all, biases_all, upb_all, layer_index, slot_here, head_width, ff_width
        )
        hidden, kept_values = forward_layer(hidden, weights_now, vectors, segments, score_scale)
        weights_kept.append(weights_now)
        states_kept.append(kept_values)
        vectors_kept.append(vectors)
    mixed_out = hidden.astype(jnp.bfloat16)
    grad_y = cot_own * valid_rows
    reduced_list = []
    gain_parts = []
    bias_parts = []
    upb_parts = []
    zero_width = jnp.zeros((D,), jnp.float32)
    zero_ff = jnp.zeros((FF,), jnp.float32)
    for layer_index in reversed(range(LAYERS)):
        weights_now = (
            lax.all_gather(w_qkv[layer_index], "dp", axis=0, tiled=True),
            lax.all_gather(w_out[layer_index], "dp", axis=1, tiled=True),
            lax.all_gather(w_up[layer_index], "dp", axis=0, tiled=True),
            lax.all_gather(w_down[layer_index], "dp", axis=1, tiled=True),
        )
        grad_y, weight_terms, small_terms = backward_layer(
            grad_y,
            weights_now,
            vectors_kept[layer_index],
            segments,
            states_kept[layer_index],
            score_scale,
        )
        (
            grad_query_bias,
            grad_value_bias,
            grad_out_bias,
            grad_gain_one,
            grad_shift_one,
            grad_upb,
            grad_down_bias,
            grad_gain_two,
            grad_shift_two,
        ) = small_terms
        query_full = lax.dynamic_update_slice_in_dim(
            zero_width, grad_query_bias, slot_here * head_width, 0
        )
        value_full = lax.dynamic_update_slice_in_dim(
            zero_width, grad_value_bias, slot_here * head_width, 0
        )
        upb_full = lax.dynamic_update_slice_in_dim(zero_ff, grad_upb, slot_here * ff_width, 0)
        gain_parts.append(jnp.stack([grad_gain_one, grad_gain_two]))
        bias_parts.append(
            jnp.stack(
                [
                    query_full,
                    value_full,
                    grad_out_bias,
                    grad_shift_one,
                    grad_down_bias,
                    grad_shift_two,
                ]
            )
        )
        upb_parts.append(upb_full)
        reduced_list.append(
            (
                lax.psum_scatter(weight_terms[0], "dp", scatter_dimension=0, tiled=True),
                lax.psum_scatter(weight_terms[1], "dp", scatter_dimension=1, tiled=True),
                lax.psum_scatter(weight_terms[2], "dp", scatter_dimension=0, tiled=True),
                lax.psum_scatter(weight_terms[3], "dp", scatter_dimension=1, tiled=True),
            )
        )
    ordered = reduced_list[::-1]
    grad_qkv = jnp.stack([entry[0] for entry in ordered])
    grad_out = jnp.stack([entry[1] for entry in ordered])
    grad_up = jnp.stack([entry[2] for entry in ordered])
    grad_down = jnp.stack([entry[3] for entry in ordered])
    grad_gains, grad_biases, grad_up_bias = (
        lax.psum_scatter(
            jnp.stack(gain_parts[::-1]), ("dp", "tensor"), scatter_dimension=2, tiled=True
        ),
        lax.psum_scatter(
            jnp.stack(bias_parts[::-1]), ("dp", "tensor"), scatter_dimension=2, tiled=True
        ),
        lax.psum_scatter(
            jnp.stack(upb_parts[::-1]), ("dp", "tensor"), scatter_dimension=1, tiled=True
        ),
    )
    return (
        mixed_out,
        grad_y,
        grad_qkv,
        grad_out,
        grad_up,
        grad_down,
        grad_gains,
        grad_biases,
        grad_up_bias,
    )


def solution(mesh):
    return jax.shard_map(
        body,
        mesh=mesh,
        in_specs=(
            P(("dp", "tensor"), None),
            P(("dp", "tensor"), None),
            P(),
            P(),
            P(None, "dp", None, "tensor"),
            P(None, "tensor", "dp"),
            P(None, "dp", "tensor"),
            P(None, "tensor", "dp"),
            P(None, None, ("dp", "tensor")),
            P(None, None, ("dp", "tensor")),
            P(None, ("dp", "tensor")),
        ),
        out_specs=(
            P(("dp", "tensor"), None),
            P(("dp", "tensor"), None),
            P(None, "dp", None, "tensor"),
            P(None, "tensor", "dp"),
            P(None, "dp", "tensor"),
            P(None, "tensor", "dp"),
            P(None, None, ("dp", "tensor")),
            P(None, None, ("dp", "tensor")),
            P(None, ("dp", "tensor")),
        ),
        check_vma=False,
    )
```

profile of v0, /device:TPU:0, one launch (start us, length us, event | category | flops | bytes accessed | tf_op | source)
XLA Modules:
  0.0 2334.3 jit_solution(2864604808661801128)
XLA Ops:
  10.2 4.1 gather_fusion.1
  14.3 5.4 gather_fusion
  19.7 3.7 select_select_fusion
  23.4 6.4 all-to-all-start
  30.7 47.5 %all-to-all-done = bf16[4,256,1024]{2,1,0:T(8,128)(2,1)} async-done(((bf16[4,256,1024]{2,1,0:T(8,128)(2,1)}), bf16[4,256,1024]{2,1,0:T(8,128)(2,1)}, u32[]{:S(2)}, u32[]{:S(2)}) %all-to-all-start) | async-done | bytes 2097184 | tf_op jit(solution)/shard_map/all_to_all | solution.py:340
  81.4 83.8 %all_gather.67 = f32[2,6,1024]{1,0,2:T(2,128)S(1)} all-gather(f32[2,6,32]{1,0,2:T(2,128)S(1)} %copy.109), channel_id=1, replica_groups=mesh['dp'=8,'tensor'=4] {'dp','tensor'}, dimensions={2}, use_global_device_ids=true | all-gather | bytes 50688 | tf_op jit(solution)/shard_map/all_gather | solution.py:334
  165.2 27.3 %fusion.154 = (f32[1,1,1024]{1,0,2:T(1,128)}, f32[1,1,1024]{1,0,2:T(1,128)}, f32[1024]{0:T(1024)S(1)}, f32[1024]{0:T(1024)S(1)}, f32[1024]{0:T(1024)S(1)}, /*ind...) fusion(f32[2,6,1024]{1,0,2:T(2,128)S(1)} %all_gather.67), kind=kLoop, calls=%fused_computation.319 | loop fusion | bytes 98304 | tf_op jit(solution)/shard_map/slice | solution.py:153
  193.5 11.1 all-gather.1
  207.2 3.9 fusion.163
  213.6 14.9 while.58
  230.0 3.7 fusion.127
  235.8 96.6 %all_gather.69 = f32[2,2,1024]{1,0,2:T(2,128)S(1)} all-gather(f32[2,2,32]{1,0,2:T(2,128)S(1)} %copy.112), channel_id=1, replica_groups=mesh['dp'=8,'tensor'=4] {'dp','tensor'}, dimensions={2}, use_global_device_ids=true | all-gather | bytes 16896 | tf_op jit(solution)/shard_map/all_gather | solution.py:333
  332.5 26.5 %slice_reduce_fusion.1 = (f32[1024]{0:T(1024)}, f32[1024]{0:T(1024)S(1)}, f32[1024]{0:T(1024)S(1)}, f32[1024]{0:T(1024)S(1)}) fusion(f32[2,2,1024]{1,0,2:T(2,128)S(1)} %all_gather.69), kind=kLoop, calls=%fused_computation.224 | loop fusion | bytes 32768 | tf_op jit(solution)/shard_map/slice | solution.py:163
  362.8 65.5 %all_gather.72 = f32[2,4096]{1,0:T(2,128)S(1)} all-gather(f32[2,128]{1,0:T(2,128)S(1)} %copy-done.90), channel_id=1, replica_groups=mesh['dp'=8,'tensor'=4] {'dp','tensor'}, dimensions={1}, use_global_device_ids=true | all-gather | bytes 33792 | tf_op jit(solution)/shard_map/all_gather | solution.py:335
  428.4 14.9 multiply_convert_fusion.3
  443.3 6.5 fusion.100
  450.6 73.3 %reduce-scatter.28.cloned.1.call-done = f32[256,1024]{1,0:T(8,128)} async-done(((f32[1024,1024]{1,0:T(8,128)}), f32[256,1024]{1,0:T(8,128)}) %reduce-scatter.28.cloned.1.call-update) | async-done | bytes 1048592 | tf_op jit(solution)/shard_map/reduce_scatter | solution.py:58
  529.0 12.4 all-gather.5
  541.4 11.7 all-gather.45.cloned.1.call-done
  554.8 46.4 %all-gather.27.cloned.1.call-done = bf16[1024,1024]{1,0:T(8,128)(2,1)} async-done(((bf16[256,1024]{1,0:T(8,128)(2,1)}), bf16[1024,1024]{1,0:T(8,128)(2,1)}) %all-gather.27.cloned.1.call-update) | async-done | bytes 2097168 | tf_op jit(solution)/shard_map/all_gather | solution.py:54
  605.3 16.5 while.59
  623.7 3.9 fusion.124
  628.4 74.9 %reduce-scatter.30.cloned.1.call-done = f32[256,1024]{1,0:T(8,128)} async-done(((f32[1024,1024]{1,0:T(8,128)}), f32[256,1024]{1,0:T(8,128)}) %reduce-scatter.30.cloned.1.call-update) | async-done | bytes 1048592 | tf_op jit(solution)/shard_map/reduce_scatter | solution.py:58
  707.3 27.1 %all-gather.47.cloned.1.call-done = bf16[1,1024,1024]{2,1,0:T(8,128)(2,1)} async-done(((bf16[1,128,1024]{2,1,0:T(8,128)(2,1)}), bf16[1,1024,1024]{2,1,0:T(8,128)(2,1)}) %all-gather.47.cloned.1.call-update) | async-done | bytes 2097168 | tf_op jit(solution)/shard_map/all_gather | solution.py:352
  734.4 48.0 %all-gather.29.cloned.1.call-done = bf16[1024,1024]{1,0:T(8,128)(2,1)} async-done(((bf16[256,1024]{1,0:T(8,128)(2,1)}), bf16[1024,1024]{1,0:T(8,128)(2,1)}) %all-gather.29.cloned.1.call-update) | async-done | bytes 2097168 | tf_op jit(solution)/shard_map/all_gather | solution.py:54
  782.4 14.9 multiply_convert_fusion.2
  797.3 14.1 all-gather.49.cloned.1.call-done
  811.4 6.5 fusion.90
  817.9 4.6 all-to-all-start.1
  822.6 104.9 %all-to-all-done.1 = bf16[4,256,1024]{2,1,0:T(8,128)(2,1)} async-done(((bf16[4,256,1024]{2,1,0:T(8,128)(2,1)}), bf16[4,256,1024]{2,1,0:T(8,128)(2,1)}, u32[]{:S(2)}, u32[]{:S(2)}) %all-to-all-start.1) | async-done | bytes 2097184 | tf_op jit(solution)/shard_map/all_to_all | solution.py:341
  929.6 3.9 reduce-scatter.32.cloned.1.call-done
  940.6 49.6 %all-gather.31.cloned.1.call-done = bf16[1024,1024]{1,0:T(8,128)(2,1)} async-done(((bf16[256,1024]{1,0:T(8,128)(2,1)}), bf16[1024,1024]{1,0:T(8,128)(2,1)}) %all-gather.31.cloned.1.call-update) | async-done | bytes 2097168 | tf_op jit(solution)/shard_map/all_gather | solution.py:62
  990.2 9.1 fusion.161
  1000.6 4.3 fusion.94
  1005.0 75.6 %reduce-scatter.34.cloned.1.call-done = f32[256,1024]{1,0:T(8,128)} async-done(((f32[1024,1024]{1,0:T(8,128)}), f32[256,1024]{1,0:T(8,128)}) %reduce-scatter.34.cloned.1.call-update) | async-done | bytes 1048592 | tf_op jit(solution)/shard_map/reduce_scatter | solution.py:66
  1086.0 46.5 %all-gather.33.cloned.1.call-done = bf16[1024,1024]{1,0:T(8,128)(2,1)} async-done(((bf16[256,1024]{1,0:T(8,128)(2,1)}), bf16[1024,1024]{1,0:T(8,128)(2,1)}) %all-gather.33.cloned.1.call-update) | async-done | bytes 2097168 | tf_op jit(solution)/shard_map/all_gather | solution.py:62
  1142.2 24.0 %while.60 = (s32[]{:T(128)}, f32[1024,4,64]{0,2,1:T(8,128)S(1)}, f32[1024,4,64]{0,2,1:T(8,128)S(1)}, f32[2,512,4,64]{1,3,2,0:T(8,128)}, bf16[2,512,4,64]{1,3,2,0...) while((s32[]{:T(128)}, f32[1024,4,64]{0,2,1:T(8,128)S(1)}, ...), condition=%wide.region_35.37_spmd.clone, body=%wide.region_33.36_spmd.clone.sunk | while | flops 1365112832 | bytes 81864960 | solution.py:142
  1171.7 5.2 convolution_bitcast_fusion.1
  1177.1 75.4 %reduce-scatter.36.cloned.1.call-done = f32[256,1024]{1,0:T(8,128)} async-done(((f32[1024,1024]{1,0:T(8,128)}), f32[256,1024]{1,0:T(8,128)}) %reduce-scatter.36.cloned.1.call-update) | async-done | bytes 1048592 | tf_op jit(solution)/shard_map/reduce_scatter | solution.py:66
  1257.0 46.5 %all-gather.35.cloned.1.call-done = bf16[1024,1024]{1,0:T(8,128)(2,1)} async-done(((bf16[256,1024]{1,0:T(8,128)(2,1)}), bf16[1024,1024]{1,0:T(8,128)(2,1)}) %all-gather.35.cloned.1.call-update) | async-done | bytes 2097168 | tf_op jit(solution)/shard_map/all_gather | solution.py:62
  1303.5 8.5 fusion.162
  1313.4 4.3 fusion.104
  1317.8 75.6 %reduce-scatter.38.cloned.1.call-done = f32[256,1024]{1,0:T(8,128)} async-done(((f32[1024,1024]{1,0:T(8,128)}), f32[256,1024]{1,0:T(8,128)}) %reduce-scatter.38.cloned.1.call-update) | async-done | bytes 1048592 | tf_op jit(solution)/shard_map/reduce_scatter | solution.py:66
  1400.9 5.9 fusion.168
  1408.5 5.9 fusion.167
  1416.1 5.9 fusion.117
  1423.6 5.9 fusion.114
  1435.0 10.3 all-gather.37.cloned.1.call-done
  1454.7 24.1 %while.61 = (s32[]{:T(128)}, f32[1024,4,64]{0,2,1:T(8,128)S(1)}, f32[1024,4,64]{0,2,1:T(8,128)S(1)}, f32[2,512,4,64]{1,3,2,0:T(8,128)}, bf16[2,512,4,64]{1,3,2,0...) while((s32[]{:T(128)}, f32[1024,4,64]{0,2,1:T(8,128)S(1)}, ...), condition=%wide.region_44.46_spmd.clone, body=%wide.region_42.45_spmd.clone.sunk | while | flops 1365112832 | bytes 81864960 | solution.py:142
  1491.7 5.1 fusion.84
  1500.3 5.4 fusion.86
  1505.8 3.8 convolution_bitcast_fusion
  1509.6 75.0 %reduce-scatter.62.cloned.1.call-done = f32[128,2]{1,0:T(8,128)} async-done(((f32[4096,2]{1,0:T(8,128)}), f32[128,2]{1,0:T(8,128)}) %reduce-scatter.62.cloned.1.call-update) | async-done | bytes 1040
  1586.0 51.5 %reduce-scatter.56.cloned.1.call-done = f32[1024,128]{1,0:T(8,128)} async-done(((f32[1024,1024]{1,0:T(8,128)}), f32[1024,128]{1,0:T(8,128)}) %reduce-scatter.56.cloned.1.call-update) | async-done | bytes 524304 | tf_op jit(solution)/shard_map/reduce_scatter | solution.py:422
  1637.5 54.9 %reduce-scatter.54.cloned.1.call-done = f32[1024,128]{1,0:T(8,128)} async-done(((f32[1024,1024]{1,0:T(8,128)}), f32[1024,128]{1,0:T(8,128)}) %reduce-scatter.54.cloned.1.call-update) | async-done | bytes 524304 | tf_op jit(solution)/shard_map/reduce_scatter | solution.py:422
  1694.7 52.4 %reduce-scatter.52.cloned.1.call-done = f32[128,1024]{1,0:T(8,128)} async-done(((f32[1024,1024]{1,0:T(8,128)}), f32[128,1024]{1,0:T(8,128)}) %reduce-scatter.52.cloned.1.call-update) | async-done | bytes 524304 | tf_op jit(solution)/shard_map/reduce_scatter | solution.py:421
  1747.2 54.9 %reduce-scatter.50.cloned.1.call-done = f32[128,1024]{1,0:T(8,128)} async-done(((f32[1024,1024]{1,0:T(8,128)}), f32[128,1024]{1,0:T(8,128)}) %reduce-scatter.50.cloned.1.call-update) | async-done | bytes 524304 | tf_op jit(solution)/shard_map/reduce_scatter | solution.py:421
  1804.4 133.9 %reduce-scatter.58.cloned.1.call-done = f32[32,4]{1,0:T(8,128)} async-done(((f32[1024,4]{1,0:T(8,128)}), f32[32,4]{1,0:T(8,128)}) %reduce-scatter.58.cloned.1.call-update) | async-done | bytes 528
  1939.7 131.6 %reduce-scatter.60.cloned.1.call-done = f32[32,12]{1,0:T(8,128)} async-done(((f32[1024,12]{1,0:T(8,128)}), f32[32,12]{1,0:T(8,128)}) %reduce-scatter.60.cloned.1.call-update) | async-done | bytes 1552
  2072.8 34.5 %reduce-scatter.48.cloned.1.call-done = f32[256,128]{1,0:T(8,128)} async-done(((f32[256,1024]{1,0:T(8,128)}), f32[256,128]{1,0:T(8,128)}) %reduce-scatter.48.cloned.1.call-update) | async-done | bytes 131088 | tf_op jit(solution)/shard_map/reduce_scatter | solution.py:420
  2107.3 39.1 %reduce-scatter.46.cloned.1.call-done = f32[256,128]{1,0:T(8,128)} async-done(((f32[256,1024]{1,0:T(8,128)}), f32[256,128]{1,0:T(8,128)}) %reduce-scatter.46.cloned.1.call-update) | async-done | bytes 131088 | tf_op jit(solution)/shard_map/reduce_scatter | solution.py:420
  2148.0 47.9 %reduce-scatter.44.cloned.1.call-done = f32[128,3,256]{2,0,1:T(8,128)} async-done(((f32[1024,3,256]{2,0,1:T(8,128)}), f32[128,3,256]{2,0,1:T(8,128)}) %reduce-scatter.44.cloned.1.call-update) | async-done | bytes 393232 | tf_op jit(solution)/shard_map/reduce_scatter | solution.py:419
  2196.0 50.0 %reduce-scatter.42.cloned.1.call-done = f32[128,3,256]{2,0,1:T(8,128)} async-done(((f32[1024,3,256]{2,0,1:T(8,128)}), f32[128,3,256]{2,0,1:T(8,128)}) %reduce-scatter.42.cloned.1.call-update) | async-done | bytes 393232 | tf_op jit(solution)/shard_map/reduce_scatter | solution.py:419
  2248.1 76.9 %reduce-scatter.40.cloned.1.call-done = f32[256,1024]{1,0:T(8,128)} async-done(((f32[1024,1024]{1,0:T(8,128)}), f32[256,1024]{1,0:T(8,128)}) %reduce-scatter.40.cloned.1.call-update) | async-done | bytes 1048592 | tf_op jit(solution)/shard_map/reduce_scatter | solution.py:66
  (498 shorter events, 213.1 us)
Async XLA Ops:
  23.4 54.8 %all-to-all-start = ((bf16[4,256,1024]{2,1,0:T(8,128)(2,1)}), bf16[4,256,1024]{2,1,0:T(8,128)(2,1)}, u32[]{:S(2)}, u32[]{:S(2)}) async-start(bf16[4,256,1024]{2,1,0:T(8,128)(2,1)} %bitcast.348), calls=%async_computation | async-start | bytes 4194304 | tf_op jit(solution)/shard_map/all_to_all | solution.py:340
  29.9 174.7 %all-gather.39.cloned.1.call-start = ((), (), s32[]{:S(2)}) async-start(), calls=%async_computation.45 | async-start | bytes 1769472 | tf_op jit(solution)/shard_map/all_gather | solution.py:350
  30.7 176.5 %all-gather.23.cloned.1.call-start = ((), (), s32[]{:S(2)}) async-start(), calls=%async_computation.21 | async-start | bytes 2621440 | tf_op jit(solution)/shard_map/all_gather | solution.py:54
  81.2 277.8 %reduce-scatter.26.cloned.1.call-start = ((), (), s32[]{:S(2)}) async-start(), calls=%async_computation.22 | async-start | bytes 5242880 | tf_op jit(solution)/shard_map/reduce_scatter | solution.py:58
  81.4 129.6 %copy-start.25 = (bf16[2,512,4,64]{1,3,2,0:T(8,128)(2,1)}, bf16[2,512,4,64]{1,3,2,0:T(8,128)(2,1)S(1)}, u32[]{:S(2)}) copy-start(bf16[2,512,4,64]{1,3,2,0:T(8,128)(2,1)S(1)} %fusion.155) | copy-start | bytes 1572868
  233.8 194.5 %all-gather.41.cloned.1.call-start = ((), (), s32[]{:S(2)}) async-start(), calls=%async_computation.46 | async-start | bytes 2359296 | tf_op jit(solution)/shard_map/all_gather | solution.py:352
  235.7 192.7 %all-gather.25.cloned.1.call-start = ((), (), s32[]{:S(2)}) async-start(), calls=%async_computation.23 | async-start | bytes 2621440 | tf_op jit(solution)/shard_map/all_gather | solution.py:54
  359.0 164.9 %copy-start.50 = (f32[1024]{0:T(1024)}, f32[1024]{0:T(1024)S(1)}, u32[]{:S(2)}) copy-start(f32[1024]{0:T(1024)S(1)} %get-tuple-element.587) | copy-start | bytes 12292
  359.0 344.3 %copy-start.52 = (f32[1024]{0:T(1024)}, f32[1024]{0:T(1024)S(1)}, u32[]{:S(2)}) copy-start(f32[1024]{0:T(1024)S(1)} %get-tuple-element.586) | copy-start | bytes 12292
  360.4 163.4 %copy-start.5 = (f32[256,1024]{1,0:T(8,128)}, f32[256,1024]{1,0:T(8,128)S(1)}, u32[]{:S(2)}) copy-start(f32[256,1024]{1,0:T(8,128)S(1)} %get-tuple-element.704) | copy-start | bytes 3145732
  360.5 163.4 %copy-start.56 = (f32[256]{0:T(256)}, f32[256]{0:T(256)S(1)}, u32[]{:S(2)}) copy-start(f32[256]{0:T(256)S(1)} %broadcast_multiply_fusion.3) | copy-start | bytes 3076
  360.7 163.1 %copy-start.60 = (f32[256]{0:T(256)}, f32[256]{0:T(256)S(1)}, u32[]{:S(2)}) copy-start(f32[256]{0:T(256)S(1)} %fusion.132) | copy-start | bytes 3076
  361.8 81.4 %all-gather.43.cloned.1.call-start = ((), (), s32[]{:S(2)}) async-start(), calls=%async_computation.47 | async-start | bytes 2359296 | tf_op jit(solution)/shard_map/all_gather | solution.py:353
  362.7 161.1 %reduce-scatter.28.cloned.1.call-start = ((), (), s32[]{:S(2)}) async-start(), calls=%async_computation.24 | async-start | bytes 5242880 | tf_op jit(solution)/shard_map/reduce_scatter | solution.py:58
  449.8 103.3 %all-gather.45.cloned.1.call-start = ((), (), s32[]{:S(2)}) async-start(), calls=%async_computation.48 | async-start | bytes 1769472 | tf_op jit(solution)/shard_map/all_gather | solution.py:350
  450.6 150.6 %all-gather.27.cloned.1.call-start = ((), (), s32[]{:S(2)}) async-start(), calls=%async_computation.25 | async-start | bytes 2621440 | tf_op jit(solution)/shard_map/all_gather | solution.py:54
  525.5 177.8 %copy-start.7 = (f32[256,1024]{1,0:T(8,128)}, f32[256,1024]{1,0:T(8,128)S(1)}, u32[]{:S(2)}) copy-start(f32[256,1024]{1,0:T(8,128)S(1)} %get-tuple-element.700) | copy-start | bytes 3145732
  525.5 177.8 %copy-start.58 = (f32[256]{0:T(256)}, f32[256]{0:T(256)S(1)}, u32[]{:S(2)}) copy-start(f32[256]{0:T(256)S(1)} %broadcast_multiply_fusion.2) | copy-start | bytes 3076
  525.8 177.5 %copy-start.62 = (f32[256]{0:T(256)}, f32[256]{0:T(256)S(1)}, u32[]{:S(2)}) copy-start(f32[256]{0:T(256)S(1)} %fusion.133) | copy-start | bytes 3076
  526.9 176.4 %reduce-scatter.30.cloned.1.call-start = ((), (), s32[]{:S(2)}) async-start(), calls=%async_computation.26 | async-start | bytes 5242880 | tf_op jit(solution)/shard_map/reduce_scatter | solution.py:58
  627.6 75.7 %copy-start.66 = (f32[1024]{0:T(1024)S(1)}, f32[1024]{0:T(1024)}, u32[]{:S(2)}) copy-start(f32[1024]{0:T(1024)} %get-tuple-element.750) | copy-start | bytes 12292
  627.6 77.6 %copy-start.54 = (f32[1024]{0:T(1024)S(1)}, f32[1024]{0:T(1024)}, u32[]{:S(2)}) copy-start(f32[1024]{0:T(1024)} %get-tuple-element.751) | copy-start | bytes 12292
  627.7 106.7 %all-gather.47.cloned.1.call-start = ((), (), s32[]{:S(2)}) async-start(), calls=%async_computation.49 | async-start | bytes 2359296 | tf_op jit(solution)/shard_map/all_gather | solution.py:352
  628.4 154.0 %all-gather.29.cloned.1.call-start = ((), (), s32[]{:S(2)}) async-start(), calls=%async_computation.27 | async-start | bytes 2621440 | tf_op jit(solution)/shard_map/all_gather | solution.py:54
  706.3 105.1 %all-gather.49.cloned.1.call-start = ((), (), s32[]{:S(2)}) async-start(), calls=%async_computation.50 | async-start | bytes 2359296 | tf_op jit(solution)/shard_map/all_gather | solution.py:353
  707.1 226.4 %reduce-scatter.32.cloned.1.call-start = ((), (), s32[]{:S(2)}) async-start(), calls=%async_computation.28 | async-start | bytes 5242880 | tf_op jit(solution)/shard_map/reduce_scatter | solution.py:58
  817.9 115.6 %copy-start.65 = (f32[1024]{0:T(1024)S(1)}, f32[1024]{0:T(1024)}, u32[]{:S(2)}) copy-start(f32[1024]{0:T(1024)} %get-tuple-element.752) | copy-start | bytes 12292
  817.9 109.6 %all-to-all-start.1 = ((bf16[4,256,1024]{2,1,0:T(8,128)(2,1)}), bf16[4,256,1024]{2,1,0:T(8,128)(2,1)}, u32[]{:S(2)}, u32[]{:S(2)}) async-start(bf16[4,256,1024]{2,1,0:T(8,128)(2,1)} %bitcast.347), calls=%async_computation.5 | async-start | bytes 4194304 | tf_op jit(solution)/shard_map/all_to_all | solution.py:341
  822.5 112.9 %copy-start.55 = (f32[1024]{0:T(1024)S(1)}, f32[1024]{0:T(1024)}, u32[]{:S(2)}) copy-start(f32[1024]{0:T(1024)} %get-tuple-element.584) | copy-start | bytes 12292
  822.5 167.7 %all-gather.31.cloned.1.call-start = ((), (), s32[]{:S(2)}) async-start(), calls=%async_computation.29 | async-start | bytes 2621440 | tf_op jit(solution)/shard_map/all_gather | solution.py:62
  822.6 113.9 %copy-start.64 = (f32[1024]{0:T(1024)S(1)}, f32[1024]{0:T(1024)}, u32[]{:S(2)}) copy-start(f32[1024]{0:T(1024)} %get-tuple-element.753) | copy-start | bytes 12292
  940.4 140.2 %reduce-scatter.34.cloned.1.call-start = ((), (), s32[]{:S(2)}) async-start(), calls=%async_computation.30 | async-start | bytes 5242880 | tf_op jit(solution)/shard_map/reduce_scatter | solution.py:66
  1004.9 127.6 %all-gather.33.cloned.1.call-start = ((), (), s32[]{:S(2)}) async-start(), calls=%async_computation.31 | async-start | bytes 2621440 | tf_op jit(solution)/shard_map/all_gather | solution.py:62
  1085.9 166.6 %reduce-scatter.36.cloned.1.call-start = ((), (), s32[]{:S(2)}) async-start(), calls=%async_computation.32 | async-start | bytes 5242880 | tf_op jit(solution)/shard_map/reduce_scatter | solution.py:66
  1176.8 75.7 %copy-start.8 = (f32[256,1024]{1,0:T(8,128)S(1)}, f32[256,1024]{1,0:T(8,128)}, u32[]{:S(2)}) copy-start(f32[256,1024]{1,0:T(8,128)} %copy-done.7) | copy-start | bytes 3145732
  1176.8 75.7 %copy-start.18 = (f32[256,1024]{1,0:T(8,128)S(1)}, f32[256,1024]{1,0:T(8,128)}, u32[]{:S(2)}) copy-start(f32[256,1024]{1,0:T(8,128)} %copy-done.17) | copy-start | bytes 3145732
  1176.8 75.7 %copy-start.53 = (f32[1024]{0:T(1024)S(1)}, f32[1024]{0:T(1024)}, u32[]{:S(2)}) copy-start(f32[1024]{0:T(1024)} %copy-done.52) | copy-start | bytes 12292
  1176.8 75.7 %copy-start.59 = (f32[256]{0:T(256)S(1)}, f32[256]{0:T(256)}, u32[]{:S(2)}) copy-start(f32[256]{0:T(256)} %copy-done.58) | copy-start | bytes 3076
  1176.8 75.7 %copy-start.63 = (f32[256]{0:T(256)S(1)}, f32[256]{0:T(256)}, u32[]{:S(2)}) copy-start(f32[256]{0:T(256)} %copy-done.62) | copy-start | bytes 3076
  1176.9 75.7 %copy-start.84 = (f32[256]{0:T(256)S(1)}, f32[256]{0:T(256)}, u32[]{:S(2)}) copy-start(f32[256]{0:T(256)} %copy-done.83) | copy-start | bytes 3076
  1176.9 78.1 %copy-start.82 = (f32[256]{0:T(256)S(1)}, f32[256]{0:T(256)}, u32[]{:S(2)}) copy-start(f32[256]{0:T(256)} %copy-done.81) | copy-start | bytes 3076
  1176.9 126.6 %copy-start.87 = (f32[1,1024]{1,0:T(1,128)S(1)}, f32[1,1024]{1,0:T(1,128)}, u32[]{:S(2)}) copy-start(f32[1,1024]{1,0:T(1,128)} %copy-done.86) | copy-start | bytes 12292
  1176.9 126.6 %all-gather.35.cloned.1.call-start = ((), (), s32[]{:S(2)}) async-start(), calls=%async_computation.33 | async-start | bytes 2621440 | tf_op jit(solution)/shard_map/all_gather | solution.py:62
  1256.9 136.4 %reduce-scatter.38.cloned.1.call-start = ((), (), s32[]{:S(2)}) async-start(), calls=%async_computation.34 | async-start | bytes 5242880 | tf_op jit(solution)/shard_map/reduce_scatter | solution.py:66
  1317.7 75.7 %copy-start.57 = (f32[256]{0:T(256)S(1)}, f32[256]{0:T(256)}, u32[]{:S(2)}) copy-start(f32[256]{0:T(256)} %copy-done.56) | copy-start | bytes 3076
  1317.7 75.7 %copy-start.61 = (f32[256]{0:T(256)S(1)}, f32[256]{0:T(256)}, u32[]{:S(2)}) copy-start(f32[256]{0:T(256)} %copy-done.60) | copy-start | bytes 3076
  1317.7 78.0 %copy-start.80 = (f32[256]{0:T(256)S(1)}, f32[256]{0:T(256)}, u32[]{:S(2)}) copy-start(f32[256]{0:T(256)} %copy-done.79) | copy-start | bytes 3076
  1317.7 81.0 %copy-start.88 = (f32[1024]{0:T(1024)S(1)}, f32[1024]{0:T(1024)}, u32[]{:S(2)}) copy-start(f32[1024]{0:T(1024)} %get-tuple-element.773) | copy-start | bytes 12292
  1317.7 127.6 %all-gather.37.cloned.1.call-start = ((), (), s32[]{:S(2)}) async-start(), calls=%async_computation.35 | async-start | bytes 2621440 | tf_op jit(solution)/shard_map/all_gather | solution.py:62
  1398.7 185.9 %reduce-scatter.62.cloned.1.call-start = ((), (), s32[]{:S(2)}) async-start(), calls=%async_computation.53 | async-start | bytes 2162688
  1400.9 236.7 %reduce-scatter.56.cloned.1.call-start = ((), (), s32[]{:S(2)}) async-start(), calls=%async_computation.44 | async-start | bytes 4718592 | tf_op jit(solution)/shard_map/reduce_scatter | solution.py:422
  1406.9 285.6 %reduce-scatter.54.cloned.1.call-start = ((), (), s32[]{:S(2)}) async-start(), calls=%async_computation.43 | async-start | bytes 4718592 | tf_op jit(solution)/shard_map/reduce_scatter | solution.py:422
  1414.5 332.7 %reduce-scatter.52.cloned.1.call-start = ((), (), s32[]{:S(2)}) async-start(), calls=%async_computation.42 | async-start | bytes 4718592 | tf_op jit(solution)/shard_map/reduce_scatter | solution.py:421
  1422.0 380.1 %reduce-scatter.50.cloned.1.call-start = ((), (), s32[]{:S(2)}) async-start(), calls=%async_computation.41 | async-start | bytes 4718592 | tf_op jit(solution)/shard_map/reduce_scatter | solution.py:421
  1429.6 508.7 %reduce-scatter.58.cloned.1.call-start = ((), (), s32[]{:S(2)}) async-start(), calls=%async_computation.51 | async-start | bytes 540672
  1434.5 636.8 %reduce-scatter.60.cloned.1.call-start = ((), (), s32[]{:S(2)}) async-start(), calls=%async_computation.52 | async-start | bytes 540672
  1484.6 622.7 %reduce-scatter.48.cloned.1.call-start = ((), (), s32[]{:S(2)}) async-start(), calls=%async_computation.40 | async-start | bytes 1179648 | tf_op jit(solution)/shard_map/reduce_scatter | solution.py:420
  1488.1 658.3 %reduce-scatter.46.cloned.1.call-start = ((), (), s32[]{:S(2)}) async-start(), calls=%async_computation.39 | async-start | bytes 1179648 | tf_op jit(solution)/shard_map/reduce_scatter | solution.py:420
  1491.5 704.5 %reduce-scatter.44.cloned.1.call-start = ((), (), s32[]{:S(2)}) async-start(), calls=%async_computation.38 | async-start | bytes 3538944 | tf_op jit(solution)/shard_map/reduce_scatter | solution.py:419
  1496.9 749.1 %reduce-scatter.42.cloned.1.call-start = ((), (), s32[]{:S(2)}) async-start(), calls=%async_computation.37 | async-start | bytes 3538944 | tf_op jit(solution)/shard_map/reduce_scatter | solution.py:419
  1505.7 819.2 %reduce-scatter.40.cloned.1.call-start = ((), (), s32[]{:S(2)}) async-start(), calls=%async_computation.36 | async-start | bytes 5242880 | tf_op jit(solution)/shard_map/reduce_scatter | solution.py:66
  1509.6 815.4 %copy-start.16 = (f32[256,1024]{1,0:T(8,128)S(1)}, f32[256,1024]{1,0:T(8,128)}, u32[]{:S(2)}) copy-start(f32[256,1024]{1,0:T(8,128)} %copy-done.15) | copy-start | bytes 3145732
  1509.6 815.3 %copy-start.78 = (f32[256]{0:T(256)S(1)}, f32[256]{0:T(256)}, u32[]{:S(2)}) copy-start(f32[256]{0:T(256)} %copy-done.77) | copy-start | bytes 3076
  1692.4 634.9 %copy-start.1 = (bf16[256,1024]{1,0:T(8,128)(2,1)S(1)}, bf16[256,1024]{1,0:T(8,128)(2,1)}, u32[]{:S(2)}) copy-start(bf16[256,1024]{1,0:T(8,128)(2,1)} %param.22) | copy-start | bytes 1572868
  (78 other events, 875.6 us)
Sparse Core Ops, SparseCore 0:
  33.2 27.1 all-gather.38
  81.3 55.9 all-gather.22
  234.0 95.4 reduce-scatter.25
  332.0 27.8 all-gather.40
  362.0 46.2 all-gather.24
  410.2 26.9 all-gather.42
  449.9 73.8 reduce-scatter.27
  525.8 27.2 all-gather.44
  555.2 45.9 all-gather.26
  627.8 75.4 reduce-scatter.29
  705.9 28.3 all-gather.46
  736.4 45.9 all-gather.28
  784.4 26.8 all-gather.48
  818.0 115.4 reduce-scatter.31
  940.5 49.6 all-gather.30
  1005.0 75.4 reduce-scatter.33
  1086.0 46.4 all-gather.32
  1177.0 75.4 reduce-scatter.35
  1257.1 46.4 all-gather.34
  1317.8 75.4 reduce-scatter.37
  1398.8 46.4 all-gather.36
  1447.6 136.8 reduce-scatter.61
  1587.9 49.5 reduce-scatter.55
  1641.1 51.2 reduce-scatter.53
  1695.8 51.3 reduce-scatter.51
  1750.7 51.3 reduce-scatter.49
  1804.2 134.0 reduce-scatter.57
  1940.6 130.7 reduce-scatter.59
  2074.5 32.7 reduce-scatter.47
  2110.3 35.9 reduce-scatter.45
  2149.7 46.1 reduce-scatter.43
  2199.7 46.2 reduce-scatter.41
  2248.1 76.7 reduce-scatter.39
where the time goes:
time: 2340 us; the launch traced here: 2330 us
  waiting for transfers between devices  1640 us (70%)
  blocking collectives  269 us (11%)
  matrix products  196 us (8%)
  local copies, waits for them, and re-layouts  132 us (6%)
  other arithmetic  70.2 us (3%)
    unnamed x36, waiting for transfers between devices  343 us
    reduce_scatter x4, waiting for transfers between devices, sum_grads(): lax.psum_scatter(partial_term, 'tensor', scatter_dimension=0, tiled=True)  303 us
    all_gather x4, waiting for transfers between devices, gather_grads(): return lax.all_gather(local_part, 'tensor', axis=0, tiled=True)  153 us
    reduce_scatter x4, waiting for transfers between devices, sum_rows(): lax.psum_scatter(partial_term, 'tensor', scatter_dimension=0, tiled=True)  152 us
    reduce_scatter x2, waiting for transfers between devices, body(): lax.psum_scatter(weight_terms[2], 'dp', scatter_dimension=0, tiled=True)  107 us
    reduce_scatter x2, waiting for transfers between devices, body(): lax.psum_scatter(weight_terms[3], 'dp', scatter_dimension=1, tiled=True)  106 us
    all_to_all x1, waiting for transfers between devices, body(): lax.all_to_all(cot_send, 'tensor', split_axis=0, concat_axis=0, tiled=True)  105 us
    reduce_scatter x2, waiting for transfers between devices, body(): lax.psum_scatter(weight_terms[0], 'dp', scatter_dimension=0, tiled=True)  97.9 us
  transfers between devices with their start and end apart: 35, of which 29 were waited for; matrix products, arithmetic and copies ran while one was open for 9% of the time, Pallas kernels for 0%

commit v1 on v0

v1 whole, which is shorter than its diff:
```python
import jax
import jax.numpy as jnp
import numpy as np
from jax import lax
from jax.sharding import Mesh, PartitionSpec as P

D = 1024
HEAD_DIM = 64
FF = 4096
LAYERS = 2
SEQ_GRP = 3

EPS = 1e-05
NEG = -1e30
ALL = ("d", "c", "zh", "zl")
SWAP = [(0, 1), (1, 0)]
bf16 = jnp.bfloat16
f32 = jnp.float32


def dot(a, b, ca, cb):
    return lax.dot_general(a, b, (((ca,), (cb,)), ((), ())), preferred_element_type=f32)


def swap(a, axis):
    return lax.ppermute(a, axis, SWAP)


def flip_d(a, bit, n_d):
    return lax.ppermute(a, "d", [(i, i ^ (1 << bit)) for i in range(n_d)])


def transpose_home(a):
    return lax.ppermute(a, ("c", "zh"), [(0, 0), (1, 2), (2, 1), (3, 3)])


def norm_parts(v):
    centred = v - jnp.mean(v, axis=-1, keepdims=True)
    r = lax.rsqrt(jnp.mean(centred * centred, axis=-1, keepdims=True) + EPS)
    return centred * r, r


def norm_back(n, r, gain, d_out):
    dn = d_out * gain
    dv = r * (
        dn - jnp.mean(dn, axis=-1, keepdims=True) - n * jnp.mean(dn * n, axis=-1, keepdims=True)
    )
    return dv, jnp.sum(d_out * n, axis=0), jnp.sum(d_out, axis=0)


def group_maps(own_len, dealt_local, group_rows):
    slot_range = jnp.arange(SEQ_GRP, dtype=jnp.int32)
    own_end = jnp.cumsum(own_len)
    own_start = own_end - own_len
    pick_table = dealt_local[:, None] == slot_range[None, :]
    dealt_len = jnp.sum(jnp.where(pick_table, own_len[None, :], 0), axis=1)
    dealt_src = jnp.sum(jnp.where(pick_table, own_start[None, :], 0), axis=1)
    dealt_end = jnp.cumsum(dealt_len)
    dealt_begin = dealt_end - dealt_len
    position = jnp.arange(group_rows, dtype=jnp.int32)
    segments = jnp.sum((position[:, None] >= dealt_end[None, :]).astype(jnp.int32), axis=1)
    seg_hit = segments[:, None] == slot_range[None, :]
    source = jnp.sum(
        jnp.where(seg_hit, dealt_src[None, :] - dealt_begin[None, :] + position[:, None], 0), axis=1
    ) + jnp.where(segments == SEQ_GRP, position, 0)
    return (segments, source)


def share_rows(own):
    far = swap(own, "zl")
    near = swap(own, "c")
    far_near = swap(far, "c")
    return own, near, far, far_near


def sum_rows(near_part, far_part, rows):
    far_own, far_near = far_part[:rows], far_part[rows:]
    chip_sum = far_own + swap(far_near.astype(bf16), "c").astype(f32)
    crossed = swap(chip_sum.astype(bf16), "zl")
    other = swap(near_part[rows:].astype(bf16), "c")
    return near_part[:rows] + other.astype(f32) + crossed.astype(f32)


def gather_weights(piece, pos, n_d):
    d, c, zh, _ = pos
    bits = list(range(n_d.bit_length() - 1))
    crossed = swap(piece, "zh")
    same = c == zh
    keep = jnp.where(same, piece, crossed)
    send = jnp.where(same, crossed, piece)
    recv = swap(send, "c")
    found = {}
    for start, order, core in ((keep, bits, c), (recv, bits[::-1], 1 - c)):
        cur, masks = start[None], [0]
        for bit in order:
            cur = jnp.concatenate([cur, flip_d(cur, bit, n_d)], 0)
            masks = masks + [m ^ (1 << bit) for m in masks]
        found[len(found)] = (cur, masks)
    stacked = jnp.concatenate([found[0][0], found[1][0]], 0)
    place_one = {m: i for i, m in enumerate(found[0][1])}
    place_two = {m: i for i, m in enumerate(found[1][1])}
    table_one = jnp.array([place_one[m] for m in range(n_d)], jnp.int32)
    table_two = jnp.array([place_two[m] for m in range(n_d)], jnp.int32)
    blocks = []
    for dd in range(n_d):
        for cc in range(2):
            mask = jnp.bitwise_xor(d, dd)
            at = jnp.where(c == cc, table_one[mask], n_d + table_two[mask])
            blocks.append(lax.dynamic_index_in_dim(stacked, at, 0, keepdims=False))
    return jnp.concatenate(blocks, 0)


def pick(a, bit_value, axis):
    return lax.dynamic_index_in_dim(a, bit_value, axis, keepdims=False)


def reduce_weights(grad, pos, n_d):
    d, c, zh, _ = pos
    bits = list(range(n_d.bit_length() - 1))
    rows, cols = grad.shape[0] // (2 * n_d), grad.shape[1]
    view = grad.reshape(n_d, 2, rows, cols)
    sums = []
    for core, order in ((c, bits[::-1]), (1 - c, bits)):
        cur = pick(view, core, 1).reshape((2,) * len(bits) + (rows, cols))
        left = list(reversed(bits))
        for bit in order:
            axis = left.index(bit)
            mine = jnp.bitwise_and(jnp.right_shift(d, bit), 1)
            send = pick(cur, 1 - mine, axis).astype(bf16)
            cur = pick(cur, mine, axis).astype(f32) + flip_d(send, bit, n_d).astype(f32)
            left.remove(bit)
        sums.append(cur)
    first, second = sums
    other = swap(second.astype(bf16), "c").astype(f32)
    same = c == zh
    keep = jnp.where(same, first, other)
    send = jnp.where(same, other, first)
    return keep + swap(send.astype(bf16), "zh").astype(f32)


def gather_small(own, pos, n_d):
    d, c, zh, zl = pos
    cur = own[None]
    for axis, me in (("zl", zl), ("zh", zh), ("c", c)):
        got = swap(cur, axis)
        cur = jnp.where(me == 0, jnp.concatenate([cur, got]), jnp.concatenate([got, cur]))
    for bit in range(n_d.bit_length() - 1):
        got = flip_d(cur, bit, n_d)
        mine = jnp.bitwise_and(jnp.right_shift(d, bit), 1)
        cur = jnp.where(mine == 0, jnp.concatenate([cur, got]), jnp.concatenate([got, cur]))
    return cur


def reduce_small(full, pos, n_d):
    d, c, zh, zl = pos
    cur = full
    for bit in reversed(range(n_d.bit_length() - 1)):
        mine = jnp.bitwise_and(jnp.right_shift(d, bit), 1)
        view = cur.reshape(2, -1, full.shape[1])
        cur = pick(view, mine, 0) + flip_d(pick(view, 1 - mine, 0), bit, n_d)
    for axis, me in (("c", c), ("zh", zh), ("zl", zl)):
        view = cur.reshape(2, -1, full.shape[1])
        cur = pick(view, me, 0) + swap(pick(view, 1 - me, 0), axis)
    return cur[0]


def heads_of(a, heads):
    return a.reshape(a.shape[0], heads, HEAD_DIM)


def attend(queries, keys, values, seg_q, seg_k, scale):
    scores = jnp.einsum("bhd,khd->hbk", queries, keys, preferred_element_type=f32) * scale
    masked = jnp.where((seg_q[:, None] == seg_k[None, :])[None], scores, NEG)
    peak = jnp.max(masked, axis=2, keepdims=True)
    exponent = jnp.exp(masked - peak)
    total = jnp.sum(exponent, axis=2, keepdims=True)
    probs = (exponent / total).astype(bf16)
    out = jnp.einsum("hbk,khd->bhd", probs, values, preferred_element_type=f32)
    return out.reshape(queries.shape[0], -1).astype(bf16), peak, total


def attend_back(queries, keys, values, seg_q, seg_k, peak, total, grad, scale):
    scores = jnp.einsum("bhd,khd->hbk", queries, keys, preferred_element_type=f32) * scale
    masked = jnp.where((seg_q[:, None] == seg_k[None, :])[None], scores, NEG)
    probs = jnp.exp(masked - peak) / total
    d_probs = jnp.einsum("bhd,khd->hbk", grad, values, preferred_element_type=f32)
    d_scores = probs * (d_probs - jnp.sum(probs * d_probs, axis=2, keepdims=True))
    low = d_scores.astype(bf16)
    d_q = jnp.einsum("hbk,khd->bhd", low, keys, preferred_element_type=f32) * scale
    d_k = jnp.einsum("hbk,bhd->khd", low, queries, preferred_element_type=f32) * scale
    d_v = jnp.einsum("hbk,bhd->khd", probs.astype(bf16), grad, preferred_element_type=f32)
    return d_q, d_k, d_v


def gelu(u):
    return jax.nn.gelu(u, approximate=False)


def body(tokens, cotangent, lengths, order, w_qkv, w_out, w_up, w_down, gains, biases, up_bias):
    rows = tokens.shape[0]
    n_d = lax.axis_size("d")
    n_dev = n_d * 8
    tensor_count = 4
    head_width = D // tensor_count
    heads = head_width // HEAD_DIM
    ff_width = FF // tensor_count
    piece = D // (2 * n_d)
    scale = HEAD_DIM ** (-0.5)
    d, c, zh, zl = (lax.axis_index(a) for a in ALL)
    pos = (d, c, zh, zl)
    slot = 2 * c + zl
    block_ids = [jnp.bitwise_xor(slot, m) for m in (0, 2, 1, 3)]

    def chunk(layer, which):
        if which == 0:
            return jnp.concatenate([w_qkv[layer].reshape(piece, -1), w_out[layer].T], 1)
        return w_up[layer] if which == 1 else w_down[layer].T

    raw = transpose_home(tokens)
    small_all = gather_small(
        jnp.concatenate([gains.reshape(-1), biases.reshape(-1), up_bias.reshape(-1)]), pos, n_d
    )
    weights = [[gather_weights(chunk(l, k), pos, n_d) for k in range(3)] for l in range(LAYERS)]
    width = D // n_dev
    up_width = FF // n_dev
    n_gain, n_bias = LAYERS * 2 * width, LAYERS * 6 * width
    gains_all = small_all[:, :n_gain].reshape(n_dev, LAYERS, 2, width)
    gains_all = gains_all.transpose(1, 2, 0, 3).reshape(LAYERS, 2, D)
    biases_all = small_all[:, n_gain : n_gain + n_bias].reshape(n_dev, LAYERS, 6, width)
    biases_all = biases_all.transpose(1, 2, 0, 3).reshape(LAYERS, 6, D)
    upb_all = small_all[:, n_gain + n_bias :].reshape(n_dev, LAYERS, up_width)
    upb_all = upb_all.transpose(1, 0, 2).reshape(LAYERS, FF)

    seq_base = (d * 2 + zh) * SEQ_GRP
    own_len = lax.dynamic_slice_in_dim(lengths, seq_base, SEQ_GRP)
    dealt_local = lax.dynamic_slice_in_dim(order, seq_base, SEQ_GRP) - seq_base
    segments, source = group_maps(own_len, dealt_local, 4 * rows)
    seg = jnp.concatenate([lax.dynamic_slice_in_dim(segments, b * rows, rows) for b in block_ids])
    src = jnp.concatenate([lax.dynamic_slice_in_dim(source, b * rows, rows) for b in block_ids])
    src_x = jnp.bitwise_xor(src // rows, slot)
    src_at = (2 * (src_x % 2) + src_x // 2) * rows + src % rows
    deal = (src_at[:, None] == jnp.arange(4 * rows, dtype=jnp.int32)[None, :]).astype(bf16)
    valid = (seg[:rows] < SEQ_GRP).astype(f32)[:, None]
    seg_near, seg_far = seg[: 2 * rows], seg[2 * rows :]

    raw_all = jnp.concatenate(share_rows(raw), 0)
    x_all = dot(deal, raw_all, 1, 0).astype(bf16)
    hidden = x_all[:rows].astype(f32)
    blocks = tuple(x_all[i * rows : (i + 1) * rows] for i in range(4))

    kept = []
    for layer in range(LAYERS):
        w_att, w_u, w_dt = weights[layer]
        w_q, w_o = w_att[:, : 3 * head_width], w_att[:, 3 * head_width :]
        bias_rows = biases_all[layer]
        q_bias = lax.dynamic_slice_in_dim(bias_rows[0], slot * head_width, head_width)
        v_bias = lax.dynamic_slice_in_dim(bias_rows[1], slot * head_width, head_width)
        u_bias = lax.dynamic_slice_in_dim(upb_all[layer], slot * ff_width, ff_width)
        add = jnp.concatenate([q_bias, jnp.zeros((head_width,), f32), v_bias])
        x_near = jnp.concatenate(blocks[:2], 0)
        x_far = jnp.concatenate(blocks[2:], 0)
        proj_near = (dot(x_near, w_q, 1, 0) + add).astype(bf16)
        proj_far = (dot(x_far, w_q, 1, 0) + add).astype(bf16)
        proj = jnp.concatenate([proj_near, proj_far], 0)
        q, k, v = (heads_of(proj[:, i * head_width : (i + 1) * head_width], heads) for i in range(3))
        att_far, peak_far, total_far = attend(q[2 * rows :], k, v, seg_far, seg, scale)
        far_part = dot(att_far, w_o, 1, 1)
        att_near, peak_near, total_near = attend(q[: 2 * rows], k, v, seg_near, seg, scale)
        near_part = dot(att_near, w_o, 1, 1)
        pre_one = hidden + sum_rows(near_part, far_part, rows) + bias_rows[2]
        n_one, r_one = norm_parts(pre_one)
        normed = n_one * gains_all[layer, 0] + bias_rows[3]
        n_blocks = share_rows(normed.astype(bf16))
        n_near = jnp.concatenate(n_blocks[:2], 0)
        n_far = jnp.concatenate(n_blocks[2:], 0)
        up_near = dot(n_near, w_u, 1, 0) + u_bias
        up_far = dot(n_far, w_u, 1, 0) + u_bias
        act_far = gelu(up_far).astype(bf16)
        far_part = dot(act_far, w_dt, 1, 1)
        act_near = gelu(up_near).astype(bf16)
        near_part = dot(act_near, w_dt, 1, 1)
        pre_two = normed + sum_rows(near_part, far_part, rows) + bias_rows[4]
        n_two, r_two = norm_parts(pre_two)
        hidden = n_two * gains_all[layer, 1] + bias_rows[5]
        if layer + 1 < LAYERS:
            blocks = share_rows(hidden.astype(bf16))
        kept.append(
            dict(
                x=(x_near, x_far), q=q, k=k, v=v, soft=((peak_near, total_near), (peak_far, total_far)),
                att=(att_near, att_far), n_one=n_one, r_one=r_one, n=(n_near, n_far),
                up=(up_near, up_far), act=(act_near, act_far), n_two=n_two, r_two=r_two,
            )
        )
    mixed = transpose_home(hidden.astype(bf16))

    raw_cot = jnp.concatenate(share_rows(transpose_home(cotangent)), 0)
    grad_y = dot(deal[:rows], raw_cot, 1, 0) * valid
    reduced = [None] * LAYERS
    smalls = [None] * LAYERS
    for layer in reversed(range(LAYERS)):
        w_att, w_u, w_dt = weights[layer]
        w_q, w_o = w_att[:, : 3 * head_width], w_att[:, 3 * head_width :]
        s = kept[layer]
        d_two, g_gain2, g_shift2 = norm_back(s["n_two"], s["r_two"], gains_all[layer, 1], grad_y)
        g_downb = jnp.sum(d_two, axis=0)
        two = share_rows(d_two.astype(bf16))
        two_near = jnp.concatenate(two[:2], 0)
        two_far = jnp.concatenate(two[2:], 0)

        def up_back(two_part, up_part):
            d_act = dot(two_part, w_dt, 1, 0)
            _, back = jax.vjp(gelu, up_part)
            (d_up,) = back(d_act)
            return d_up.astype(bf16), jnp.sum(d_up, axis=0)

        up_far, sum_far = up_back(two_far, s["up"][1])
        far_part = dot(up_far, w_u, 1, 1)
        up_near, sum_near = up_back(two_near, s["up"][0])
        near_part = dot(up_near, w_u, 1, 1)
        g_upb = sum_far + sum_near
        d_normed = d_two + sum_rows(near_part, far_part, rows)
        d_one, g_gain1, g_shift1 = norm_back(s["n_one"], s["r_one"], gains_all[layer, 0], d_normed)
        g_outb = jnp.sum(d_one, axis=0)
        one = share_rows(d_one.astype(bf16))
        one_near = jnp.concatenate(one[:2], 0)
        one_far = jnp.concatenate(one[2:], 0)
        g_down = (dot(s["act"][0], two_near, 0, 0) + dot(s["act"][1], two_far, 0, 0)).T
        g_up = dot(s["n"][0], up_near, 0, 0) + dot(s["n"][1], up_far, 0, 0)
        d_att_far = heads_of(dot(one_far, w_o, 1, 0).astype(bf16), heads)
        d_att_near = heads_of(dot(one_near, w_o, 1, 0).astype(bf16), heads)
        q, k, v = s["q"], s["k"], s["v"]
        dq_far, dk_far, dv_far = attend_back(
            q[2 * rows :], k, v, seg_far, seg, *s["soft"][1], d_att_far, scale
        )
        dq_near, dk_near, dv_near = attend_back(
            q[: 2 * rows], k, v, seg_near, seg, *s["soft"][0], d_att_near, scale
        )
        d_q = jnp.concatenate([dq_near, dq_far], 0).reshape(4 * rows, head_width)
        d_k = (dk_far + dk_near).reshape(4 * rows, head_width)
        d_v = (dv_far + dv_near).reshape(4 * rows, head_width)
        g_qb, g_vb = jnp.sum(d_q, axis=0), jnp.sum(d_v, axis=0)
        d_proj = jnp.concatenate([d_q.astype(bf16), d_k.astype(bf16), d_v.astype(bf16)], 1)
        far_part = dot(d_proj[2 * rows :], w_q, 1, 1)
        near_part = dot(d_proj[: 2 * rows], w_q, 1, 1)
        grad_y = d_one + sum_rows(near_part, far_part, rows)
        g_qkv = dot(s["x"][0], d_proj[: 2 * rows], 0, 0) + dot(s["x"][1], d_proj[2 * rows :], 0, 0)
        g_out = dot(one_near, s["att"][0], 0, 0) + dot(one_far, s["att"][1], 0, 0)
        reduced[layer] = (
            reduce_weights(jnp.concatenate([g_qkv, g_out], 1).astype(bf16), pos, n_d),
            reduce_weights(g_up.astype(bf16), pos, n_d),
            reduce_weights(g_down.astype(bf16), pos, n_d),
        )
        place = lambda vec, full: lax.dynamic_update_slice_in_dim(
            jnp.zeros((full,), f32), vec, slot * vec.shape[0], 0
        )
        smalls[layer] = (
            jnp.stack([g_gain1, g_gain2]),
            jnp.stack([place(g_qb, D), place(g_vb, D), g_outb, g_shift1, g_downb, g_shift2]),
            place(g_upb, FF),
        )
    tokens_grad = transpose_home(grad_y.astype(bf16)).astype(f32)

    def by_device(a, per):
        return jnp.moveaxis(a.reshape(a.shape[:-1] + (n_dev, per)), -2, 0).reshape(n_dev, -1)

    small_terms = jnp.concatenate(
        [
            by_device(jnp.stack([s[0] for s in smalls]), width),
            by_device(jnp.stack([s[1] for s in smalls]), width),
            by_device(jnp.stack([s[2] for s in smalls]), up_width),
        ],
        1,
    )
    small_sum = reduce_small(small_terms, pos, n_d)
    g_gains = small_sum[:n_gain].reshape(LAYERS, 2, width)
    g_biases = small_sum[n_gain : n_gain + n_bias].reshape(LAYERS, 6, width)
    g_upb = small_sum[n_gain + n_bias :].reshape(LAYERS, up_width)
    g_qkv = jnp.stack([r[0][:, : 3 * head_width].reshape(piece, 3, head_width) for r in reduced])
    g_out = jnp.stack([r[0][:, 3 * head_width :].T for r in reduced])
    g_up = jnp.stack([r[1] for r in reduced])
    g_down = jnp.stack([r[2].T for r in reduced])
    return mixed, tokens_grad, g_qkv, g_out, g_up, g_down, g_gains, g_biases, g_upb


def solution(mesh):
    n_dp, n_t = mesh.shape["dp"], mesh.shape["tensor"]
    fine = Mesh(mesh.devices.reshape(n_dp // 2, 2, n_t // 2, 2), ALL)
    dp, t = ("d", "c"), ("zh", "zl")
    return jax.shard_map(
        body,
        mesh=fine,
        in_specs=(
            P(ALL, None),
            P(ALL, None),
            P(),
            P(),
            P(None, dp, None, t),
            P(None, t, dp),
            P(None, dp, t),
            P(None, t, dp),
            P(None, None, ALL),
            P(None, None, ALL),
            P(None, ALL),
        ),
        out_specs=(
            P(ALL, None),
            P(ALL, None),
            P(None, dp, None, t),
            P(None, t, dp),
            P(None, dp, t),
            P(None, t, dp),
            P(None, None, ALL),
            P(None, None, ALL),
            P(None, ALL),
        ),
        check_vma=False,
    )
```

time: 2340 us -> 891 us (0.38)
  waiting for transfers between devices: 1640 us -> 340 us
  blocking collectives: 269 us -> 0 us
  starting transfers between devices: 13.7 us -> 111 us
  other arithmetic: 70.2 us -> 93.7 us
    reduce_scatter x16 -> x0, waiting for transfers between devices: 841 us -> none  [the longest x4 303 us: sum_grads(): lax.psum_scatter(partial_term, 'tensor', scatter_dimension=0, tiled=True)]
    unnamed x36 -> x0, waiting for transfers between devices: 343 us -> none
    ppermute x0 -> x137, waiting for transfers between devices: none -> 340 us  [the longest x81 189 us: swap(): return lax.ppermute(a, axis, SWAP)]
    all_gather x14 -> x0, waiting for transfers between devices: 300 us -> none  [the longest x4 153 us: gather_grads(): return lax.all_gather(local_part, 'tensor', axis=0, tiled=True)]
    all_gather x5 -> x0, blocking collectives: 269 us -> none  [the longest x1 96.6 us: body(): lax.all_gather(gains, ('dp', 'tensor'), axis=2, tiled=True)]
    all_to_all x2 -> x0, waiting for transfers between devices: 152 us -> none  [the longest x1 105 us: body(): lax.all_to_all(cot_send, 'tensor', split_axis=0, concat_axis=0, tiled=True)]
    ppermute x0 -> x137, starting transfers between devices: none -> 111 us  [the longest x52 52.9 us: flip_d(): return lax.ppermute(a, 'd', [(i, i ^ 1 << bit) for i in range(n_d)])]
    slice x9 -> x43, local copies, waits for them, and re-layouts: 56.4 us -> 16.7 us  [the longest x8 5.62 us: sum_rows(): far_own, far_near = (far_part[:rows], far_part[rows:])]
  transfers between devices with their start and end apart: 35 -> 137, of which waited for: 29 -> 56; matrix products, arithmetic and copies ran while one was open for 9% -> 40% of each run, Pallas kernels for 0% -> 0%
where the time goes in v1:
time: 891 us; the launch traced here: 879 us
  waiting for transfers between devices  340 us (38%)
  matrix products  200 us (22%)
  local copies, waits for them, and re-layouts  126 us (14%)
  starting transfers between devices  111 us (12%)
  other arithmetic  93.7 us (11%)
    ppermute x81, waiting for transfers between devices, swap(): return lax.ppermute(a, axis, SWAP)  189 us
    ppermute x52, waiting for transfers between devices, flip_d(): return lax.ppermute(a, 'd', [(i, i ^ 1 << bit) for i in range(n_d)])  152 us
    dot_general x50, matrix products, dot(): lax.dot_general(a, b, (((ca,), (cb,)), ((), ())), preferred_element_type=...  115 us
    ppermute x52, starting transfers between devices, flip_d(): return lax.ppermute(a, 'd', [(i, i ^ 1 << bit) for i in range(n_d)])  52.9 us
    unnamed x479, local copies, waits for them, and re-layouts  46.6 us
    ppermute x81, starting transfers between devices, swap(): return lax.ppermute(a, axis, SWAP)  40.6 us
    dot_general x4, matrix products, attend_back(): jnp.einsum('bhd,khd->hbk', grad, values, preferred_element_type=f32)  24.9 us
    sub x4, matrix products, attend(): exponent = jnp.exp(masked - peak)  23.5 us
  transfers between devices with their start and end apart: 137, of which 56 were waited for; matrix products, arithmetic and copies ran while one was open for 40% of the time, Pallas kernels for 0%

profile of v1, /device:TPU:0, one launch (start us, length us, event | category | flops | bytes accessed | tf_op | source)
XLA Modules:
  0.0 878.6 jit_solution(10100751965909646066)
XLA Ops:
  22.2 33.2 %collective-permute-done.11 = f32[2,768]{1,0:T(2,128)S(1)} collective-permute-done((f32[2,768]{1,0:T(2,128)S(1)}, f32[2,768]{1,0:T(2,128)S(1)}, u32[]{:S(2)}, u32[]{:S(2)}) %collective-permute-start.11) | collective-permute-done | bytes 6176 | tf_op jit(solution)/shard_map/ppermute | solution.py:26
  86.2 7.5 collective-permute-done.49
  98.1 4.9 collective-permute-done.38
  104.6 4.0 collective-permute-done.26
  108.6 5.6 collective-permute-done.56
  120.8 3.2 collective-permute-done.23
  124.5 5.1 collective-permute-done.8
  131.8 3.5 collective-permute-done.41
  136.5 4.3 collective-permute-done.29
  141.6 4.9 collective-permute-done.59
  148.6 25.9 %collective-permute-done.53 = bf16[1,128,1024]{1,2,0:T(8,128)(2,1)S(1)} collective-permute-done((bf16[1,128,1024]{1,2,0:T(8,128)(2,1)S(1)}, bf16[1,128,1024]{1,2,0:T(8,128)(2,1)S(1)}, u32[]{:S(2)}, u32[]{:S(2)}) %collective-permute-start.53) | collective-permute-done | bytes 262176 | tf_op jit(solution)/shard_map/ppermute | solution.py:30
  174.6 5.6 collective-permute-start.67
  185.9 11.1 %collective-permute-done.27 = bf16[2,128,1024]{1,2,0:T(8,128)(2,1)S(1)} collective-permute-done((bf16[2,128,1024]{1,2,0:T(8,128)(2,1)S(1)}, bf16[2,128,1024]{1,2,0:T(8,128)(2,1)S(1)}, u32[]{:S(2)}, u32[]{:S(2)}) %collective-permute-start.27) | collective-permute-done | bytes 524320 | tf_op jit(solution)/shard_map/ppermute | solution.py:30
  198.7 9.5 %collective-permute-done.57 = bf16[2,128,1024]{1,2,0:T(8,128)(2,1)S(1)} collective-permute-done((bf16[2,128,1024]{1,2,0:T(8,128)(2,1)S(1)}, bf16[2,128,1024]{1,2,0:T(8,128)(2,1)S(1)}, u32[]{:S(2)}, u32[]{:S(2)}) %collective-permute-start.57) | collective-permute-done | bytes 524320 | tf_op jit(solution)/shard_map/ppermute | solution.py:30
  210.0 8.6 collective-permute-done.51
  230.0 6.0 fusion.339
  235.9 4.9 fusion.107
  244.0 6.4 fusion.340
  250.5 5.1 fusion.104
  263.8 9.7 %collective-permute-done.17 = bf16[256,1024]{1,0:T(8,128)(2,1)S(1)} collective-permute-done((bf16[256,1024]{1,0:T(8,128)(2,1)S(1)}, bf16[256,1024]{1,0:T(8,128)(2,1)S(1)}, u32[]{:S(2)}, u32[]{:S(2)}) %collective-permute-start.17) | collective-permute-done | bytes 524320 | tf_op jit(solution)/shard_map/ppermute | solution.py:26
  276.4 12.8 %collective-permute-done.32 = bf16[256,1024]{1,0:T(8,128)(2,1)S(1)} collective-permute-done((bf16[256,1024]{1,0:T(8,128)(2,1)S(1)}, bf16[256,1024]{1,0:T(8,128)(2,1)S(1)}, u32[]{:S(2)}, u32[]{:S(2)}) %collective-permute-start.32) | collective-permute-done | bytes 524320 | tf_op jit(solution)/shard_map/ppermute | solution.py:26
  292.5 13.2 %multiply_convert_fusion.7 = (bf16[512,1024]{1,0:T(8,128)(2,1)S(1)}, f32[512,1024]{1,0:T(8,128)}, bf16[512,1024]{1,0:T(8,128)(2,1)S(1)}, f32[512,1024]{1,0:T(8,128)}, f32[512,1024]{1,0:T(8,128)}) fusion(f32[1024]{0:T(1024)S(1)} %copy-done.165, f32[512,1024]{1,0:T(8,128)S(1)} %fusion.346, bf16[1024,1024]{0,1:T(8,128)(2,1)S(1)} %bitcast_dynamic-update-slice_fusion.32, ...), kind=kOutput, calls=%fused_computation.130 | convolution fusion | flops 1145044992 | bytes 13635584 | tf_op jit(solution)/shard_map/dot_general | solution.py:22
  312.5 12.3 %collective-permute-done.35 = bf16[256,1024]{1,0:T(8,128)(2,1)S(1)} collective-permute-done((bf16[256,1024]{1,0:T(8,128)(2,1)S(1)}, bf16[256,1024]{1,0:T(8,128)(2,1)S(1)}, u32[]{:S(2)}, u32[]{:S(2)}) %collective-permute-start.35) | collective-permute-done | bytes 524320 | tf_op jit(solution)/shard_map/ppermute | solution.py:26
  330.4 8.7 collective-permute-done.43
  345.4 5.8 fusion.341
  351.2 5.0 fusion.113
  360.5 5.3 fusion.342
  365.8 5.0 fusion.110
  375.2 13.1 %collective-permute-done.47 = bf16[256,1024]{1,0:T(8,128)(2,1)S(1)} collective-permute-done((bf16[256,1024]{1,0:T(8,128)(2,1)S(1)}, bf16[256,1024]{1,0:T(8,128)(2,1)S(1)}, u32[]{:S(2)}, u32[]{:S(2)}) %collective-permute-start.47) | collective-permute-done | bytes 524320 | tf_op jit(solution)/shard_map/ppermute | solution.py:26
  391.2 11.7 %collective-permute-done.62 = bf16[256,1024]{1,0:T(8,128)(2,1)S(1)} collective-permute-done((bf16[256,1024]{1,0:T(8,128)(2,1)S(1)}, bf16[256,1024]{1,0:T(8,128)(2,1)S(1)}, u32[]{:S(2)}, u32[]{:S(2)}) %collective-permute-start.62) | collective-permute-done | bytes 524320 | tf_op jit(solution)/shard_map/ppermute | solution.py:26
  406.3 13.2 %multiply_convert_fusion.5 = (bf16[512,1024]{1,0:T(8,128)(2,1)S(1)}, f32[512,1024]{1,0:T(8,128)}, bf16[512,1024]{1,0:T(8,128)(2,1)S(1)}, f32[512,1024]{1,0:T(8,128)}, f32[512,1024]{1,0:T(8,128)}) fusion(f32[1024]{0:T(1024)S(1)} %copy-done.167, f32[512,1024]{1,0:T(8,128)S(1)} %fusion.349, bf16[1024,1024]{0,1:T(8,128)(2,1)S(1)} %bitcast_dynamic-update-slice_fusion.8, ...), kind=kOutput, calls=%fused_computation.96 | convolution fusion | flops 1145044992 | bytes 13635584 | tf_op jit(solution)/shard_map/dot_general | solution.py:22
  428.7 7.5 collective-permute-done.69
  436.2 10.7 %collective-permute-done.65 = bf16[256,1024]{1,0:T(8,128)(2,1)} collective-permute-done((bf16[256,1024]{1,0:T(8,128)(2,1)}, bf16[256,1024]{1,0:T(8,128)(2,1)}, u32[]{:S(2)}, u32[]{:S(2)}) %collective-permute-start.65) | collective-permute-done | bytes 524320 | tf_op jit(solution)/shard_map/ppermute | solution.py:26
  454.3 5.4 collective-permute-start.66
  461.1 5.3 fusion.343
  468.7 5.4 collective-permute-done.73
  476.5 4.6 fusion.193
  498.6 4.1 add_convert_fusion
  521.3 4.6 collective-permute-done.126
  527.7 3.9 collective-permute-done.117
  546.2 15.0 %collective-permute-done.119 = bf16[128,1024]{0,1:T(8,128)(2,1)} collective-permute-done((bf16[128,1024]{0,1:T(8,128)(2,1)}, bf16[128,1024]{0,1:T(8,128)(2,1)}, u32[]{:S(2)}, u32[]{:S(2)}) %collective-permute-start.119) | collective-permute-done | bytes 262176 | tf_op jit(solution)/shard_map/ppermute | solution.py:26
  563.2 3.6 collective-permute-done.131
  570.5 8.2 multiply_reduce_fusion.3
  578.8 4.9 multiply_convert_fusion.3
  591.7 4.2 multiply_reduce_fusion.2
  595.9 4.5 multiply_convert_fusion.2
  631.1 7.0 collective-permute-done.102
  654.5 5.8 collective-permute-done.107
  661.1 4.6 fusion.344
  668.0 3.4 collective-permute-done.85
  673.9 4.6 fusion.190
  691.1 4.1 add_convert_fusion.1
  717.0 5.2 collective-permute-done.120
  722.8 5.0 collective-permute-done.111
  750.1 4.5 collective-permute-done.113
  757.1 7.0 collective-permute-done.125
  768.2 8.2 multiply_reduce_fusion.1
  776.4 4.9 multiply_convert_fusion.1
  789.0 4.3 multiply_reduce_fusion
  793.3 4.2 multiply_convert_fusion
  835.8 4.2 collective-permute-done.98
  844.1 5.1 collective-permute-done.99
  855.5 5.5 collective-permute-start.95
  861.0 11.3 %collective-permute-done.101 = bf16[128,1024]{0,1:T(8,128)(2,1)S(1)} collective-permute-done((bf16[128,1024]{0,1:T(8,128)(2,1)S(1)}, bf16[128,1024]{0,1:T(8,128)(2,1)S(1)}, u32[]{:S(2)}, u32[]{:S(2)}) %collective-permute-start.101) | collective-permute-done | bytes 262176 | tf_op jit(solution)/shard_map/ppermute | solution.py:26
  (1109 shorter events, 404.3 us)
Async XLA Ops:
  2.9 16.5 %collective-permute-start.10 = (f32[1,768]{1,0:T(1,128)S(1)}, f32[1,768]{1,0:T(1,128)S(1)}, u32[]{:S(2)}, u32[]{:S(2)}) collective-permute-start(f32[1,768]{1,0:T(1,128)S(1)} %broadcast_in_dim.101), channel_id=1, source_target_pairs={{0,1},{1,0},{2,3},{3,2},{4,5},{5,4},{6,7},{7,6},{8,9},{9,8},{10,11... | collective-permute-start | bytes 9224 | tf_op jit(solution)/shard_map/ppermute | solution.py:26
  7.3 73.0 %collective-permute-start.19 = (bf16[128,1024]{0,1:T(8,128)(2,1)S(1)}, bf16[128,1024]{0,1:T(8,128)(2,1)S(1)}, u32[]{:S(2)}, u32[]{:S(2)}) collective-permute-start(bf16[128,1024]{0,1:T(8,128)(2,1)S(1)} %bitcast.614), channel_id=1, source_target_pairs={{0,2},{2,0},{1,3},{3,1},{4,6},{6,4},{5,7},{7,5},{8,10},{10,8},{9,1... | collective-permute-start | bytes 786440 | tf_op jit(solution)/shard_map/ppermute | solution.py:26
  11.8 71.5 %collective-permute-start.4 = (bf16[128,1024]{0,1:T(8,128)(2,1)}, bf16[128,1024]{0,1:T(8,128)(2,1)S(1)}, u32[]{:S(2)}, u32[]{:S(2)}) collective-permute-start(bf16[128,1024]{0,1:T(8,128)(2,1)} %pad_maximum_fusion.48), channel_id=1, source_target_pairs={{0,2},{2,0},{1,3},{3,1},{4,6},{6,4},{5,7},{7,5},{8,10},{10,8},{9,1... | collective-permute-start | bytes 786440 | tf_op jit(solution)/shard_map/ppermute | solution.py:26
  12.3 73.5 %collective-permute-start.37 = (bf16[128,1024]{0,1:T(8,128)(2,1)S(1)}, bf16[128,1024]{0,1:T(8,128)(2,1)S(1)}, u32[]{:S(2)}, u32[]{:S(2)}) collective-permute-start(bf16[128,1024]{0,1:T(8,128)(2,1)S(1)} %pad_maximum_fusion.49), channel_id=1, source_target_pairs={{0,2},{2,0},{1,3},{3,1},{4,6},{6,4},{5,7},{7,5},{8,10},{10,8},{9,1... | collective-permute-start | bytes 786440 | tf_op jit(solution)/shard_map/ppermute | solution.py:26
  15.8 69.2 %collective-permute-start.55 = (bf16[128,1024]{0,1:T(8,128)(2,1)}, bf16[128,1024]{0,1:T(8,128)(2,1)S(1)}, u32[]{:S(2)}, u32[]{:S(2)}) collective-permute-start(bf16[128,1024]{0,1:T(8,128)(2,1)} %get-tuple-element.165), channel_id=1, source_target_pairs={{0,2},{2,0},{1,3},{3,1},{4,6},{6,4},{5,7},{7,5},{8,10},{10,8},{9,1... | collective-permute-start | bytes 786440 | tf_op jit(solution)/shard_map/ppermute | solution.py:26
  19.5 36.0 %collective-permute-start.11 = (f32[2,768]{1,0:T(2,128)S(1)}, f32[2,768]{1,0:T(2,128)S(1)}, u32[]{:S(2)}, u32[]{:S(2)}) collective-permute-start(f32[2,768]{1,0:T(2,128)S(1)} %maximum_select_fusion.4), channel_id=1, source_target_pairs={{0,2},{2,0},{1,3},{3,1},{4,6},{6,4},{5,7},{7,5},{8,10},{10,8},{9,1... | collective-permute-start | bytes 18440 | tf_op jit(solution)/shard_map/ppermute | solution.py:26
  66.4 18.7 %collective-permute-start.25 = (bf16[128,1024]{0,1:T(8,128)(2,1)}, bf16[128,1024]{0,1:T(8,128)(2,1)S(1)}, u32[]{:S(2)}, u32[]{:S(2)}) collective-permute-start(bf16[128,1024]{0,1:T(8,128)(2,1)} %get-tuple-element.166), channel_id=1, source_target_pairs={{0,2},{2,0},{1,3},{3,1},{4,6},{6,4},{5,7},{7,5},{8,10},{10,8},{9,1... | collective-permute-start | bytes 786440 | tf_op jit(solution)/shard_map/ppermute | solution.py:26
  85.0 29.3 %collective-permute-start.22 = (bf16[128,1024]{0,1:T(8,128)(2,1)S(1)}, bf16[128,1024]{0,1:T(8,128)(2,1)S(1)}, u32[]{:S(2)}, u32[]{:S(2)}) collective-permute-start(bf16[128,1024]{0,1:T(8,128)(2,1)S(1)} %broadcast_select_fusion.4), channel_id=1, source_target_pairs={{0,4},{4,0},{1,5},{5,1},{2,6},{6,2},{3,7},{7,3},{8,12},{12,8},{9,1... | collective-permute-start | bytes 786440 | tf_op jit(solution)/shard_map/ppermute | solution.py:26
  85.9 29.0 %collective-permute-start.7 = (bf16[128,1024]{0,1:T(8,128)(2,1)S(1)}, bf16[128,1024]{0,1:T(8,128)(2,1)S(1)}, u32[]{:S(2)}, u32[]{:S(2)}) collective-permute-start(bf16[128,1024]{0,1:T(8,128)(2,1)S(1)} %broadcast_select_fusion.5), channel_id=1, source_target_pairs={{0,4},{4,0},{1,5},{5,1},{2,6},{6,2},{3,7},{7,3},{8,12},{12,8},{9,1... | collective-permute-start | bytes 786440 | tf_op jit(solution)/shard_map/ppermute | solution.py:26
  96.5 17.7 %collective-permute-start.56 = (bf16[1,128,1024]{1,2,0:T(8,128)(2,1)S(1)}, bf16[1,128,1024]{1,2,0:T(8,128)(2,1)S(1)}, u32[]{:S(2)}, u32[]{:S(2)}) collective-permute-start(bf16[1,128,1024]{1,2,0:T(8,128)(2,1)S(1)} %get-tuple-element.97), channel_id=1, source_target_pairs={{0,8},{8,0},{16,24},{24,16},{1,9},{9,1},{17,25},{25,17},{2,10},{10... | collective-permute-start | bytes 786440 | tf_op jit(solution)/shard_map/ppermute | solution.py:30
  118.6 16.7 %collective-permute-start.41 = (bf16[1,128,1024]{1,2,0:T(8,128)(2,1)S(1)}, bf16[1,128,1024]{1,2,0:T(8,128)(2,1)S(1)}, u32[]{:S(2)}, u32[]{:S(2)}) collective-permute-start(bf16[1,128,1024]{1,2,0:T(8,128)(2,1)S(1)} %bitcast.640), channel_id=1, source_target_pairs={{0,16},{8,24},{16,0},{24,8},{1,17},{9,25},{17,1},{25,9},{2,18},{10... | collective-permute-start | bytes 786440 | tf_op jit(solution)/shard_map/ppermute | solution.py:30
  120.3 20.6 %collective-permute-start.29 = (bf16[1,128,1024]{1,2,0:T(8,128)(2,1)S(1)}, bf16[1,128,1024]{1,2,0:T(8,128)(2,1)S(1)}, u32[]{:S(2)}, u32[]{:S(2)}) collective-permute-start(bf16[1,128,1024]{1,2,0:T(8,128)(2,1)S(1)} %bitcast.638), channel_id=1, source_target_pairs={{0,16},{8,24},{16,0},{24,8},{1,17},{9,25},{17,1},{25,9},{2,18},{10... | collective-permute-start | bytes 786440 | tf_op jit(solution)/shard_map/ppermute | solution.py:30
  124.0 22.5 %collective-permute-start.59 = (bf16[1,128,1024]{1,2,0:T(8,128)(2,1)S(1)}, bf16[1,128,1024]{1,2,0:T(8,128)(2,1)S(1)}, u32[]{:S(2)}, u32[]{:S(2)}) collective-permute-start(bf16[1,128,1024]{1,2,0:T(8,128)(2,1)S(1)} %bitcast.636), channel_id=1, source_target_pairs={{0,16},{8,24},{16,0},{24,8},{1,17},{9,25},{17,1},{25,9},{2,18},{10... | collective-permute-start | bytes 786440 | tf_op jit(solution)/shard_map/ppermute | solution.py:30
  129.6 51.4 %collective-permute-start.21 = (bf16[2,128,1024]{1,2,0:T(8,128)(2,1)S(1)}, bf16[2,128,1024]{1,2,0:T(8,128)(2,1)S(1)}, u32[]{:S(2)}, u32[]{:S(2)}) collective-permute-start(bf16[2,128,1024]{1,2,0:T(8,128)(2,1)S(1)} %pad_maximum_fusion.36), channel_id=1, source_target_pairs={{0,16},{8,24},{16,0},{24,8},{1,17},{9,25},{17,1},{25,9},{2,18},{10... | collective-permute-start | bytes 1572872 | tf_op jit(solution)/shard_map/ppermute | solution.py:30
  130.2 51.4 %collective-permute-start.6 = (bf16[2,128,1024]{1,2,0:T(8,128)(2,1)S(1)}, bf16[2,128,1024]{1,2,0:T(8,128)(2,1)S(1)}, u32[]{:S(2)}, u32[]{:S(2)}) collective-permute-start(bf16[2,128,1024]{1,2,0:T(8,128)(2,1)S(1)} %pad_maximum_fusion.34), channel_id=1, source_target_pairs={{0,16},{8,24},{16,0},{24,8},{1,17},{9,25},{17,1},{25,9},{2,18},{10... | collective-permute-start | bytes 1572872 | tf_op jit(solution)/shard_map/ppermute | solution.py:30
  135.2 39.3 %collective-permute-start.53 = (bf16[1,128,1024]{1,2,0:T(8,128)(2,1)S(1)}, bf16[1,128,1024]{1,2,0:T(8,128)(2,1)S(1)}, u32[]{:S(2)}, u32[]{:S(2)}) collective-permute-start(bf16[1,128,1024]{1,2,0:T(8,128)(2,1)S(1)} %bitcast.630), channel_id=1, source_target_pairs={{0,16},{8,24},{16,0},{24,8},{1,17},{9,25},{17,1},{25,9},{2,18},{10... | collective-permute-start | bytes 786440 | tf_op jit(solution)/shard_map/ppermute | solution.py:30
  140.9 42.4 %collective-permute-start = (bf16[256,1024]{1,0:T(8,128)(2,1)S(1)}, bf16[256,1024]{1,0:T(8,128)(2,1)S(1)}, u32[]{:S(2)}, u32[]{:S(2)}) collective-permute-start(bf16[256,1024]{1,0:T(8,128)(2,1)S(1)} %copy-done.172), channel_id=1, source_target_pairs={{0,0},{2,4},{4,2},{6,6},{1,1},{3,5},{5,3},{7,7},{8,8},{10,12},{12,... | collective-permute-start | bytes 1572872 | tf_op jit(solution)/shard_map/ppermute | solution.py:34
  146.5 39.3 %collective-permute-start.39 = (bf16[2,128,1024]{1,2,0:T(8,128)(2,1)S(1)}, bf16[2,128,1024]{1,2,0:T(8,128)(2,1)S(1)}, u32[]{:S(2)}, u32[]{:S(2)}) collective-permute-start(bf16[2,128,1024]{1,2,0:T(8,128)(2,1)S(1)} %pad_maximum_fusion.40), channel_id=1, source_target_pairs={{0,16},{8,24},{16,0},{24,8},{1,17},{9,25},{17,1},{25,9},{2,18},{10... | collective-permute-start | bytes 1572872 | tf_op jit(solution)/shard_map/ppermute | solution.py:30
  174.6 246.5 %collective-permute-start.67 = (bf16[256,1024]{1,0:T(8,128)(2,1)}, bf16[256,1024]{1,0:T(8,128)(2,1)}, u32[]{:S(2)}, u32[]{:S(2)}) collective-permute-start(bf16[256,1024]{1,0:T(8,128)(2,1)} %param.24), channel_id=1, source_target_pairs={{0,0},{2,4},{4,2},{6,6},{1,1},{3,5},{5,3},{7,7},{8,8},{10,12},{12,... | collective-permute-start | bytes 1572872 | tf_op jit(solution)/shard_map/ppermute | solution.py:34
  181.0 16.0 %collective-permute-start.27 = (bf16[2,128,1024]{1,2,0:T(8,128)(2,1)S(1)}, bf16[2,128,1024]{1,2,0:T(8,128)(2,1)S(1)}, u32[]{:S(2)}, u32[]{:S(2)}) collective-permute-start(bf16[2,128,1024]{1,2,0:T(8,128)(2,1)S(1)} %pad_maximum_fusion.38), channel_id=1, source_target_pairs={{0,16},{8,24},{16,0},{24,8},{1,17},{9,25},{17,1},{25,9},{2,18},{10... | collective-permute-start | bytes 1572872 | tf_op jit(solution)/shard_map/ppermute | solution.py:30
  181.6 26.7 %collective-permute-start.57 = (bf16[2,128,1024]{1,2,0:T(8,128)(2,1)S(1)}, bf16[2,128,1024]{1,2,0:T(8,128)(2,1)S(1)}, u32[]{:S(2)}, u32[]{:S(2)}) collective-permute-start(bf16[2,128,1024]{1,2,0:T(8,128)(2,1)S(1)} %pad_maximum_fusion.44), channel_id=1, source_target_pairs={{0,16},{8,24},{16,0},{24,8},{1,17},{9,25},{17,1},{25,9},{2,18},{10... | collective-permute-start | bytes 1572872 | tf_op jit(solution)/shard_map/ppermute | solution.py:30
  183.3 35.3 %collective-permute-start.51 = (bf16[2,128,1024]{1,2,0:T(8,128)(2,1)S(1)}, bf16[2,128,1024]{1,2,0:T(8,128)(2,1)S(1)}, u32[]{:S(2)}, u32[]{:S(2)}) collective-permute-start(bf16[2,128,1024]{1,2,0:T(8,128)(2,1)S(1)} %pad_maximum_fusion.42), channel_id=1, source_target_pairs={{0,16},{8,24},{16,0},{24,8},{1,17},{9,25},{17,1},{25,9},{2,18},{10... | collective-permute-start | bytes 1572872 | tf_op jit(solution)/shard_map/ppermute | solution.py:30
  185.8 34.6 %collective-permute-start.2 = (bf16[256,1024]{1,0:T(8,128)(2,1)S(1)}, bf16[256,1024]{1,0:T(8,128)(2,1)S(1)}, u32[]{:S(2)}, u32[]{:S(2)}) collective-permute-start(bf16[256,1024]{1,0:T(8,128)(2,1)S(1)} %collective-permute-done), channel_id=1, source_target_pairs={{0,1},{1,0},{2,3},{3,2},{4,5},{5,4},{6,7},{7,6},{8,9},{9,8},{10,11... | collective-permute-start | bytes 1572872 | tf_op jit(solution)/shard_map/ppermute | solution.py:26
  197.0 21.7 %collective-permute-start.24 = (bf16[2,128,1024]{1,2,0:T(8,128)(2,1)S(1)}, bf16[2,128,1024]{1,2,0:T(8,128)(2,1)S(1)}, u32[]{:S(2)}, u32[]{:S(2)}) collective-permute-start(bf16[2,128,1024]{1,2,0:T(8,128)(2,1)S(1)} %pad_maximum_fusion.37), channel_id=1, source_target_pairs={{0,8},{8,0},{16,24},{24,16},{1,9},{9,1},{17,25},{25,17},{2,10},{10... | collective-permute-start | bytes 1572872 | tf_op jit(solution)/shard_map/ppermute | solution.py:30
  218.8 40.5 %collective-permute-start.42 = (bf16[2,128,1024]{1,2,0:T(8,128)(2,1)}, bf16[2,128,1024]{1,2,0:T(8,128)(2,1)}, u32[]{:S(2)}, u32[]{:S(2)}) collective-permute-start(bf16[2,128,1024]{1,2,0:T(8,128)(2,1)} %pad_maximum_fusion.41), channel_id=1, source_target_pairs={{0,8},{8,0},{16,24},{24,16},{1,9},{9,1},{17,25},{25,17},{2,10},{10... | collective-permute-start | bytes 1572872 | tf_op jit(solution)/shard_map/ppermute | solution.py:30
  220.4 41.5 %collective-permute-start.30 = (bf16[2,128,1024]{1,2,0:T(8,128)(2,1)}, bf16[2,128,1024]{1,2,0:T(8,128)(2,1)}, u32[]{:S(2)}, u32[]{:S(2)}) collective-permute-start(bf16[2,128,1024]{1,2,0:T(8,128)(2,1)} %pad_maximum_fusion.39), channel_id=1, source_target_pairs={{0,8},{8,0},{16,24},{24,16},{1,9},{9,1},{17,25},{25,17},{2,10},{10... | collective-permute-start | bytes 1572872 | tf_op jit(solution)/shard_map/ppermute | solution.py:30
  259.3 67.5 %collective-permute-start.60 = (bf16[2,128,1024]{1,2,0:T(8,128)(2,1)S(1)}, bf16[2,128,1024]{1,2,0:T(8,128)(2,1)S(1)}, u32[]{:S(2)}, u32[]{:S(2)}) collective-permute-start(bf16[2,128,1024]{1,2,0:T(8,128)(2,1)S(1)} %copy-done.105), channel_id=1, source_target_pairs={{0,8},{8,0},{16,24},{24,16},{1,9},{9,1},{17,25},{25,17},{2,10},{10... | collective-permute-start | bytes 1572872 | tf_op jit(solution)/shard_map/ppermute | solution.py:30
  262.0 65.6 %collective-permute-start.54 = (bf16[2,128,1024]{1,2,0:T(8,128)(2,1)S(1)}, bf16[2,128,1024]{1,2,0:T(8,128)(2,1)S(1)}, u32[]{:S(2)}, u32[]{:S(2)}) collective-permute-start(bf16[2,128,1024]{1,2,0:T(8,128)(2,1)S(1)} %copy-done.106), channel_id=1, source_target_pairs={{0,8},{8,0},{16,24},{24,16},{1,9},{9,1},{17,25},{25,17},{2,10},{10... | collective-permute-start | bytes 1572872 | tf_op jit(solution)/shard_map/ppermute | solution.py:30
  426.2 20.6 %collective-permute-start.65 = (bf16[256,1024]{1,0:T(8,128)(2,1)}, bf16[256,1024]{1,0:T(8,128)(2,1)}, u32[]{:S(2)}, u32[]{:S(2)}) collective-permute-start(bf16[256,1024]{1,0:T(8,128)(2,1)} %fusion.135), channel_id=1, source_target_pairs={{0,1},{1,0},{2,3},{3,2},{4,5},{5,4},{6,7},{7,6},{8,9},{9,8},{10,11... | collective-permute-start | bytes 1572872 | tf_op jit(solution)/shard_map/ppermute | solution.py:26
  428.5 20.7 %collective-permute-start.68 = (bf16[256,1024]{1,0:T(8,128)(2,1)}, bf16[256,1024]{1,0:T(8,128)(2,1)S(1)}, u32[]{:S(2)}, u32[]{:S(2)}) collective-permute-start(bf16[256,1024]{1,0:T(8,128)(2,1)} %collective-permute-done.67), channel_id=1, source_target_pairs={{0,4},{4,0},{1,5},{5,1},{2,6},{6,2},{3,7},{7,3},{8,12},{12,8},{9,1... | collective-permute-start | bytes 1572872 | tf_op jit(solution)/shard_map/ppermute | solution.py:26
  453.8 20.3 %collective-permute-start.73 = (bf16[256,1024]{1,0:T(8,128)(2,1)}, bf16[256,1024]{1,0:T(8,128)(2,1)}, u32[]{:S(2)}, u32[]{:S(2)}) collective-permute-start(bf16[256,1024]{1,0:T(8,128)(2,1)} %convert_element_type.657), channel_id=1, source_target_pairs={{0,1},{1,0},{2,3},{3,2},{4,5},{5,4},{6,7},{7,6},{8,9},{9,8},{10,11... | collective-permute-start | bytes 1572872 | tf_op jit(solution)/shard_map/ppermute | solution.py:26
  454.3 21.0 %collective-permute-start.66 = (bf16[256,1024]{1,0:T(8,128)(2,1)}, bf16[256,1024]{1,0:T(8,128)(2,1)}, u32[]{:S(2)}, u32[]{:S(2)}) collective-permute-start(bf16[256,1024]{1,0:T(8,128)(2,1)} %get-tuple-element.136), channel_id=1, source_target_pairs={{0,0},{2,4},{4,2},{6,6},{1,1},{3,5},{5,3},{7,7},{8,8},{10,12},{12,... | collective-permute-start | bytes 1572872 | tf_op jit(solution)/shard_map/ppermute | solution.py:34
  468.7 66.7 %collective-permute-start.72 = (bf16[256,1024]{1,0:T(8,128)(2,1)}, bf16[256,1024]{1,0:T(8,128)(2,1)}, u32[]{:S(2)}, u32[]{:S(2)}) collective-permute-start(bf16[256,1024]{1,0:T(8,128)(2,1)} %slice.695), channel_id=1, source_target_pairs={{0,4},{4,0},{1,5},{5,1},{2,6},{6,2},{3,7},{7,3},{8,12},{12,8},{9,1... | collective-permute-start | bytes 1572872 | tf_op jit(solution)/shard_map/ppermute | solution.py:26
  486.0 25.0 %collective-permute-start.75 = (bf16[256,1024]{1,0:T(8,128)(2,1)}, bf16[256,1024]{1,0:T(8,128)(2,1)}, u32[]{:S(2)}, u32[]{:S(2)}) collective-permute-start(bf16[256,1024]{1,0:T(8,128)(2,1)} %slice.694), channel_id=1, source_target_pairs={{0,4},{4,0},{1,5},{5,1},{2,6},{6,2},{3,7},{7,3},{8,12},{12,8},{9,1... | collective-permute-start | bytes 1572872 | tf_op jit(solution)/shard_map/ppermute | solution.py:26
  491.2 23.0 %collective-permute-start.116 = (bf16[2,128,1024]{1,2,0:T(8,128)(2,1)}, bf16[2,128,1024]{1,2,0:T(8,128)(2,1)}, u32[]{:S(2)}, u32[]{:S(2)}) collective-permute-start(bf16[2,128,1024]{1,2,0:T(8,128)(2,1)} %bitcast.655), channel_id=1, source_target_pairs={{0,8},{8,0},{16,24},{24,16},{1,9},{9,1},{17,25},{25,17},{2,10},{10... | collective-permute-start | bytes 1572872 | tf_op jit(solution)/shard_map/ppermute | solution.py:30
  498.1 17.4 %collective-permute-start.114 = (bf16[2,128,1024]{1,2,0:T(8,128)(2,1)}, bf16[2,128,1024]{1,2,0:T(8,128)(2,1)}, u32[]{:S(2)}, u32[]{:S(2)}) collective-permute-start(bf16[2,128,1024]{1,2,0:T(8,128)(2,1)} %dynamic-slice_bitcast_fusion.2), channel_id=1, source_target_pairs={{0,16},{8,24},{16,0},{24,8},{1,17},{9,25},{17,1},{25,9},{2,18},{10... | collective-permute-start | bytes 1572872 | tf_op jit(solution)/shard_map/ppermute | solution.py:30
  514.2 21.8 %collective-permute-start.76 = (bf16[256,1024]{1,0:T(8,128)(2,1)S(1)}, bf16[256,1024]{1,0:T(8,128)(2,1)S(1)}, u32[]{:S(2)}, u32[]{:S(2)}) collective-permute-start(bf16[256,1024]{1,0:T(8,128)(2,1)S(1)} %fusion.132), channel_id=1, source_target_pairs={{0,1},{1,0},{2,3},{3,2},{4,5},{5,4},{6,7},{7,6},{8,9},{9,8},{10,11... | collective-permute-start | bytes 1572872 | tf_op jit(solution)/shard_map/ppermute | solution.py:26
  515.5 16.1 %collective-permute-start.117 = (bf16[128,1024]{0,1:T(8,128)(2,1)S(1)}, bf16[128,1024]{0,1:T(8,128)(2,1)S(1)}, u32[]{:S(2)}, u32[]{:S(2)}) collective-permute-start(bf16[128,1024]{0,1:T(8,128)(2,1)S(1)} %fusion.252), channel_id=1, source_target_pairs={{0,16},{8,24},{16,0},{24,8},{1,17},{9,25},{17,1},{25,9},{2,18},{10... | collective-permute-start | bytes 786440 | tf_op jit(solution)/shard_map/ppermute | solution.py:30
  519.6 19.4 %collective-permute-start.115 = (bf16[128,1024]{0,1:T(8,128)(2,1)S(1)}, bf16[128,1024]{0,1:T(8,128)(2,1)S(1)}, u32[]{:S(2)}, u32[]{:S(2)}) collective-permute-start(bf16[128,1024]{0,1:T(8,128)(2,1)S(1)} %fusion.251), channel_id=1, source_target_pairs={{0,8},{8,0},{16,24},{24,16},{1,9},{9,1},{17,25},{25,17},{2,10},{10... | collective-permute-start | bytes 786440 | tf_op jit(solution)/shard_map/ppermute | solution.py:30
  539.0 29.8 %collective-permute-start.77 = (bf16[256,1024]{1,0:T(8,128)(2,1)}, bf16[256,1024]{1,0:T(8,128)(2,1)}, u32[]{:S(2)}, u32[]{:S(2)}) collective-permute-start(bf16[256,1024]{1,0:T(8,128)(2,1)} %convert_element_type.664), channel_id=1, source_target_pairs={{0,4},{4,0},{1,5},{5,1},{2,6},{6,2},{3,7},{7,3},{8,12},{12,8},{9,1... | collective-permute-start | bytes 1572872 | tf_op jit(solution)/shard_map/ppermute | solution.py:26
  539.9 21.3 %collective-permute-start.119 = (bf16[128,1024]{0,1:T(8,128)(2,1)}, bf16[128,1024]{0,1:T(8,128)(2,1)}, u32[]{:S(2)}, u32[]{:S(2)}) collective-permute-start(bf16[128,1024]{0,1:T(8,128)(2,1)} %fusion.208), channel_id=1, source_target_pairs={{0,2},{2,0},{1,3},{3,1},{4,6},{6,4},{5,7},{7,5},{8,10},{10,8},{9,1... | collective-permute-start | bytes 786440 | tf_op jit(solution)/shard_map/ppermute | solution.py:26
  541.5 25.2 %collective-permute-start.131 = (bf16[128,1024]{0,1:T(8,128)(2,1)}, bf16[128,1024]{0,1:T(8,128)(2,1)}, u32[]{:S(2)}, u32[]{:S(2)}) collective-permute-start(bf16[128,1024]{0,1:T(8,128)(2,1)} %fusion.214), channel_id=1, source_target_pairs={{0,2},{2,0},{1,3},{3,1},{4,6},{6,4},{5,7},{7,5},{8,10},{10,8},{9,1... | collective-permute-start | bytes 786440 | tf_op jit(solution)/shard_map/ppermute | solution.py:26
  543.8 40.0 %collective-permute-start.78 = (bf16[256,1024]{1,0:T(8,128)(2,1)}, bf16[256,1024]{1,0:T(8,128)(2,1)}, u32[]{:S(2)}, u32[]{:S(2)}) collective-permute-start(bf16[256,1024]{1,0:T(8,128)(2,1)} %convert_element_type.664), channel_id=1, source_target_pairs={{0,1},{1,0},{2,3},{3,2},{4,5},{5,4},{6,7},{7,6},{8,9},{9,8},{10,11... | collective-permute-start | bytes 1572872 | tf_op jit(solution)/shard_map/ppermute | solution.py:26
  609.4 15.3 %collective-permute-start.81 = (bf16[256,1024]{1,0:T(8,128)(2,1)}, bf16[256,1024]{1,0:T(8,128)(2,1)}, u32[]{:S(2)}, u32[]{:S(2)}) collective-permute-start(bf16[256,1024]{1,0:T(8,128)(2,1)} %slice.692), channel_id=1, source_target_pairs={{0,4},{4,0},{1,5},{5,1},{2,6},{6,2},{3,7},{7,3},{8,12},{12,8},{9,1... | collective-permute-start | bytes 1572872 | tf_op jit(solution)/shard_map/ppermute | solution.py:26
  620.4 23.0 %collective-permute-start.80 = (bf16[256,1024]{1,0:T(8,128)(2,1)}, bf16[256,1024]{1,0:T(8,128)(2,1)}, u32[]{:S(2)}, u32[]{:S(2)}) collective-permute-start(bf16[256,1024]{1,0:T(8,128)(2,1)} %slice.693), channel_id=1, source_target_pairs={{0,4},{4,0},{1,5},{5,1},{2,6},{6,2},{3,7},{7,3},{8,12},{12,8},{9,1... | collective-permute-start | bytes 1572872 | tf_op jit(solution)/shard_map/ppermute | solution.py:26
  626.3 17.1 %collective-permute-start.82 = (bf16[256,1024]{1,0:T(8,128)(2,1)S(1)}, bf16[256,1024]{1,0:T(8,128)(2,1)S(1)}, u32[]{:S(2)}, u32[]{:S(2)}) collective-permute-start(bf16[256,1024]{1,0:T(8,128)(2,1)S(1)} %fusion.129), channel_id=1, source_target_pairs={{0,1},{1,0},{2,3},{3,2},{4,5},{5,4},{6,7},{7,6},{8,9},{9,8},{10,11... | collective-permute-start | bytes 1572872 | tf_op jit(solution)/shard_map/ppermute | solution.py:26
  650.9 20.6 %collective-permute-start.85 = (bf16[256,1024]{1,0:T(8,128)(2,1)}, bf16[256,1024]{1,0:T(8,128)(2,1)}, u32[]{:S(2)}, u32[]{:S(2)}) collective-permute-start(bf16[256,1024]{1,0:T(8,128)(2,1)} %convert_element_type.679), channel_id=1, source_target_pairs={{0,1},{1,0},{2,3},{3,2},{4,5},{5,4},{6,7},{7,6},{8,9},{9,8},{10,11... | collective-permute-start | bytes 1572872 | tf_op jit(solution)/shard_map/ppermute | solution.py:26
  668.0 63.5 %collective-permute-start.84 = (bf16[256,1024]{1,0:T(8,128)(2,1)}, bf16[256,1024]{1,0:T(8,128)(2,1)}, u32[]{:S(2)}, u32[]{:S(2)}) collective-permute-start(bf16[256,1024]{1,0:T(8,128)(2,1)} %slice.691), channel_id=1, source_target_pairs={{0,4},{4,0},{1,5},{5,1},{2,6},{6,2},{3,7},{7,3},{8,12},{12,8},{9,1... | collective-permute-start | bytes 1572872 | tf_op jit(solution)/shard_map/ppermute | solution.py:26
  683.4 23.8 %collective-permute-start.87 = (bf16[256,1024]{1,0:T(8,128)(2,1)}, bf16[256,1024]{1,0:T(8,128)(2,1)}, u32[]{:S(2)}, u32[]{:S(2)}) collective-permute-start(bf16[256,1024]{1,0:T(8,128)(2,1)} %slice.690), channel_id=1, source_target_pairs={{0,4},{4,0},{1,5},{5,1},{2,6},{6,2},{3,7},{7,3},{8,12},{12,8},{9,1... | collective-permute-start | bytes 1572872 | tf_op jit(solution)/shard_map/ppermute | solution.py:26
  687.6 21.7 %collective-permute-start.110 = (bf16[2,128,1024]{1,2,0:T(8,128)(2,1)}, bf16[2,128,1024]{1,2,0:T(8,128)(2,1)}, u32[]{:S(2)}, u32[]{:S(2)}) collective-permute-start(bf16[2,128,1024]{1,2,0:T(8,128)(2,1)} %bitcast.168), channel_id=1, source_target_pairs={{0,8},{8,0},{16,24},{24,16},{1,9},{9,1},{17,25},{25,17},{2,10},{10... | collective-permute-start | bytes 1572872 | tf_op jit(solution)/shard_map/ppermute | solution.py:30
  689.6 21.0 %collective-permute-start.108 = (bf16[2,128,1024]{1,2,0:T(8,128)(2,1)}, bf16[2,128,1024]{1,2,0:T(8,128)(2,1)}, u32[]{:S(2)}, u32[]{:S(2)}) collective-permute-start(bf16[2,128,1024]{1,2,0:T(8,128)(2,1)} %dynamic-slice_bitcast_fusion.3), channel_id=1, source_target_pairs={{0,16},{8,24},{16,0},{24,8},{1,17},{9,25},{17,1},{25,9},{2,18},{10... | collective-permute-start | bytes 1572872 | tf_op jit(solution)/shard_map/ppermute | solution.py:30
  709.3 22.9 %collective-permute-start.88 = (bf16[256,1024]{1,0:T(8,128)(2,1)S(1)}, bf16[256,1024]{1,0:T(8,128)(2,1)S(1)}, u32[]{:S(2)}, u32[]{:S(2)}) collective-permute-start(bf16[256,1024]{1,0:T(8,128)(2,1)S(1)} %fusion.126), channel_id=1, source_target_pairs={{0,1},{1,0},{2,3},{3,2},{4,5},{5,4},{6,7},{7,6},{8,9},{9,8},{10,11... | collective-permute-start | bytes 1572872 | tf_op jit(solution)/shard_map/ppermute | solution.py:26
  710.6 17.2 %collective-permute-start.111 = (bf16[128,1024]{0,1:T(8,128)(2,1)S(1)}, bf16[128,1024]{0,1:T(8,128)(2,1)S(1)}, u32[]{:S(2)}, u32[]{:S(2)}) collective-permute-start(bf16[128,1024]{0,1:T(8,128)(2,1)S(1)} %fusion.250), channel_id=1, source_target_pairs={{0,16},{8,24},{16,0},{24,8},{1,17},{9,25},{17,1},{25,9},{2,18},{10... | collective-permute-start | bytes 786440 | tf_op jit(solution)/shard_map/ppermute | solution.py:30
  714.2 22.1 %collective-permute-start.109 = (bf16[128,1024]{0,1:T(8,128)(2,1)S(1)}, bf16[128,1024]{0,1:T(8,128)(2,1)S(1)}, u32[]{:S(2)}, u32[]{:S(2)}) collective-permute-start(bf16[128,1024]{0,1:T(8,128)(2,1)S(1)} %fusion.249), channel_id=1, source_target_pairs={{0,8},{8,0},{16,24},{24,16},{1,9},{9,1},{17,25},{25,17},{2,10},{10... | collective-permute-start | bytes 786440 | tf_op jit(solution)/shard_map/ppermute | solution.py:30
  736.4 45.0 %collective-permute-start.90 = (bf16[256,1024]{1,0:T(8,128)(2,1)}, bf16[256,1024]{1,0:T(8,128)(2,1)}, u32[]{:S(2)}, u32[]{:S(2)}) collective-permute-start(bf16[256,1024]{1,0:T(8,128)(2,1)} %convert_element_type.686), channel_id=1, source_target_pairs={{0,1},{1,0},{2,3},{3,2},{4,5},{5,4},{6,7},{7,6},{8,9},{9,8},{10,11... | collective-permute-start | bytes 1572872 | tf_op jit(solution)/shard_map/ppermute | solution.py:26
  736.4 29.9 %collective-permute-start.89 = (bf16[256,1024]{1,0:T(8,128)(2,1)}, bf16[256,1024]{1,0:T(8,128)(2,1)}, u32[]{:S(2)}, u32[]{:S(2)}) collective-permute-start(bf16[256,1024]{1,0:T(8,128)(2,1)} %convert_element_type.686), channel_id=1, source_target_pairs={{0,4},{4,0},{1,5},{5,1},{2,6},{6,2},{3,7},{7,3},{8,12},{12,8},{9,1... | collective-permute-start | bytes 1572872 | tf_op jit(solution)/shard_map/ppermute | solution.py:26
  737.2 17.4 %collective-permute-start.113 = (bf16[128,1024]{0,1:T(8,128)(2,1)}, bf16[128,1024]{0,1:T(8,128)(2,1)}, u32[]{:S(2)}, u32[]{:S(2)}) collective-permute-start(bf16[128,1024]{0,1:T(8,128)(2,1)} %fusion.205), channel_id=1, source_target_pairs={{0,2},{2,0},{1,3},{3,1},{4,6},{6,4},{5,7},{7,5},{8,10},{10,8},{9,1... | collective-permute-start | bytes 786440 | tf_op jit(solution)/shard_map/ppermute | solution.py:26
  741.4 22.7 %collective-permute-start.125 = (bf16[128,1024]{0,1:T(8,128)(2,1)}, bf16[128,1024]{0,1:T(8,128)(2,1)}, u32[]{:S(2)}, u32[]{:S(2)}) collective-permute-start(bf16[128,1024]{0,1:T(8,128)(2,1)} %fusion.211), channel_id=1, source_target_pairs={{0,2},{2,0},{1,3},{3,1},{4,6},{6,4},{5,7},{7,5},{8,10},{10,8},{9,1... | collective-permute-start | bytes 786440 | tf_op jit(solution)/shard_map/ppermute | solution.py:26
  809.4 22.1 %collective-permute-start.93 = (bf16[256,1024]{1,0:T(8,128)(2,1)}, bf16[256,1024]{1,0:T(8,128)(2,1)}, u32[]{:S(2)}, u32[]{:S(2)}) collective-permute-start(bf16[256,1024]{1,0:T(8,128)(2,1)} %slice.688), channel_id=1, source_target_pairs={{0,4},{4,0},{1,5},{5,1},{2,6},{6,2},{3,7},{7,3},{8,12},{12,8},{9,1... | collective-permute-start | bytes 1572872 | tf_op jit(solution)/shard_map/ppermute | solution.py:26
  810.8 42.1 %collective-permute-start.92 = (bf16[256,1024]{1,0:T(8,128)(2,1)}, bf16[256,1024]{1,0:T(8,128)(2,1)}, u32[]{:S(2)}, u32[]{:S(2)}) collective-permute-start(bf16[256,1024]{1,0:T(8,128)(2,1)} %slice.689), channel_id=1, source_target_pairs={{0,4},{4,0},{1,5},{5,1},{2,6},{6,2},{3,7},{7,3},{8,12},{12,8},{9,1... | collective-permute-start | bytes 1572872 | tf_op jit(solution)/shard_map/ppermute | solution.py:26
  831.4 17.9 %collective-permute-start.136 = (f32[1,768]{1,0:T(1,128)S(1)}, f32[1,768]{1,0:T(1,128)S(1)}, u32[]{:S(2)}, u32[]{:S(2)}) collective-permute-start(f32[1,768]{1,0:T(1,128)S(1)} %constant_dynamic-slice_fusion.27), channel_id=1, source_target_pairs={{0,1},{1,0},{2,3},{3,2},{4,5},{5,4},{6,7},{7,6},{8,9},{9,8},{10,11... | collective-permute-start | bytes 9224 | tf_op jit(solution)/shard_map/ppermute | solution.py:26
  833.9 19.0 %collective-permute-start.94 = (bf16[256,1024]{1,0:T(8,128)(2,1)}, bf16[256,1024]{1,0:T(8,128)(2,1)}, u32[]{:S(2)}, u32[]{:S(2)}) collective-permute-start(bf16[256,1024]{1,0:T(8,128)(2,1)} %fusion.122), channel_id=1, source_target_pairs={{0,1},{1,0},{2,3},{3,2},{4,5},{5,4},{6,7},{7,6},{8,9},{9,8},{10,11... | collective-permute-start | bytes 1572872 | tf_op jit(solution)/shard_map/ppermute | solution.py:26
  851.4 20.9 %collective-permute-start.101 = (bf16[128,1024]{0,1:T(8,128)(2,1)S(1)}, bf16[128,1024]{0,1:T(8,128)(2,1)S(1)}, u32[]{:S(2)}, u32[]{:S(2)}) collective-permute-start(bf16[128,1024]{0,1:T(8,128)(2,1)S(1)} %fusion.200), channel_id=1, source_target_pairs={{0,2},{2,0},{1,3},{3,1},{4,6},{6,4},{5,7},{7,5},{8,10},{10,8},{9,1... | collective-permute-start | bytes 786440 | tf_op jit(solution)/shard_map/ppermute | solution.py:26
  855.5 18.9 %collective-permute-start.95 = (bf16[256,1024]{1,0:T(8,128)(2,1)}, bf16[256,1024]{1,0:T(8,128)(2,1)}, u32[]{:S(2)}, u32[]{:S(2)}) collective-permute-start(bf16[256,1024]{1,0:T(8,128)(2,1)} %fusion.125), channel_id=1, source_target_pairs={{0,0},{2,4},{4,2},{6,6},{1,1},{3,5},{5,3},{7,7},{8,8},{10,12},{12,... | collective-permute-start | bytes 1572872 | tf_op jit(solution)/shard_map/ppermute | solution.py:34
  (271 other events, 2913.8 us)

commit v2 on v1

v2 whole, which is shorter than its diff:
```python
import functools

import jax
import jax.numpy as jnp
from jax import lax
from jax.experimental import pallas as pl
from jax.experimental.pallas import tpu as pltpu
from jax.sharding import Mesh, PartitionSpec as P

D = 1024
HEAD_DIM = 64
FF = 4096
LAYERS = 2
SEQ_GRP = 3

EPS = 1e-05
NEG = -1e30
ALL = ("d", "c", "zh", "zl")
SWAP = [(0, 1), (1, 0)]
bf16 = jnp.bfloat16
f32 = jnp.float32
MIB = 1 << 20

TAIL_STEP = 0.24
TAIL = (
    0.0912286469891869,
    0.14294535326111468,
    -0.11556713177962434,
    0.5630756863681534,
    -0.5892310046041954,
    0.5271447780474939,
    -0.11959632556906954,
)
INV_SQRT_2PI = 0.3989422804014327


def nn(a, b):
    return lax.dot_general(a, b, (((1,), (0,)), ((), ())), preferred_element_type=f32)


def nt(a, b):
    return lax.dot_general(a, b, (((1,), (1,)), ((), ())), preferred_element_type=f32)


def tn(a, b):
    return lax.dot_general(a, b, (((0,), (0,)), ((), ())), preferred_element_type=f32)


def stack_rows(refs):
    return jnp.concatenate([r[...] for r in refs], 0)


def params(limit):
    return pltpu.CompilerParams(vmem_limit_bytes=limit * MIB)


def cost(flops, nbytes, exps=0):
    return pl.CostEstimate(flops=int(flops), bytes_accessed=int(nbytes), transcendentals=int(exps))


def struct(shape, dtype):
    return jax.ShapeDtypeStruct(shape, dtype)


def gelu_parts(u):
    z = jnp.abs(u)
    bell = jnp.exp(-0.5 * (u * u))
    below = 1.0 + TAIL_STEP * z
    t = pl.reciprocal(below, approx=True)
    t = t * (2.0 - below * t)
    poly = jnp.full_like(t, TAIL[-1])
    for coef in TAIL[-2::-1]:
        poly = poly * t + coef
    tail = bell * (poly * t)
    phi = jnp.where(u > 0.0, 1.0 - tail, tail)
    return u * phi, phi + u * (INV_SQRT_2PI * bell)


def project_kernel(n_x, *refs):
    x_refs, (w_ref, add_ref, out_ref) = refs[:n_x], refs[n_x:]
    out_ref[...] = (nn(stack_rows(x_refs), w_ref[...]) + add_ref[...]).astype(bf16)


def project(blocks, w_att, add, width):
    rows = sum(b.shape[0] for b in blocks)
    d = w_att.shape[0]
    return pl.pallas_call(
        functools.partial(project_kernel, len(blocks)),
        grid=(3,),
        in_specs=[pl.BlockSpec(b.shape, lambda i: (0, 0)) for b in blocks]
        + [pl.BlockSpec((d, width), lambda i: (0, i)), pl.BlockSpec((1, width), lambda i: (0, i))],
        out_specs=pl.BlockSpec((rows, width), lambda i: (0, i)),
        out_shape=struct((rows, 3 * width), bf16),
        compiler_params=params(32),
        cost_estimate=cost(6 * rows * d * width, 4 * MIB),
        name="project",
    )(*blocks, w_att, add)


def attend_kernel(scale, heads, q_ref, kn_ref, kf_ref, vn_ref, vf_ref, segq_ref, segk_ref, w_ref, *outs):
    att_ref, lse_ref, one_ref, two_ref = outs
    q = q_ref[...] * jnp.asarray(scale, bf16)
    rows, width = q.shape
    ks, vs = (kn_ref, kf_ref), (vn_ref, vf_ref)
    kv_rows = kn_ref.shape[0]
    lane = lax.broadcasted_iota(jnp.int32, (1, width), 1) // HEAD_DIM
    stat_lane = lax.broadcasted_iota(jnp.int32, (1, 128), 1)
    out = jnp.zeros((rows, width), f32)
    lse = jnp.zeros((rows, 128), f32)
    segq = segq_ref[...]
    masks = [
        jnp.where(segq == segk_ref[:, i * kv_rows : (i + 1) * kv_rows], 0.0, NEG) for i in range(2)
    ]
    for h in range(heads):
        hit = lane == h
        qh = jnp.where(hit, q, jnp.zeros_like(q))
        scores = [nt(qh, ks[i][...]) + masks[i] for i in range(2)]
        peak = jnp.maximum(*[jnp.max(s, axis=1, keepdims=True) for s in scores])
        exps = [jnp.exp(s - peak) for s in scores]
        total = sum(jnp.sum(e, axis=1, keepdims=True) for e in exps)
        inv = 1.0 / total
        head_out = sum(nn((exps[i] * inv).astype(bf16), vs[i][...]) for i in range(2))
        out = jnp.where(hit, head_out, out)
        lse = jnp.where(stat_lane == h, peak + jnp.log(total), lse)
    low = out.astype(bf16)
    att_ref[...] = low
    lse_ref[...] = lse
    part = nt(low, w_ref[...])
    half = rows // 2
    one_ref[...] = part[:half].astype(one_ref.dtype)
    two_ref[...] = part[half:].astype(two_ref.dtype)


def attend(proj_q, proj, seg_q, seg_k, w_att, scale, heads, one_type):
    rows, width = proj_q.shape[0], heads * HEAD_DIM
    kv_rows = proj[0].shape[0]
    d = w_att.shape[0]
    whole = lambda *at: (lambda i: at)
    return pl.pallas_call(
        functools.partial(attend_kernel, scale, heads),
        grid=(1,),
        in_specs=[pl.BlockSpec((rows, width), whole(0, 0))]
        + [pl.BlockSpec((kv_rows, width), whole(0, 1))] * 2
        + [pl.BlockSpec((kv_rows, width), whole(0, 2))] * 2
        + [
            pl.BlockSpec((rows, 1), whole(0, 0)),
            pl.BlockSpec((1, 2 * kv_rows), whole(0, 0)),
            pl.BlockSpec((d, width), whole(0, 3)),
        ],
        out_specs=[
            pl.BlockSpec((rows, width), whole(0, 0)),
            pl.BlockSpec((rows, 128), whole(0, 0)),
            pl.BlockSpec((rows // 2, d), whole(0, 0)),
            pl.BlockSpec((rows // 2, d), whole(0, 0)),
        ],
        out_shape=[
            struct((rows, width), bf16),
            struct((rows, 128), f32),
            struct((rows // 2, d), one_type),
            struct((rows // 2, d), bf16),
        ],
        compiler_params=params(40),
        cost_estimate=cost(16 * rows * kv_rows * 2 * width, 6 * MIB, rows * kv_rows * 2 * heads),
        name="attend",
    )(proj_q, *proj, *proj, seg_q, seg_k, w_att)


def attend_back_kernel(scale, heads, last, *refs):
    q_ref, kn_ref, kf_ref, vn_ref, vf_ref, segq_ref, segk_ref, lse_ref, a_ref, b_ref, w_ref = refs[:11]
    q = q_ref[...]
    rows, width = q.shape
    ks, vs = (kn_ref, kf_ref), (vn_ref, vf_ref)
    kv_rows = kn_ref.shape[0]
    if last:
        dqn_ref, sumq_ref, dk_in, dv_in, wq_ref = refs[11:16]
        near_ref, far_ref, sums_ref, one_ref, two_ref, dk_ref, dv_ref = refs[16:]
    else:
        dqn_ref, sumq_ref, dk_ref, dv_ref = refs[11:]
    lane = lax.broadcasted_iota(jnp.int32, (1, width), 1) // HEAD_DIM
    grad = nn(stack_rows((a_ref, b_ref)), w_ref[...]).astype(bf16)
    segq = segq_ref[...]
    masks = [
        jnp.where(segq == segk_ref[:, i * kv_rows : (i + 1) * kv_rows], 0.0, NEG) for i in range(2)
    ]
    sc = jnp.asarray(scale, bf16)
    zero = jnp.zeros_like(q)
    dq = jnp.zeros((rows, width), f32)
    for h in range(heads):
        hit = lane == h
        qh = jnp.where(hit, q, zero) * sc
        gh = jnp.where(hit, grad, zero)
        lse = lse_ref[:, h : h + 1]
        probs = [jnp.exp(nt(qh, ks[i][...]) + masks[i] - lse) for i in range(2)]
        d_probs = [nt(gh, vs[i][...]) for i in range(2)]
        dot_sum = sum(jnp.sum(p * g, axis=1, keepdims=True) for p, g in zip(probs, d_probs))
        dq_h = 0.0
        for i in range(2):
            low = (probs[i] * (d_probs[i] - dot_sum)).astype(bf16)
            at = pl.ds(i * kv_rows, kv_rows)
            d_k, d_v = tn(low, qh), tn(probs[i].astype(bf16), gh)
            if h > 0:
                d_k, d_v = d_k + dk_ref[at, :], d_v + dv_ref[at, :]
            elif last:
                d_k, d_v = d_k + dk_in[at, :], d_v + dv_in[at, :]
            dk_ref[at, :] = d_k
            dv_ref[at, :] = d_v
            dq_h = dq_h + nn(low, ks[i][...])
        dq = jnp.where(hit, dq_h, dq)
    dq = dq * scale
    sum_q = jnp.sum(dq, axis=0, keepdims=True)
    if not last:
        dqn_ref[...] = dq.astype(bf16)
        sumq_ref[...] = sum_q
        return
    sums_ref[0:1, :] = sum_q + sumq_ref[...]
    sums_ref[1:2, :] = jnp.sum(dv_ref[...], axis=0, keepdims=True)
    near_ref[:, :width] = dqn_ref[...]
    far_ref[:, :width] = dq.astype(bf16)
    for i, ref in enumerate((near_ref, far_ref)):
        at = pl.ds(i * kv_rows, kv_rows)
        ref[:, width : 2 * width] = dk_ref[at, :].astype(bf16)
        ref[:, 2 * width :] = dv_ref[at, :].astype(bf16)
    part = nt(far_ref[...], wq_ref[...]).astype(bf16)
    half = rows // 2
    one_ref[...] = part[:half]
    two_ref[...] = part[half:]


def attend_back(proj_q, proj, seg_q, seg_k, lse, one, w_att, scale, heads, earlier=None):
    rows, width = proj_q.shape[0], heads * HEAD_DIM
    kv_rows = proj[0].shape[0]
    d = w_att.shape[0]
    last = earlier is not None
    whole = lambda *at: (lambda i: at)
    in_specs = (
        [pl.BlockSpec((rows, width), whole(0, 0))]
        + [pl.BlockSpec((kv_rows, width), whole(0, 1))] * 2
        + [pl.BlockSpec((kv_rows, width), whole(0, 2))] * 2
        + [
            pl.BlockSpec((rows, 1), whole(0, 0)),
            pl.BlockSpec((1, 2 * kv_rows), whole(0, 0)),
            pl.BlockSpec((rows, 128), whole(0, 0)),
            pl.BlockSpec((rows // 2, d), whole(0, 0)),
            pl.BlockSpec((rows // 2, d), whole(0, 0)),
            pl.BlockSpec((d, width), whole(0, 3)),
        ]
    )
    args = [proj_q, *proj, *proj, seg_q, seg_k, lse, *one, w_att]
    acc = pltpu.VMEM((2 * kv_rows, width), f32)
    if last:
        in_specs += [
            pl.BlockSpec((rows, width), whole(0, 0)),
            pl.BlockSpec((1, width), whole(0, 0)),
            pl.BlockSpec((2 * kv_rows, width), whole(0, 0)),
            pl.BlockSpec((2 * kv_rows, width), whole(0, 0)),
            pl.BlockSpec((d, 3 * width), whole(0, 0)),
        ]
        args += [*earlier, w_att]
        out_shape = [
            struct((kv_rows, 3 * width), bf16),
            struct((kv_rows, 3 * width), bf16),
            struct((2, width), f32),
            struct((rows // 2, d), bf16),
            struct((rows // 2, d), bf16),
        ]
        scratch = [acc, acc]
    else:
        out_shape = [
            struct((rows, width), bf16),
            struct((1, width), f32),
            struct((2 * kv_rows, width), f32),
            struct((2 * kv_rows, width), f32),
        ]
        scratch = []
    return pl.pallas_call(
        functools.partial(attend_back_kernel, scale, heads, last),
        grid=(1,),
        in_specs=in_specs,
        out_specs=[pl.BlockSpec(o.shape, whole(0, 0)) for o in out_shape],
        out_shape=out_shape,
        scratch_shapes=scratch,
        compiler_params=params(48),
        cost_estimate=cost(40 * rows * kv_rows * 2 * width, 8 * MIB, rows * kv_rows * 2 * heads),
        name="attend_back",
    )(*args)


def ffn_kernel(a_ref, b_ref, up_ref, down_ref, bias_ref, act_ref, slope_ref, one_ref, two_ref, x, acc):
    step = pl.program_id(0)

    @pl.when(step == 0)
    def _():
        x[...] = stack_rows((a_ref, b_ref))

    value, slope = gelu_parts(nn(x[...], up_ref[...]) + bias_ref[...])
    low = value.astype(bf16)
    act_ref[...] = low
    slope_ref[...] = slope
    part = nt(low, down_ref[...])

    @pl.when(step == 0)
    def _():
        acc[...] = part

    @pl.when(step > 0)
    def _():
        acc[...] += part

    @pl.when(step == pl.num_programs(0) - 1)
    def _():
        half = acc.shape[0] // 2
        one_ref[...] = acc[:half].astype(one_ref.dtype)
        two_ref[...] = acc[half:].astype(two_ref.dtype)


def ffn(blocks, w_ud, bias, one_type, tile=256):
    rows, d = 2 * blocks[0].shape[0], w_ud.shape[0]
    ff = w_ud.shape[1] // 2
    steps = ff // tile
    fixed = lambda i: (0, 0)
    moving = lambda i: (0, i)
    return pl.pallas_call(
        ffn_kernel,
        grid=(steps,),
        in_specs=[
            pl.BlockSpec((rows // 2, d), fixed),
            pl.BlockSpec((rows // 2, d), fixed),
            pl.BlockSpec((d, tile), moving),
            pl.BlockSpec((d, tile), lambda i: (0, i + steps)),
            pl.BlockSpec((1, tile), moving),
        ],
        out_specs=[
            pl.BlockSpec((rows, tile), moving),
            pl.BlockSpec((rows, tile), moving),
            pl.BlockSpec((rows // 2, d), fixed),
            pl.BlockSpec((rows // 2, d), fixed),
        ],
        out_shape=[
            struct((rows, ff), bf16),
            struct((rows, ff), f32),
            struct((rows // 2, d), one_type),
            struct((rows // 2, d), bf16),
        ],
        scratch_shapes=[pltpu.VMEM((rows, d), bf16), pltpu.VMEM((rows, d), f32)],
        compiler_params=params(40),
        cost_estimate=cost(4 * rows * d * ff, 9 * MIB, rows * ff * 2),
        name="ffn",
    )(*blocks, w_ud, w_ud, bias)


def ffn_back_kernel(a_ref, b_ref, up_ref, down_ref, slope_ref, low_ref, sum_ref, one_ref, two_ref, x, acc):
    step = pl.program_id(0)

    @pl.when(step == 0)
    def _():
        x[...] = stack_rows((a_ref, b_ref))

    d_up = nn(x[...], down_ref[...]) * slope_ref[...]
    low = d_up.astype(bf16)
    low_ref[...] = low
    sum_ref[...] = jnp.sum(d_up, axis=0, keepdims=True)
    part = nt(low, up_ref[...])

    @pl.when(step == 0)
    def _():
        acc[...] = part

    @pl.when(step > 0)
    def _():
        acc[...] += part

    @pl.when(step == pl.num_programs(0) - 1)
    def _():
        half = acc.shape[0] // 2
        one_ref[...] = acc[:half].astype(one_ref.dtype)
        two_ref[...] = acc[half:].astype(two_ref.dtype)


def ffn_back(blocks, w_ud, slope, one_type, tile=256):
    rows, d = 2 * blocks[0].shape[0], w_ud.shape[0]
    ff = w_ud.shape[1] // 2
    steps = ff // tile
    fixed = lambda i: (0, 0)
    moving = lambda i: (0, i)
    return pl.pallas_call(
        ffn_back_kernel,
        grid=(steps,),
        in_specs=[
            pl.BlockSpec((rows // 2, d), fixed),
            pl.BlockSpec((rows // 2, d), fixed),
            pl.BlockSpec((d, tile), moving),
            pl.BlockSpec((d, tile), lambda i: (0, i + steps)),
            pl.BlockSpec((rows, tile), moving),
        ],
        out_specs=[
            pl.BlockSpec((rows, tile), moving),
            pl.BlockSpec((1, tile), moving),
            pl.BlockSpec((rows // 2, d), fixed),
            pl.BlockSpec((rows // 2, d), fixed),
        ],
        out_shape=[
            struct((rows, ff), bf16),
            struct((1, ff), f32),
            struct((rows // 2, d), one_type),
            struct((rows // 2, d), bf16),
        ],
        scratch_shapes=[pltpu.VMEM((rows, d), bf16), pltpu.VMEM((rows, d), f32)],
        compiler_params=params(40),
        cost_estimate=cost(4 * rows * d * ff, 9 * MIB),
        name="ffn_back",
    )(*blocks, w_ud, w_ud, slope)


def grad_kernel(n_d, order_ref, *refs):
    outs = refs[12:]
    tile = D // (2 * n_d)
    per = n_d // 2
    for g, out in enumerate(outs):
        for pair in range(0, per, 2):
            at = [pl.multiple_of(order_ref[g * per + pair + k] * tile, tile) for k in range(2)]
            col = 0
            for p in range(2):
                a_refs, (near, far) = refs[6 * p : 6 * p + 4], refs[6 * p + 4 : 6 * p + 6]
                width = near.shape[1]
                total = 0.0
                for half, b_ref in ((0, near), (2, far)):
                    sel = jnp.concatenate(
                        [
                            jnp.concatenate([a[:, pl.ds(s, tile)] for s in at], 1)
                            for a in a_refs[half : half + 2]
                        ],
                        0,
                    )
                    total = total + tn(sel, b_ref[...])
                for k in range(2):
                    out[pair + k, :, col : col + width] = total[k * tile : (k + 1) * tile].astype(bf16)
                col += width


def weight_grad(pairs, order, n_d):
    flat = [r for a, b in pairs for r in (*a, *b)]
    cols = sum(b[0].shape[1] for _, b in pairs)
    tile = D // (2 * n_d)
    per = n_d // 2
    rows = sum(b.shape[0] for b in pairs[0][1])
    if tile % 128 or per % 2:
        full = jnp.concatenate(
            [dot(jnp.concatenate(a, 0), jnp.concatenate(b, 0), 0, 0) for a, b in pairs], 1
        )
        tiles = jnp.take(full.astype(bf16).reshape(2 * n_d, tile, cols), order, axis=0)
        return [tiles[g * per : (g + 1) * per] for g in range(4)]
    vmem = pl.BlockSpec(memory_space=pltpu.VMEM)
    return pl.pallas_call(
        functools.partial(grad_kernel, n_d),
        in_specs=[pl.BlockSpec(memory_space=pltpu.SMEM)] + [vmem] * len(flat),
        out_specs=[vmem] * 4,
        out_shape=[struct((per, tile, cols), bf16)] * 4,
        compiler_params=params(48),
        cost_estimate=cost(2 * rows * D * cols, 12 * MIB),
        name="weight_grad",
    )(order, *flat)


def place_kernel(counts, dest_ref, *refs):
    ins, out_ref = refs[: len(counts)], refs[len(counts)]
    k = 0
    for ref, count in zip(ins, counts):
        for i in range(count):
            out_ref[dest_ref[k]] = ref[i]
            k += 1


def place_tiles(stacks, dest):
    counts = [s.shape[0] for s in stacks]
    total = sum(counts)
    rows, cols = stacks[0].shape[1:]
    vmem = pl.BlockSpec(memory_space=pltpu.VMEM)
    out = pl.pallas_call(
        functools.partial(place_kernel, counts),
        in_specs=[pl.BlockSpec(memory_space=pltpu.SMEM)] + [vmem] * len(stacks),
        out_specs=vmem,
        out_shape=struct((total, rows, cols), bf16),
        compiler_params=params(32),
        cost_estimate=cost(0, 4 * total * rows * cols),
        name="place_tiles",
    )(dest, *stacks)
    return out.reshape(total * rows, cols)


def dot(a, b, ca, cb):
    return lax.dot_general(a, b, (((ca,), (cb,)), ((), ())), preferred_element_type=f32)


def swap(a, axis):
    return lax.ppermute(a, axis, SWAP)


def flip_d(a, bit, n_d):
    return lax.ppermute(a, "d", [(i, i ^ (1 << bit)) for i in range(n_d)])


def transpose_home(a):
    return lax.ppermute(a, ("c", "zh"), [(0, 0), (1, 2), (2, 1), (3, 3)])


def after(a, *marks):
    return lax.optimization_barrier((a,) + marks)[0]


def share_rows(own):
    far = swap(own, "zl")
    near = swap(own, "c")
    far_near = swap(far, "c")
    return own, near, far, far_near


def sum_rows(near_own, near_other, far_own, far_other):
    chip_sum = far_own.astype(f32) + swap(far_other, "c").astype(f32)
    crossed = swap(chip_sum.astype(bf16), "zl")
    other = swap(near_other, "c")
    return near_own + other.astype(f32) + crossed.astype(f32)


def masks_of(order):
    masks = [0]
    for bit in order:
        masks = masks + [m ^ (1 << bit) for m in masks]
    return masks


class Gather:
    def __init__(self, piece, pos, n_d):
        self.piece, self.pos, self.n_d = piece, pos, n_d
        self.bits = list(range(n_d.bit_length() - 1))

    def cross(self, *marks):
        _, c, zh, _ = self.pos
        piece = after(self.piece, *marks) if marks else self.piece
        self.crossed = swap(piece, "zh")
        same = c == zh
        self.one = [jnp.where(same, piece, self.crossed)[None]]
        self.two = [swap(jnp.where(same, self.crossed, piece), "c")[None]]
        self.step = 0

    def spread(self, *marks):
        one, two = (p[0] if len(p) == 1 else jnp.concatenate(p, 0) for p in (self.one, self.two))
        if marks:
            one, two = lax.optimization_barrier((one, two) + marks)[:2]
        bit_one, bit_two = self.bits[self.step], self.bits[-1 - self.step]
        self.got = flip_d(one, bit_one, self.n_d)
        self.one = [one, self.got]
        self.two = [two, flip_d(two, bit_two, self.n_d)]
        self.step += 1

    def whole(self):
        while self.step < len(self.bits):
            self.spread()
        d, c, _, _ = self.pos
        dest = [2 * jnp.bitwise_xor(d, m) + c for m in masks_of(self.bits)]
        dest += [2 * jnp.bitwise_xor(d, m) + 1 - c for m in masks_of(self.bits[::-1])]
        return place_tiles(self.one + self.two, jnp.stack(dest).astype(jnp.int32))


def grad_order(pos, n_d):
    d, c, _, _ = pos
    bits = list(range(n_d.bit_length() - 1))
    half = n_d // 2
    order = []
    for core, masks in ((c, masks_of(bits)), (1 - c, masks_of(bits[::-1]))):
        order += [2 * jnp.bitwise_xor(d, m) + core for m in masks[half:] + masks[:half]]
    return jnp.stack(order).astype(jnp.int32)


def reduce_weights(stacks, pos, n_d):
    _, c, zh, _ = pos
    bits = list(range(n_d.bit_length() - 1))
    sums = []
    for send, keep, order in ((*stacks[:2], bits[::-1]), (*stacks[2:], bits)):
        for step, bit in enumerate(order):
            got = flip_d(send, bit, n_d)
            total = keep.astype(f32) + got.astype(f32)
            half = total.shape[0] // 2
            if step + 1 < len(order):
                send, keep = total[half:].astype(bf16), total[:half]
        sums.append(total[0])
    first, second = sums
    other = swap(second.astype(bf16), "c").astype(f32)
    same = c == zh
    keep = jnp.where(same, first, other)
    send = jnp.where(same, other, first)
    return keep + swap(send.astype(bf16), "zh").astype(f32)


def gather_small(own, pos, n_d):
    d, c, zh, zl = pos
    cur = own
    for axis, me in (("zl", zl), ("zh", zh), ("c", c)):
        got = swap(cur, axis)
        cur = jnp.where(me == 0, jnp.concatenate([cur, got]), jnp.concatenate([got, cur]))
    for bit in range(n_d.bit_length() - 1):
        got = flip_d(cur, bit, n_d)
        mine = jnp.bitwise_and(jnp.right_shift(d, bit), 1)
        cur = jnp.where(mine == 0, jnp.concatenate([cur, got]), jnp.concatenate([got, cur]))
    return cur


def pick(a, at, axis):
    return lax.dynamic_index_in_dim(a, at, axis, keepdims=False)


def reduce_small(full, pos, n_d):
    d, c, zh, zl = pos
    cur = full
    for bit in reversed(range(n_d.bit_length() - 1)):
        mine = jnp.bitwise_and(jnp.right_shift(d, bit), 1)
        view = cur.reshape(2, -1, full.shape[1])
        cur = pick(view, mine, 0) + flip_d(pick(view, 1 - mine, 0), bit, n_d)
    for axis, me in (("c", c), ("zh", zh), ("zl", zl)):
        view = cur.reshape(2, -1, full.shape[1])
        cur = pick(view, me, 0) + swap(pick(view, 1 - me, 0), axis)
    return cur


def norm_parts(v):
    centred = v - jnp.mean(v, axis=-1, keepdims=True)
    r = lax.rsqrt(jnp.mean(centred * centred, axis=-1, keepdims=True) + EPS)
    return centred * r, r


def column_sum(a):
    return jnp.sum(a, axis=0, keepdims=True)


def norm_back(n, r, gain, d_out):
    dn = d_out * gain
    dv = r * (
        dn - jnp.mean(dn, axis=-1, keepdims=True) - n * jnp.mean(dn * n, axis=-1, keepdims=True)
    )
    return dv, column_sum(d_out * n), column_sum(d_out)


def group_maps(own_len, dealt_local, group_rows):
    slot_range = jnp.arange(SEQ_GRP, dtype=jnp.int32)
    own_end = jnp.cumsum(own_len)
    own_start = own_end - own_len
    pick_table = dealt_local[:, None] == slot_range[None, :]
    dealt_len = jnp.sum(jnp.where(pick_table, own_len[None, :], 0), axis=1)
    dealt_src = jnp.sum(jnp.where(pick_table, own_start[None, :], 0), axis=1)
    dealt_end = jnp.cumsum(dealt_len)
    dealt_begin = dealt_end - dealt_len
    position = jnp.arange(group_rows, dtype=jnp.int32)
    segments = jnp.sum((position[:, None] >= dealt_end[None, :]).astype(jnp.int32), axis=1)
    seg_hit = segments[:, None] == slot_range[None, :]
    source = jnp.sum(
        jnp.where(seg_hit, dealt_src[None, :] - dealt_begin[None, :] + position[:, None], 0), axis=1
    ) + jnp.where(segments == SEQ_GRP, position, 0)
    return (segments, source)


def body(tokens, cotangent, lengths, order, w_qkv, w_out, w_up, w_down, gains, biases, up_bias):
    rows = tokens.shape[0]
    n_d = lax.axis_size("d")
    n_dev = n_d * 8
    head_width = D // 4
    heads = head_width // HEAD_DIM
    ff_width = FF // 4
    piece = D // (2 * n_d)
    scale = HEAD_DIM ** (-0.5)
    d, c, zh, zl = (lax.axis_index(a) for a in ALL)
    pos = (d, c, zh, zl)
    slot = 2 * c + zl
    block_ids = [jnp.bitwise_xor(slot, m) for m in (0, 2, 1, 3)]

    def chunk(layer, which):
        if which == 0:
            return jnp.concatenate([w_qkv[layer].reshape(piece, -1), w_out[layer].T], 1)
        return jnp.concatenate([w_up[layer], w_down[layer].T], 1)

    raw = transpose_home(tokens)
    g_a0, g_f0, g_a1, g_f1 = (Gather(chunk(l, k), pos, n_d) for l in range(LAYERS) for k in range(2))
    g_a0.cross()
    small_all = gather_small(
        jnp.concatenate(
            [gains.reshape(1, -1), biases.reshape(1, -1), up_bias.reshape(1, -1)], 1
        ),
        pos,
        n_d,
    )
    g_f0.cross(g_a0.crossed)
    w_a0 = g_a0.whole()
    weights = [[w_a0, None], [None, None]]
    width = D // n_dev
    up_width = FF // n_dev
    n_vec = LAYERS * 8
    vectors = small_all[:, : n_vec * width].reshape(n_dev, n_vec, width)
    vectors = vectors.transpose(1, 0, 2).reshape(n_vec, D)
    ups = small_all[:, n_vec * width :].reshape(n_dev, LAYERS, up_width)
    ups = ups.transpose(1, 0, 2).reshape(LAYERS, FF)

    def gain(layer, i):
        return vectors[2 * layer + i][None]

    def bias(layer, i):
        return vectors[2 * LAYERS + 6 * layer + i][None]

    def part_of(row, size):
        return lax.dynamic_slice(row, (0, slot * size), (1, size))

    seq_base = (d * 2 + zh) * SEQ_GRP
    own_len = lax.dynamic_slice_in_dim(lengths, seq_base, SEQ_GRP)
    dealt_local = lax.dynamic_slice_in_dim(order, seq_base, SEQ_GRP) - seq_base
    segments, source = group_maps(own_len, dealt_local, 4 * rows)
    seg = jnp.concatenate([lax.dynamic_slice_in_dim(segments, b * rows, rows) for b in block_ids])
    src = jnp.concatenate([lax.dynamic_slice_in_dim(source, b * rows, rows) for b in block_ids])
    src_x = jnp.bitwise_xor(src // rows, slot)
    src_at = (2 * (src_x % 2) + src_x // 2) * rows + src % rows
    deal = (src_at[:, None] == jnp.arange(4 * rows, dtype=jnp.int32)[None, :]).astype(bf16)
    valid = (seg[:rows] < SEQ_GRP).astype(f32)[:, None]
    seg_col, seg_row = seg[:, None], seg[None, :]
    seg_near, seg_far = seg_col[: 2 * rows], seg_col[2 * rows :]
    tile_order = grad_order(pos, n_d)

    raw_all = jnp.concatenate(share_rows(raw), 0)
    blocks = tuple(
        dot(deal[i * rows : (i + 1) * rows], raw_all, 1, 0).astype(bf16) for i in range(4)
    )
    hidden = blocks[0].astype(f32)

    kept = []
    for layer in range(LAYERS):
        first = layer == 0
        w_att = weights[layer][0]
        add = jnp.concatenate(
            [
                part_of(bias(layer, 0), head_width),
                jnp.zeros((1, head_width), f32),
                part_of(bias(layer, 1), head_width),
            ],
            1,
        )
        proj_near = project(blocks[:2], w_att, add, head_width)
        proj_far = project(blocks[2:], w_att, add, head_width)
        proj = (proj_near, proj_far)
        if first:
            g_f0.spread(w_att)
            g_f0.spread(proj_far)
            g_a1.cross(proj_far)
        else:
            g_f1.spread(proj_far)
        att_far, lse_far, far_own, far_other = attend(
            proj_far, proj, seg_far, seg_row, w_att, scale, heads, bf16
        )
        att_near, lse_near, near_own, near_other = attend(
            proj_near, proj, seg_near, seg_row, w_att, scale, heads, f32
        )
        pre_one = hidden + sum_rows(near_own, near_other, far_own, far_other) + bias(layer, 2)
        n_one, r_one = norm_parts(pre_one)
        normed = n_one * gain(layer, 0) + bias(layer, 3)
        normed_low = normed.astype(bf16)
        if first:
            g_f1.cross(normed_low)
            g_a1.spread(normed_low)
            weights[0][1] = g_f0.whole()
        else:
            weights[1][1] = g_f1.whole()
        w_ud = weights[layer][1]
        n_blocks = share_rows(normed_low)
        u_bias = part_of(ups[layer : layer + 1], ff_width)
        act_near, slope_near, near_own, near_other = ffn(n_blocks[:2], w_ud, u_bias, f32)
        if first:
            g_a1.spread(act_near)
        act_far, slope_far, far_own, far_other = ffn(n_blocks[2:], w_ud, u_bias, bf16)
        if first:
            g_f1.spread(far_own)
        pre_two = normed + sum_rows(near_own, near_other, far_own, far_other) + bias(layer, 4)
        n_two, r_two = norm_parts(pre_two)
        hidden = n_two * gain(layer, 1) + bias(layer, 5)
        hidden_low = hidden.astype(bf16)
        kept.append(
            dict(
                x=blocks, proj=proj, lse=(lse_near, lse_far), att=(att_near, att_far),
                n_one=n_one, r_one=r_one, n=n_blocks, slope=(slope_near, slope_far),
                act=(act_near, act_far), n_two=n_two, r_two=r_two,
            )
        )
        if first:
            weights[1][0] = g_a1.whole()
            blocks = share_rows(hidden_low)
    mixed = transpose_home(hidden_low)

    raw_cot = jnp.concatenate(share_rows(transpose_home(cotangent)), 0)
    grad_y = dot(deal[:rows], raw_cot, 1, 0) * valid
    reduced = [None] * LAYERS
    vector_sums = [None] * LAYERS
    up_sums = [None] * LAYERS

    def spot(vec, full):
        return lax.dynamic_update_slice(jnp.zeros((1, full), f32), vec, (0, slot * vec.shape[1]))

    for layer in reversed(range(LAYERS)):
        w_att, w_ud = weights[layer]
        s = kept[layer]
        d_two, g_gain2, g_shift2 = norm_back(s["n_two"], s["r_two"], gain(layer, 1), grad_y)
        two = share_rows(d_two.astype(bf16))
        up_near, sum_near, near_own, near_other = ffn_back(two[:2], w_ud, s["slope"][0], f32)
        up_far, sum_far, far_own, far_other = ffn_back(two[2:], w_ud, s["slope"][1], bf16)
        d_normed = d_two + sum_rows(near_own, near_other, far_own, far_other)
        d_one, g_gain1, g_shift1 = norm_back(s["n_one"], s["r_one"], gain(layer, 0), d_normed)
        one = share_rows(d_one.astype(bf16))
        g_ff = weight_grad(((s["n"], (up_near, up_far)), (two, s["act"])), tile_order, n_d)
        earlier = attend_back(
            s["proj"][0], s["proj"], seg_near, seg_row, s["lse"][0], one[:2], w_att, scale, heads
        )
        d_near, d_far, sums, far_own, far_other = attend_back(
            s["proj"][1], s["proj"], seg_far, seg_row, s["lse"][1], one[2:], w_att, scale, heads,
            earlier,
        )
        w_q = w_att[:, : 3 * head_width]
        near_own = dot(d_near[:rows], w_q, 1, 1)
        near_other = dot(d_near[rows:], w_q, 1, 1).astype(bf16)
        grad_y = d_one + sum_rows(near_own, near_other, far_own, far_other)
        g_att = weight_grad(((s["x"], (d_near, d_far)), (one, s["att"])), tile_order, n_d)
        reduced[layer] = (reduce_weights(g_att, pos, n_d), reduce_weights(g_ff, pos, n_d))
        vector_sums[layer] = (
            [g_gain1, g_gain2],
            [
                spot(sums[0:1], D), spot(sums[1:2], D), column_sum(d_one),
                g_shift1, column_sum(d_two), g_shift2,
            ],
        )
        up_sums[layer] = spot(sum_near + sum_far, FF)
    tokens_grad = transpose_home(grad_y.astype(bf16)).astype(f32)

    terms = jnp.concatenate(
        [g for s in vector_sums for g in s[0]] + [b for s in vector_sums for b in s[1]], 0
    )
    small_terms = jnp.concatenate(
        [
            terms.reshape(n_vec, n_dev, width).transpose(1, 0, 2).reshape(n_dev, n_vec * width),
            jnp.concatenate(up_sums, 0)
            .reshape(LAYERS, n_dev, up_width)
            .transpose(1, 0, 2)
            .reshape(n_dev, LAYERS * up_width),
        ],
        1,
    )
    small_sum = reduce_small(small_terms, pos, n_d)
    n_gain = LAYERS * 2 * width
    g_gains = small_sum[:, :n_gain].reshape(LAYERS, 2, width)
    g_biases = small_sum[:, n_gain : n_vec * width].reshape(LAYERS, 6, width)
    g_upb = small_sum[:, n_vec * width :].reshape(LAYERS, up_width)
    g_qkv = jnp.stack([r[0][:, : 3 * head_width].reshape(piece, 3, head_width) for r in reduced])
    g_out = jnp.stack([r[0][:, 3 * head_width :].T for r in reduced])
    g_up = jnp.stack([r[1][:, :ff_width] for r in reduced])
    g_down = jnp.stack([r[1][:, ff_width:].T for r in reduced])
    return mixed, tokens_grad, g_qkv, g_out, g_up, g_down, g_gains, g_biases, g_upb


def solution(mesh):
    n_dp, n_t = mesh.shape["dp"], mesh.shape["tensor"]
    fine = Mesh(mesh.devices.reshape(n_dp // 2, 2, n_t // 2, 2), ALL)
    dp, t = ("d", "c"), ("zh", "zl")
    return jax.shard_map(
        body,
        mesh=fine,
        in_specs=(
            P(ALL, None),
            P(ALL, None),
            P(),
            P(),
            P(None, dp, None, t),
            P(None, t, dp),
            P(None, dp, t),
            P(None, t, dp),
            P(None, None, ALL),
            P(None, None, ALL),
            P(None, ALL),
        ),
        out_specs=(
            P(ALL, None),
            P(ALL, None),
            P(None, dp, None, t),
            P(None, t, dp),
            P(None, dp, t),
            P(None, t, dp),
            P(None, None, ALL),
            P(None, None, ALL),
            P(None, ALL),
        ),
        check_vma=False,
    )
```

time: 891 us -> 706 us (0.79)
  matrix products: 200 us -> 15.2 us
  Pallas kernels: 0 us -> 167 us
  waiting for transfers between devices: 340 us -> 234 us
  local copies, waits for them, and re-layouts: 126 us -> 104 us
  starting transfers between devices: 111 us -> 92.6 us
  other arithmetic: 93.7 us -> 78.3 us
    pallas_call x0 -> x28, Pallas kernels: none -> 167 us  [the longest x4 42.3 us: attend_back(): pl.pallas_call(functools.partial(attend_back_kernel, scale, heads, last),...]
    dot_general x50 -> x9, matrix products: 115 us -> 15.2 us  [dot(): lax.dot_general(a, b, (((ca,), (cb,)), ((), ())), preferred_element_type=...]
    ppermute x52 -> x36, waiting for transfers between devices: 152 us -> 64.1 us  [flip_d(): return lax.ppermute(a, 'd', [(i, i ^ 1 << bit) for i in range(n_d)])]
    dot_general x20 -> x0, matrix products: 61 us -> none  [the longest x4 24.9 us: attend_back(): jnp.einsum('bhd,khd->hbk', grad, values, preferred_element_type=f32)]
    dynamic_slice x29 -> x4, local copies, waits for them, and re-layouts: 24.6 us -> 0.02 us  [part_of(): return lax.dynamic_slice(row, (0, slot * size), (1, size))]
    sub x4 -> x0, matrix products: 23.5 us -> none  [attend(): exponent = jnp.exp(masked - peak)]
    ppermute x81 -> x73, waiting for transfers between devices: 189 us -> 169 us  [swap(): return lax.ppermute(a, axis, SWAP)]
    convert_element_type x7 -> x3, other arithmetic: 19.4 us -> 0.76 us  [the longest x2 0.51 us: body(): normed_low = normed.astype(bf16)]
  transfers between devices with their start and end apart: 137 -> 113, of which waited for: 56 -> 32; matrix products, arithmetic and copies ran while one was open for 40% -> 20% of each run, Pallas kernels for 0% -> 22%
where the time goes in v2:
time: 706 us; the launch traced here: 695 us
  waiting for transfers between devices  234 us (33%)
  Pallas kernels  167 us (24%)
  local copies, waits for them, and re-layouts  104 us (15%)
  starting transfers between devices  92.6 us (13%)
  other arithmetic  78.3 us (11%)
  matrix products  15.2 us (2%)
    ppermute x73, waiting for transfers between devices, swap(): return lax.ppermute(a, axis, SWAP)  169 us
    unnamed x428, local copies, waits for them, and re-layouts  64.8 us
    ppermute x36, waiting for transfers between devices, flip_d(): return lax.ppermute(a, 'd', [(i, i ^ 1 << bit) for i in range(n_d)])  64.1 us
    pallas_call x4, Pallas kernels, attend_back(): pl.pallas_call(functools.partial(attend_back_kernel, scale, heads, last),...  42.3 us
    ppermute x73, starting transfers between devices, swap(): return lax.ppermute(a, axis, SWAP)  41.1 us
    ppermute x36, starting transfers between devices, flip_d(): return lax.ppermute(a, 'd', [(i, i ^ 1 << bit) for i in range(n_d)])  41 us
    pallas_call x4, Pallas kernels, ffn(): pl.pallas_call(ffn_kernel, grid=(steps,), in_specs=[pl.BlockSpec((rows //...  38.4 us
    pallas_call x4, Pallas kernels, ffn_back(): pl.pallas_call(ffn_back_kernel, grid=(steps,), in_specs=[pl.BlockSpec((ro...  30.5 us
  transfers between devices with their start and end apart: 113, of which 32 were waited for; matrix products, arithmetic and copies ran while one was open for 20% of the time, Pallas kernels for 22%

profile of v2, /device:TPU:0, one launch (start us, length us, event | category | flops | bytes accessed | tf_op | source)
XLA Modules:
  0.0 694.9 jit_solution(4055983784501712890)
XLA Ops:
  3.0 3.0 collective-permute-start.10
  6.0 5.4 collective-permute-start
  19.9 3.0 collective-permute-start.11
  23.5 11.4 %collective-permute-done.11 = f32[2,768]{1,0:T(2,128)S(1)} collective-permute-done((f32[2,768]{1,0:T(2,128)S(1)}, f32[2,768]{1,0:T(2,128)S(1)}, u32[]{:S(2)}, u32[]{:S(2)}) %collective-permute-start.11) | collective-permute-done | bytes 6176 | tf_op jit(solution)/shard_map/ppermute | solution.py:495
  56.0 2.8 collective-permute-done.2
  61.9 2.5 collective-permute-done.6.refs_1_
  74.0 4.6 attend.5
  78.7 6.4 collective-permute-done.19
  86.1 4.6 attend.4
  96.8 11.3 %collective-permute-done.17 = bf16[256,1024]{1,0:T(8,128)(2,1)} collective-permute-done((bf16[256,1024]{1,0:T(8,128)(2,1)}, bf16[256,1024]{1,0:T(8,128)(2,1)}, u32[]{:S(2)}, u32[]{:S(2)}) %collective-permute-start.17) | collective-permute-done | bytes 524320 | tf_op jit(solution)/shard_map/ppermute | solution.py:495
  113.3 10.1 %collective-permute-done.26.a_ref.refs_2_ = bf16[256,1024]{1,0:T(8,128)(2,1)} collective-permute-done((bf16[256,1024]{1,0:T(8,128)(2,1)S(1)}, bf16[256,1024]{1,0:T(8,128)(2,1)}, u32[]{:S(2)}, u32[]{:S(2)}) %collective-permute-start.26) | collective-permute-done | bytes 524320 | tf_op jit(solution)/shard_map/ppermute | solution.py:495
  124.1 12.3 %collective-permute-done.23.refs_1_ = bf16[2,128,2048]{2,1,0:T(8,128)(2,1)} collective-permute-done((bf16[2,128,2048]{2,1,0:T(8,128)(2,1)S(1)}, bf16[2,128,2048]{2,1,0:T(8,128)(2,1)}, u32[]{:S(2)}, u32[]{:S(2)}) %collective-permute-start.23) | collective-permute-done | bytes 1048608 | tf_op jit(solution)/shard_map/ppermute | solution.py:499
  138.5 11.2 %ffn.5 = (bf16[512,1024]{1,0:T(8,128)(2,1)S(1)}, f32[512,1024]{1,0:T(8,128)S(1)}, bf16[256,1024]{1,0:T(8,128)(2,1)S(1)}, bf16[256,1024]{1,0:T(8,128)(2,1)}) custom-call(bf16[256,1024]{1,0:T(8,128)(2,1)} %collective-permute-done.26.a_ref.refs_2_, bf16[256,1024]{1,0:T(8,128)(2,1)S(1)} %collective-permute-done.27.b_ref.refs_3_, ...), custom_call_target="tpu_custom_call" | custom-call | flops 2147483648 | bytes 9437184 | tf_op jit(solution)/shard_map/ffn/pallas_call | solution.py:322
  153.5 2.2 copy-done.1
  155.7 9.5 %ffn.4 = (bf16[512,1024]{1,0:T(8,128)(2,1)S(1)}, f32[512,1024]{1,0:T(8,128)S(1)}, f32[256,1024]{1,0:T(8,128)S(1)}, bf16[256,1024]{1,0:T(8,128)(2,1)S(1)}) custom-call(bf16[256,1024]{1,0:T(8,128)(2,1)S(1)} %fusion.57.a_ref.refs_0_, bf16[256,1024]{1,0:T(8,128)(2,1)} %collective-permute-done.18.b_ref.refs_1_, bf16[1024,2048]{1,0:T(8,128)(2,1)S(1)} %bitcast.149, ...), custom_call_target="tpu_custom_call" | custom-call | flops 2147483648 | bytes 9437184 | tf_op jit(solution)/shard_map/ffn/pallas_call | solution.py:322
  166.8 2.2 add_convert_fusion.7
  174.3 9.1 %collective-permute-done.29 = bf16[256,1024]{1,0:T(8,128)(2,1)} collective-permute-done((bf16[256,1024]{1,0:T(8,128)(2,1)}, bf16[256,1024]{1,0:T(8,128)(2,1)}, u32[]{:S(2)}, u32[]{:S(2)}) %collective-permute-start.29) | collective-permute-done | bytes 524320 | tf_op jit(solution)/shard_map/ppermute | solution.py:495
  191.0 4.5 collective-permute-done.34
  198.1 11.3 %collective-permute-done.37.refs_0_.refs_2_ = bf16[256,1024]{1,0:T(8,128)(2,1)S(1)} collective-permute-done((bf16[256,1024]{1,0:T(8,128)(2,1)S(1)}, bf16[256,1024]{1,0:T(8,128)(2,1)S(1)}, u32[]{:S(2)}, u32[]{:S(2)}) %collective-permute-start.37) | collective-permute-done | bytes 524320 | tf_op jit(solution)/shard_map/ppermute | solution.py:495
  209.4 2.9 collective-permute-done.43
  216.8 4.6 attend.7
  225.6 4.6 attend.6
  232.5 4.9 collective-permute-done.45
  242.2 4.7 collective-permute-done.41
  249.5 13.3 %collective-permute-done.50.a_ref.refs_2_ = bf16[256,1024]{1,0:T(8,128)(2,1)S(1)} collective-permute-done((bf16[256,1024]{1,0:T(8,128)(2,1)S(1)}, bf16[256,1024]{1,0:T(8,128)(2,1)S(1)}, u32[]{:S(2)}, u32[]{:S(2)}) %collective-permute-start.50) | collective-permute-done | bytes 524320 | tf_op jit(solution)/shard_map/ppermute | solution.py:495
  266.8 9.0 %ffn.7 = (bf16[512,1024]{1,0:T(8,128)(2,1)S(1)}, f32[512,1024]{1,0:T(8,128)S(1)}, bf16[256,1024]{1,0:T(8,128)(2,1)S(1)}, bf16[256,1024]{1,0:T(8,128)(2,1)S(1)}) custom-call(bf16[256,1024]{1,0:T(8,128)(2,1)S(1)} %collective-permute-done.50.a_ref.refs_2_, bf16[256,1024]{1,0:T(8,128)(2,1)S(1)} %collective-permute-done.51.b_ref.refs_3_, ...), custom_call_target="tpu_custom_call" | custom-call | flops 2147483648 | bytes 9437184 | tf_op jit(solution)/shard_map/ffn/pallas_call | solution.py:322
  279.9 8.6 %ffn.6 = (bf16[512,1024]{1,0:T(8,128)(2,1)S(1)}, f32[512,1024]{1,0:T(8,128)S(1)}, f32[256,1024]{1,0:T(8,128)S(1)}, bf16[256,1024]{1,0:T(8,128)(2,1)S(1)}) custom-call(bf16[256,1024]{1,0:T(8,128)(2,1)S(1)} %fusion.59.a_ref.refs_0_, bf16[256,1024]{1,0:T(8,128)(2,1)S(1)} %collective-permute-done.42.b_ref.refs_1_, bf16[1024,2048]{1,0:T(8,128)(2,1)S(1)} %bitcast.157, ...), custom_call_target="tpu_custom_call" | custom-call | flops 2147483648 | bytes 9437184 | tf_op jit(solution)/shard_map/ffn/pallas_call | solution.py:322
  293.9 11.8 %collective-permute-done.53 = bf16[256,1024]{1,0:T(8,128)(2,1)} collective-permute-done((bf16[256,1024]{1,0:T(8,128)(2,1)}, bf16[256,1024]{1,0:T(8,128)(2,1)}, u32[]{:S(2)}, u32[]{:S(2)}) %collective-permute-start.53) | collective-permute-done | bytes 524320 | tf_op jit(solution)/shard_map/ppermute | solution.py:495
  305.7 2.1 fusion.96
  308.1 2.4 multiply_reduce_fusion
  314.5 11.5 %collective-permute-done.61.a_ref.refs_8_ = bf16[256,1024]{1,0:T(8,128)(2,1)} collective-permute-done((bf16[256,1024]{1,0:T(8,128)(2,1)S(1)}, bf16[256,1024]{1,0:T(8,128)(2,1)}, u32[]{:S(2)}, u32[]{:S(2)}) %collective-permute-start.61) | collective-permute-done | bytes 524320 | tf_op jit(solution)/shard_map/ppermute | solution.py:495
  326.9 2.2 copy-done.5
  331.8 6.7 ffn_back.4
  340.3 8.7 %ffn_back.5 = (bf16[512,1024]{1,0:T(8,128)(2,1)S(1)}, f32[1,1024]{1,0:T(1,128)S(1)}, bf16[256,1024]{1,0:T(8,128)(2,1)S(1)}, bf16[256,1024]{1,0:T(8,128)(2,1)}) custom-call(bf16[256,1024]{1,0:T(8,128)(2,1)} %collective-permute-done.61.a_ref.refs_8_, bf16[256,1024]{1,0:T(8,128)(2,1)} %collective-permute-done.62.b_ref.refs_9_, ...), custom_call_target="tpu_custom_call" | custom-call | flops 2147483648 | bytes 9437184 | tf_op jit(solution)/shard_map/ffn_back/pallas_call | solution.py:385
  350.1 8.3 %weight_grad.7 = (bf16[2,128,2048]{2,1,0:T(8,128)(2,1)S(1)}, bf16[2,128,2048]{2,1,0:T(8,128)(2,1)}, bf16[2,128,2048]{2,1,0:T(8,128)(2,1)}, bf16[2,128,2048]{2,1,0:T(8,128)(2,1)}) custom-call(s32[8]{0:T(128)S(1)} %stack.116.order_ref, bf16[256,1024]{1,0:T(8,128)(2,1)S(1)} %fusion.59.a_ref.refs_0_, bf16[256,1024]{1,0:T(8,128)(2,1)S(1)} %copy-done.55, ...), custom_call_target="tpu_custom_call" | custom-call | flops 4294967296 | bytes 12582912 | tf_op jit(solution)/shard_map/weight_grad/pallas_call | solution.py:453
  362.6 2.9 collective-permute-start.63
  369.9 15.4 %collective-permute-done.104 = bf16[2,128,2048]{2,1,0:T(8,128)(2,1)} collective-permute-done((bf16[2,128,2048]{2,1,0:T(8,128)(2,1)}, bf16[2,128,2048]{2,1,0:T(8,128)(2,1)}, u32[]{:S(2)}, u32[]{:S(2)}) %collective-permute-start.104) | collective-permute-done | bytes 1048608 | tf_op jit(solution)/shard_map/ppermute | solution.py:499
  398.8 5.6 collective-permute-done.65.refs_8_
  407.0 9.0 %attend_back.4 = (bf16[512,256]{1,0:T(8,128)(2,1)S(1)}, f32[1,256]{1,0:T(1,128)S(1)}, f32[1024,256]{1,0:T(8,128)S(1)}, f32[1024,256]{1,0:T(8,128)S(1)}) custom-call(bf16[512,768]{1,0:T(8,128)(2,1)S(1)} %copy-done.29, bf16[512,768]{1,0:T(8,128)(2,1)S(1)} %copy-done.29, bf16[512,768]{1,0:T(8,128)(2,1)S(1)} %copy-done.31, bf16[512,768]{1,0:T(8,128)(2,1)S(1)} %copy-done.29, ...), custom_call_target="tpu_custom_call" | custom-call | flops 5368709120 | bytes 8388608 | tf_op jit(solution)/shard_map/attend_back/pallas_call | solution.py:275
  417.9 11.7 %attend_back.5 = (bf16[512,768]{1,0:T(8,128)(2,1)S(1)}, bf16[512,768]{1,0:T(8,128)(2,1)S(1)}, f32[2,256]{1,0:T(2,128)S(1)}, bf16[256,1024]{1,0:T(8,128)(2,1)S(1)}, bf16[256,1024]{1,0:T(8,128)(2,1)S(1)}) custom-call(bf16[512,768]{1,0:T(8,128)(2,1)S(1)} %copy-done.31, bf16[512,768]{1,0:T(8,128)(2,1)S(1)} %copy-done.29, bf16[512,768]{1,0:T(8,128)(2,1)S(1)} %copy-done.31, ...), custom_call_target="tpu_custom_call" | custom-call | flops 5368709120 | bytes 8388608 | tf_op jit(solution)/shard_map/attend_back/pallas_call | solution.py:275
  429.8 2.9 fusion.49
  432.7 2.2 collective-permute-start.107
  438.0 4.9 weight_grad.5
  450.3 12.1 %collective-permute-done.70 = bf16[256,1024]{1,0:T(8,128)(2,1)} collective-permute-done((bf16[256,1024]{1,0:T(8,128)(2,1)}, bf16[256,1024]{1,0:T(8,128)(2,1)}, u32[]{:S(2)}, u32[]{:S(2)}) %collective-permute-start.70) | collective-permute-done | bytes 524320 | tf_op jit(solution)/shard_map/ppermute | solution.py:495
  462.4 3.1 multiply_reduce_fusion.2
  471.7 7.9 %collective-permute-done.73.a_ref.refs_8_ = bf16[256,1024]{1,0:T(8,128)(2,1)S(1)} collective-permute-done((bf16[256,1024]{1,0:T(8,128)(2,1)S(1)}, bf16[256,1024]{1,0:T(8,128)(2,1)S(1)}, u32[]{:S(2)}, u32[]{:S(2)}) %collective-permute-start.73) | collective-permute-done | bytes 524320 | tf_op jit(solution)/shard_map/ppermute | solution.py:495
  482.5 7.5 %ffn_back.7 = (bf16[512,1024]{1,0:T(8,128)(2,1)S(1)}, f32[1,1024]{1,0:T(1,128)S(1)}, bf16[256,1024]{1,0:T(8,128)(2,1)S(1)}, bf16[256,1024]{1,0:T(8,128)(2,1)}) custom-call(bf16[256,1024]{1,0:T(8,128)(2,1)S(1)} %collective-permute-done.73.a_ref.refs_8_, bf16[256,1024]{1,0:T(8,128)(2,1)S(1)} %collective-permute-done.74.b_ref.refs_9_, ...), custom_call_target="tpu_custom_call" | custom-call | flops 2147483648 | bytes 9437184 | tf_op jit(solution)/shard_map/ffn_back/pallas_call | solution.py:385
  496.5 2.4 copy-done.3
  500.5 7.5 %ffn_back.6 = (bf16[512,1024]{1,0:T(8,128)(2,1)S(1)}, f32[1,1024]{1,0:T(1,128)S(1)}, f32[256,1024]{1,0:T(8,128)S(1)}, bf16[256,1024]{1,0:T(8,128)(2,1)}) custom-call(bf16[256,1024]{1,0:T(8,128)(2,1)S(1)} %convert_element_type.362.a_ref.refs_6_, bf16[256,1024]{1,0:T(8,128)(2,1)S(1)} %collective-permute-done.71.b_ref.refs_7_, ...), custom_call_target="tpu_custom_call" | custom-call | flops 2147483648 | bytes 9437184 | tf_op jit(solution)/shard_map/ffn_back/pallas_call | solution.py:385
  508.2 2.2 add_convert_fusion.1
  520.0 8.5 %weight_grad.6 = (bf16[2,128,2048]{2,1,0:T(8,128)(2,1)}, bf16[2,128,2048]{2,1,0:T(8,128)(2,1)}, bf16[2,128,2048]{2,1,0:T(8,128)(2,1)}, bf16[2,128,2048]{2,1,0:T(8,128)(2,1)}) custom-call(s32[8]{0:T(128)S(1)} %stack.116.order_ref, bf16[256,1024]{1,0:T(8,128)(2,1)S(1)} %fusion.57.a_ref.refs_0_, bf16[256,1024]{1,0:T(8,128)(2,1)} %collective-permute-done.18.b_ref.refs_1_, ...), custom_call_target="tpu_custom_call" | custom-call | flops 4294967296 | bytes 12582912 | tf_op jit(solution)/shard_map/weight_grad/pallas_call | solution.py:453
  535.8 9.9 %collective-permute-done.77.refs_8_ = bf16[256,1024]{1,0:T(8,128)(2,1)} collective-permute-done((bf16[256,1024]{1,0:T(8,128)(2,1)S(1)}, bf16[256,1024]{1,0:T(8,128)(2,1)}, u32[]{:S(2)}, u32[]{:S(2)}) %collective-permute-start.77) | collective-permute-done | bytes 524320 | tf_op jit(solution)/shard_map/ppermute | solution.py:495
  545.7 8.0 %collective-permute-done.98 = bf16[2,128,2048]{2,1,0:T(8,128)(2,1)} collective-permute-done((bf16[2,128,2048]{2,1,0:T(8,128)(2,1)}, bf16[2,128,2048]{2,1,0:T(8,128)(2,1)}, u32[]{:S(2)}, u32[]{:S(2)}) %collective-permute-start.98) | collective-permute-done | bytes 1048608 | tf_op jit(solution)/shard_map/ppermute | solution.py:499
  562.2 9.4 %attend_back.6 = (bf16[512,256]{1,0:T(8,128)(2,1)S(1)}, f32[1,256]{1,0:T(1,128)S(1)}, f32[1024,256]{1,0:T(8,128)S(1)}, f32[1024,256]{1,0:T(8,128)S(1)}) custom-call(bf16[512,768]{1,0:T(8,128)(2,1)S(1)} %copy-done.27, bf16[512,768]{1,0:T(8,128)(2,1)S(1)} %copy-done.27, bf16[512,768]{1,0:T(8,128)(2,1)S(1)} %copy-done.25, bf16[512,768]{1,0:T(8,128)(2,1)S(1)} %copy-done.27, ...), custom_call_target="tpu_custom_call" | custom-call | flops 5368709120 | bytes 8388608 | tf_op jit(solution)/shard_map/attend_back/pallas_call | solution.py:275
  573.7 12.2 %attend_back.7 = (bf16[512,768]{1,0:T(8,128)(2,1)S(1)}, bf16[512,768]{1,0:T(8,128)(2,1)S(1)}, f32[2,256]{1,0:T(2,128)S(1)}, bf16[256,1024]{1,0:T(8,128)(2,1)S(1)}, bf16[256,1024]{1,0:T(8,128)(2,1)}) custom-call(bf16[512,768]{1,0:T(8,128)(2,1)S(1)} %copy-done.25, bf16[512,768]{1,0:T(8,128)(2,1)S(1)} %copy-done.27, bf16[512,768]{1,0:T(8,128)(2,1)S(1)} %copy-done.25, ...), custom_call_target="tpu_custom_call" | custom-call | flops 5368709120 | bytes 8388608 | tf_op jit(solution)/shard_map/attend_back/pallas_call | solution.py:275
  599.0 8.3 %collective-permute-done.109 = f32[8,768]{1,0:T(8,128)S(1)} collective-permute-done((f32[8,768]{1,0:T(8,128)S(1)}, f32[8,768]{1,0:T(8,128)S(1)}, u32[]{:S(2)}, u32[]{:S(2)}) %collective-permute-start.109) | collective-permute-done | bytes 24608 | tf_op jit(solution)/shard_map/ppermute | solution.py:499
  610.0 2.4 fusion.43
  620.8 5.0 weight_grad.4
  631.5 2.2 fusion.47
  647.9 11.0 %collective-permute-done.101 = bf16[128,2048]{1,0:T(8,128)(2,1)} collective-permute-done((bf16[128,2048]{1,0:T(8,128)(2,1)}, bf16[128,2048]{1,0:T(8,128)(2,1)}, u32[]{:S(2)}, u32[]{:S(2)}) %collective-permute-start.101) | collective-permute-done | bytes 524320 | tf_op jit(solution)/shard_map/ppermute | solution.py:495
  663.4 2.5 copy.74
  665.9 2.3 pad_maximum_fusion.4
  669.7 2.8 fusion.37
  674.3 15.0 %collective-permute-done.89 = bf16[128,1024]{1,0:T(8,128)(2,1)S(1)} collective-permute-done((bf16[128,1024]{1,0:T(8,128)(2,1)S(1)}, bf16[128,1024]{1,0:T(8,128)(2,1)S(1)}, u32[]{:S(2)}, u32[]{:S(2)}) %collective-permute-start.89) | collective-permute-done | bytes 262176 | tf_op jit(solution)/shard_map/ppermute | solution.py:495
  (850 shorter events, 260.4 us)
Async XLA Ops:
  3.0 16.9 %collective-permute-start.10 = (f32[1,768]{1,0:T(1,128)S(1)}, f32[1,768]{1,0:T(1,128)S(1)}, u32[]{:S(2)}, u32[]{:S(2)}) collective-permute-start(f32[1,768]{1,0:T(1,128)S(1)} %pad_maximum_fusion.16), channel_id=1, source_target_pairs={{0,1},{1,0},{2,3},{3,2},{4,5},{5,4},{6,7},{7,6},{8,9},{9,8},{10,11... | collective-permute-start | bytes 9224 | tf_op jit(solution)/shard_map/ppermute | solution.py:495
  6.0 41.4 %collective-permute-start = (bf16[256,1024]{1,0:T(8,128)(2,1)}, bf16[256,1024]{1,0:T(8,128)(2,1)}, u32[]{:S(2)}, u32[]{:S(2)}) collective-permute-start(bf16[256,1024]{1,0:T(8,128)(2,1)} %param.11), channel_id=1, source_target_pairs={{0,0},{2,4},{4,2},{6,6},{1,1},{3,5},{5,3},{7,7},{8,8},{10,12},{12,... | collective-permute-start | bytes 1572872 | tf_op jit(solution)/shard_map/ppermute | solution.py:503
  15.0 22.7 %collective-permute-start.4 = (bf16[128,1024]{1,0:T(8,128)(2,1)S(1)}, bf16[128,1024]{1,0:T(8,128)(2,1)}, u32[]{:S(2)}, u32[]{:S(2)}) collective-permute-start(bf16[128,1024]{1,0:T(8,128)(2,1)S(1)} %pad_maximum_fusion.13), channel_id=1, source_target_pairs={{0,2},{2,0},{1,3},{3,1},{4,6},{6,4},{5,7},{7,5},{8,10},{10,8},{9,1... | collective-permute-start | bytes 786440 | tf_op jit(solution)/shard_map/ppermute | solution.py:495
  19.9 15.0 %collective-permute-start.11 = (f32[2,768]{1,0:T(2,128)S(1)}, f32[2,768]{1,0:T(2,128)S(1)}, u32[]{:S(2)}, u32[]{:S(2)}) collective-permute-start(f32[2,768]{1,0:T(2,128)S(1)} %maximum_select_fusion.4), channel_id=1, source_target_pairs={{0,2},{2,0},{1,3},{3,1},{4,6},{6,4},{5,7},{7,5},{8,10},{10,8},{9,1... | collective-permute-start | bytes 18440 | tf_op jit(solution)/shard_map/ppermute | solution.py:495
  58.8 26.3 %collective-permute-start.19 = (bf16[128,2048]{1,0:T(8,128)(2,1)S(1)}, bf16[128,2048]{1,0:T(8,128)(2,1)S(1)}, u32[]{:S(2)}, u32[]{:S(2)}) collective-permute-start(bf16[128,2048]{1,0:T(8,128)(2,1)S(1)} %pad_maximum_fusion.9), channel_id=1, source_target_pairs={{0,2},{2,0},{1,3},{3,1},{4,6},{6,4},{5,7},{7,5},{8,10},{10,8},{9,1... | collective-permute-start | bytes 1572872 | tf_op jit(solution)/shard_map/ppermute | solution.py:495
  93.8 14.2 %collective-permute-start.17 = (bf16[256,1024]{1,0:T(8,128)(2,1)}, bf16[256,1024]{1,0:T(8,128)(2,1)}, u32[]{:S(2)}, u32[]{:S(2)}) collective-permute-start(bf16[256,1024]{1,0:T(8,128)(2,1)} %add_convert_fusion.8), channel_id=1, source_target_pairs={{0,1},{1,0},{2,3},{3,2},{4,5},{5,4},{6,7},{7,6},{8,9},{9,8},{10,11... | collective-permute-start | bytes 1572872 | tf_op jit(solution)/shard_map/ppermute | solution.py:495
  95.4 15.2 %collective-permute-start.21 = (bf16[1,128,2048]{2,1,0:T(8,128)(2,1)S(1)}, bf16[1,128,2048]{2,1,0:T(8,128)(2,1)S(1)}, u32[]{:S(2)}, u32[]{:S(2)}) collective-permute-start(bf16[1,128,2048]{2,1,0:T(8,128)(2,1)S(1)} %get-tuple-element.111), channel_id=1, source_target_pairs={{0,8},{8,0},{16,24},{24,16},{1,9},{9,1},{17,25},{25,17},{2,10},{10... | collective-permute-start | bytes 1572872 | tf_op jit(solution)/shard_map/ppermute | solution.py:499
  96.2 14.5 %collective-permute-start.22 = (bf16[1,128,2048]{2,1,0:T(8,128)(2,1)}, bf16[1,128,2048]{2,1,0:T(8,128)(2,1)S(1)}, u32[]{:S(2)}, u32[]{:S(2)}) collective-permute-start(bf16[1,128,2048]{2,1,0:T(8,128)(2,1)} %bitcast.27), channel_id=1, source_target_pairs={{0,16},{8,24},{16,0},{24,8},{1,17},{9,25},{17,1},{25,9},{2,18},{10... | collective-permute-start | bytes 1572872 | tf_op jit(solution)/shard_map/ppermute | solution.py:499
  111.9 24.5 %collective-permute-start.23 = (bf16[2,128,2048]{2,1,0:T(8,128)(2,1)S(1)}, bf16[2,128,2048]{2,1,0:T(8,128)(2,1)}, u32[]{:S(2)}, u32[]{:S(2)}) collective-permute-start(bf16[2,128,2048]{2,1,0:T(8,128)(2,1)S(1)} %pad_maximum_fusion.refs_0_), channel_id=1, source_target_pairs={{0,16},{8,24},{16,0},{24,8},{1,17},{9,25},{17,1},{25,9},{2,18},{10... | collective-permute-start | bytes 3145736 | tf_op jit(solution)/shard_map/ppermute | solution.py:499
  112.4 24.2 %collective-permute-start.24 = (bf16[2,128,2048]{2,1,0:T(8,128)(2,1)S(1)}, bf16[2,128,2048]{2,1,0:T(8,128)(2,1)}, u32[]{:S(2)}, u32[]{:S(2)}) collective-permute-start(bf16[2,128,2048]{2,1,0:T(8,128)(2,1)S(1)} %pad_maximum_fusion.1.refs_2_), channel_id=1, source_target_pairs={{0,8},{8,0},{16,24},{24,16},{1,9},{9,1},{17,25},{25,17},{2,10},{10... | collective-permute-start | bytes 3145736 | tf_op jit(solution)/shard_map/ppermute | solution.py:499
  123.4 15.0 %collective-permute-start.27 = (bf16[256,1024]{1,0:T(8,128)(2,1)}, bf16[256,1024]{1,0:T(8,128)(2,1)S(1)}, u32[]{:S(2)}, u32[]{:S(2)}) collective-permute-start(bf16[256,1024]{1,0:T(8,128)(2,1)} %collective-permute-done.26.a_ref.refs_2_), channel_id=1, source_target_pairs={{0,4},{4,0},{1,5},{5,1},{2,6},{6,2},{3,7},{7,3},{8,12},{12,8},{9,1... | collective-permute-start | bytes 1572872 | tf_op jit(solution)/shard_map/ppermute | solution.py:495
  123.5 30.0 %collective-permute-start.18 = (bf16[256,1024]{1,0:T(8,128)(2,1)S(1)}, bf16[256,1024]{1,0:T(8,128)(2,1)}, u32[]{:S(2)}, u32[]{:S(2)}) collective-permute-start(bf16[256,1024]{1,0:T(8,128)(2,1)S(1)} %fusion.57.a_ref.refs_0_), channel_id=1, source_target_pairs={{0,4},{4,0},{1,5},{5,1},{2,6},{6,2},{3,7},{7,3},{8,12},{12,8},{9,1... | collective-permute-start | bytes 1572872 | tf_op jit(solution)/shard_map/ppermute | solution.py:495
  151.0 15.8 %collective-permute-start.28 = (bf16[256,1024]{1,0:T(8,128)(2,1)}, bf16[256,1024]{1,0:T(8,128)(2,1)}, u32[]{:S(2)}, u32[]{:S(2)}) collective-permute-start(bf16[256,1024]{1,0:T(8,128)(2,1)} %get-tuple-element.118), channel_id=1, source_target_pairs={{0,4},{4,0},{1,5},{5,1},{2,6},{6,2},{3,7},{7,3},{8,12},{12,8},{9,1... | collective-permute-start | bytes 1572872 | tf_op jit(solution)/shard_map/ppermute | solution.py:495
  151.5 18.1 %collective-permute-start.31 = (bf16[128,1024]{1,0:T(8,128)(2,1)S(1)}, bf16[128,1024]{1,0:T(8,128)(2,1)S(1)}, u32[]{:S(2)}, u32[]{:S(2)}) collective-permute-start(bf16[128,1024]{1,0:T(8,128)(2,1)S(1)} %pad_maximum_fusion.14), channel_id=1, source_target_pairs={{0,2},{2,0},{1,3},{3,1},{4,6},{6,4},{5,7},{7,5},{8,10},{10,8},{9,1... | collective-permute-start | bytes 786440 | tf_op jit(solution)/shard_map/ppermute | solution.py:495
  169.0 14.4 %collective-permute-start.29 = (bf16[256,1024]{1,0:T(8,128)(2,1)}, bf16[256,1024]{1,0:T(8,128)(2,1)}, u32[]{:S(2)}, u32[]{:S(2)}) collective-permute-start(bf16[256,1024]{1,0:T(8,128)(2,1)} %add_convert_fusion.7), channel_id=1, source_target_pairs={{0,1},{1,0},{2,3},{3,2},{4,5},{5,4},{6,7},{7,6},{8,9},{9,8},{10,11... | collective-permute-start | bytes 1572872 | tf_op jit(solution)/shard_map/ppermute | solution.py:495
  173.5 16.5 %collective-permute-start.33 = (bf16[1,128,1024]{2,1,0:T(8,128)(2,1)}, bf16[1,128,1024]{2,1,0:T(8,128)(2,1)S(1)}, u32[]{:S(2)}, u32[]{:S(2)}) collective-permute-start(bf16[1,128,1024]{2,1,0:T(8,128)(2,1)} %get-tuple-element.120), channel_id=1, source_target_pairs={{0,8},{8,0},{16,24},{24,16},{1,9},{9,1},{17,25},{25,17},{2,10},{10... | collective-permute-start | bytes 786440 | tf_op jit(solution)/shard_map/ppermute | solution.py:499
  186.1 23.3 %collective-permute-start.37 = (bf16[256,1024]{1,0:T(8,128)(2,1)S(1)}, bf16[256,1024]{1,0:T(8,128)(2,1)S(1)}, u32[]{:S(2)}, u32[]{:S(2)}) collective-permute-start(bf16[256,1024]{1,0:T(8,128)(2,1)S(1)} %fusion.58.refs_0_), channel_id=1, source_target_pairs={{0,1},{1,0},{2,3},{3,2},{4,5},{5,4},{6,7},{7,6},{8,9},{9,8},{10,11... | collective-permute-start | bytes 1572872 | tf_op jit(solution)/shard_map/ppermute | solution.py:495
  186.9 25.4 %collective-permute-start.43 = (bf16[128,2048]{1,0:T(8,128)(2,1)S(1)}, bf16[128,2048]{1,0:T(8,128)(2,1)S(1)}, u32[]{:S(2)}, u32[]{:S(2)}) collective-permute-start(bf16[128,2048]{1,0:T(8,128)(2,1)S(1)} %copy-done.144), channel_id=1, source_target_pairs={{0,2},{2,0},{1,3},{3,1},{4,6},{6,4},{5,7},{7,5},{8,10},{10,8},{9,1... | collective-permute-start | bytes 1572872 | tf_op jit(solution)/shard_map/ppermute | solution.py:495
  195.6 16.8 %collective-permute-start.35 = (bf16[2,128,1024]{2,1,0:T(8,128)(2,1)S(1)}, bf16[2,128,1024]{2,1,0:T(8,128)(2,1)S(1)}, u32[]{:S(2)}, u32[]{:S(2)}) collective-permute-start(bf16[2,128,1024]{2,1,0:T(8,128)(2,1)S(1)} %pad_maximum_fusion.10.refs_0_), channel_id=1, source_target_pairs={{0,16},{8,24},{16,0},{24,8},{1,17},{9,25},{17,1},{25,9},{2,18},{10... | collective-permute-start | bytes 1572872 | tf_op jit(solution)/shard_map/ppermute | solution.py:499
  197.2 15.3 %collective-permute-start.36 = (bf16[2,128,1024]{2,1,0:T(8,128)(2,1)S(1)}, bf16[2,128,1024]{2,1,0:T(8,128)(2,1)S(1)}, u32[]{:S(2)}, u32[]{:S(2)}) collective-permute-start(bf16[2,128,1024]{2,1,0:T(8,128)(2,1)S(1)} %pad_maximum_fusion.11.refs_2_), channel_id=1, source_target_pairs={{0,8},{8,0},{16,24},{24,16},{1,9},{9,1},{17,25},{25,17},{2,10},{10... | collective-permute-start | bytes 1572872 | tf_op jit(solution)/shard_map/ppermute | solution.py:499
  198.1 15.1 %collective-permute-start.30 = (bf16[256,1024]{1,0:T(8,128)(2,1)S(1)}, bf16[256,1024]{1,0:T(8,128)(2,1)S(1)}, u32[]{:S(2)}, u32[]{:S(2)}) collective-permute-start(bf16[256,1024]{1,0:T(8,128)(2,1)S(1)} %fusion.58.refs_0_), channel_id=1, source_target_pairs={{0,4},{4,0},{1,5},{5,1},{2,6},{6,2},{3,7},{7,3},{8,12},{12,8},{9,1... | collective-permute-start | bytes 1572872 | tf_op jit(solution)/shard_map/ppermute | solution.py:495
  224.1 14.4 %collective-permute-start.46 = (bf16[1,128,2048]{2,1,0:T(8,128)(2,1)}, bf16[1,128,2048]{2,1,0:T(8,128)(2,1)}, u32[]{:S(2)}, u32[]{:S(2)}) collective-permute-start(bf16[1,128,2048]{2,1,0:T(8,128)(2,1)} %bitcast.41), channel_id=1, source_target_pairs={{0,16},{8,24},{16,0},{24,8},{1,17},{9,25},{17,1},{25,9},{2,18},{10... | collective-permute-start | bytes 1572872 | tf_op jit(solution)/shard_map/ppermute | solution.py:499
  232.2 14.6 %collective-permute-start.41 = (bf16[256,1024]{1,0:T(8,128)(2,1)}, bf16[256,1024]{1,0:T(8,128)(2,1)}, u32[]{:S(2)}, u32[]{:S(2)}) collective-permute-start(bf16[256,1024]{1,0:T(8,128)(2,1)} %add_convert_fusion.6), channel_id=1, source_target_pairs={{0,1},{1,0},{2,3},{3,2},{4,5},{5,4},{6,7},{7,6},{8,9},{9,8},{10,11... | collective-permute-start | bytes 1572872 | tf_op jit(solution)/shard_map/ppermute | solution.py:495
  239.8 26.2 %collective-permute-start.47 = (bf16[2,128,2048]{2,1,0:T(8,128)(2,1)S(1)}, bf16[2,128,2048]{2,1,0:T(8,128)(2,1)S(1)}, u32[]{:S(2)}, u32[]{:S(2)}) collective-permute-start(bf16[2,128,2048]{2,1,0:T(8,128)(2,1)S(1)} %pad_maximum_fusion.2.refs_0_), channel_id=1, source_target_pairs={{0,16},{8,24},{16,0},{24,8},{1,17},{9,25},{17,1},{25,9},{2,18},{10... | collective-permute-start | bytes 3145736 | tf_op jit(solution)/shard_map/ppermute | solution.py:499
  241.3 24.6 %collective-permute-start.48 = (bf16[2,128,2048]{2,1,0:T(8,128)(2,1)S(1)}, bf16[2,128,2048]{2,1,0:T(8,128)(2,1)S(1)}, u32[]{:S(2)}, u32[]{:S(2)}) collective-permute-start(bf16[2,128,2048]{2,1,0:T(8,128)(2,1)S(1)} %pad_maximum_fusion.3.refs_2_), channel_id=1, source_target_pairs={{0,8},{8,0},{16,24},{24,16},{1,9},{9,1},{17,25},{25,17},{2,10},{10... | collective-permute-start | bytes 3145736 | tf_op jit(solution)/shard_map/ppermute | solution.py:499
  262.8 15.4 %collective-permute-start.55 = (bf16[256,1024]{1,0:T(8,128)(2,1)S(1)}, bf16[256,1024]{1,0:T(8,128)(2,1)}, u32[]{:S(2)}, u32[]{:S(2)}) collective-permute-start(bf16[256,1024]{1,0:T(8,128)(2,1)S(1)} %copy-done.205), channel_id=1, source_target_pairs={{0,0},{2,4},{4,2},{6,6},{1,1},{3,5},{5,3},{7,7},{8,8},{10,12},{12,... | collective-permute-start | bytes 1572872 | tf_op jit(solution)/shard_map/ppermute | solution.py:503
  264.3 15.6 %collective-permute-start.42 = (bf16[256,1024]{1,0:T(8,128)(2,1)S(1)}, bf16[256,1024]{1,0:T(8,128)(2,1)S(1)}, u32[]{:S(2)}, u32[]{:S(2)}) collective-permute-start(bf16[256,1024]{1,0:T(8,128)(2,1)S(1)} %fusion.59.a_ref.refs_0_), channel_id=1, source_target_pairs={{0,4},{4,0},{1,5},{5,1},{2,6},{6,2},{3,7},{7,3},{8,12},{12,8},{9,1... | collective-permute-start | bytes 1572872 | tf_op jit(solution)/shard_map/ppermute | solution.py:495
  278.3 15.1 %collective-permute-start.57 = (bf16[256,1024]{1,0:T(8,128)(2,1)}, bf16[256,1024]{1,0:T(8,128)(2,1)}, u32[]{:S(2)}, u32[]{:S(2)}) collective-permute-start(bf16[256,1024]{1,0:T(8,128)(2,1)} %collective-permute-done.55), channel_id=1, source_target_pairs={{0,1},{1,0},{2,3},{3,2},{4,5},{5,4},{6,7},{7,6},{8,9},{9,8},{10,11... | collective-permute-start | bytes 1572872 | tf_op jit(solution)/shard_map/ppermute | solution.py:495
  291.4 14.3 %collective-permute-start.53 = (bf16[256,1024]{1,0:T(8,128)(2,1)}, bf16[256,1024]{1,0:T(8,128)(2,1)}, u32[]{:S(2)}, u32[]{:S(2)}) collective-permute-start(bf16[256,1024]{1,0:T(8,128)(2,1)} %add_convert_fusion.5), channel_id=1, source_target_pairs={{0,1},{1,0},{2,3},{3,2},{4,5},{5,4},{6,7},{7,6},{8,9},{9,8},{10,11... | collective-permute-start | bytes 1572872 | tf_op jit(solution)/shard_map/ppermute | solution.py:495
  293.3 14.8 %collective-permute-start.56 = (bf16[256,1024]{1,0:T(8,128)(2,1)}, bf16[256,1024]{1,0:T(8,128)(2,1)S(1)}, u32[]{:S(2)}, u32[]{:S(2)}) collective-permute-start(bf16[256,1024]{1,0:T(8,128)(2,1)} %collective-permute-done.55), channel_id=1, source_target_pairs={{0,4},{4,0},{1,5},{5,1},{2,6},{6,2},{3,7},{7,3},{8,12},{12,8},{9,1... | collective-permute-start | bytes 1572872 | tf_op jit(solution)/shard_map/ppermute | solution.py:495
  293.4 14.7 %collective-permute-start.58 = (bf16[256,1024]{1,0:T(8,128)(2,1)}, bf16[256,1024]{1,0:T(8,128)(2,1)S(1)}, u32[]{:S(2)}, u32[]{:S(2)}) collective-permute-start(bf16[256,1024]{1,0:T(8,128)(2,1)} %collective-permute-done.57), channel_id=1, source_target_pairs={{0,4},{4,0},{1,5},{5,1},{2,6},{6,2},{3,7},{7,3},{8,12},{12,8},{9,1... | collective-permute-start | bytes 1572872 | tf_op jit(solution)/shard_map/ppermute | solution.py:495
  326.0 14.3 %collective-permute-start.62 = (bf16[256,1024]{1,0:T(8,128)(2,1)}, bf16[256,1024]{1,0:T(8,128)(2,1)}, u32[]{:S(2)}, u32[]{:S(2)}) collective-permute-start(bf16[256,1024]{1,0:T(8,128)(2,1)} %collective-permute-done.61.a_ref.refs_8_), channel_id=1, source_target_pairs={{0,4},{4,0},{1,5},{5,1},{2,6},{6,2},{3,7},{7,3},{8,12},{12,8},{9,1... | collective-permute-start | bytes 1572872 | tf_op jit(solution)/shard_map/ppermute | solution.py:495
  359.5 25.9 %collective-permute-start.104 = (bf16[2,128,2048]{2,1,0:T(8,128)(2,1)}, bf16[2,128,2048]{2,1,0:T(8,128)(2,1)}, u32[]{:S(2)}, u32[]{:S(2)}) collective-permute-start(bf16[2,128,2048]{2,1,0:T(8,128)(2,1)} %get-tuple-element.196), channel_id=1, source_target_pairs={{0,8},{8,0},{16,24},{24,16},{1,9},{9,1},{17,25},{25,17},{2,10},{10... | collective-permute-start | bytes 3145736 | tf_op jit(solution)/shard_map/ppermute | solution.py:499
  367.6 22.2 %collective-permute-start.60 = (bf16[256,1024]{1,0:T(8,128)(2,1)}, bf16[256,1024]{1,0:T(8,128)(2,1)S(1)}, u32[]{:S(2)}, u32[]{:S(2)}) collective-permute-start(bf16[256,1024]{1,0:T(8,128)(2,1)} %copy-done.93), channel_id=1, source_target_pairs={{0,4},{4,0},{1,5},{5,1},{2,6},{6,2},{3,7},{7,3},{8,12},{12,8},{9,1... | collective-permute-start | bytes 1572872 | tf_op jit(solution)/shard_map/ppermute | solution.py:495
  367.6 25.2 %collective-permute-start.102 = (bf16[2,128,2048]{2,1,0:T(8,128)(2,1)}, bf16[2,128,2048]{2,1,0:T(8,128)(2,1)S(1)}, u32[]{:S(2)}, u32[]{:S(2)}) collective-permute-start(bf16[2,128,2048]{2,1,0:T(8,128)(2,1)} %copy-done.86), channel_id=1, source_target_pairs={{0,16},{8,24},{16,0},{24,8},{1,17},{9,25},{17,1},{25,9},{2,18},{10... | collective-permute-start | bytes 3145736 | tf_op jit(solution)/shard_map/ppermute | solution.py:499
  369.4 20.3 %collective-permute-start.64 = (bf16[256,1024]{1,0:T(8,128)(2,1)S(1)}, bf16[256,1024]{1,0:T(8,128)(2,1)S(1)}, u32[]{:S(2)}, u32[]{:S(2)}) collective-permute-start(bf16[256,1024]{1,0:T(8,128)(2,1)S(1)} %add_convert_fusion.3), channel_id=1, source_target_pairs={{0,1},{1,0},{2,3},{3,2},{4,5},{5,4},{6,7},{7,6},{8,9},{9,8},{10,11... | collective-permute-start | bytes 1572872 | tf_op jit(solution)/shard_map/ppermute | solution.py:495
  389.2 15.2 %collective-permute-start.105 = (bf16[1,128,2048]{2,1,0:T(8,128)(2,1)}, bf16[1,128,2048]{2,1,0:T(8,128)(2,1)}, u32[]{:S(2)}, u32[]{:S(2)}) collective-permute-start(bf16[1,128,2048]{2,1,0:T(8,128)(2,1)} %slice.522), channel_id=1, source_target_pairs={{0,16},{8,24},{16,0},{24,8},{1,17},{9,25},{17,1},{25,9},{2,18},{10... | collective-permute-start | bytes 1572872 | tf_op jit(solution)/shard_map/ppermute | solution.py:499
  395.4 34.3 %collective-permute-start.103 = (bf16[1,128,2048]{2,1,0:T(8,128)(2,1)}, bf16[1,128,2048]{2,1,0:T(8,128)(2,1)}, u32[]{:S(2)}, u32[]{:S(2)}) collective-permute-start(bf16[1,128,2048]{2,1,0:T(8,128)(2,1)} %slice.523), channel_id=1, source_target_pairs={{0,8},{8,0},{16,24},{24,16},{1,9},{9,1},{17,25},{25,17},{2,10},{10... | collective-permute-start | bytes 1572872 | tf_op jit(solution)/shard_map/ppermute | solution.py:499
  405.9 23.8 %collective-permute-start.106 = (bf16[128,2048]{1,0:T(8,128)(2,1)S(1)}, bf16[128,2048]{1,0:T(8,128)(2,1)S(1)}, u32[]{:S(2)}, u32[]{:S(2)}) collective-permute-start(bf16[128,2048]{1,0:T(8,128)(2,1)S(1)} %fusion.67), channel_id=1, source_target_pairs={{0,4},{4,0},{1,5},{5,1},{2,6},{6,2},{3,7},{7,3},{8,12},{12,8},{9,1... | collective-permute-start | bytes 1572872 | tf_op jit(solution)/shard_map/ppermute | solution.py:495
  432.7 33.6 %collective-permute-start.107 = (bf16[128,2048]{1,0:T(8,128)(2,1)}, bf16[128,2048]{1,0:T(8,128)(2,1)}, u32[]{:S(2)}, u32[]{:S(2)}) collective-permute-start(bf16[128,2048]{1,0:T(8,128)(2,1)} %fusion.49), channel_id=1, source_target_pairs={{0,2},{2,0},{1,3},{3,1},{4,6},{6,4},{5,7},{7,5},{8,10},{10,8},{9,1... | collective-permute-start | bytes 1572872 | tf_op jit(solution)/shard_map/ppermute | solution.py:495
  437.6 24.9 %collective-permute-start.70 = (bf16[256,1024]{1,0:T(8,128)(2,1)}, bf16[256,1024]{1,0:T(8,128)(2,1)}, u32[]{:S(2)}, u32[]{:S(2)}) collective-permute-start(bf16[256,1024]{1,0:T(8,128)(2,1)} %add_convert_fusion.2), channel_id=1, source_target_pairs={{0,1},{1,0},{2,3},{3,2},{4,5},{5,4},{6,7},{7,6},{8,9},{9,8},{10,11... | collective-permute-start | bytes 1572872 | tf_op jit(solution)/shard_map/ppermute | solution.py:495
  444.4 24.7 %collective-permute-start.92 = (bf16[2,128,1024]{2,1,0:T(8,128)(2,1)}, bf16[2,128,1024]{2,1,0:T(8,128)(2,1)}, u32[]{:S(2)}, u32[]{:S(2)}) collective-permute-start(bf16[2,128,1024]{2,1,0:T(8,128)(2,1)} %get-tuple-element.181), channel_id=1, source_target_pairs={{0,8},{8,0},{16,24},{24,16},{1,9},{9,1},{17,25},{25,17},{2,10},{10... | collective-permute-start | bytes 1572872 | tf_op jit(solution)/shard_map/ppermute | solution.py:499
  445.6 34.0 %collective-permute-start.90 = (bf16[2,128,1024]{2,1,0:T(8,128)(2,1)}, bf16[2,128,1024]{2,1,0:T(8,128)(2,1)}, u32[]{:S(2)}, u32[]{:S(2)}) collective-permute-start(bf16[2,128,1024]{2,1,0:T(8,128)(2,1)} %get-tuple-element.179), channel_id=1, source_target_pairs={{0,16},{8,24},{16,0},{24,8},{1,17},{9,25},{17,1},{25,9},{2,18},{10... | collective-permute-start | bytes 1572872 | tf_op jit(solution)/shard_map/ppermute | solution.py:499
  482.1 14.5 %collective-permute-start.71 = (bf16[256,1024]{1,0:T(8,128)(2,1)S(1)}, bf16[256,1024]{1,0:T(8,128)(2,1)S(1)}, u32[]{:S(2)}, u32[]{:S(2)}) collective-permute-start(bf16[256,1024]{1,0:T(8,128)(2,1)S(1)} %convert_element_type.362.a_ref.refs_6_), channel_id=1, source_target_pairs={{0,4},{4,0},{1,5},{5,1},{2,6},{6,2},{3,7},{7,3},{8,12},{12,8},{9,1... | collective-permute-start | bytes 1572872 | tf_op jit(solution)/shard_map/ppermute | solution.py:495
  491.9 16.3 %collective-permute-start.75 = (bf16[256,1024]{1,0:T(8,128)(2,1)}, bf16[256,1024]{1,0:T(8,128)(2,1)}, u32[]{:S(2)}, u32[]{:S(2)}) collective-permute-start(bf16[256,1024]{1,0:T(8,128)(2,1)} %get-tuple-element.158), channel_id=1, source_target_pairs={{0,4},{4,0},{1,5},{5,1},{2,6},{6,2},{3,7},{7,3},{8,12},{12,8},{9,1... | collective-permute-start | bytes 1572872 | tf_op jit(solution)/shard_map/ppermute | solution.py:495
  493.9 18.2 %collective-permute-start.95 = (bf16[128,1024]{1,0:T(8,128)(2,1)}, bf16[128,1024]{1,0:T(8,128)(2,1)}, u32[]{:S(2)}, u32[]{:S(2)}) collective-permute-start(bf16[128,1024]{1,0:T(8,128)(2,1)} %fusion.65), channel_id=1, source_target_pairs={{0,2},{2,0},{1,3},{3,1},{4,6},{6,4},{5,7},{7,5},{8,10},{10,8},{9,1... | collective-permute-start | bytes 786440 | tf_op jit(solution)/shard_map/ppermute | solution.py:495
  508.0 21.1 %collective-permute-start.72 = (bf16[256,1024]{1,0:T(8,128)(2,1)}, bf16[256,1024]{1,0:T(8,128)(2,1)}, u32[]{:S(2)}, u32[]{:S(2)}) collective-permute-start(bf16[256,1024]{1,0:T(8,128)(2,1)} %get-tuple-element.155), channel_id=1, source_target_pairs={{0,4},{4,0},{1,5},{5,1},{2,6},{6,2},{3,7},{7,3},{8,12},{12,8},{9,1... | collective-permute-start | bytes 1572872 | tf_op jit(solution)/shard_map/ppermute | solution.py:495
  510.4 18.7 %collective-permute-start.76 = (bf16[256,1024]{1,0:T(8,128)(2,1)}, bf16[256,1024]{1,0:T(8,128)(2,1)}, u32[]{:S(2)}, u32[]{:S(2)}) collective-permute-start(bf16[256,1024]{1,0:T(8,128)(2,1)} %add_convert_fusion.1), channel_id=1, source_target_pairs={{0,1},{1,0},{2,3},{3,2},{4,5},{5,4},{6,7},{7,6},{8,9},{9,8},{10,11... | collective-permute-start | bytes 1572872 | tf_op jit(solution)/shard_map/ppermute | solution.py:495
  528.4 25.2 %collective-permute-start.98 = (bf16[2,128,2048]{2,1,0:T(8,128)(2,1)}, bf16[2,128,2048]{2,1,0:T(8,128)(2,1)}, u32[]{:S(2)}, u32[]{:S(2)}) collective-permute-start(bf16[2,128,2048]{2,1,0:T(8,128)(2,1)} %get-tuple-element.188), channel_id=1, source_target_pairs={{0,8},{8,0},{16,24},{24,16},{1,9},{9,1},{17,25},{25,17},{2,10},{10... | collective-permute-start | bytes 3145736 | tf_op jit(solution)/shard_map/ppermute | solution.py:499
  533.5 57.8 %collective-permute-start.96 = (bf16[2,128,2048]{2,1,0:T(8,128)(2,1)}, bf16[2,128,2048]{2,1,0:T(8,128)(2,1)}, u32[]{:S(2)}, u32[]{:S(2)}) collective-permute-start(bf16[2,128,2048]{2,1,0:T(8,128)(2,1)} %get-tuple-element.186), channel_id=1, source_target_pairs={{0,16},{8,24},{16,0},{24,8},{1,17},{9,25},{17,1},{25,9},{2,18},{10... | collective-permute-start | bytes 3145736 | tf_op jit(solution)/shard_map/ppermute | solution.py:499
  535.8 26.4 %collective-permute-start.79 = (bf16[256,1024]{1,0:T(8,128)(2,1)S(1)}, bf16[256,1024]{1,0:T(8,128)(2,1)}, u32[]{:S(2)}, u32[]{:S(2)}) collective-permute-start(bf16[256,1024]{1,0:T(8,128)(2,1)S(1)} %convert_element_type.368.refs_8_.refs_6_), channel_id=1, source_target_pairs={{0,4},{4,0},{1,5},{5,1},{2,6},{6,2},{3,7},{7,3},{8,12},{12,8},{9,1... | collective-permute-start | bytes 1572872 | tf_op jit(solution)/shard_map/ppermute | solution.py:495
  545.7 27.9 %collective-permute-start.78 = (bf16[256,1024]{1,0:T(8,128)(2,1)}, bf16[256,1024]{1,0:T(8,128)(2,1)}, u32[]{:S(2)}, u32[]{:S(2)}) collective-permute-start(bf16[256,1024]{1,0:T(8,128)(2,1)} %collective-permute-done.77.refs_8_), channel_id=1, source_target_pairs={{0,4},{4,0},{1,5},{5,1},{2,6},{6,2},{3,7},{7,3},{8,12},{12,8},{9,1... | collective-permute-start | bytes 1572872 | tf_op jit(solution)/shard_map/ppermute | solution.py:495
  557.9 38.5 %collective-permute-start.99 = (bf16[1,128,2048]{2,1,0:T(8,128)(2,1)}, bf16[1,128,2048]{2,1,0:T(8,128)(2,1)}, u32[]{:S(2)}, u32[]{:S(2)}) collective-permute-start(bf16[1,128,2048]{2,1,0:T(8,128)(2,1)} %slice.524), channel_id=1, source_target_pairs={{0,16},{8,24},{16,0},{24,8},{1,17},{9,25},{17,1},{25,9},{2,18},{10... | collective-permute-start | bytes 1572872 | tf_op jit(solution)/shard_map/ppermute | solution.py:499
  594.3 34.5 %collective-permute-start.97 = (bf16[1,128,2048]{2,1,0:T(8,128)(2,1)}, bf16[1,128,2048]{2,1,0:T(8,128)(2,1)}, u32[]{:S(2)}, u32[]{:S(2)}) collective-permute-start(bf16[1,128,2048]{2,1,0:T(8,128)(2,1)} %slice.525), channel_id=1, source_target_pairs={{0,8},{8,0},{16,24},{24,16},{1,9},{9,1},{17,25},{25,17},{2,10},{10... | collective-permute-start | bytes 1572872 | tf_op jit(solution)/shard_map/ppermute | solution.py:499
  598.5 31.4 %collective-permute-start.100 = (bf16[128,2048]{1,0:T(8,128)(2,1)}, bf16[128,2048]{1,0:T(8,128)(2,1)}, u32[]{:S(2)}, u32[]{:S(2)}) collective-permute-start(bf16[128,2048]{1,0:T(8,128)(2,1)} %fusion.66), channel_id=1, source_target_pairs={{0,4},{4,0},{1,5},{5,1},{2,6},{6,2},{3,7},{7,3},{8,12},{12,8},{9,1... | collective-permute-start | bytes 1572872 | tf_op jit(solution)/shard_map/ppermute | solution.py:495
  598.5 38.6 %collective-permute-start.81 = (bf16[256,1024]{1,0:T(8,128)(2,1)}, bf16[256,1024]{1,0:T(8,128)(2,1)}, u32[]{:S(2)}, u32[]{:S(2)}) collective-permute-start(bf16[256,1024]{1,0:T(8,128)(2,1)} %get-tuple-element.167), channel_id=1, source_target_pairs={{0,4},{4,0},{1,5},{5,1},{2,6},{6,2},{3,7},{7,3},{8,12},{12,8},{9,1... | collective-permute-start | bytes 1572872 | tf_op jit(solution)/shard_map/ppermute | solution.py:495
  612.5 57.2 %collective-permute-start.80 = (bf16[256,1024]{1,0:T(8,128)(2,1)}, bf16[256,1024]{1,0:T(8,128)(2,1)}, u32[]{:S(2)}, u32[]{:S(2)}) collective-permute-start(bf16[256,1024]{1,0:T(8,128)(2,1)} %fusion.43), channel_id=1, source_target_pairs={{0,4},{4,0},{1,5},{5,1},{2,6},{6,2},{3,7},{7,3},{8,12},{12,8},{9,1... | collective-permute-start | bytes 1572872 | tf_op jit(solution)/shard_map/ppermute | solution.py:495
  628.8 15.3 %collective-permute-start.84 = (bf16[2,128,1024]{2,1,0:T(8,128)(2,1)}, bf16[2,128,1024]{2,1,0:T(8,128)(2,1)}, u32[]{:S(2)}, u32[]{:S(2)}) collective-permute-start(bf16[2,128,1024]{2,1,0:T(8,128)(2,1)} %get-tuple-element.172), channel_id=1, source_target_pairs={{0,16},{8,24},{16,0},{24,8},{1,17},{9,25},{17,1},{25,9},{2,18},{10... | collective-permute-start | bytes 1572872 | tf_op jit(solution)/shard_map/ppermute | solution.py:499
  633.7 25.3 %collective-permute-start.101 = (bf16[128,2048]{1,0:T(8,128)(2,1)}, bf16[128,2048]{1,0:T(8,128)(2,1)}, u32[]{:S(2)}, u32[]{:S(2)}) collective-permute-start(bf16[128,2048]{1,0:T(8,128)(2,1)} %fusion.47), channel_id=1, source_target_pairs={{0,2},{2,0},{1,3},{3,1},{4,6},{6,4},{5,7},{7,5},{8,10},{10,8},{9,1... | collective-permute-start | bytes 1572872 | tf_op jit(solution)/shard_map/ppermute | solution.py:495
  639.2 30.5 %collective-permute-start.82 = (bf16[256,1024]{1,0:T(8,128)(2,1)}, bf16[256,1024]{1,0:T(8,128)(2,1)}, u32[]{:S(2)}, u32[]{:S(2)}) collective-permute-start(bf16[256,1024]{1,0:T(8,128)(2,1)} %add_convert_fusion), channel_id=1, source_target_pairs={{0,1},{1,0},{2,3},{3,2},{4,5},{5,4},{6,7},{7,6},{8,9},{9,8},{10,11... | collective-permute-start | bytes 1572872 | tf_op jit(solution)/shard_map/ppermute | solution.py:495
  642.5 19.0 %collective-permute-start.87 = (bf16[1,128,1024]{2,1,0:T(8,128)(2,1)S(1)}, bf16[1,128,1024]{2,1,0:T(8,128)(2,1)S(1)}, u32[]{:S(2)}, u32[]{:S(2)}) collective-permute-start(bf16[1,128,1024]{2,1,0:T(8,128)(2,1)S(1)} %slice.528), channel_id=1, source_target_pairs={{0,16},{8,24},{16,0},{24,8},{1,17},{9,25},{17,1},{25,9},{2,18},{10... | collective-permute-start | bytes 786440 | tf_op jit(solution)/shard_map/ppermute | solution.py:499
  647.0 21.2 %collective-permute-start.85 = (bf16[1,128,1024]{2,1,0:T(8,128)(2,1)}, bf16[1,128,1024]{2,1,0:T(8,128)(2,1)}, u32[]{:S(2)}, u32[]{:S(2)}) collective-permute-start(bf16[1,128,1024]{2,1,0:T(8,128)(2,1)} %slice.529), channel_id=1, source_target_pairs={{0,8},{8,0},{16,24},{24,16},{1,9},{9,1},{17,25},{25,17},{2,10},{10... | collective-permute-start | bytes 786440 | tf_op jit(solution)/shard_map/ppermute | solution.py:499
  669.6 19.8 %collective-permute-start.89 = (bf16[128,1024]{1,0:T(8,128)(2,1)S(1)}, bf16[128,1024]{1,0:T(8,128)(2,1)S(1)}, u32[]{:S(2)}, u32[]{:S(2)}) collective-permute-start(bf16[128,1024]{1,0:T(8,128)(2,1)S(1)} %fusion.63), channel_id=1, source_target_pairs={{0,2},{2,0},{1,3},{3,1},{4,6},{6,4},{5,7},{7,5},{8,10},{10,8},{9,1... | collective-permute-start | bytes 786440 | tf_op jit(solution)/shard_map/ppermute | solution.py:495
  672.5 20.3 %collective-permute-start.83 = (bf16[256,1024]{1,0:T(8,128)(2,1)}, bf16[256,1024]{1,0:T(8,128)(2,1)S(1)}, u32[]{:S(2)}, u32[]{:S(2)}) collective-permute-start(bf16[256,1024]{1,0:T(8,128)(2,1)} %fusion.37), channel_id=1, source_target_pairs={{0,0},{2,4},{4,2},{6,6},{1,1},{3,5},{5,3},{7,7},{8,8},{10,12},{12,... | collective-permute-start | bytes 1572872 | tf_op jit(solution)/shard_map/ppermute | solution.py:503
  (255 other events, 2171.5 us)

commit v3 on v2

v3 whole, which is shorter than its diff:
```python
import functools

import jax
import jax.numpy as jnp
from jax import lax
from jax.experimental import pallas as pl
from jax.experimental.pallas import tpu as pltpu
from jax.sharding import Mesh, PartitionSpec as P

D = 1024
HEAD_DIM = 64
FF = 4096
LAYERS = 2
SEQ_GRP = 3

EPS = 1e-05
NEG = -1e30
ALL = ("d", "c", "zh", "zl")
SWAP = [(0, 1), (1, 0)]
bf16 = jnp.bfloat16
f32 = jnp.float32
MIB = 1 << 20

TAIL_STEP = 0.24
TAIL = (
    0.0912286469891869,
    0.14294535326111468,
    -0.11556713177962434,
    0.5630756863681534,
    -0.5892310046041954,
    0.5271447780474939,
    -0.11959632556906954,
)
INV_SQRT_2PI = 0.3989422804014327


def nn(a, b):
    return lax.dot_general(a, b, (((1,), (0,)), ((), ())), preferred_element_type=f32)


def nt(a, b):
    return lax.dot_general(a, b, (((1,), (1,)), ((), ())), preferred_element_type=f32)


def tn(a, b):
    return lax.dot_general(a, b, (((0,), (0,)), ((), ())), preferred_element_type=f32)


def stack_rows(refs):
    return jnp.concatenate([r[...] for r in refs], 0)


def params(limit):
    return pltpu.CompilerParams(vmem_limit_bytes=limit * MIB)


def cost(flops, nbytes, exps=0):
    return pl.CostEstimate(flops=int(flops), bytes_accessed=int(nbytes), transcendentals=int(exps))


def struct(shape, dtype):
    return jax.ShapeDtypeStruct(shape, dtype)


def hbm(shape, dtype):
    return pltpu.HBM(shape, dtype)


def far(*arrays):
    return [pltpu.with_memory_space_constraint(a, pltpu.HBM) for a in arrays]


SCALARS = pl.BlockSpec(memory_space=pltpu.SMEM)
ROWS = pl.BlockSpec(memory_space=pltpu.HBM)


def full(a):
    shape = a.shape
    return pl.BlockSpec(shape, lambda *_: (0,) * len(shape))


def blocks_in(arrays):
    return [full(a) for a in arrays]


def gelu_parts(u):
    z = jnp.abs(u)
    bell = jnp.exp(-0.5 * (u * u))
    below = 1.0 + TAIL_STEP * z
    t = pl.reciprocal(below, approx=True)
    t = t * (2.0 - below * t)
    poly = jnp.full_like(t, TAIL[-1])
    for coef in TAIL[-2::-1]:
        poly = poly * t + coef
    tail = bell * (poly * t)
    phi = jnp.where(u > 0.0, 1.0 - tail, tail)
    return u * phi, phi + u * (INV_SQRT_2PI * bell)


def whole(*at):
    return lambda i: at


def project_kernel(*refs):
    x_refs, (w_ref, add_ref, out_ref, x_ref) = refs[:2], refs[2:]

    @pl.when(pl.program_id(0) == 0)
    def _():
        x_ref[...] = stack_rows(x_refs)

    out_ref[...] = (nn(x_ref[...], w_ref[0]) + add_ref[...]).astype(bf16)


def project(x, w_qkv, add):
    rows = 2 * x[0].shape[0]
    _, d, width = w_qkv.shape
    return pl.pallas_call(
        project_kernel,
        grid=(3,),
        in_specs=blocks_in(x)
        + [pl.BlockSpec((1, d, width), lambda i: (i, 0, 0)), pl.BlockSpec((1, width), lambda i: (0, i))],
        out_specs=[pl.BlockSpec((rows, width), lambda i: (0, i)), pl.BlockSpec((rows, d), whole(0, 0))],
        out_shape=[struct((rows, 3 * width), bf16), hbm((rows, d), bf16)],
        compiler_params=params(12),
        cost_estimate=cost(6 * rows * d * width, 4 * MIB),
        name="project",
    )(*x, w_qkv, add)


def input_grad_kernel(g_ref, w_ref, mine_ref, theirs_ref):
    width = w_ref.shape[2]
    part = sum(nt(g_ref[:, j * width : (j + 1) * width], w_ref[j]) for j in range(3))
    half = part.shape[0] // 2
    mine_ref[...] = part[:half]
    theirs_ref[...] = part[half:].astype(bf16)


def input_grad(d_proj, w_qkv):
    rows = d_proj.shape[0]
    _, d, width = w_qkv.shape
    outs = [struct((rows // 2, d), f32), struct((rows // 2, d), bf16)]
    return pl.pallas_call(
        input_grad_kernel,
        grid=(1,),
        in_specs=blocks_in((d_proj, w_qkv)),
        out_specs=blocks_in(outs),
        out_shape=outs,
        compiler_params=params(16),
        cost_estimate=cost(6 * rows * d * width, 4 * MIB),
        name="input_grad",
    )(d_proj, w_qkv)


def attend_kernel(scale, heads, q_ref, k0_ref, k1_ref, v0_ref, v1_ref, segq_ref, segk_ref, w_ref, *outs):
    att_ref, lse_ref, mine_ref, theirs_ref = outs
    q = q_ref[...] * jnp.asarray(scale, bf16)
    rows, width = q.shape
    ks, vs = (k0_ref, k1_ref), (v0_ref, v1_ref)
    kv_rows = k0_ref.shape[0]
    lane = lax.broadcasted_iota(jnp.int32, (1, width), 1) // HEAD_DIM
    stat_lane = lax.broadcasted_iota(jnp.int32, (1, 128), 1)
    out = jnp.zeros((rows, width), f32)
    lse = jnp.zeros((rows, 128), f32)
    segq = segq_ref[...]
    masks = [
        jnp.where(segq == segk_ref[:, i * kv_rows : (i + 1) * kv_rows], 0.0, NEG) for i in range(2)
    ]
    for h in range(heads):
        hit = lane == h
        qh = jnp.where(hit, q, jnp.zeros_like(q))
        scores = [nt(qh, ks[i][...]) + masks[i] for i in range(2)]
        peak = jnp.maximum(*[jnp.max(s, axis=1, keepdims=True) for s in scores])
        exps = [jnp.exp(s - peak) for s in scores]
        total = sum(jnp.sum(e, axis=1, keepdims=True) for e in exps)
        inv = 1.0 / total
        head_out = sum(nn((exps[i] * inv).astype(bf16), vs[i][...]) for i in range(2))
        out = jnp.where(hit, head_out, out)
        lse = jnp.where(stat_lane == h, peak + jnp.log(total), lse)
    low = out.astype(bf16)
    att_ref[...] = low
    lse_ref[...] = lse
    part = nn(low, w_ref[...])
    half = rows // 2
    mine_ref[...] = part[:half]
    theirs_ref[...] = part[half:].astype(bf16)


def attend(proj_q, proj, seg_q, seg_k, w_out, scale, heads):
    rows, width = proj_q.shape[0], heads * HEAD_DIM
    d = w_out.shape[1]
    return pl.pallas_call(
        functools.partial(attend_kernel, scale, heads),
        grid=(1,),
        in_specs=[pl.BlockSpec((rows, width), whole(0, 0))]
        + [pl.BlockSpec((rows, width), whole(0, 1))] * 2
        + [pl.BlockSpec((rows, width), whole(0, 2))] * 2
        + [
            pl.BlockSpec((rows, 1), whole(0, 0)),
            pl.BlockSpec((1, 2 * rows), whole(0, 0)),
            pl.BlockSpec((width, d), whole(0, 0)),
        ],
        out_specs=[
            pl.BlockSpec((rows, width), whole(0, 0)),
            pl.BlockSpec((rows, 128), whole(0, 0)),
            pl.BlockSpec((rows // 2, d), whole(0, 0)),
            pl.BlockSpec((rows // 2, d), whole(0, 0)),
        ],
        out_shape=[
            hbm((rows, width), bf16),
            hbm((rows, 128), f32),
            struct((rows // 2, d), f32),
            struct((rows // 2, d), bf16),
        ],
        compiler_params=params(28),
        cost_estimate=cost(32 * rows * rows * width, 6 * MIB, rows * rows * 2 * heads),
        name="attend",
    )(proj_q, *proj, *proj, seg_q, seg_k, w_out)


def attend_back_kernel(scale, heads, last, *refs):
    q_ref, k0_ref, k1_ref, v0_ref, v1_ref, segq_ref, segk_ref, lse_ref = refs[:8]
    one_refs, w_ref, refs = refs[8:10], refs[10], refs[11:]
    q = q_ref[...]
    rows, width = q.shape
    ks, vs = (k0_ref, k1_ref), (v0_ref, v1_ref)
    if last:
        dq0_ref, sumq_ref, dk_in, dv_in = refs[:4]
        g0_ref, g1_ref, sums_ref, keep_ref, dk_ref, dv_ref = refs[4:]
    else:
        dq0_ref, sumq_ref, dk_ref, dv_ref, keep_ref = refs
    lane = lax.broadcasted_iota(jnp.int32, (1, width), 1) // HEAD_DIM
    one = stack_rows(one_refs)
    keep_ref[...] = one
    grad = nt(one, w_ref[...]).astype(bf16)
    segq = segq_ref[...]
    masks = [jnp.where(segq == segk_ref[:, i * rows : (i + 1) * rows], 0.0, NEG) for i in range(2)]
    sc = jnp.asarray(scale, bf16)
    zero = jnp.zeros_like(q)
    dq = jnp.zeros((rows, width), f32)
    for h in range(heads):
        hit = lane == h
        qh = jnp.where(hit, q, zero) * sc
        gh = jnp.where(hit, grad, zero)
        lse = lse_ref[:, h : h + 1]
        probs = [jnp.exp(nt(qh, ks[i][...]) + masks[i] - lse) for i in range(2)]
        d_probs = [nt(gh, vs[i][...]) for i in range(2)]
        dot_sum = sum(jnp.sum(p * g, axis=1, keepdims=True) for p, g in zip(probs, d_probs))
        dq_h = 0.0
        for i in range(2):
            low = (probs[i] * (d_probs[i] - dot_sum)).astype(bf16)
            at = pl.ds(i * rows, rows)
            d_k, d_v = tn(low, qh), tn(probs[i].astype(bf16), gh)
            if h > 0:
                d_k, d_v = d_k + dk_ref[at, :], d_v + dv_ref[at, :]
            elif last:
                d_k, d_v = d_k + dk_in[at, :], d_v + dv_in[at, :]
            dk_ref[at, :] = d_k
            dv_ref[at, :] = d_v
            dq_h = dq_h + nn(low, ks[i][...])
        dq = jnp.where(hit, dq_h, dq)
    dq = dq * scale
    sum_q = jnp.sum(dq, axis=0, keepdims=True)
    if not last:
        dq0_ref[...] = dq.astype(bf16)
        sumq_ref[...] = sum_q
        return
    sums_ref[0:1, :] = sum_q + sumq_ref[...]
    sums_ref[1:2, :] = jnp.sum(dv_ref[...], axis=0, keepdims=True)
    g0_ref[:, :width] = dq0_ref[...]
    g1_ref[:, :width] = dq.astype(bf16)
    for i, ref in enumerate((g0_ref, g1_ref)):
        at = pl.ds(i * rows, rows)
        ref[:, width : 2 * width] = dk_ref[at, :].astype(bf16)
        ref[:, 2 * width :] = dv_ref[at, :].astype(bf16)


def attend_back(proj_q, proj, seg_q, seg_k, lse, one, w_out, scale, heads, earlier=None):
    rows, width = proj_q.shape[0], heads * HEAD_DIM
    d = w_out.shape[1]
    last = earlier is not None
    in_specs = (
        [pl.BlockSpec((rows, width), whole(0, 0))]
        + [pl.BlockSpec((rows, width), whole(0, 1))] * 2
        + [pl.BlockSpec((rows, width), whole(0, 2))] * 2
        + [
            pl.BlockSpec((rows, 1), whole(0, 0)),
            pl.BlockSpec((1, 2 * rows), whole(0, 0)),
            pl.BlockSpec((rows, 128), whole(0, 0)),
        ]
        + blocks_in(one)
        + [pl.BlockSpec((width, d), whole(0, 0))]
    )
    args = [proj_q, *proj, *proj, seg_q, seg_k, lse, *one, w_out]
    keep = [hbm((rows, d), bf16)]
    sums = [struct((2 * rows, width), f32)] * 2
    if last:
        in_specs += [pl.BlockSpec(e.shape, whole(0, 0)) for e in earlier]
        args += [*earlier]
        out_shape = [struct((rows, 3 * width), bf16)] * 2 + [struct((2, width), f32)] + keep
        scratch = [pltpu.VMEM(o.shape, f32) for o in sums]
    else:
        out_shape = [struct((rows, width), bf16), struct((1, width), f32)] + sums + keep
        scratch = []
    return pl.pallas_call(
        functools.partial(attend_back_kernel, scale, heads, last),
        grid=(1,),
        in_specs=in_specs,
        out_specs=[pl.BlockSpec(o.shape, whole(0, 0)) for o in out_shape],
        out_shape=out_shape,
        scratch_shapes=scratch,
        compiler_params=params(40),
        cost_estimate=cost(80 * rows * rows * width, 8 * MIB, rows * rows * 2 * heads),
        name="attend_back",
    )(*args)


def ffn_kernel(*refs):
    x_refs, refs = refs[:2], refs[2:]
    up_ref, down_ref, bias_ref, act_ref, slope_ref, mine_ref, theirs_ref, x, acc = refs
    step = pl.program_id(0)

    @pl.when(step == 0)
    def _():
        x[...] = stack_rows(x_refs)

    value, slope = gelu_parts(nn(x[...], up_ref[...]) + bias_ref[...])
    low = value.astype(bf16)
    act_ref[...] = low
    slope_ref[...] = slope
    add_up(step, nn(low, down_ref[...]), acc, mine_ref, theirs_ref)


def add_up(step, part, acc, mine_ref, theirs_ref):
    @pl.when(step == 0)
    def _():
        acc[...] = part

    @pl.when(step > 0)
    def _():
        acc[...] += part

    @pl.when(step == pl.num_programs(0) - 1)
    def _():
        half = acc.shape[0] // 2
        mine_ref[...] = acc[:half]
        theirs_ref[...] = acc[half:].astype(bf16)


def ffn(x, w_up, w_down, bias, tile=1024):
    rows, d = 2 * x[0].shape[0], x[0].shape[1]
    half = rows // 2
    ff = w_up.shape[1]
    moving = lambda i: (0, i)
    return pl.pallas_call(
        ffn_kernel,
        grid=(ff // tile,),
        in_specs=[
            *blocks_in(x),
            pl.BlockSpec((d, tile), moving),
            pl.BlockSpec((tile, d), lambda i: (i, 0)),
            pl.BlockSpec((1, tile), moving),
        ],
        out_specs=[
            pl.BlockSpec((rows, tile), moving),
            pl.BlockSpec((rows, tile), moving),
            pl.BlockSpec((half, d), whole(0, 0)),
            pl.BlockSpec((half, d), whole(0, 0)),
            pl.BlockSpec((rows, d), whole(0, 0)),
        ],
        out_shape=[
            hbm((rows, ff), bf16),
            hbm((rows, ff), f32),
            struct((half, d), f32),
            struct((half, d), bf16),
            hbm((rows, d), bf16),
        ],
        scratch_shapes=[pltpu.VMEM((rows, d), f32)],
        compiler_params=params(20),
        cost_estimate=cost(4 * rows * d * ff, 9 * MIB, rows * ff * 2),
        name="ffn",
    )(*x, w_up, w_down, bias)


def ffn_back_kernel(*refs):
    x_refs, refs = refs[:2], refs[2:]
    up_ref, down_ref, slope_ref, low_ref, sum_ref, mine_ref, theirs_ref, x, acc = refs
    step = pl.program_id(0)

    @pl.when(step == 0)
    def _():
        x[...] = stack_rows(x_refs)

    d_up = nt(x[...], down_ref[...]) * slope_ref[...]
    low = d_up.astype(bf16)
    low_ref[...] = low
    sum_ref[...] = jnp.sum(d_up, axis=0, keepdims=True)
    add_up(step, nt(low, up_ref[...]), acc, mine_ref, theirs_ref)


def ffn_back(x, w_up, w_down, slope, tile=1024):
    rows, d = 2 * x[0].shape[0], x[0].shape[1]
    half = rows // 2
    ff = w_up.shape[1]
    moving = lambda i: (0, i)
    return pl.pallas_call(
        ffn_back_kernel,
        grid=(ff // tile,),
        in_specs=[
            *blocks_in(x),
            pl.BlockSpec((d, tile), moving),
            pl.BlockSpec((tile, d), lambda i: (i, 0)),
            pl.BlockSpec((rows, tile), moving),
        ],
        out_specs=[
            pl.BlockSpec((rows, tile), moving),
            pl.BlockSpec((1, tile), moving),
            pl.BlockSpec((half, d), whole(0, 0)),
            pl.BlockSpec((half, d), whole(0, 0)),
            pl.BlockSpec((rows, d), whole(0, 0)),
        ],
        out_shape=[
            hbm((rows, ff), bf16),
            struct((1, ff), f32),
            struct((half, d), f32),
            struct((half, d), bf16),
            hbm((rows, d), bf16),
        ],
        scratch_shapes=[pltpu.VMEM((rows, d), f32)],
        compiler_params=params(20),
        cost_estimate=cost(4 * rows * d * ff, 9 * MIB),
        name="ffn_back",
    )(*x, w_up, w_down, *far(slope))


def lines_of(field, head_width, ff_width):
    return {"qkv": 3 * head_width, "out": head_width, "up": ff_width, "down": ff_width}[field]


def pack_kernel(fields, *refs):
    out_ref, at = refs[-1], 0
    for field, ref in zip(fields, refs):
        if field == "qkv":
            for j in range(3):
                for h in range(0, ref.shape[3], 128):
                    out_ref[at : at + 128, :] = ref[0, j, :, h : h + 128]
                    at += 128
        elif field == "up":
            for h in range(0, ref.shape[2], 128):
                out_ref[at : at + 128, :] = ref[0, :, h : h + 128]
                at += 128
        else:
            out_ref[at : at + ref.shape[1], :] = ref[0]
            at += ref.shape[1]


def pack(fields, args, layer):
    ins = [args[f] for f in fields]
    piece = args["up"].shape[1]
    if piece != 128:
        flat = {
            "qkv": lambda a: a[layer].transpose(0, 2, 1).reshape(-1, piece),
            "up": lambda a: a[layer].T,
            "out": lambda a: a[layer],
            "down": lambda a: a[layer],
        }
        return jnp.concatenate([flat[f](a) for f, a in zip(fields, ins)], 0)
    lines = sum(a.size // a.shape[0] for a in ins) // piece
    return pl.pallas_call(
        functools.partial(pack_kernel, fields),
        grid=(1,),
        in_specs=[
            pl.BlockSpec((1,) + a.shape[1:], whole(layer, *([0] * (a.ndim - 1)))) for a in ins
        ],
        out_specs=pl.BlockSpec((lines, piece), whole(0, 0)),
        out_shape=struct((lines, piece), bf16),
        compiler_params=params(8),
        cost_estimate=cost(0, 4 * lines * piece),
        name="pack",
    )(*far(*ins))


def maps_kernel(group_rows, lengths_ref, order_ref, spot_ref, src_ref, segc_ref, segr_ref):
    group, slot, rows = spot_ref[0], spot_ref[1], group_rows // 4
    base = group * SEQ_GRP
    lens = [lengths_ref[base + i] for i in range(SEQ_GRP)]
    starts = [0, lens[0], lens[0] + lens[1]]
    end, ends, shifts = 0, [], []
    for j in range(SEQ_GRP):
        seq = order_ref[base + j] - base
        length, start = lens[SEQ_GRP - 1], starts[SEQ_GRP - 1]
        for i in range(SEQ_GRP - 1):
            length = jnp.where(seq == i, lens[i], length)
            start = jnp.where(seq == i, starts[i], start)
        shifts.append(start - end)
        end = end + length
        ends.append(end)

    def turn(x):
        return x % 2 * 2 + x // 2

    def position(shape, axis):
        at = lax.broadcasted_iota(jnp.int32, shape, axis)
        return jnp.bitwise_xor(turn(at // rows), slot) * rows + at % rows

    def segment(place):
        return sum((place >= e).astype(jnp.int32) for e in ends)

    segr_ref[...] = segment(position(segr_ref.shape, 1))
    place = position(segc_ref.shape, 0)
    seg = segment(place)
    segc_ref[...] = seg
    source = place
    for j in range(SEQ_GRP):
        source = jnp.where(seg == j, place + shifts[j], source)
    src_ref[...] = turn(jnp.bitwise_xor(source // rows, slot)) * rows + source % rows


def maps(lengths, order, spot, group_rows):
    outs = [struct((group_rows, 1), jnp.int32)] * 2 + [struct((1, group_rows), jnp.int32)]
    return pl.pallas_call(
        functools.partial(maps_kernel, group_rows),
        grid=(1,),
        in_specs=[SCALARS] * 3,
        out_specs=blocks_in(outs),
        out_shape=outs,
        compiler_params=params(8),
        cost_estimate=cost(100 * group_rows, 8 * group_rows),
        name="maps",
    )(lengths, order, spot)


def tile_at(where_ref, spec):
    masked, d, core = spec
    d = jnp.bitwise_xor(where_ref[0], d) if masked else d
    tile = 2 * d + jnp.bitwise_xor(where_ref[1], core)
    return pl.ds(pl.multiple_of(tile * 128, 128), 128)


def tile_order(where, specs):
    return jnp.stack([2 * (where[0] ^ d if m else d) + (where[1] ^ core) for m, d, core in specs])


def place_kernel(fields, counts, specs, where_ref, *refs):
    ins, outs = refs[: len(counts)], refs[len(counts) :]
    k = 0
    for ref, count in zip(ins, counts):
        for i in range(count):
            here = tile_at(where_ref, specs[k])
            at = 0
            for field, out in zip(fields, outs):
                if field == "qkv":
                    for j in range(3):
                        for h in range(0, out.shape[2], 128):
                            out[j, here, h : h + 128] = ref[i, at : at + 128, :]
                            at += 128
                elif field == "up":
                    for h in range(0, out.shape[1], 128):
                        out[here, h : h + 128] = ref[i, at : at + 128, :]
                        at += 128
                else:
                    out[:, here] = ref[i, at : at + out.shape[0], :]
                    at += out.shape[0]
            k += 1


def place(fields, stacks, specs, where, head_width, ff_width):
    counts = [s.shape[0] for s in stacks]
    piece = stacks[0].shape[2]
    if piece != 128:
        tiles = jnp.take(jnp.concatenate(stacks, 0), jnp.argsort(tile_order(where, specs)), axis=0)
        flat = tiles.transpose(1, 0, 2).reshape(-1, D)
        found, at = [], 0
        for f in fields:
            lines = lines_of(f, head_width, ff_width)
            part = flat[at : at + lines]
            at += lines
            if f == "qkv":
                part = part.reshape(3, head_width, D).transpose(0, 2, 1)
            found.append(part.T if f == "up" else part)
        return found
    shapes = {
        "qkv": (3, D, head_width),
        "out": (head_width, D),
        "up": (D, ff_width),
        "down": (ff_width, D),
    }
    outs = [struct(shapes[f], bf16) for f in fields]
    return pl.pallas_call(
        functools.partial(place_kernel, fields, counts, specs),
        grid=(1,),
        in_specs=[SCALARS] + blocks_in(stacks),
        out_specs=blocks_in(outs),
        out_shape=outs,
        compiler_params=params(20),
        cost_estimate=cost(0, 4 * sum(s.size for s in stacks)),
        name="place",
    )(where, *stacks)


def grad_kernel(fields, counts, specs, where_ref, *refs):
    count = len(fields)
    ins, refs = refs[: 4 * count], refs[4 * count :]
    outs, bufs, sems = refs[: len(counts)], refs[len(counts) : -1], refs[-1]
    rows = ins[0].shape[0]
    copies = []
    for n in range(4 * count):
        there = bufs[n // 2].at[pl.ds(n % 2 * rows, rows), :]
        copies.append(pltpu.make_async_copy(ins[n], there, sems.at[n]))
        copies[-1].start()
    spots = [(out, i) for out, total in zip(outs, counts) for i in range(total)]
    at = 0
    for n, field in enumerate(fields):
        for copy in copies[4 * n : 4 * n + 4]:
            copy.wait()
        a_ref, b_ref = bufs[2 * n : 2 * n + 2]
        b = b_ref[...]
        lines = b.shape[1]
        for g in range(0, len(specs), 4):
            a = jnp.concatenate([a_ref[:, tile_at(where_ref, t)] for t in specs[g : g + 4]], 1)
            by_rows = field in ("qkv", "up")
            total = (tn(a, b) if by_rows else tn(b, a)).astype(bf16)
            for k, (out, i) in enumerate(spots[g : g + 4]):
                tile = slice(k * 128, (k + 1) * 128)
                if by_rows:
                    for h in range(0, lines, 128):
                        out[i, at + h : at + h + 128, :] = total[tile, h : h + 128]
                else:
                    out[i, at : at + lines, :] = total[:, tile]
        at += lines


def weight_grad(fields, pairs, specs, counts, where):
    flat = [r for a, b in pairs for r in (*a, *b)]
    lines = sum(b[0].shape[1] for _, b in pairs)
    rows = sum(b.shape[0] for b in pairs[0][1])
    piece = D // len(specs)
    if piece != 128:
        products = [dot(jnp.concatenate(b, 0), jnp.concatenate(a, 0), 0, 0) for a, b in pairs]
        tiles = jnp.concatenate(products, 0).astype(bf16).reshape(lines, len(specs), piece)
        tiles = jnp.take(tiles.transpose(1, 0, 2), tile_order(where, specs), axis=0)
        ends = [sum(counts[: i + 1]) for i in range(len(counts))]
        return [tiles[e - n : e] for e, n in zip(ends, counts)]
    kind = struct if len(counts) > 1 else hbm
    outs = [kind((n, lines, piece), bf16) for n in counts]
    bufs = [pltpu.VMEM((rows, r.shape[1]), bf16) for r in flat[::2]]
    return pl.pallas_call(
        functools.partial(grad_kernel, fields, counts, specs),
        grid=(1,),
        in_specs=[SCALARS] + [ROWS] * len(flat),
        out_specs=blocks_in(outs),
        out_shape=outs,
        scratch_shapes=bufs + [pltpu.SemaphoreType.DMA((len(flat),))],
        compiler_params=params(32),
        cost_estimate=cost(2 * rows * D * lines, 12 * MIB),
        name="weight_grad",
    )(where, *far(*flat))


def finish_kernel(fields, has_prev, keep_ref, got_ref, *refs):
    outs = refs[len(fields) if has_prev else 0 :]
    at = 0
    for field, out in zip(fields, outs):
        if field == "qkv":
            for j in range(3):
                for h in range(0, out.shape[3], 128):
                    out[0, j, :, h : h + 128] = keep_ref[at : at + 128, :] + got_ref[at : at + 128, :].astype(f32)
                    at += 128
        elif field == "up":
            for h in range(0, out.shape[2], 128):
                out[0, :, h : h + 128] = keep_ref[at : at + 128, :] + got_ref[at : at + 128, :].astype(f32)
                at += 128
        else:
            n = out.shape[1]
            out[0] = keep_ref[at : at + n, :] + got_ref[at : at + n, :].astype(f32)
            at += n


def finish(fields, keep, got, layer, prev, head_width, ff_width):
    piece = keep.shape[1]
    shapes = {
        "qkv": (3, piece, head_width),
        "out": (head_width, piece),
        "up": (piece, ff_width),
        "down": (ff_width, piece),
    }
    if piece != 128:
        total, at, found = keep + got.astype(f32), 0, []
        for n, f in enumerate(fields):
            lines = lines_of(f, head_width, ff_width)
            part = total[at : at + lines]
            at += lines
            if f == "qkv":
                part = part.reshape(3, head_width, piece).transpose(0, 2, 1)
            part = part.T if f == "up" else part
            base = jnp.zeros((LAYERS,) + shapes[f], f32) if prev is None else prev[n]
            found.append(base.at[layer].set(part))
        return found
    outs = [struct((LAYERS,) + shapes[f], f32) for f in fields]
    specs = [
        pl.BlockSpec((1,) + o.shape[1:], whole(layer, *([0] * (len(o.shape) - 1)))) for o in outs
    ]
    return pl.pallas_call(
        functools.partial(finish_kernel, fields, prev is not None),
        grid=(1,),
        in_specs=[pl.BlockSpec(keep.shape, whole(0, 0))] * 2
        + ([] if prev is None else [pl.BlockSpec(memory_space=pl.ANY)] * len(outs)),
        out_specs=specs,
        out_shape=outs,
        input_output_aliases={} if prev is None else {2 + n: n for n in range(len(outs))},
        compiler_params=params(16),
        cost_estimate=cost(0, 10 * keep.size),
        name="finish",
    )(keep, got, *([] if prev is None else prev))


def deal_kernel(src_ref, *refs):
    raw, outs = stack_rows(refs[:4]), refs[4:]
    rows = outs[0].shape[0]
    spot = lax.broadcasted_iota(jnp.int32, (1, raw.shape[0]), 1)
    hit = src_ref[...] == spot
    dealt = nn(jnp.where(hit, 1.0, 0.0).astype(bf16), raw)
    for i in range(4):
        outs[i][...] = dealt[i * rows : (i + 1) * rows].astype(bf16)
    outs[4][...] = dealt[:rows]


def deal_rows(src, raw):
    rows, d = raw[0].shape
    outs = [struct((rows, d), bf16)] * 4 + [struct((rows, d), f32)]
    outs = pl.pallas_call(
        deal_kernel,
        grid=(1,),
        in_specs=blocks_in((src, *raw)),
        out_specs=blocks_in(outs),
        out_shape=outs,
        compiler_params=params(20),
        cost_estimate=cost(32 * rows * rows * d, 6 * MIB),
        name="deal_rows",
    )(src, *raw)
    return outs[:2], outs[2:4], outs[4]


def total_of(refs):
    total = refs[0][...]
    for ref in refs[1:]:
        total = total + ref[...].astype(f32)
    return total


def norm_kernel(n_terms, bias_row, gain_row, shift_row, *refs):
    terms, (vec_ref, y_ref, low_ref, n_ref, r_ref) = refs[:n_terms], refs[n_terms:]
    row = lambda i: vec_ref[i : i + 1, :]
    v = total_of(terms) + row(bias_row)
    centred = v - jnp.mean(v, axis=-1, keepdims=True)
    r = lax.rsqrt(jnp.mean(centred * centred, axis=-1, keepdims=True) + EPS)
    n = centred * r
    y = n * row(gain_row) + row(shift_row)
    y_ref[...] = y
    low_ref[...] = y.astype(bf16)
    n_ref[...] = n
    r_ref[...] = r


def term_specs(terms):
    shape = terms[0].shape
    return [pl.BlockSpec(shape, whole(0, 0)) for _ in terms]


def norm(terms, vectors, bias_row, gain_row, shift_row):
    shape = terms[0].shape
    outs = [struct(shape, f32), struct(shape, bf16), hbm(shape, f32), struct((shape[0], 1), f32)]
    return pl.pallas_call(
        functools.partial(norm_kernel, len(terms), bias_row, gain_row, shift_row),
        grid=(1,),
        in_specs=term_specs(terms) + [full(vectors)],
        out_specs=blocks_in(outs),
        out_shape=outs,
        compiler_params=params(8),
        cost_estimate=cost(20 * terms[0].size, 2 * MIB),
        name="norm",
    )(*terms, vectors)


def norm_back_kernel(n_terms, gain_row, has_sums, *refs):
    terms, refs = refs[:n_terms], refs[n_terms:]
    n_ref, r_ref, vec_ref = refs[:3]
    dv_ref, low_ref, sums_ref = refs[-3:]
    d_out, n = total_of(terms), n_ref[...]
    dn = d_out * vec_ref[gain_row : gain_row + 1, :]
    dv = r_ref[...] * (
        dn - jnp.mean(dn, axis=-1, keepdims=True) - n * jnp.mean(dn * n, axis=-1, keepdims=True)
    )
    dv_ref[...] = dv
    low_ref[...] = dv.astype(bf16)
    for i, a in enumerate((d_out * n, d_out, dv)):
        column = jnp.sum(a, axis=0, keepdims=True)
        sums_ref[i : i + 1, :] = column + refs[3][i : i + 1, :] if has_sums else column


def norm_back(terms, n, r, vectors, gain_row, sums=None):
    shape = terms[0].shape
    outs = [struct(shape, f32), struct(shape, bf16), struct((3, shape[1]), f32)]
    more = [] if sums is None else [sums]
    return pl.pallas_call(
        functools.partial(norm_back_kernel, len(terms), gain_row, sums is not None),
        grid=(1,),
        in_specs=term_specs(terms) + blocks_in((n, r, vectors, *more)),
        out_specs=blocks_in(outs),
        out_shape=outs,
        compiler_params=params(8),
        cost_estimate=cost(20 * terms[0].size, 3 * MIB),
        name="norm_back",
    )(*terms, n, r, vectors, *more)


def dot(a, b, ca, cb):
    return lax.dot_general(a, b, (((ca,), (cb,)), ((), ())), preferred_element_type=f32)


def swap(a, axis):
    return lax.ppermute(a, axis, SWAP)


def flip_d(a, bit, n_d):
    return lax.ppermute(a, "d", [(i, i ^ (1 << bit)) for i in range(n_d)])


def to_home(a):
    return lax.ppermute(a, ("c", "zh"), [(1, 2), (2, 1)])


def after(a, *marks):
    return lax.optimization_barrier((a,) + marks)[0]


def send_rows(own):
    return (own, swap(own, "c")), swap(own, "zl")


def far_rows(far, *marks):
    if marks:
        far = after(far, *marks)
    return far, swap(far, "c")


def chip_sum(mine, theirs, *arrivals):
    other = swap(after(theirs, *arrivals) if arrivals else theirs, "c")
    return mine, other


def cross_sum(terms):
    total = (terms[0] + terms[1].astype(f32)).astype(bf16)
    return total, swap(total, "zl")


def masks_of(order):
    masks = [0]
    for bit in order:
        masks = masks + [m ^ (1 << bit) for m in masks]
    return masks


def absolute_specs(n_d):
    return [(False, d, core) for d in range(n_d) for core in range(2)]


def reduce_specs(n_d):
    bits = list(range(n_d.bit_length() - 1))
    half = n_d // 2
    order = []
    for core, masks in ((0, masks_of(bits)), (1, masks_of(bits[::-1]))):
        order += [(True, m, core) for m in masks[half:] + masks[:half]]
    return order


class Gather:
    def __init__(self, fields, args, layer, pos, where, n_d):
        self.fields, self.pos, self.where, self.n_d = fields, pos, where, n_d
        self.widths = args["out"].shape[1], args["down"].shape[1]
        self.tile = pack(fields, args, layer)
        self.crossed = []

    def cross(self, *marks, parts=1):
        lines = self.tile.shape[0] // parts
        part = self.tile[len(self.crossed) * lines : (len(self.crossed) + 1) * lines]
        self.crossed.append(swap(after(part, *marks) if marks else part, "zh"))
        return self.crossed[-1]

    def cores(self, *marks):
        _, c, zh, _ = self.pos
        same = c == zh
        crossed = jnp.concatenate(self.crossed, 0) if len(self.crossed) > 1 else self.crossed[0]
        crossed = after(crossed, *marks) if marks else crossed
        self.own = jnp.where(same, self.tile, crossed)
        self.other = swap(jnp.where(same, crossed, self.tile), "c")
        return self.other

    def collect(self, *marks):
        both = jnp.stack([self.own, self.other])
        if marks:
            both = after(both, *marks)
        self.stacks = [lax.all_gather(both, "d", axis=0, tiled=True)]
        self.specs = absolute_specs(self.n_d)
        return self.stacks[0]

    def weights(self):
        found = place(self.fields, self.stacks, self.specs, self.where, *self.widths)
        return dict(zip(self.fields, found))


class Reduce:
    def __init__(self, fields, pairs, pos, where, n_d, by_halves):
        self.fields, self.pos, self.n_d, self.step = fields, pos, n_d, 0
        specs = reduce_specs(n_d) if by_halves else absolute_specs(n_d)
        counts = [n_d // 2] * 4 if by_halves else [2 * n_d]
        self.stacks = weight_grad(fields, pairs, specs, counts, where)

    def collect(self, *marks):
        both = lax.psum_scatter(after(self.stacks[0], *marks), "d", scatter_dimension=0, tiled=True)
        self.first, self.second = both[0], both[1]
        return both

    def halve(self, *marks):
        bits = list(range(self.n_d.bit_length() - 1))
        if self.step == len(bits):
            return []
        if self.step == 0:
            self.sends, self.keeps = [self.stacks[0], self.stacks[2]], [self.stacks[1], self.stacks[3]]
        sends = lax.optimization_barrier((*self.sends, *marks))[:2] if marks else self.sends
        orders = (bits[::-1], bits)
        gots = [flip_d(a, o[self.step], self.n_d) for a, o in zip(sends, orders)]
        self.step += 1
        half = self.keeps[0].shape[0] // 2
        if self.step < len(bits):
            self.sends = [
                (k[half:].astype(f32) + g[half:].astype(f32)).astype(bf16)
                for k, g in zip(self.keeps, gots)
            ]
            self.keeps = [k[:half].astype(f32) + g[:half].astype(f32) for k, g in zip(self.keeps, gots)]
        else:
            self.first, self.second = (k[0].astype(f32) + g[0].astype(f32) for k, g in zip(self.keeps, gots))
        return gots

    def cores(self, *marks):
        while len(self.stacks) > 1 and self.step < self.n_d.bit_length() - 1:
            self.halve()
        second = self.second.astype(bf16)
        self.other = swap(after(second, *marks) if marks else second, "c")
        self.crossed, self.at = [], 0
        return self.other

    def cross(self, lines, *marks):
        _, c, zh, _ = self.pos
        same = c == zh
        part = slice(self.at, self.at + lines)
        send = jnp.where(same, self.other[part], self.first[part].astype(bf16))
        self.crossed.append(swap(after(send, *marks) if marks else send, "zh"))
        self.at += lines
        return self.crossed[-1]

    def finish(self, outs, layer, widths, *marks):
        _, c, zh, _ = self.pos
        got = jnp.concatenate(self.crossed, 0) if len(self.crossed) > 1 else self.crossed[0]
        first = after(self.first, *marks) if marks else self.first
        keep = jnp.where(c == zh, first.astype(f32), self.other.astype(f32))
        prev = None if outs[self.fields[0]] is None else [outs[f] for f in self.fields]
        outs.update(zip(self.fields, finish(self.fields, keep, got, layer, prev, *widths)))


def gather_small(own, pos, n_d):
    d, c, _, zl = pos
    cur = own
    for axis, me in (("zl", zl), ("c", c)):
        got = swap(cur, axis)
        cur = jnp.where(me == 0, jnp.concatenate([cur, got]), jnp.concatenate([got, cur]))
    for bit in range(n_d.bit_length() - 1):
        got = flip_d(cur, bit, n_d)
        mine = jnp.bitwise_and(jnp.right_shift(d, bit), 1)
        cur = jnp.where(mine == 0, jnp.concatenate([cur, got]), jnp.concatenate([got, cur]))
    return cur


def pick(a, at, axis):
    return lax.dynamic_index_in_dim(a, at, axis, keepdims=False)


def halve_small(cur, me, send):
    view = cur.reshape(2, -1, cur.shape[1])
    return pick(view, me, 0) + send(pick(view, 1 - me, 0))


def body(tokens, cotangent, lengths, order, w_qkv, w_out, w_up, w_down, gains, biases, up_bias):
    rows = tokens.shape[0]
    n_d = lax.axis_size("d")
    n_dev = n_d * 8
    head_width = D // 4
    heads = head_width // HEAD_DIM
    ff_width = FF // 4
    widths = (head_width, ff_width)
    scale = HEAD_DIM ** (-0.5)
    d, c, zh, zl = (lax.axis_index(a) for a in ALL)
    pos = (d, c, zh, zl)
    slot = 2 * c + zl
    where = jnp.stack([d, c]).astype(jnp.int32)
    stay = c == zh
    args = {"qkv": w_qkv.transpose(0, 2, 1, 3), "out": w_out, "up": w_up, "down": w_down}

    def gather(fields, layer):
        return Gather(fields, args, layer, pos, where, n_d)

    g_a0 = gather(("qkv", "out"), 0)
    a0_crossed = g_a0.cross()
    g_f0, g_a1, g_f1 = gather(("up", "down"), 0), gather(("qkv", "out"), 1), gather(("up", "down"), 1)
    small_own = jnp.concatenate([a.reshape(1, -1) for a in (gains, biases, up_bias)], 1)
    src, seg_col, seg_row = maps(
        lengths, order, jnp.stack([d * 2 + zh, slot]).astype(jnp.int32), 4 * rows
    )
    seg_near, seg_far = seg_col[: 2 * rows], seg_col[2 * rows :]
    g_a0.cores(src, small_own, *[g.tile for g in (g_f0, g_a1, g_f1)])
    g_a0.collect()
    raw_got = to_home(after(tokens, a0_crossed))
    raw = jnp.where(stay, tokens, raw_got)
    raw_near, raw_far = send_rows(raw)
    f0_crossed = g_f0.cross(raw_got)
    x_near, x_far, hidden = deal_rows(src, [*raw_near, *far_rows(raw_far)])
    small_near = gather_small(after(small_own, g_a0.other), pos, n_d)
    small_far = swap(small_near, "zh")
    width = D // n_dev
    up_width = FF // n_dev
    n_vec = LAYERS * 8
    small_all = jnp.where(zh == 0, jnp.stack([small_near, small_far]), jnp.stack([small_far, small_near]))
    small_all = small_all.reshape(2, n_d * 2, 2, -1)
    vectors = small_all[..., : n_vec * width].reshape(2, n_d * 2, 2, n_vec, width)
    vectors = vectors.transpose(3, 1, 0, 2, 4).reshape(n_vec, D)
    ups = small_all[..., n_vec * width :].reshape(2, n_d * 2, 2, LAYERS, up_width)
    ups = ups.transpose(3, 1, 0, 2, 4).reshape(LAYERS, FF)
    ups = lax.dynamic_slice(ups, (0, slot * ff_width), (LAYERS, ff_width))
    own_vectors = lax.dynamic_slice(vectors, (0, slot * head_width), (n_vec, head_width))
    gain_row = lambda layer, i: 2 * layer + i
    bias_row = lambda layer, i: 2 * LAYERS + 6 * layer + i
    f0_other = g_f0.cores(x_near[0])
    g_f0.collect()
    a1_crossed = g_a1.cross(f0_other)
    weights = [g_a0.weights(), {}]

    kept = []
    x_sent = None
    for layer in range(LAYERS):
        first = layer == 0
        w = weights[layer]
        q_row, v_row = bias_row(layer, 0), bias_row(layer, 1)
        add = jnp.concatenate(
            [
                own_vectors[q_row : q_row + 1],
                jnp.zeros((1, head_width), f32),
                own_vectors[v_row : v_row + 1],
            ],
            1,
        )
        proj_near, keep_near = project(x_near, w["qkv"], add)
        if not first:
            x_far = far_rows(x_sent, keep_near)
        proj_far, keep_far = project(x_far, w["qkv"], add)
        proj = (proj_near, proj_far)
        x_kept = (keep_near, keep_far)
        due = [a1_crossed] if first else []
        if not first:
            cot_got = to_home(after(cotangent, proj_far))
        att_far, lse_far, mine, theirs = attend(
            proj_far, proj, seg_far, seg_row, w["out"], scale, heads
        )
        chip, crossed = cross_sum(chip_sum(mine, theirs, *due))
        att_near, lse_near, mine, theirs = attend(
            after(proj_near, chip), proj, seg_near, seg_row, w["out"], scale, heads
        )
        due = [crossed] if first else [crossed, cot_got]
        terms = (*chip_sum(mine, theirs, *due), crossed)
        at = [bias_row(layer, 2), gain_row(layer, 0), bias_row(layer, 3)]
        normed, low, n_one, r_one = norm((hidden, *terms), vectors, *at)
        n_near, n_sent = send_rows(low)
        due = [n_sent]
        if first:
            w.update(g_f0.weights())
            g_a1.cores(low)
            g_a1.collect()
            due += [g_f1.cross(low, parts=2)]
        else:
            w.update(g_f1.weights())
        u_bias = ups[layer : layer + 1]
        act_near, slope_near, mine_near, theirs_near, keep_near = ffn(n_near, w["up"], w["down"], u_bias)
        near = chip_sum(mine_near, theirs_near, *due)
        n_far = far_rows(n_sent, keep_near)
        due = []
        if first:
            due += [g_f1.cross(keep_near, parts=2)]
        else:
            cot = jnp.where(stay, cotangent, cot_got)
            cot_near, cot_sent = send_rows(after(cot, keep_near))
            due += [cot_sent]
        act_far, slope_far, mine, theirs, keep_far = ffn(n_far, w["up"], w["down"], u_bias)
        chip, crossed = cross_sum(chip_sum(mine, theirs, *due))
        if first:
            g_f1.cores(chip)
            g_f1.collect()
        at = [bias_row(layer, 4), gain_row(layer, 1), bias_row(layer, 5)]
        hidden, low, n_two, r_two = norm((normed, *near, crossed), vectors, *at)
        kept.append(
            dict(
                x=x_kept, proj=proj, lse=(lse_near, lse_far), att=(att_near, att_far),
                one=(n_one, r_one), n=(keep_near, keep_far), slope=(slope_near, slope_far),
                act=(act_near, act_far), two=(n_two, r_two),
            )
        )
        if first:
            weights[1].update(g_a1.weights())
            x_near, x_sent = send_rows(low)
    last_low = low

    deal = (src[:rows] == jnp.arange(4 * rows, dtype=jnp.int32)[None, :]).astype(bf16)
    cot = jnp.concatenate([*cot_near, *far_rows(cot_sent)], 0)
    valid = (seg_near[:rows] < SEQ_GRP).astype(f32)
    grad_y = (dot(deal, cot, 1, 0) * valid,)
    vector_sums = [None] * LAYERS
    up_sums = [None] * LAYERS
    late = None

    def spot(vec, full_width):
        return lax.dynamic_update_slice(jnp.zeros((1, full_width), f32), vec, (0, slot * vec.shape[1]))

    for layer in reversed(range(LAYERS)):
        w, k = weights[layer], kept[layer]
        d_two, low, sums_two = norm_back(grad_y, *k["two"], vectors, gain_row(layer, 1))
        two_near, two_sent = send_rows(low)
        if late:
            late[0].cores(low)
        up_near, sum_near, mine_near, theirs_near, keep_two_near = ffn_back(
            two_near, w["up"], w["down"], k["slope"][0]
        )
        near = chip_sum(mine_near, theirs_near, two_sent)
        two_far = far_rows(two_sent, up_near)
        due = []
        if late:
            due += [late[0].cross(ff_width, up_near)]
        up_far, sum_far, mine, theirs, keep_two_far = ffn_back(
            two_far, w["up"], w["down"], k["slope"][1]
        )
        chip, crossed = cross_sum(chip_sum(mine, theirs, *due))
        two_pair = ((keep_two_near, keep_two_far), (k["act"][0], after(k["act"][1], chip)))
        up_pair = (k["n"], (up_near, after(up_far, chip)))
        due = []
        if late:
            due += [late[0].cross(ff_width, chip)]
            r_down = Reduce(("down",), (two_pair,), pos, where, n_d, True)
            down_got = r_down.halve()
            up_pair = (up_pair[0], (up_near, after(up_far, r_down.stacks[0])))
            r_ff = Reduce(("up",), (up_pair,), pos, where, n_d, True)
            up_got = r_ff.halve()
        else:
            r_ff = Reduce(("up", "down"), (up_pair, two_pair), pos, where, n_d, False)
        d_two = after(d_two, r_ff.stacks[0], *due)
        d_one, low, sums_one = norm_back((d_two, *near, crossed), *k["one"], vectors, gain_row(layer, 0))
        one_near, one_sent = send_rows(low)
        if not late:
            r_ff.collect(low)
        *earlier, keep_one_near = attend_back(
            k["proj"][0], k["proj"], seg_near, seg_row, k["lse"][0], one_near, w["out"], scale, heads
        )
        one_far = far_rows(one_sent, earlier[0])
        due = []
        if late:
            earlier[0] = after(earlier[0], *down_got, *up_got)
            due += r_down.halve(earlier[0]) + r_ff.halve(earlier[0])
            late[1].cores(earlier[0])
            due += [late[1].cross(4 * head_width, earlier[0])]
        else:
            mixed_got = to_home(after(last_low, earlier[0]))
            due += [mixed_got]
        d_near, d_far, head_sums, keep_one_far = attend_back(
            k["proj"][1], k["proj"], seg_far, seg_row, k["lse"][1], one_far, w["out"], scale, heads,
            earlier,
        )
        d_far = after(d_far, *due)
        mine, theirs = input_grad(d_far, w["qkv"])
        chip, crossed = cross_sum(chip_sum(mine, theirs))
        att_pairs = ((k["x"], (d_near, after(d_far, chip))), ((keep_one_near, keep_one_far), k["att"]))
        if late:
            r_att = Reduce(("qkv", "out"), att_pairs, pos, where, n_d, True)
            r_att.halve()
            d_near = after(d_near, r_att.stacks[0])
            near = chip_sum(*input_grad(d_near, w["qkv"]))
        else:
            near = chip_sum(*input_grad(after(d_near, chip), w["qkv"]))
            r_att = Reduce(("qkv", "out"), att_pairs, pos, where, n_d, False)
            late = (r_ff, r_att)
            d_one = after(d_one, r_att.stacks[0])
            r_att.collect(crossed)
        grad_y = (d_one, *near, crossed)
        vector_sums[layer] = (
            [sums_one[0:1], sums_two[0:1]],
            [
                spot(head_sums[0:1], D), spot(head_sums[1:2], D), sums_one[2:3],
                sums_one[1:2], sums_two[2:3], sums_two[1:2],
            ],
        )
        up_sums[layer] = spot(sum_near + sum_far, FF)

    r_down.cores(d_far)
    down_crossed = r_down.cross(ff_width)
    r_ff.cores(d_far)
    up_crossed = r_ff.cross(ff_width, down_crossed)
    att_got = r_att.halve(down_crossed)
    base, mine, other, crossed = grad_y
    own_grad = (base + mine + other.astype(f32) + crossed.astype(f32)).astype(bf16)
    grad_got = to_home(after(own_grad, *att_got))
    r_att.cores(up_crossed)
    r_att.cross(4 * head_width)
    outs = {f: None for f in ("qkv", "out", "up", "down")}
    for r in late:
        r.finish(outs, 1, widths, *att_got)
    r_down.finish(outs, 0, widths, *att_got)
    r_ff.finish(outs, 0, widths, *att_got)
    r_att.finish(outs, 0, widths)
    tokens_grad = jnp.where(stay, own_grad, grad_got).astype(f32)
    mixed = jnp.where(stay, last_low, after(mixed_got, *att_got))

    terms = jnp.concatenate(
        [g for s in vector_sums for g in s[0]] + [b for s in vector_sums for b in s[1]], 0
    )
    small = jnp.concatenate(
        [
            terms.reshape(n_vec, n_dev, width).transpose(1, 0, 2).reshape(n_dev, n_vec * width),
            jnp.concatenate(up_sums, 0)
            .reshape(LAYERS, n_dev, up_width)
            .transpose(1, 0, 2)
            .reshape(n_dev, LAYERS * up_width),
        ],
        1,
    )
    n_small = small.shape[1]
    small = after(small, *att_got).reshape(n_d, 2, 4 * n_small)
    small = pick(small, c, 1) + swap(pick(small, 1 - c, 1), "c")
    small = small.reshape(n_d, 2, 2, n_small)
    small = pick(small, zl, 2) + swap(pick(small, 1 - zl, 2), "zl")
    small = small.reshape(n_d, 2 * n_small)
    for bit in reversed(range(n_d.bit_length() - 1)):
        mine = jnp.bitwise_and(jnp.right_shift(d, bit), 1)
        small = halve_small(small, mine, lambda a, bit=bit: flip_d(a, bit, n_d))
    small_sum = halve_small(small.reshape(2, n_small), zh, lambda a: swap(a, "zh"))
    n_gain = LAYERS * 2 * width
    g_gains = small_sum[:, :n_gain].reshape(LAYERS, 2, width)
    g_biases = small_sum[:, n_gain : n_vec * width].reshape(LAYERS, 6, width)
    g_upb = small_sum[:, n_vec * width :].reshape(LAYERS, up_width)
    g_qkv = outs["qkv"].transpose(0, 2, 1, 3)
    return mixed, tokens_grad, g_qkv, outs["out"], outs["up"], outs["down"], g_gains, g_biases, g_upb


def solution(mesh):
    n_dp, n_t = mesh.shape["dp"], mesh.shape["tensor"]
    fine = Mesh(mesh.devices.reshape(n_dp // 2, 2, n_t // 2, 2), ALL)
    dp, t = ("d", "c"), ("zh", "zl")
    return jax.shard_map(
        body,
        mesh=fine,
        in_specs=(
            P(ALL, None),
            P(ALL, None),
            P(),
            P(),
            P(None, dp, None, t),
            P(None, t, dp),
            P(None, dp, t),
            P(None, t, dp),
            P(None, None, ALL),
            P(None, None, ALL),
            P(None, ALL),
        ),
        out_specs=(
            P(ALL, None),
            P(ALL, None),
            P(None, dp, None, t),
            P(None, t, dp),
            P(None, dp, t),
            P(None, t, dp),
            P(None, None, ALL),
            P(None, None, ALL),
            P(None, ALL),
        ),
        check_vma=False,
    )
```

time: 706 us -> 599 us (0.85)
  local copies, waits for them, and re-layouts: 104 us -> 49 us
  other arithmetic: 78.3 us -> 31.5 us
  matrix products: 15.2 us -> 0.78 us
  between operations: 3.67 us -> 16.2 us
  Pallas kernels: 167 us -> 175 us
    ppermute x36 -> x16, waiting for transfers between devices: 64.1 us -> 23.1 us  [flip_d(): return lax.ppermute(a, 'd', [(i, i ^ 1 << bit) for i in range(n_d)])]
    ppermute x73 -> x77, waiting for transfers between devices: 169 us -> 208 us  [swap(): return lax.ppermute(a, axis, SWAP)]
    unnamed x428 -> x271, local copies, waits for them, and re-layouts: 64.8 us -> 40 us
    ppermute x73 -> x77, starting transfers between devices: 41.1 us -> 64.1 us  [swap(): return lax.ppermute(a, axis, SWAP)]
    ppermute x36 -> x16, starting transfers between devices: 41 us -> 19.1 us  [flip_d(): return lax.ppermute(a, 'd', [(i, i ^ 1 << bit) for i in range(n_d)])]
    add x18 -> x5, other arithmetic: 18 us -> 0.08 us  [the longest x3 0.05 us: halve_small(): return pick(view, me, 0) + send(pick(view, 1 - me, 0))]
    pallas_call x20 -> x44, Pallas kernels: 107 us -> 123 us  [the longest x5 34.4 us: weight_grad(): pl.pallas_call(functools.partial(grad_kernel, fields, counts, specs), gri...]
    reduce_sum x17 -> x0, other arithmetic: 14.6 us -> none  [the longest x4 7.61 us: norm_parts(): centred = v - jnp.mean(v, axis=-1, keepdims=True)]
  transfers between devices with their start and end apart: 113 -> 103, of which waited for: 32 -> 56; matrix products, arithmetic and copies ran while one was open for 20% -> 7% of each run, Pallas kernels for 22% -> 28%
where the time goes in v3:
time: 599 us; the launch traced here: 592 us
  waiting for transfers between devices  231 us (39%)
  Pallas kernels  175 us (29%)
  starting transfers between devices  87.9 us (15%)
  local copies, waits for them, and re-layouts  49 us (8%)
  other arithmetic  31.5 us (5%)
  between operations  16.2 us (3%)
    ppermute x77, waiting for transfers between devices, swap(): return lax.ppermute(a, axis, SWAP)  208 us
    ppermute x77, starting transfers between devices, swap(): return lax.ppermute(a, axis, SWAP)  64.1 us
    unnamed x271, local copies, waits for them, and re-layouts  40 us
    pallas_call x5, Pallas kernels, weight_grad(): pl.pallas_call(functools.partial(grad_kernel, fields, counts, specs), gri...  34.4 us
    pallas_call x4, Pallas kernels, attend_back(): pl.pallas_call(functools.partial(attend_back_kernel, scale, heads, last),...  33.6 us
    ppermute x16, waiting for transfers between devices, flip_d(): return lax.ppermute(a, 'd', [(i, i ^ 1 << bit) for i in range(n_d)])  23.1 us
    pallas_call x4, Pallas kernels, ffn(): pl.pallas_call(ffn_kernel, grid=(ff // tile,), in_specs=[*blocks_in(x), p...  23.1 us
    pallas_call x4, Pallas kernels, ffn_back(): pl.pallas_call(ffn_back_kernel, grid=(ff // tile,), in_specs=[*blocks_in(...  20.3 us
  transfers between devices with their start and end apart: 103, of which 56 were waited for; matrix products, arithmetic and copies ran while one was open for 7% of the time, Pallas kernels for 28%

profile of v3, /device:TPU:0, one launch (start us, length us, event | category | flops | bytes accessed | tf_op | source)
XLA Modules:
  0.0 591.9 jit_solution(1300105759168313990)
XLA Ops:
  8.2 4.1 collective-permute-start
  19.4 5.0 collective-permute-done
  29.7 13.6 %collective-permute-start.2 = (bf16[256,1024]{1,0:T(8,128)(2,1)S(1)}, bf16[256,1024]{1,0:T(8,128)(2,1)S(1)}, u32[]{:S(2)}, u32[]{:S(2)}) collective-permute-start(bf16[256,1024]{1,0:T(8,128)(2,1)S(1)} %broadcast_select_fusion.4.refs_0_), channel_id=1, source_target_pairs={{0,4},{4,0},{1,5},{5,1},{2,6},{6,2},{3,7},{7,3},{8,12},{12,8},{9,1... | collective-permute-start | bytes 1572872 | tf_op jit(solution)/shard_map/ppermute | solution.py:821
  43.3 7.9 %collective-permute-start.4 = (bf16[256,1024]{1,0:T(8,128)(2,1)S(1)}, bf16[256,1024]{1,0:T(8,128)(2,1)S(1)}, u32[]{:S(2)}, u32[]{:S(2)}) collective-permute-start(bf16[256,1024]{1,0:T(8,128)(2,1)S(1)} %collective-permute-done.3.refs_2_), channel_id=1, source_target_pairs={{0,4},{4,0},{1,5},{5,1},{2,6},{6,2},{3,7},{7,3},{8,12},{12,8},{9,1... | collective-permute-start | bytes 1572872 | tf_op jit(solution)/shard_map/ppermute | solution.py:821
  53.8 2.4 deal_rows.1
  56.2 20.8 %collective-permute-done.11 = bf16[2048,128]{1,0:T(8,128)(2,1)S(1)} collective-permute-done((bf16[2048,128]{1,0:T(8,128)(2,1)S(1)}, bf16[2048,128]{1,0:T(8,128)(2,1)S(1)}, u32[]{:S(2)}, u32[]{:S(2)}) %collective-permute-start.11) | collective-permute-done | bytes 524320 | tf_op jit(solution)/shard_map/ppermute | solution.py:821
  80.3 3.6 collective-permute-done.6
  90.6 2.5 collective-permute-done.9
  93.8 4.3 collective-permute-done.10
  105.4 2.9 project.4
  108.2 2.4 project.5
  110.7 4.8 attend.4
  117.6 2.4 collective-permute-start.15
  120.0 4.8 attend.5
  124.8 7.4 %collective-permute-done.15.refs_3_ = bf16[256,1024]{1,0:T(8,128)(2,1)S(1)} collective-permute-done((bf16[256,1024]{1,0:T(8,128)(2,1)S(1)}, bf16[256,1024]{1,0:T(8,128)(2,1)S(1)}, u32[]{:S(2)}, u32[]{:S(2)}) %collective-permute-start.15) | collective-permute-done | bytes 524320 | tf_op jit(solution)/shard_map/ppermute | solution.py:821
  140.2 2.2 copy-done
  146.5 6.6 %ffn.4 = (bf16[512,1024]{1,0:T(8,128)(2,1)}, f32[512,1024]{1,0:T(8,128)}, f32[256,1024]{1,0:T(8,128)S(1)}, bf16[256,1024]{1,0:T(8,128)(2,1)}, bf16[512,1024]{1,0:T(8,128)(2,1)}) custom-call(bf16[256,1024]{1,0:T(8,128)(2,1)} %get-tuple-element.256.refs_0_, bf16[256,1024]{1,0:T(8,128)(2,1)S(1)} %copy-done.67, ...), custom_call_target="tpu_custom_call" | custom-call | flops 2147483648 | bytes 9437184 | tf_op jit(solution)/shard_map/ffn/pallas_call | solution.py:354
  155.0 5.5 ffn.5
  160.5 7.9 %collective-permute-done.22 = bf16[1024,128]{1,0:T(8,128)(2,1)S(1)} collective-permute-done((bf16[1024,128]{1,0:T(8,128)(2,1)S(1)}, bf16[1024,128]{1,0:T(8,128)(2,1)S(1)}, u32[]{:S(2)}, u32[]{:S(2)}) %collective-permute-start.22) | collective-permute-done | bytes 262176 | tf_op jit(solution)/shard_map/ppermute | solution.py:821
  168.4 13.9 %collective-permute-done.19 = bf16[1024,128]{1,0:T(8,128)(2,1)S(1)} collective-permute-done((bf16[1024,128]{1,0:T(8,128)(2,1)S(1)}, bf16[1024,128]{1,0:T(8,128)(2,1)S(1)}, u32[]{:S(2)}, u32[]{:S(2)}) %collective-permute-start.19) | collective-permute-done | bytes 262176 | tf_op jit(solution)/shard_map/ppermute | solution.py:821
  188.8 12.4 %collective-permute-done.24.refs_3_ = bf16[256,1024]{1,0:T(8,128)(2,1)S(1)} collective-permute-done((bf16[256,1024]{1,0:T(8,128)(2,1)}, bf16[256,1024]{1,0:T(8,128)(2,1)S(1)}, u32[]{:S(2)}, u32[]{:S(2)}) %collective-permute-start.24) | collective-permute-done | bytes 524320 | tf_op jit(solution)/shard_map/ppermute | solution.py:821
  207.5 3.9 project.6
  211.3 7.8 %collective-permute-done.27.refs_0_ = bf16[256,1024]{1,0:T(8,128)(2,1)S(1)} collective-permute-done((bf16[256,1024]{1,0:T(8,128)(2,1)}, bf16[256,1024]{1,0:T(8,128)(2,1)S(1)}, u32[]{:S(2)}, u32[]{:S(2)}) %collective-permute-start.27) | collective-permute-done | bytes 524320 | tf_op jit(solution)/shard_map/ppermute | solution.py:821
  221.1 2.5 project.7
  223.5 4.7 attend.6
  230.7 4.7 attend.7
  235.4 14.5 %collective-permute-done.30.refs_3_ = bf16[256,1024]{1,0:T(8,128)(2,1)S(1)} collective-permute-done((bf16[256,1024]{1,0:T(8,128)(2,1)S(1)}, bf16[256,1024]{1,0:T(8,128)(2,1)S(1)}, u32[]{:S(2)}, u32[]{:S(2)}) %collective-permute-start.30) | collective-permute-done | bytes 524320 | tf_op jit(solution)/shard_map/ppermute | solution.py:821
  254.4 2.2 copy-done.1
  258.3 5.4 ffn.6
  263.7 4.4 collective-permute-done.35.refs_0_
  270.0 5.6 ffn.7
  275.5 7.0 %collective-permute-done.38 = bf16[256,1024]{1,0:T(8,128)(2,1)S(1)} collective-permute-done((bf16[256,1024]{1,0:T(8,128)(2,1)S(1)}, bf16[256,1024]{1,0:T(8,128)(2,1)S(1)}, u32[]{:S(2)}, u32[]{:S(2)}) %collective-permute-start.38) | collective-permute-done | bytes 524320 | tf_op jit(solution)/shard_map/ppermute | solution.py:821
  287.8 10.8 %collective-permute-done.40.refs_3_ = bf16[256,1024]{1,0:T(8,128)(2,1)S(1)} collective-permute-done((bf16[256,1024]{1,0:T(8,128)(2,1)S(1)}, bf16[256,1024]{1,0:T(8,128)(2,1)S(1)}, u32[]{:S(2)}, u32[]{:S(2)}) %collective-permute-start.40) | collective-permute-done | bytes 524320 | tf_op jit(solution)/shard_map/ppermute | solution.py:821
  304.6 5.1 ffn_back.4
  310.7 6.3 %collective-permute-done.44.refs_0_ = bf16[256,1024]{1,0:T(8,128)(2,1)S(1)} collective-permute-done((bf16[256,1024]{1,0:T(8,128)(2,1)S(1)}, bf16[256,1024]{1,0:T(8,128)(2,1)S(1)}, u32[]{:S(2)}, u32[]{:S(2)}) %collective-permute-start.44) | collective-permute-done | bytes 524320 | tf_op jit(solution)/shard_map/ppermute | solution.py:821
  319.0 4.9 ffn_back.5
  327.0 9.9 %weight_grad.5 = bf16[8,2048,128]{2,1,0:T(8,128)(2,1)} custom-call(s32[2]{0:T(128)S(1)} %pad_add_fusion.1.where_ref, bf16[512,1024]{1,0:T(8,128)(2,1)} %get-tuple-element.293.refs_0_, bf16[512,1024]{1,0:T(8,128)(2,1)} %get-tuple-element.304.refs_1_, bf16[512,1024]{1,0:T(8,128)(2,1)} %get-tuple-element.307.refs_2_, ...), custom_call_target="tpu_custom_call" | custom-call | flops 4294967296 | bytes 12582912 | tf_op jit(solution)/shard_map/weight_grad/pallas_call | solution.py:646
  337.7 3.2 collective-permute-done.48.refs_3_
  352.7 7.9 %attend_back.4 = (bf16[512,256]{1,0:T(8,128)(2,1)S(1)}, f32[1,256]{1,0:T(1,128)S(1)}, f32[1024,256]{1,0:T(8,128)S(1)}, f32[1024,256]{1,0:T(8,128)S(1)}, bf16[512,1024]{1,0:T(8,128)(2,1)}) custom-call(bf16[512,768]{1,0:T(8,128)(2,1)S(1)} %copy-done.77, bf16[512,768]{1,0:T(8,128)(2,1)S(1)} %copy-done.77, bf16[512,768]{1,0:T(8,128)(2,1)S(1)} %copy-done.79, ...), custom_call_target="tpu_custom_call" | custom-call | flops 5368709120 | bytes 8388608 | tf_op jit(solution)/shard_map/attend_back/pallas_call | solution.py:304
  360.6 2.2 collective-permute-done.51.refs_8_
  364.8 8.6 %attend_back.5 = (bf16[512,768]{1,0:T(8,128)(2,1)S(1)}, bf16[512,768]{1,0:T(8,128)(2,1)S(1)}, f32[2,256]{1,0:T(2,128)S(1)}, bf16[512,1024]{1,0:T(8,128)(2,1)}) custom-call(bf16[512,768]{1,0:T(8,128)(2,1)S(1)} %copy-done.79, bf16[512,768]{1,0:T(8,128)(2,1)S(1)} %copy-done.77, bf16[512,768]{1,0:T(8,128)(2,1)S(1)} %copy-done.79, ...), custom_call_target="tpu_custom_call" | custom-call | flops 5368709120 | bytes 8388608 | tf_op jit(solution)/shard_map/attend_back/pallas_call | solution.py:304
  374.4 6.8 %collective-permute-start.53 = (bf16[256,1024]{1,0:T(8,128)(2,1)S(1)}, bf16[256,1024]{1,0:T(8,128)(2,1)S(1)}, u32[]{:S(2)}, u32[]{:S(2)}) collective-permute-start(bf16[256,1024]{1,0:T(8,128)(2,1)S(1)} %get-tuple-element.342), channel_id=1, source_target_pairs={{0,4},{4,0},{1,5},{5,1},{2,6},{6,2},{3,7},{7,3},{8,12},{12,8},{9,1... | collective-permute-start | bytes 1572872 | tf_op jit(solution)/shard_map/ppermute | solution.py:821
  383.8 7.4 %weight_grad.6 = bf16[8,1024,128]{2,1,0:T(8,128)(2,1)} custom-call(s32[2]{0:T(128)S(1)} %pad_add_fusion.1.where_ref, bf16[512,1024]{1,0:T(8,128)(2,1)} %get-tuple-element.274.refs_0_, bf16[512,1024]{1,0:T(8,128)(2,1)} %get-tuple-element.332.refs_1_, bf16[512,768]{1,0:T(8,128)(2,1)} %copy-done.17, bf16[512,768]{1,0:T(8,128)(2,1)} %copy-done.19, ...), custom_call_target="tpu_custom_call" | custom-call | flops 2147483648 | bytes 12582912 | tf_op jit(solution)/shard_map/weight_grad/pallas_call | solution.py:646
  391.3 6.9 %collective-permute-done.55.refs_3_ = bf16[256,1024]{1,0:T(8,128)(2,1)S(1)} collective-permute-done((bf16[256,1024]{1,0:T(8,128)(2,1)}, bf16[256,1024]{1,0:T(8,128)(2,1)S(1)}, u32[]{:S(2)}, u32[]{:S(2)}) %collective-permute-start.55) | collective-permute-done | bytes 524320 | tf_op jit(solution)/shard_map/ppermute | solution.py:821
  411.5 5.4 ffn_back.6
  416.8 3.3 collective-permute-done.57.refs_0_
  422.1 4.9 ffn_back.7
  427.0 8.3 %collective-permute-done.60 = bf16[1024,128]{1,0:T(8,128)(2,1)S(1)} collective-permute-done((bf16[1024,128]{1,0:T(8,128)(2,1)S(1)}, bf16[1024,128]{1,0:T(8,128)(2,1)S(1)}, u32[]{:S(2)}, u32[]{:S(2)}) %collective-permute-start.60) | collective-permute-done | bytes 262176 | tf_op jit(solution)/shard_map/ppermute | solution.py:821
  438.2 2.4 collective-permute-start.62
  440.6 6.0 %weight_grad.7 = (bf16[2,1024,128]{2,1,0:T(8,128)(2,1)S(1)}, bf16[2,1024,128]{2,1,0:T(8,128)(2,1)S(1)}, bf16[2,1024,128]{2,1,0:T(8,128)(2,1)}, bf16[2,1024,128]{2,1,0:T(8,128)(2,1)S(1)}) custom-call(s32[2]{0:T(128)S(1)} %pad_add_fusion.1.where_ref, bf16[512,1024]{1,0:T(8,128)(2,1)} %get-tuple-element.362.refs_0_, ...), custom_call_target="tpu_custom_call" | custom-call | flops 2147483648 | bytes 12582912 | tf_op jit(solution)/shard_map/weight_grad/pallas_call | solution.py:646
  453.0 5.3 weight_grad.8
  466.7 6.4 %collective-permute-done.71 = bf16[2,1024,128]{2,1,0:T(8,128)(2,1)S(1)} collective-permute-done((bf16[2,1024,128]{2,1,0:T(8,128)(2,1)S(1)}, bf16[2,1024,128]{2,1,0:T(8,128)(2,1)S(1)}, u32[]{:S(2)}, u32[]{:S(2)}) %collective-permute-start.71) | collective-permute-done | bytes 524320 | tf_op jit(solution)/shard_map/ppermute | solution.py:825
  473.2 8.3 %attend_back.6 = (bf16[512,256]{1,0:T(8,128)(2,1)S(1)}, f32[1,256]{1,0:T(1,128)S(1)}, f32[1024,256]{1,0:T(8,128)S(1)}, f32[1024,256]{1,0:T(8,128)S(1)}, bf16[512,1024]{1,0:T(8,128)(2,1)}) custom-call(bf16[512,768]{1,0:T(8,128)(2,1)S(1)} %copy-done.73, bf16[512,768]{1,0:T(8,128)(2,1)S(1)} %copy-done.73, bf16[512,768]{1,0:T(8,128)(2,1)S(1)} %copy-done.75, ...), custom_call_target="tpu_custom_call" | custom-call | flops 5368709120 | bytes 8388608 | tf_op jit(solution)/shard_map/attend_back/pallas_call | solution.py:304
  486.3 4.7 collective-permute-done.73
  493.6 2.6 collective-permute-done.75
  497.0 8.8 %attend_back.7 = (bf16[512,768]{1,0:T(8,128)(2,1)S(1)}, bf16[512,768]{1,0:T(8,128)(2,1)S(1)}, f32[2,256]{1,0:T(2,128)S(1)}, bf16[512,1024]{1,0:T(8,128)(2,1)}) custom-call(bf16[512,768]{1,0:T(8,128)(2,1)S(1)} %copy-done.75, bf16[512,768]{1,0:T(8,128)(2,1)S(1)} %copy-done.73, bf16[512,768]{1,0:T(8,128)(2,1)S(1)} %copy-done.75, ...), custom_call_target="tpu_custom_call" | custom-call | flops 5368709120 | bytes 8388608 | tf_op jit(solution)/shard_map/attend_back/pallas_call | solution.py:304
  509.1 5.8 weight_grad.9
  523.9 8.3 %collective-permute-done.82.got_ref = bf16[1024,128]{1,0:T(8,128)(2,1)S(1)} collective-permute-done((bf16[1024,128]{1,0:T(8,128)(2,1)S(1)}, bf16[1024,128]{1,0:T(8,128)(2,1)S(1)}, u32[]{:S(2)}, u32[]{:S(2)}) %collective-permute-start.82) | collective-permute-done | bytes 262176 | tf_op jit(solution)/shard_map/ppermute | solution.py:821
  534.5 6.4 %collective-permute-done.86 = bf16[256,1024]{1,0:T(8,128)(2,1)S(1)} collective-permute-done((bf16[256,1024]{1,0:T(8,128)(2,1)S(1)}, bf16[256,1024]{1,0:T(8,128)(2,1)S(1)}, u32[]{:S(2)}, u32[]{:S(2)}) %collective-permute-start.86) | collective-permute-done | bytes 524320 | tf_op jit(solution)/shard_map/ppermute | solution.py:821
  544.2 2.9 collective-permute-done.89.got_ref
  550.2 2.5 collective-permute-done.93
  560.4 6.6 %collective-permute-start.96 = (f32[1,768]{1,0:T(1,128)S(1)}, f32[1,768]{1,0:T(1,128)S(1)}, u32[]{:S(2)}, u32[]{:S(2)}) collective-permute-start(f32[1,768]{1,0:T(1,128)S(1)} %fusion.20), channel_id=1, source_target_pairs={{0,2},{2,0},{1,3},{3,1},{4,6},{6,4},{5,7},{7,5},{8,10},{10,8},{9,1... | collective-permute-start | bytes 9224 | tf_op jit(solution)/shard_map/ppermute | solution.py:821
  576.1 2.1 select_convert_fusion
  578.1 5.9 collective-permute-done.91.got_ref
  (590 shorter events, 188.5 us)
Async XLA Ops:
  7.2 93.1 %all-gather.5.cloned.1.call-start = ((), (), s32[]{:S(2)}) async-start(), calls=%async_computation.2 | async-start | bytes 2621440 | tf_op jit(solution)/shard_map/all_gather | solution.py:902
  8.2 16.1 %collective-permute-start = (bf16[1024,128]{1,0:T(8,128)(2,1)S(1)}, bf16[1024,128]{1,0:T(8,128)(2,1)}, u32[]{:S(2)}, u32[]{:S(2)}) collective-permute-start(bf16[1024,128]{1,0:T(8,128)(2,1)S(1)} %pack.4), channel_id=1, source_target_pairs={{0,2},{2,0},{1,3},{3,1},{4,6},{6,4},{5,7},{7,5},{8,10},{10,8},{9,1... | collective-permute-start | bytes 786440 | tf_op jit(solution)/shard_map/ppermute | solution.py:821
  27.8 112.4 %all-gather.7.cloned.1.call-start = ((), (), s32[]{:S(2)}) async-start(), calls=%async_computation.3 | async-start | bytes 5242880 | tf_op jit(solution)/shard_map/all_gather | solution.py:902
  29.0 14.3 %collective-permute-start.3 = (bf16[256,1024]{1,0:T(8,128)(2,1)S(1)}, bf16[256,1024]{1,0:T(8,128)(2,1)S(1)}, u32[]{:S(2)}, u32[]{:S(2)}) collective-permute-start(bf16[256,1024]{1,0:T(8,128)(2,1)S(1)} %broadcast_select_fusion.4.refs_0_), channel_id=1, source_target_pairs={{0,1},{1,0},{2,3},{3,2},{4,5},{5,4},{6,7},{7,6},{8,9},{9,8},{10,11... | collective-permute-start | bytes 1572872 | tf_op jit(solution)/shard_map/ppermute | solution.py:821
  29.7 22.3 %collective-permute-start.2 = (bf16[256,1024]{1,0:T(8,128)(2,1)S(1)}, bf16[256,1024]{1,0:T(8,128)(2,1)S(1)}, u32[]{:S(2)}, u32[]{:S(2)}) collective-permute-start(bf16[256,1024]{1,0:T(8,128)(2,1)S(1)} %broadcast_select_fusion.4.refs_0_), channel_id=1, source_target_pairs={{0,4},{4,0},{1,5},{5,1},{2,6},{6,2},{3,7},{7,3},{8,12},{12,8},{9,1... | collective-permute-start | bytes 1572872 | tf_op jit(solution)/shard_map/ppermute | solution.py:821
  43.3 9.5 %collective-permute-start.4 = (bf16[256,1024]{1,0:T(8,128)(2,1)S(1)}, bf16[256,1024]{1,0:T(8,128)(2,1)S(1)}, u32[]{:S(2)}, u32[]{:S(2)}) collective-permute-start(bf16[256,1024]{1,0:T(8,128)(2,1)S(1)} %collective-permute-done.3.refs_2_), channel_id=1, source_target_pairs={{0,4},{4,0},{1,5},{5,1},{2,6},{6,2},{3,7},{7,3},{8,12},{12,8},{9,1... | collective-permute-start | bytes 1572872 | tf_op jit(solution)/shard_map/ppermute | solution.py:821
  51.2 25.8 %collective-permute-start.11 = (bf16[2048,128]{1,0:T(8,128)(2,1)S(1)}, bf16[2048,128]{1,0:T(8,128)(2,1)S(1)}, u32[]{:S(2)}, u32[]{:S(2)}) collective-permute-start(bf16[2048,128]{1,0:T(8,128)(2,1)S(1)} %pack.5), channel_id=1, source_target_pairs={{0,2},{2,0},{1,3},{3,1},{4,6},{6,4},{5,7},{7,5},{8,10},{10,8},{9,1... | collective-permute-start | bytes 1572872 | tf_op jit(solution)/shard_map/ppermute | solution.py:821
  80.2 124.7 %all-gather.9.cloned.1.call-start = ((), (), s32[]{:S(2)}) async-start(), calls=%async_computation.4 | async-start | bytes 2621440 | tf_op jit(solution)/shard_map/all_gather | solution.py:902
  99.6 15.9 %collective-permute-start.13 = (bf16[1024,128]{1,0:T(8,128)(2,1)S(1)}, bf16[1024,128]{1,0:T(8,128)(2,1)S(1)}, u32[]{:S(2)}, u32[]{:S(2)}) collective-permute-start(bf16[1024,128]{1,0:T(8,128)(2,1)S(1)} %pack.6), channel_id=1, source_target_pairs={{0,2},{2,0},{1,3},{3,1},{4,6},{6,4},{5,7},{7,5},{8,10},{10,8},{9,1... | collective-permute-start | bytes 786440 | tf_op jit(solution)/shard_map/ppermute | solution.py:821
  117.6 14.6 %collective-permute-start.15 = (bf16[256,1024]{1,0:T(8,128)(2,1)S(1)}, bf16[256,1024]{1,0:T(8,128)(2,1)S(1)}, u32[]{:S(2)}, u32[]{:S(2)}) collective-permute-start(bf16[256,1024]{1,0:T(8,128)(2,1)S(1)} %add_convert_fusion.8), channel_id=1, source_target_pairs={{0,1},{1,0},{2,3},{3,2},{4,5},{5,4},{6,7},{7,6},{8,9},{9,8},{10,11... | collective-permute-start | bytes 1572872 | tf_op jit(solution)/shard_map/ppermute | solution.py:821
  136.8 7.4 %collective-permute-start.17 = (bf16[256,1024]{1,0:T(8,128)(2,1)}, bf16[256,1024]{1,0:T(8,128)(2,1)S(1)}, u32[]{:S(2)}, u32[]{:S(2)}) collective-permute-start(bf16[256,1024]{1,0:T(8,128)(2,1)} %get-tuple-element.256.refs_0_), channel_id=1, source_target_pairs={{0,4},{4,0},{1,5},{5,1},{2,6},{6,2},{3,7},{7,3},{8,12},{12,8},{9,1... | collective-permute-start | bytes 1572872 | tf_op jit(solution)/shard_map/ppermute | solution.py:821
  137.1 16.0 %collective-permute-start.18 = (bf16[256,1024]{1,0:T(8,128)(2,1)}, bf16[256,1024]{1,0:T(8,128)(2,1)S(1)}, u32[]{:S(2)}, u32[]{:S(2)}) collective-permute-start(bf16[256,1024]{1,0:T(8,128)(2,1)} %get-tuple-element.256.refs_0_), channel_id=1, source_target_pairs={{0,1},{1,0},{2,3},{3,2},{4,5},{5,4},{6,7},{7,6},{8,9},{9,8},{10,11... | collective-permute-start | bytes 1572872 | tf_op jit(solution)/shard_map/ppermute | solution.py:821
  139.8 114.6 %all-gather.11.cloned.1.call-start = ((), (), s32[]{:S(2)}) async-start(), calls=%async_computation.5 | async-start | bytes 5242880 | tf_op jit(solution)/shard_map/all_gather | solution.py:902
  153.1 15.3 %collective-permute-start.22 = (bf16[1024,128]{1,0:T(8,128)(2,1)S(1)}, bf16[1024,128]{1,0:T(8,128)(2,1)S(1)}, u32[]{:S(2)}, u32[]{:S(2)}) collective-permute-start(bf16[1024,128]{1,0:T(8,128)(2,1)S(1)} %get-tuple-element.267), channel_id=1, source_target_pairs={{0,2},{2,0},{1,3},{3,1},{4,6},{6,4},{5,7},{7,5},{8,10},{10,8},{9,1... | collective-permute-start | bytes 786440 | tf_op jit(solution)/shard_map/ppermute | solution.py:821
  168.4 14.0 %collective-permute-start.23 = (bf16[256,1024]{1,0:T(8,128)(2,1)S(1)}, bf16[256,1024]{1,0:T(8,128)(2,1)S(1)}, u32[]{:S(2)}, u32[]{:S(2)}) collective-permute-start(bf16[256,1024]{1,0:T(8,128)(2,1)S(1)} %get-tuple-element.268), channel_id=1, source_target_pairs={{0,4},{4,0},{1,5},{5,1},{2,6},{6,2},{3,7},{7,3},{8,12},{12,8},{9,1... | collective-permute-start | bytes 1572872 | tf_op jit(solution)/shard_map/ppermute | solution.py:821
  168.4 14.0 %collective-permute-start.19 = (bf16[1024,128]{1,0:T(8,128)(2,1)S(1)}, bf16[1024,128]{1,0:T(8,128)(2,1)S(1)}, u32[]{:S(2)}, u32[]{:S(2)}) collective-permute-start(bf16[1024,128]{1,0:T(8,128)(2,1)S(1)} %get-tuple-element.261), channel_id=1, source_target_pairs={{0,2},{2,0},{1,3},{3,1},{4,6},{6,4},{5,7},{7,5},{8,10},{10,8},{9,1... | collective-permute-start | bytes 786440 | tf_op jit(solution)/shard_map/ppermute | solution.py:821
  186.6 219.5 %reduce-scatter.3.cloned.1.call-start = ((), (), s32[]{:S(2)}) async-start(), calls=%async_computation.6 | async-start | bytes 5242880 | tf_op jit(solution)/shard_map/reduce_scatter | solution.py:919
  186.8 14.4 %collective-permute-start.24 = (bf16[256,1024]{1,0:T(8,128)(2,1)}, bf16[256,1024]{1,0:T(8,128)(2,1)S(1)}, u32[]{:S(2)}, u32[]{:S(2)}) collective-permute-start(bf16[256,1024]{1,0:T(8,128)(2,1)} %add_convert_fusion.7), channel_id=1, source_target_pairs={{0,1},{1,0},{2,3},{3,2},{4,5},{5,4},{6,7},{7,6},{8,9},{9,8},{10,11... | collective-permute-start | bytes 1572872 | tf_op jit(solution)/shard_map/ppermute | solution.py:821
  204.6 14.5 %collective-permute-start.27 = (bf16[256,1024]{1,0:T(8,128)(2,1)}, bf16[256,1024]{1,0:T(8,128)(2,1)S(1)}, u32[]{:S(2)}, u32[]{:S(2)}) collective-permute-start(bf16[256,1024]{1,0:T(8,128)(2,1)} %get-tuple-element.270.refs_0_), channel_id=1, source_target_pairs={{0,1},{1,0},{2,3},{3,2},{4,5},{5,4},{6,7},{7,6},{8,9},{9,8},{10,11... | collective-permute-start | bytes 1572872 | tf_op jit(solution)/shard_map/ppermute | solution.py:821
  228.4 7.0 %collective-permute-start.31 = (bf16[256,1024]{1,0:T(8,128)(2,1)S(1)}, bf16[256,1024]{1,0:T(8,128)(2,1)S(1)}, u32[]{:S(2)}, u32[]{:S(2)}) collective-permute-start(bf16[256,1024]{1,0:T(8,128)(2,1)S(1)} %copy-done.108), channel_id=1, source_target_pairs={{2,4},{4,2},{3,5},{5,3},{10,12},{12,10},{11,13},{13,11},{18,20},{2... | collective-permute-start | bytes 1572872 | tf_op jit(solution)/shard_map/ppermute | solution.py:829
  230.4 19.6 %collective-permute-start.30 = (bf16[256,1024]{1,0:T(8,128)(2,1)S(1)}, bf16[256,1024]{1,0:T(8,128)(2,1)S(1)}, u32[]{:S(2)}, u32[]{:S(2)}) collective-permute-start(bf16[256,1024]{1,0:T(8,128)(2,1)S(1)} %add_convert_fusion.6), channel_id=1, source_target_pairs={{0,1},{1,0},{2,3},{3,2},{4,5},{5,4},{6,7},{7,6},{8,9},{9,8},{10,11... | collective-permute-start | bytes 1572872 | tf_op jit(solution)/shard_map/ppermute | solution.py:821
  254.1 14.0 %collective-permute-start.35 = (bf16[256,1024]{1,0:T(8,128)(2,1)S(1)}, bf16[256,1024]{1,0:T(8,128)(2,1)S(1)}, u32[]{:S(2)}, u32[]{:S(2)}) collective-permute-start(bf16[256,1024]{1,0:T(8,128)(2,1)S(1)} %get-tuple-element.286.refs_0_), channel_id=1, source_target_pairs={{0,1},{1,0},{2,3},{3,2},{4,5},{5,4},{6,7},{7,6},{8,9},{9,8},{10,11... | collective-permute-start | bytes 1572872 | tf_op jit(solution)/shard_map/ppermute | solution.py:821
  268.1 14.4 %collective-permute-start.38 = (bf16[256,1024]{1,0:T(8,128)(2,1)S(1)}, bf16[256,1024]{1,0:T(8,128)(2,1)S(1)}, u32[]{:S(2)}, u32[]{:S(2)}) collective-permute-start(bf16[256,1024]{1,0:T(8,128)(2,1)S(1)} %broadcast_select_fusion.3), channel_id=1, source_target_pairs={{0,1},{1,0},{2,3},{3,2},{4,5},{5,4},{6,7},{7,6},{8,9},{9,8},{10,11... | collective-permute-start | bytes 1572872 | tf_op jit(solution)/shard_map/ppermute | solution.py:821
  284.6 14.0 %collective-permute-start.40 = (bf16[256,1024]{1,0:T(8,128)(2,1)S(1)}, bf16[256,1024]{1,0:T(8,128)(2,1)S(1)}, u32[]{:S(2)}, u32[]{:S(2)}) collective-permute-start(bf16[256,1024]{1,0:T(8,128)(2,1)S(1)} %add_convert_fusion.5), channel_id=1, source_target_pairs={{0,1},{1,0},{2,3},{3,2},{4,5},{5,4},{6,7},{7,6},{8,9},{9,8},{10,11... | collective-permute-start | bytes 1572872 | tf_op jit(solution)/shard_map/ppermute | solution.py:821
  302.7 14.3 %collective-permute-start.44 = (bf16[256,1024]{1,0:T(8,128)(2,1)S(1)}, bf16[256,1024]{1,0:T(8,128)(2,1)S(1)}, u32[]{:S(2)}, u32[]{:S(2)}) collective-permute-start(bf16[256,1024]{1,0:T(8,128)(2,1)S(1)} %get-tuple-element.305.refs_0_), channel_id=1, source_target_pairs={{0,1},{1,0},{2,3},{3,2},{4,5},{5,4},{6,7},{7,6},{8,9},{9,8},{10,11... | collective-permute-start | bytes 1572872 | tf_op jit(solution)/shard_map/ppermute | solution.py:821
  324.0 12.9 %collective-permute-start.47 = (bf16[256,1024]{1,0:T(8,128)(2,1)}, bf16[256,1024]{1,0:T(8,128)(2,1)S(1)}, u32[]{:S(2)}, u32[]{:S(2)}) collective-permute-start(bf16[256,1024]{1,0:T(8,128)(2,1)} %get-tuple-element.322), channel_id=1, source_target_pairs={{0,4},{4,0},{1,5},{5,1},{2,6},{6,2},{3,7},{7,3},{8,12},{12,8},{9,1... | collective-permute-start | bytes 1572872 | tf_op jit(solution)/shard_map/ppermute | solution.py:821
  326.7 14.2 %collective-permute-start.48 = (bf16[256,1024]{1,0:T(8,128)(2,1)}, bf16[256,1024]{1,0:T(8,128)(2,1)S(1)}, u32[]{:S(2)}, u32[]{:S(2)}) collective-permute-start(bf16[256,1024]{1,0:T(8,128)(2,1)} %add_convert_fusion.4), channel_id=1, source_target_pairs={{0,1},{1,0},{2,3},{3,2},{4,5},{5,4},{6,7},{7,6},{8,9},{9,8},{10,11... | collective-permute-start | bytes 1572872 | tf_op jit(solution)/shard_map/ppermute | solution.py:821
  347.5 102.3 %reduce-scatter.5.cloned.1.call-start = ((), (), s32[]{:S(2)}) async-start(), calls=%async_computation.7 | async-start | bytes 2621440 | tf_op jit(solution)/shard_map/reduce_scatter | solution.py:919
  348.6 14.3 %collective-permute-start.51 = (bf16[256,1024]{1,0:T(8,128)(2,1)S(1)}, bf16[256,1024]{1,0:T(8,128)(2,1)S(1)}, u32[]{:S(2)}, u32[]{:S(2)}) collective-permute-start(bf16[256,1024]{1,0:T(8,128)(2,1)S(1)} %copy-done.69), channel_id=1, source_target_pairs={{0,1},{1,0},{2,3},{3,2},{4,5},{5,4},{6,7},{7,6},{8,9},{9,8},{10,11... | collective-permute-start | bytes 1572872 | tf_op jit(solution)/shard_map/ppermute | solution.py:821
  362.9 10.5 %collective-permute-start.50 = (bf16[256,1024]{1,0:T(8,128)(2,1)S(1)}, bf16[256,1024]{1,0:T(8,128)(2,1)S(1)}, u32[]{:S(2)}, u32[]{:S(2)}) collective-permute-start(bf16[256,1024]{1,0:T(8,128)(2,1)S(1)} %copy-done.27), channel_id=1, source_target_pairs={{2,4},{4,2},{3,5},{5,3},{10,12},{12,10},{11,13},{13,11},{18,20},{2... | collective-permute-start | bytes 1572872 | tf_op jit(solution)/shard_map/ppermute | solution.py:829
  374.4 8.4 %collective-permute-start.53 = (bf16[256,1024]{1,0:T(8,128)(2,1)S(1)}, bf16[256,1024]{1,0:T(8,128)(2,1)S(1)}, u32[]{:S(2)}, u32[]{:S(2)}) collective-permute-start(bf16[256,1024]{1,0:T(8,128)(2,1)S(1)} %get-tuple-element.342), channel_id=1, source_target_pairs={{0,4},{4,0},{1,5},{5,1},{2,6},{6,2},{3,7},{7,3},{8,12},{12,8},{9,1... | collective-permute-start | bytes 1572872 | tf_op jit(solution)/shard_map/ppermute | solution.py:821
  383.7 14.5 %collective-permute-start.55 = (bf16[256,1024]{1,0:T(8,128)(2,1)}, bf16[256,1024]{1,0:T(8,128)(2,1)S(1)}, u32[]{:S(2)}, u32[]{:S(2)}) collective-permute-start(bf16[256,1024]{1,0:T(8,128)(2,1)} %add_convert_fusion.3), channel_id=1, source_target_pairs={{0,1},{1,0},{2,3},{3,2},{4,5},{5,4},{6,7},{7,6},{8,9},{9,8},{10,11... | collective-permute-start | bytes 1572872 | tf_op jit(solution)/shard_map/ppermute | solution.py:821
  405.8 14.4 %collective-permute-start.57 = (bf16[256,1024]{1,0:T(8,128)(2,1)}, bf16[256,1024]{1,0:T(8,128)(2,1)S(1)}, u32[]{:S(2)}, u32[]{:S(2)}) collective-permute-start(bf16[256,1024]{1,0:T(8,128)(2,1)} %get-tuple-element.356.refs_0_), channel_id=1, source_target_pairs={{0,1},{1,0},{2,3},{3,2},{4,5},{5,4},{6,7},{7,6},{8,9},{9,8},{10,11... | collective-permute-start | bytes 1572872 | tf_op jit(solution)/shard_map/ppermute | solution.py:821
  408.2 12.0 %collective-permute-start.59 = (bf16[2048,128]{1,0:T(8,128)(2,1)S(1)}, bf16[2048,128]{1,0:T(8,128)(2,1)S(1)}, u32[]{:S(2)}, u32[]{:S(2)}) collective-permute-start(bf16[2048,128]{1,0:T(8,128)(2,1)S(1)} %get-tuple-element.369), channel_id=1, source_target_pairs={{0,4},{4,0},{1,5},{5,1},{2,6},{6,2},{3,7},{7,3},{8,12},{12,8},{9,1... | collective-permute-start | bytes 1572872 | tf_op jit(solution)/shard_map/ppermute | solution.py:821
  420.3 15.0 %collective-permute-start.60 = (bf16[1024,128]{1,0:T(8,128)(2,1)S(1)}, bf16[1024,128]{1,0:T(8,128)(2,1)S(1)}, u32[]{:S(2)}, u32[]{:S(2)}) collective-permute-start(bf16[1024,128]{1,0:T(8,128)(2,1)S(1)} %get-tuple-element.370), channel_id=1, source_target_pairs={{0,2},{2,0},{1,3},{3,1},{4,6},{6,4},{5,7},{7,5},{8,10},{10,8},{9,1... | collective-permute-start | bytes 786440 | tf_op jit(solution)/shard_map/ppermute | solution.py:821
  421.7 38.4 %collective-permute-start.63 = (bf16[256,1024]{1,0:T(8,128)(2,1)}, bf16[256,1024]{1,0:T(8,128)(2,1)S(1)}, u32[]{:S(2)}, u32[]{:S(2)}) collective-permute-start(bf16[256,1024]{1,0:T(8,128)(2,1)} %get-tuple-element.380), channel_id=1, source_target_pairs={{0,4},{4,0},{1,5},{5,1},{2,6},{6,2},{3,7},{7,3},{8,12},{12,8},{9,1... | collective-permute-start | bytes 1572872 | tf_op jit(solution)/shard_map/ppermute | solution.py:821
  438.2 22.4 %collective-permute-start.64 = (bf16[256,1024]{1,0:T(8,128)(2,1)}, bf16[256,1024]{1,0:T(8,128)(2,1)S(1)}, u32[]{:S(2)}, u32[]{:S(2)}) collective-permute-start(bf16[256,1024]{1,0:T(8,128)(2,1)} %add_convert_fusion.2), channel_id=1, source_target_pairs={{0,1},{1,0},{2,3},{3,2},{4,5},{5,4},{6,7},{7,6},{8,9},{9,8},{10,11... | collective-permute-start | bytes 1572872 | tf_op jit(solution)/shard_map/ppermute | solution.py:821
  438.2 20.2 %collective-permute-start.62 = (bf16[1024,128]{1,0:T(8,128)(2,1)S(1)}, bf16[1024,128]{1,0:T(8,128)(2,1)}, u32[]{:S(2)}, u32[]{:S(2)}) collective-permute-start(bf16[1024,128]{1,0:T(8,128)(2,1)S(1)} %get-tuple-element.376), channel_id=1, source_target_pairs={{0,2},{2,0},{1,3},{3,1},{4,6},{6,4},{5,7},{7,5},{8,10},{10,8},{9,1... | collective-permute-start | bytes 786440 | tf_op jit(solution)/shard_map/ppermute | solution.py:821
  448.3 15.2 %collective-permute-start.69 = (bf16[2,1024,128]{2,1,0:T(8,128)(2,1)}, bf16[2,1024,128]{2,1,0:T(8,128)(2,1)}, u32[]{:S(2)}, u32[]{:S(2)}) collective-permute-start(bf16[2,1024,128]{2,1,0:T(8,128)(2,1)} %get-tuple-element.387), channel_id=1, source_target_pairs={{0,8},{8,0},{16,24},{24,16},{1,9},{9,1},{17,25},{25,17},{2,10},{10... | collective-permute-start | bytes 1572872 | tf_op jit(solution)/shard_map/ppermute | solution.py:825
  451.6 15.1 %collective-permute-start.68 = (bf16[2,1024,128]{2,1,0:T(8,128)(2,1)}, bf16[2,1024,128]{2,1,0:T(8,128)(2,1)S(1)}, u32[]{:S(2)}, u32[]{:S(2)}) collective-permute-start(bf16[2,1024,128]{2,1,0:T(8,128)(2,1)} %copy-done.65), channel_id=1, source_target_pairs={{0,16},{8,24},{16,0},{24,8},{1,17},{9,25},{17,1},{25,9},{2,18},{10... | collective-permute-start | bytes 1572872 | tf_op jit(solution)/shard_map/ppermute | solution.py:825
  458.4 14.7 %collective-permute-start.71 = (bf16[2,1024,128]{2,1,0:T(8,128)(2,1)S(1)}, bf16[2,1024,128]{2,1,0:T(8,128)(2,1)S(1)}, u32[]{:S(2)}, u32[]{:S(2)}) collective-permute-start(bf16[2,1024,128]{2,1,0:T(8,128)(2,1)S(1)} %get-tuple-element.388), channel_id=1, source_target_pairs={{0,8},{8,0},{16,24},{24,16},{1,9},{9,1},{17,25},{25,17},{2,10},{10... | collective-permute-start | bytes 1572872 | tf_op jit(solution)/shard_map/ppermute | solution.py:825
  460.1 21.6 %collective-permute-start.70 = (bf16[2,1024,128]{2,1,0:T(8,128)(2,1)S(1)}, bf16[2,1024,128]{2,1,0:T(8,128)(2,1)S(1)}, u32[]{:S(2)}, u32[]{:S(2)}) collective-permute-start(bf16[2,1024,128]{2,1,0:T(8,128)(2,1)S(1)} %get-tuple-element.375), channel_id=1, source_target_pairs={{0,16},{8,24},{16,0},{24,8},{1,17},{9,25},{17,1},{25,9},{2,18},{10... | collective-permute-start | bytes 1572872 | tf_op jit(solution)/shard_map/ppermute | solution.py:825
  462.6 10.6 %collective-permute-start.66 = (bf16[256,1024]{1,0:T(8,128)(2,1)S(1)}, bf16[256,1024]{1,0:T(8,128)(2,1)S(1)}, u32[]{:S(2)}, u32[]{:S(2)}) collective-permute-start(bf16[256,1024]{1,0:T(8,128)(2,1)S(1)} %get-tuple-element.383.refs_8_), channel_id=1, source_target_pairs={{0,4},{4,0},{1,5},{5,1},{2,6},{6,2},{3,7},{7,3},{8,12},{12,8},{9,1... | collective-permute-start | bytes 1572872 | tf_op jit(solution)/shard_map/ppermute | solution.py:821
  463.4 20.0 %collective-permute-start.65 = (bf16[256,1024]{1,0:T(8,128)(2,1)S(1)}, bf16[256,1024]{1,0:T(8,128)(2,1)S(1)}, u32[]{:S(2)}, u32[]{:S(2)}) collective-permute-start(bf16[256,1024]{1,0:T(8,128)(2,1)S(1)} %get-tuple-element.383.refs_8_), channel_id=1, source_target_pairs={{0,1},{1,0},{2,3},{3,2},{4,5},{5,4},{6,7},{7,6},{8,9},{9,8},{10,11... | collective-permute-start | bytes 1572872 | tf_op jit(solution)/shard_map/ppermute | solution.py:821
  481.8 9.2 %collective-permute-start.73 = (bf16[1,1024,128]{2,1,0:T(8,128)(2,1)S(1)}, bf16[1,1024,128]{2,1,0:T(8,128)(2,1)S(1)}, u32[]{:S(2)}, u32[]{:S(2)}) collective-permute-start(bf16[1,1024,128]{2,1,0:T(8,128)(2,1)S(1)} %add_convert_fusion.16), channel_id=1, source_target_pairs={{0,16},{8,24},{16,0},{24,8},{1,17},{9,25},{17,1},{25,9},{2,18},{10... | collective-permute-start | bytes 786440 | tf_op jit(solution)/shard_map/ppermute | solution.py:825
  483.5 13.5 %collective-permute-start.67 = (bf16[256,1024]{1,0:T(8,128)(2,1)S(1)}, bf16[256,1024]{1,0:T(8,128)(2,1)S(1)}, u32[]{:S(2)}, u32[]{:S(2)}) collective-permute-start(bf16[256,1024]{1,0:T(8,128)(2,1)S(1)} %collective-permute-done.65.refs_8_), channel_id=1, source_target_pairs={{0,4},{4,0},{1,5},{5,1},{2,6},{6,2},{3,7},{7,3},{8,12},{12,8},{9,1... | collective-permute-start | bytes 1572872 | tf_op jit(solution)/shard_map/ppermute | solution.py:821
  483.7 22.1 %collective-permute-start.74 = (bf16[1,1024,128]{2,1,0:T(8,128)(2,1)S(1)}, bf16[1,1024,128]{2,1,0:T(8,128)(2,1)S(1)}, u32[]{:S(2)}, u32[]{:S(2)}) collective-permute-start(bf16[1,1024,128]{2,1,0:T(8,128)(2,1)S(1)} %add_convert_fusion.15), channel_id=1, source_target_pairs={{0,8},{8,0},{16,24},{24,16},{1,9},{9,1},{17,25},{25,17},{2,10},{10... | collective-permute-start | bytes 786440 | tf_op jit(solution)/shard_map/ppermute | solution.py:825
  485.2 11.0 %collective-permute-start.75 = (bf16[1,1024,128]{2,1,0:T(8,128)(2,1)S(1)}, bf16[1,1024,128]{2,1,0:T(8,128)(2,1)S(1)}, u32[]{:S(2)}, u32[]{:S(2)}) collective-permute-start(bf16[1,1024,128]{2,1,0:T(8,128)(2,1)S(1)} %add_convert_fusion.14), channel_id=1, source_target_pairs={{0,16},{8,24},{16,0},{24,8},{1,17},{9,25},{17,1},{25,9},{2,18},{10... | collective-permute-start | bytes 786440 | tf_op jit(solution)/shard_map/ppermute | solution.py:825
  485.8 20.1 %collective-permute-start.72 = (bf16[1,1024,128]{2,1,0:T(8,128)(2,1)S(1)}, bf16[1,1024,128]{2,1,0:T(8,128)(2,1)S(1)}, u32[]{:S(2)}, u32[]{:S(2)}) collective-permute-start(bf16[1,1024,128]{2,1,0:T(8,128)(2,1)S(1)} %add_convert_fusion.17), channel_id=1, source_target_pairs={{0,8},{8,0},{16,24},{24,16},{1,9},{9,1},{17,25},{25,17},{2,10},{10... | collective-permute-start | bytes 786440 | tf_op jit(solution)/shard_map/ppermute | solution.py:825
  491.0 14.9 %collective-permute-start.77 = (bf16[1024,128]{1,0:T(8,128)(2,1)S(1)}, bf16[1024,128]{1,0:T(8,128)(2,1)S(1)}, u32[]{:S(2)}, u32[]{:S(2)}) collective-permute-start(bf16[1024,128]{1,0:T(8,128)(2,1)S(1)} %broadcast_select_fusion.5), channel_id=1, source_target_pairs={{0,2},{2,0},{1,3},{3,1},{4,6},{6,4},{5,7},{7,5},{8,10},{10,8},{9,1... | collective-permute-start | bytes 786440 | tf_op jit(solution)/shard_map/ppermute | solution.py:821
  507.7 8.9 %collective-permute-start.81 = (bf16[1024,128]{1,0:T(8,128)(2,1)}, bf16[1024,128]{1,0:T(8,128)(2,1)S(1)}, u32[]{:S(2)}, u32[]{:S(2)}) collective-permute-start(bf16[1024,128]{1,0:T(8,128)(2,1)} %fusion.12), channel_id=1, source_target_pairs={{0,4},{4,0},{1,5},{5,1},{2,6},{6,2},{3,7},{7,3},{8,12},{12,8},{9,1... | collective-permute-start | bytes 786440 | tf_op jit(solution)/shard_map/ppermute | solution.py:821
  508.2 14.6 %collective-permute-start.88 = (bf16[1024,128]{1,0:T(8,128)(2,1)}, bf16[1024,128]{1,0:T(8,128)(2,1)S(1)}, u32[]{:S(2)}, u32[]{:S(2)}) collective-permute-start(bf16[1024,128]{1,0:T(8,128)(2,1)} %fusion.14), channel_id=1, source_target_pairs={{0,4},{4,0},{1,5},{5,1},{2,6},{6,2},{3,7},{7,3},{8,12},{12,8},{9,1... | collective-permute-start | bytes 786440 | tf_op jit(solution)/shard_map/ppermute | solution.py:821
  514.9 17.3 %collective-permute-start.80 = (bf16[2,1024,128]{2,1,0:T(8,128)(2,1)S(1)}, bf16[2,1024,128]{2,1,0:T(8,128)(2,1)S(1)}, u32[]{:S(2)}, u32[]{:S(2)}) collective-permute-start(bf16[2,1024,128]{2,1,0:T(8,128)(2,1)S(1)} %get-tuple-element.417), channel_id=1, source_target_pairs={{0,8},{8,0},{16,24},{24,16},{1,9},{9,1},{17,25},{25,17},{2,10},{10... | collective-permute-start | bytes 1572872 | tf_op jit(solution)/shard_map/ppermute | solution.py:825
  517.5 14.7 %collective-permute-start.82 = (bf16[1024,128]{1,0:T(8,128)(2,1)S(1)}, bf16[1024,128]{1,0:T(8,128)(2,1)S(1)}, u32[]{:S(2)}, u32[]{:S(2)}) collective-permute-start(bf16[1024,128]{1,0:T(8,128)(2,1)S(1)} %get-tuple-element.471), channel_id=1, source_target_pairs={{0,2},{2,0},{1,3},{3,1},{4,6},{6,4},{5,7},{7,5},{8,10},{10,8},{9,1... | collective-permute-start | bytes 786440 | tf_op jit(solution)/shard_map/ppermute | solution.py:821
  518.3 14.0 %collective-permute-start.79 = (bf16[2,1024,128]{2,1,0:T(8,128)(2,1)S(1)}, bf16[2,1024,128]{2,1,0:T(8,128)(2,1)S(1)}, u32[]{:S(2)}, u32[]{:S(2)}) collective-permute-start(bf16[2,1024,128]{2,1,0:T(8,128)(2,1)S(1)} %get-tuple-element.415), channel_id=1, source_target_pairs={{0,16},{8,24},{16,0},{24,8},{1,17},{9,25},{17,1},{25,9},{2,18},{10... | collective-permute-start | bytes 1572872 | tf_op jit(solution)/shard_map/ppermute | solution.py:825
  520.0 20.9 %collective-permute-start.86 = (bf16[256,1024]{1,0:T(8,128)(2,1)S(1)}, bf16[256,1024]{1,0:T(8,128)(2,1)S(1)}, u32[]{:S(2)}, u32[]{:S(2)}) collective-permute-start(bf16[256,1024]{1,0:T(8,128)(2,1)S(1)} %add_convert_fusion.1), channel_id=1, source_target_pairs={{0,1},{1,0},{2,3},{3,2},{4,5},{5,4},{6,7},{7,6},{8,9},{9,8},{10,11... | collective-permute-start | bytes 1572872 | tf_op jit(solution)/shard_map/ppermute | solution.py:821
  522.8 11.7 %collective-permute-start.85 = (bf16[256,1024]{1,0:T(8,128)(2,1)S(1)}, bf16[256,1024]{1,0:T(8,128)(2,1)S(1)}, u32[]{:S(2)}, u32[]{:S(2)}) collective-permute-start(bf16[256,1024]{1,0:T(8,128)(2,1)S(1)} %get-tuple-element.425), channel_id=1, source_target_pairs={{0,4},{4,0},{1,5},{5,1},{2,6},{6,2},{3,7},{7,3},{8,12},{12,8},{9,1... | collective-permute-start | bytes 1572872 | tf_op jit(solution)/shard_map/ppermute | solution.py:821
  532.2 15.0 %collective-permute-start.89 = (bf16[1024,128]{1,0:T(8,128)(2,1)}, bf16[1024,128]{1,0:T(8,128)(2,1)S(1)}, u32[]{:S(2)}, u32[]{:S(2)}) collective-permute-start(bf16[1024,128]{1,0:T(8,128)(2,1)} %get-tuple-element.428), channel_id=1, source_target_pairs={{0,2},{2,0},{1,3},{3,1},{4,6},{6,4},{5,7},{7,5},{8,10},{10,8},{9,1... | collective-permute-start | bytes 786440 | tf_op jit(solution)/shard_map/ppermute | solution.py:821
  532.4 9.7 %collective-permute-start.83 = (bf16[1,1024,128]{2,1,0:T(8,128)(2,1)S(1)}, bf16[1,1024,128]{2,1,0:T(8,128)(2,1)S(1)}, u32[]{:S(2)}, u32[]{:S(2)}) collective-permute-start(bf16[1,1024,128]{2,1,0:T(8,128)(2,1)S(1)} %add_convert_fusion.13), channel_id=1, source_target_pairs={{0,8},{8,0},{16,24},{24,16},{1,9},{9,1},{17,25},{25,17},{2,10},{10... | collective-permute-start | bytes 786440 | tf_op jit(solution)/shard_map/ppermute | solution.py:825
  533.0 9.1 %collective-permute-start.84 = (bf16[1,1024,128]{2,1,0:T(8,128)(2,1)S(1)}, bf16[1,1024,128]{2,1,0:T(8,128)(2,1)}, u32[]{:S(2)}, u32[]{:S(2)}) collective-permute-start(bf16[1,1024,128]{2,1,0:T(8,128)(2,1)S(1)} %add_convert_fusion.12), channel_id=1, source_target_pairs={{0,16},{8,24},{16,0},{24,8},{1,17},{9,25},{17,1},{25,9},{2,18},{10... | collective-permute-start | bytes 786440 | tf_op jit(solution)/shard_map/ppermute | solution.py:825
  547.2 25.7 %collective-permute-start.90 = (bf16[1024,128]{1,0:T(8,128)(2,1)}, bf16[1024,128]{1,0:T(8,128)(2,1)}, u32[]{:S(2)}, u32[]{:S(2)}) collective-permute-start(bf16[1024,128]{1,0:T(8,128)(2,1)} %fusion.13), channel_id=1, source_target_pairs={{0,4},{4,0},{1,5},{5,1},{2,6},{6,2},{3,7},{7,3},{8,12},{12,8},{9,1... | collective-permute-start | bytes 786440 | tf_op jit(solution)/shard_map/ppermute | solution.py:821
  547.2 28.9 %collective-permute-start.87 = (bf16[256,1024]{1,0:T(8,128)(2,1)}, bf16[256,1024]{1,0:T(8,128)(2,1)}, u32[]{:S(2)}, u32[]{:S(2)}) collective-permute-start(bf16[256,1024]{1,0:T(8,128)(2,1)} %add_convert_fusion), channel_id=1, source_target_pairs={{2,4},{4,2},{3,5},{5,3},{10,12},{12,10},{11,13},{13,11},{18,20},{2... | collective-permute-start | bytes 1572872 | tf_op jit(solution)/shard_map/ppermute | solution.py:829
  560.4 10.6 %collective-permute-start.96 = (f32[1,768]{1,0:T(1,128)S(1)}, f32[1,768]{1,0:T(1,128)S(1)}, u32[]{:S(2)}, u32[]{:S(2)}) collective-permute-start(f32[1,768]{1,0:T(1,128)S(1)} %fusion.20), channel_id=1, source_target_pairs={{0,2},{2,0},{1,3},{3,1},{4,6},{6,4},{5,7},{7,5},{8,10},{10,8},{9,1... | collective-permute-start | bytes 9224 | tf_op jit(solution)/shard_map/ppermute | solution.py:821
  574.0 10.0 %collective-permute-start.91 = (bf16[1024,128]{1,0:T(8,128)(2,1)S(1)}, bf16[1024,128]{1,0:T(8,128)(2,1)S(1)}, u32[]{:S(2)}, u32[]{:S(2)}) collective-permute-start(bf16[1024,128]{1,0:T(8,128)(2,1)S(1)} %fusion.15), channel_id=1, source_target_pairs={{0,2},{2,0},{1,3},{3,1},{4,6},{6,4},{5,7},{7,5},{8,10},{10,8},{9,1... | collective-permute-start | bytes 786440 | tf_op jit(solution)/shard_map/ppermute | solution.py:821
  (173 other events, 1183.0 us)
Sparse Core Ops, SparseCore 0:
  28.0 37.2 all-gather.4
  80.3 53.0 all-gather.6
  139.9 34.6 all-gather.8
  186.7 52.8 all-gather.10
  347.7 52.5 reduce-scatter.2
  403.3 35.1 reduce-scatter.4

commit v4 on v3

--- a/solution.py
+++ b/solution.py
@@ -453,27 +453,29 @@
             at += ref.shape[1]
 
 
-def pack(fields, args, layer):
+def pack(parts, args):
+    fields = [f for f, _ in parts]
     ins = [args[f] for f in fields]
     piece = args["up"].shape[1]
     if piece != 128:
         flat = {
-            "qkv": lambda a: a[layer].transpose(0, 2, 1).reshape(-1, piece),
-            "up": lambda a: a[layer].T,
-            "out": lambda a: a[layer],
-            "down": lambda a: a[layer],
+            "qkv": lambda a, l: a[l].transpose(0, 2, 1).reshape(-1, piece),
+            "up": lambda a, l: a[l].T,
+            "out": lambda a, l: a[l],
+            "down": lambda a, l: a[l],
         }
-        return jnp.concatenate([flat[f](a) for f, a in zip(fields, ins)], 0)
+        return jnp.concatenate([flat[f](args[f], l) for f, l in parts], 0)
     lines = sum(a.size // a.shape[0] for a in ins) // piece
     return pl.pallas_call(
         functools.partial(pack_kernel, fields),
         grid=(1,),
         in_specs=[
-            pl.BlockSpec((1,) + a.shape[1:], whole(layer, *([0] * (a.ndim - 1)))) for a in ins
+            pl.BlockSpec((1,) + args[f].shape[1:], whole(l, *([0] * (args[f].ndim - 1))))
+            for f, l in parts
         ],
         out_specs=pl.BlockSpec((lines, piece), whole(0, 0)),
         out_shape=struct((lines, piece), bf16),
-        compiler_params=params(8),
+        compiler_params=params(12),
         cost_estimate=cost(0, 4 * lines * piece),
         name="pack",
     )(*far(*ins))
@@ -594,7 +596,7 @@
         compiler_params=params(20),
         cost_estimate=cost(0, 4 * sum(s.size for s in stacks)),
         name="place",
-    )(where, *stacks)
+    )(where, *far(*stacks))
 
 
 def grad_kernel(fields, counts, specs, where_ref, *refs):
@@ -874,31 +876,21 @@
 
 
 class Gather:
-    def __init__(self, fields, args, layer, pos, where, n_d):
+    def __init__(self, fields, tile, crossed, widths, pos, where, n_d):
         self.fields, self.pos, self.where, self.n_d = fields, pos, where, n_d
-        self.widths = args["out"].shape[1], args["down"].shape[1]
-        self.tile = pack(fields, args, layer)
-        self.crossed = []
-
-    def cross(self, *marks, parts=1):
-        lines = self.tile.shape[0] // parts
-        part = self.tile[len(self.crossed) * lines : (len(self.crossed) + 1) * lines]
-        self.crossed.append(swap(after(part, *marks) if marks else part, "zh"))
-        return self.crossed[-1]
+        self.widths, self.tile, self.crossed = widths, tile, crossed
 
     def cores(self, *marks):
         _, c, zh, _ = self.pos
         same = c == zh
-        crossed = jnp.concatenate(self.crossed, 0) if len(self.crossed) > 1 else self.crossed[0]
-        crossed = after(crossed, *marks) if marks else crossed
+        crossed = after(self.crossed, *marks) if marks else self.crossed
         self.own = jnp.where(same, self.tile, crossed)
         self.other = swap(jnp.where(same, crossed, self.tile), "c")
         return self.other
 
     def collect(self, *marks):
-        both = jnp.stack([self.own, self.other])
-        if marks:
-            both = after(both, *marks)
+        self.both = jnp.stack([self.own, self.other])
+        both = after(self.both, *marks) if marks else self.both
         self.stacks = [lax.all_gather(both, "d", axis=0, tiled=True)]
         self.specs = absolute_specs(self.n_d)
         return self.stacks[0]
@@ -1005,25 +997,32 @@
     stay = c == zh
     args = {"qkv": w_qkv.transpose(0, 2, 1, 3), "out": w_out, "up": w_up, "down": w_down}
 
-    def gather(fields, layer):
-        return Gather(fields, args, layer, pos, where, n_d)
-
-    g_a0 = gather(("qkv", "out"), 0)
-    a0_crossed = g_a0.cross()
-    g_f0, g_a1, g_f1 = gather(("up", "down"), 0), gather(("qkv", "out"), 1), gather(("up", "down"), 1)
+    tile_a0 = pack((("qkv", 0), ("out", 0)), args)
+    a0_crossed = swap(tile_a0, "zh")
+    g_a0 = Gather(("qkv", "out"), tile_a0, a0_crossed, widths, pos, where, n_d)
+    rest = [("up", 0), ("down", 0), ("qkv", 1), ("out", 1), ("up", 1), ("down", 1)]
+    tile_rest = pack(rest, args)
     small_own = jnp.concatenate([a.reshape(1, -1) for a in (gains, biases, up_bias)], 1)
     src, seg_col, seg_row = maps(
         lengths, order, jnp.stack([d * 2 + zh, slot]).astype(jnp.int32), 4 * rows
     )
     seg_near, seg_far = seg_col[: 2 * rows], seg_col[2 * rows :]
-    g_a0.cores(src, small_own, *[g.tile for g in (g_f0, g_a1, g_f1)])
+    g_a0.cores(src, small_own, tile_rest)
     g_a0.collect()
     raw_got = to_home(after(tokens, a0_crossed))
     raw = jnp.where(stay, tokens, raw_got)
     raw_near, raw_far = send_rows(raw)
-    f0_crossed = g_f0.cross(raw_got)
+    rest_crossed = swap(after(tile_rest, raw_got), "zh")
+    gathers, at = [], 0
+    for n in range(0, len(rest), 2):
+        fields = (rest[n][0], rest[n + 1][0])
+        lines = sum(lines_of(f, *widths) for f in fields)
+        part = slice(at, at + lines)
+        gathers.append(Gather(fields, tile_rest[part], rest_crossed[part], widths, pos, where, n_d))
+        at += lines
+    g_f0, g_a1, g_f1 = gathers
     x_near, x_far, hidden = deal_rows(src, [*raw_near, *far_rows(raw_far)])
-    small_near = gather_small(after(small_own, g_a0.other), pos, n_d)
+    small_near = gather_small(after(small_own, x_near[0]), pos, n_d)
     small_far = swap(small_near, "zh")
     width = D // n_dev
     up_width = FF // n_dev
@@ -1038,9 +1037,10 @@
     own_vectors = lax.dynamic_slice(vectors, (0, slot * head_width), (n_vec, head_width))
     gain_row = lambda layer, i: 2 * layer + i
     bias_row = lambda layer, i: 2 * LAYERS + 6 * layer + i
-    f0_other = g_f0.cores(x_near[0])
+    f0_other = g_f0.cores(small_near)
     g_f0.collect()
-    a1_crossed = g_a1.cross(f0_other)
+    cot_got = to_home(after(cotangent, f0_other, small_far))
+    cot_near, cot_sent = send_rows(jnp.where(stay, cotangent, cot_got))
     weights = [g_a0.weights(), {}]
 
     kept = []
@@ -1057,15 +1057,15 @@
             ],
             1,
         )
+        if first:
+            x_near = (after(x_near[0], g_f0.both), x_near[1])
         proj_near, keep_near = project(x_near, w["qkv"], add)
         if not first:
             x_far = far_rows(x_sent, keep_near)
         proj_far, keep_far = project(x_far, w["qkv"], add)
         proj = (proj_near, proj_far)
         x_kept = (keep_near, keep_far)
-        due = [a1_crossed] if first else []
-        if not first:
-            cot_got = to_home(after(cotangent, proj_far))
+        due = [cot_got] if first else []
         att_far, lse_far, mine, theirs = attend(
             proj_far, proj, seg_far, seg_row, w["out"], scale, heads
         )
@@ -1073,8 +1073,8 @@
         att_near, lse_near, mine, theirs = attend(
             after(proj_near, chip), proj, seg_near, seg_row, w["out"], scale, heads
         )
-        due = [crossed] if first else [crossed, cot_got]
-        terms = (*chip_sum(mine, theirs, *due), crossed)
+        terms = chip_sum(mine, theirs, crossed)
+        terms = (*terms, crossed)
         at = [bias_row(layer, 2), gain_row(layer, 0), bias_row(layer, 3)]
         normed, low, n_one, r_one = norm((hidden, *terms), vectors, *at)
         n_near, n_sent = send_rows(low)
@@ -1083,7 +1083,6 @@
             w.update(g_f0.weights())
             g_a1.cores(low)
             g_a1.collect()
-            due += [g_f1.cross(low, parts=2)]
         else:
             w.update(g_f1.weights())
         u_bias = ups[layer : layer + 1]
@@ -1091,12 +1090,6 @@
         near = chip_sum(mine_near, theirs_near, *due)
         n_far = far_rows(n_sent, keep_near)
         due = []
-        if first:
-            due += [g_f1.cross(keep_near, parts=2)]
-        else:
-            cot = jnp.where(stay, cotangent, cot_got)
-            cot_near, cot_sent = send_rows(after(cot, keep_near))
-            due += [cot_sent]
         act_far, slope_far, mine, theirs, keep_far = ffn(n_far, w["up"], w["down"], u_bias)
         chip, crossed = cross_sum(chip_sum(mine, theirs, *due))
         if first:
@@ -1179,6 +1172,10 @@
             k["proj"][1], k["proj"], seg_far, seg_row, k["lse"][1], one_far, w["out"], scale, heads,
             earlier,
         )
+        if late:
+            outs = {f: None for f in ("qkv", "out", "up", "down")}
+            late[0].finish(outs, 1, widths, earlier[0])
+            due += [outs["up"]]
         d_far = after(d_far, *due)
         mine, theirs = input_grad(d_far, w["qkv"])
         chip, crossed = cross_sum(chip_sum(mine, theirs))
@@ -1190,6 +1187,7 @@
             near = chip_sum(*input_grad(d_near, w["qkv"]))
         else:
             near = chip_sum(*input_grad(after(d_near, chip), w["qkv"]))
+            att_pairs = ((k["x"], (after(d_near, near[1]), d_far)), att_pairs[1])
             r_att = Reduce(("qkv", "out"), att_pairs, pos, where, n_d, False)
             late = (r_ff, r_att)
             d_one = after(d_one, r_att.stacks[0])
@@ -1214,9 +1212,7 @@
     grad_got = to_home(after(own_grad, *att_got))
     r_att.cores(up_crossed)
     r_att.cross(4 * head_width)
-    outs = {f: None for f in ("qkv", "out", "up", "down")}
-    for r in late:
-        r.finish(outs, 1, widths, *att_got)
+    late[1].finish(outs, 1, widths, *att_got)
     r_down.finish(outs, 0, widths, *att_got)
     r_ff.finish(outs, 0, widths, *att_got)
     r_att.finish(outs, 0, widths)

time: 599 us -> 588 us (0.982)
  waiting for transfers between devices: 231 us -> 209 us
  Pallas kernels: 175 us -> 182 us
    ppermute x77 -> x74, waiting for transfers between devices: 208 us -> 177 us  [swap(): return lax.ppermute(a, axis, SWAP)]
    all_gather x4, waiting for transfers between devices: 0.02 us -> 7.75 us  [collect(): self.stacks = [lax.all_gather(both, 'd', axis=0, tiled=True)]]
    ppermute x77 -> x74, starting transfers between devices: 64.1 us -> 66.4 us  [swap(): return lax.ppermute(a, axis, SWAP)]
    unnamed x271 -> x279, local copies, waits for them, and re-layouts: 40 us -> 40.6 us
  transfers between devices with their start and end apart: 103 -> 100, of which waited for: 56 -> 56; matrix products, arithmetic and copies ran while one was open for 7% -> 8% of each run, Pallas kernels for 28% -> 29%
where the time goes in v4:
time: 588 us; the launch traced here: 582 us
  waiting for transfers between devices  209 us (36%)
  Pallas kernels  182 us (31%)
  starting transfers between devices  89.6 us (15%)
  local copies, waits for them, and re-layouts  54.7 us (9%)
  other arithmetic  29.4 us (5%)
  between operations  16.1 us (3%)
    ppermute x74, waiting for transfers between devices, swap(): return lax.ppermute(a, axis, SWAP)  177 us
    ppermute x74, starting transfers between devices, swap(): return lax.ppermute(a, axis, SWAP)  66.4 us
    unnamed x279, local copies, waits for them, and re-layouts  40.6 us
    pallas_call x5, Pallas kernels, weight_grad(): pl.pallas_call(functools.partial(grad_kernel, fields, counts, specs), gri...  33.8 us
    pallas_call x4, Pallas kernels, attend_back(): pl.pallas_call(functools.partial(attend_back_kernel, scale, heads, last),...  33.5 us
    pallas_call x4, Pallas kernels, ffn(): pl.pallas_call(ffn_kernel, grid=(ff // tile,), in_specs=[*blocks_in(x), p...  25.3 us
    ppermute x16, waiting for transfers between devices, flip_d(): return lax.ppermute(a, 'd', [(i, i ^ 1 << bit) for i in range(n_d)])  24.3 us
    pallas_call x4, Pallas kernels, ffn_back(): pl.pallas_call(ffn_back_kernel, grid=(ff // tile,), in_specs=[*blocks_in(...  20 us
  transfers between devices with their start and end apart: 100, of which 56 were waited for; matrix products, arithmetic and copies ran while one was open for 8% of the time, Pallas kernels for 29%

profile of v4, /device:TPU:0, one launch (start us, length us, event | category | flops | bytes accessed | tf_op | source)
XLA Modules:
  0.0 581.8 jit_solution(3654554047318021881)
XLA Ops:
  8.2 4.1 collective-permute-start
  12.3 11.9 %collective-permute-done = bf16[1024,128]{1,0:T(8,128)(2,1)S(1)} collective-permute-done((bf16[1024,128]{1,0:T(8,128)(2,1)S(1)}, bf16[1024,128]{1,0:T(8,128)(2,1)S(1)}, u32[]{:S(2)}, u32[]{:S(2)}) %collective-permute-start) | collective-permute-done | bytes 262176 | tf_op jit(solution)/shard_map/ppermute | solution.py:823
  32.4 4.6 collective-permute-start.3
  38.0 6.9 %collective-permute-start.5 = (bf16[5120,128]{1,0:T(8,128)(2,1)S(1)}, bf16[5120,128]{1,0:T(8,128)(2,1)}, u32[]{:S(2)}, u32[]{:S(2)}) collective-permute-start(bf16[5120,128]{1,0:T(8,128)(2,1)S(1)} %pack.3), channel_id=1, source_target_pairs={{0,2},{2,0},{1,3},{3,1},{4,6},{6,4},{5,7},{7,5},{8,10},{10,8},{9,1... | collective-permute-start | bytes 3932168 | tf_op jit(solution)/shard_map/ppermute | solution.py:823
  44.8 6.8 %collective-permute-done.3.refs_2_ = bf16[256,1024]{1,0:T(8,128)(2,1)S(1)} collective-permute-done((bf16[256,1024]{1,0:T(8,128)(2,1)S(1)}, bf16[256,1024]{1,0:T(8,128)(2,1)S(1)}, u32[]{:S(2)}, u32[]{:S(2)}) %collective-permute-start.3) | collective-permute-done | bytes 524320 | tf_op jit(solution)/shard_map/ppermute | solution.py:823
  51.6 4.9 collective-permute-start.4
  60.1 2.4 deal_rows.1
  65.7 8.5 %collective-permute-done.6 = f32[1,768]{1,0:T(1,128)S(1)} collective-permute-done((f32[1,768]{1,0:T(1,128)S(1)}, f32[1,768]{1,0:T(1,128)S(1)}, u32[]{:S(2)}, u32[]{:S(2)}) %collective-permute-start.6) | collective-permute-done | bytes 3104 | tf_op jit(solution)/shard_map/ppermute | solution.py:823
  74.2 3.6 collective-permute-start.7
  84.0 2.3 collective-permute-done.9
  86.9 15.5 %collective-permute-done.5 = bf16[5120,128]{1,0:T(8,128)(2,1)} collective-permute-done((bf16[5120,128]{1,0:T(8,128)(2,1)S(1)}, bf16[5120,128]{1,0:T(8,128)(2,1)}, u32[]{:S(2)}, u32[]{:S(2)}) %collective-permute-start.5) | collective-permute-done | bytes 1310752 | tf_op jit(solution)/shard_map/ppermute | solution.py:823
  108.0 5.2 collective-permute-done.12
  121.3 2.4 project.4
  123.7 2.4 project.5
  126.1 4.8 attend.4
  133.2 2.6 collective-permute-start.15
  135.7 4.8 attend.5
  140.5 7.6 %collective-permute-done.15.refs_3_ = bf16[256,1024]{1,0:T(8,128)(2,1)S(1)} collective-permute-done((bf16[256,1024]{1,0:T(8,128)(2,1)S(1)}, bf16[256,1024]{1,0:T(8,128)(2,1)S(1)}, u32[]{:S(2)}, u32[]{:S(2)}) %collective-permute-start.15) | collective-permute-done | bytes 524320 | tf_op jit(solution)/shard_map/ppermute | solution.py:823
  156.1 3.7 all-gather.7.cloned.1.call-done.refs_0_
  159.9 3.3 place.5
  163.2 7.5 %ffn.4 = (bf16[512,1024]{1,0:T(8,128)(2,1)}, f32[512,1024]{1,0:T(8,128)}, f32[256,1024]{1,0:T(8,128)S(1)}, bf16[256,1024]{1,0:T(8,128)(2,1)S(1)}, bf16[512,1024]{1,0:T(8,128)(2,1)}) custom-call(bf16[256,1024]{1,0:T(8,128)(2,1)} %get-tuple-element.252.refs_0_, bf16[256,1024]{1,0:T(8,128)(2,1)} %collective-permute-done.17.refs_1_, ...), custom_call_target="tpu_custom_call" | custom-call | flops 2147483648 | bytes 9437184 | tf_op jit(solution)/shard_map/ffn/pallas_call | solution.py:354
  174.4 5.4 ffn.5
  188.0 12.4 %collective-permute-done.22.refs_3_ = bf16[256,1024]{1,0:T(8,128)(2,1)S(1)} collective-permute-done((bf16[256,1024]{1,0:T(8,128)(2,1)S(1)}, bf16[256,1024]{1,0:T(8,128)(2,1)S(1)}, u32[]{:S(2)}, u32[]{:S(2)}) %collective-permute-start.22) | collective-permute-done | bytes 524320 | tf_op jit(solution)/shard_map/ppermute | solution.py:823
  205.8 3.9 project.6
  209.7 7.1 %collective-permute-done.25.refs_0_ = bf16[256,1024]{1,0:T(8,128)(2,1)S(1)} collective-permute-done((bf16[256,1024]{1,0:T(8,128)(2,1)}, bf16[256,1024]{1,0:T(8,128)(2,1)S(1)}, u32[]{:S(2)}, u32[]{:S(2)}) %collective-permute-start.25) | collective-permute-done | bytes 524320 | tf_op jit(solution)/shard_map/ppermute | solution.py:823
  218.7 2.6 project.7
  221.3 4.8 attend.6
  229.7 4.8 attend.7
  234.5 7.7 %collective-permute-done.28.refs_3_ = bf16[256,1024]{1,0:T(8,128)(2,1)S(1)} collective-permute-done((bf16[256,1024]{1,0:T(8,128)(2,1)S(1)}, bf16[256,1024]{1,0:T(8,128)(2,1)S(1)}, u32[]{:S(2)}, u32[]{:S(2)}) %collective-permute-start.28) | collective-permute-done | bytes 524320 | tf_op jit(solution)/shard_map/ppermute | solution.py:823
  247.5 4.0 all-gather.11.cloned.1.call-done.refs_0_
  251.5 3.3 place.7
  254.9 7.0 %ffn.6 = (bf16[512,1024]{1,0:T(8,128)(2,1)}, f32[512,1024]{1,0:T(8,128)}, f32[256,1024]{1,0:T(8,128)S(1)}, bf16[256,1024]{1,0:T(8,128)(2,1)S(1)}, bf16[512,1024]{1,0:T(8,128)(2,1)}) custom-call(bf16[256,1024]{1,0:T(8,128)(2,1)} %get-tuple-element.278.refs_0_, bf16[256,1024]{1,0:T(8,128)(2,1)S(1)} %collective-permute-done.30.refs_1_, ...), custom_call_target="tpu_custom_call" | custom-call | flops 2147483648 | bytes 9437184 | tf_op jit(solution)/shard_map/ffn/pallas_call | solution.py:354
  263.8 5.4 ffn.7
  270.1 6.2 %collective-permute-done.38 = bf16[256,1024]{1,0:T(8,128)(2,1)S(1)} collective-permute-done((bf16[256,1024]{1,0:T(8,128)(2,1)S(1)}, bf16[256,1024]{1,0:T(8,128)(2,1)S(1)}, u32[]{:S(2)}, u32[]{:S(2)}) %collective-permute-start.38) | collective-permute-done | bytes 524320 | tf_op jit(solution)/shard_map/ppermute | solution.py:823
  281.4 9.8 %collective-permute-done.36.refs_3_ = bf16[256,1024]{1,0:T(8,128)(2,1)S(1)} collective-permute-done((bf16[256,1024]{1,0:T(8,128)(2,1)S(1)}, bf16[256,1024]{1,0:T(8,128)(2,1)S(1)}, u32[]{:S(2)}, u32[]{:S(2)}) %collective-permute-start.36) | collective-permute-done | bytes 524320 | tf_op jit(solution)/shard_map/ppermute | solution.py:823
  297.1 5.2 ffn_back.4
  303.3 6.3 %collective-permute-done.41.refs_0_ = bf16[256,1024]{1,0:T(8,128)(2,1)S(1)} collective-permute-done((bf16[256,1024]{1,0:T(8,128)(2,1)S(1)}, bf16[256,1024]{1,0:T(8,128)(2,1)S(1)}, u32[]{:S(2)}, u32[]{:S(2)}) %collective-permute-start.41) | collective-permute-done | bytes 524320 | tf_op jit(solution)/shard_map/ppermute | solution.py:823
  311.5 5.1 ffn_back.5
  320.9 9.6 %weight_grad.5 = bf16[8,2048,128]{2,1,0:T(8,128)(2,1)} custom-call(s32[2]{0:T(128)S(1)} %pad_add_fusion.1.where_ref, bf16[512,1024]{1,0:T(8,128)(2,1)} %get-tuple-element.285.refs_0_, bf16[512,1024]{1,0:T(8,128)(2,1)} %get-tuple-element.294.refs_1_, bf16[512,1024]{1,0:T(8,128)(2,1)} %get-tuple-element.297.refs_2_, ...), custom_call_target="tpu_custom_call" | custom-call | flops 4294967296 | bytes 12582912 | tf_op jit(solution)/shard_map/weight_grad/pallas_call | solution.py:648
  345.5 7.9 %attend_back.4 = (bf16[512,256]{1,0:T(8,128)(2,1)S(1)}, f32[1,256]{1,0:T(1,128)S(1)}, f32[1024,256]{1,0:T(8,128)S(1)}, f32[1024,256]{1,0:T(8,128)S(1)}, bf16[512,1024]{1,0:T(8,128)(2,1)}) custom-call(bf16[512,768]{1,0:T(8,128)(2,1)S(1)} %copy-done.82, bf16[512,768]{1,0:T(8,128)(2,1)S(1)} %copy-done.82, bf16[512,768]{1,0:T(8,128)(2,1)S(1)} %copy-done.84, ...), custom_call_target="tpu_custom_call" | custom-call | flops 5368709120 | bytes 8388608 | tf_op jit(solution)/shard_map/attend_back/pallas_call | solution.py:304
  357.6 8.6 %attend_back.5 = (bf16[512,768]{1,0:T(8,128)(2,1)S(1)}, bf16[512,768]{1,0:T(8,128)(2,1)S(1)}, f32[2,256]{1,0:T(2,128)S(1)}, bf16[512,1024]{1,0:T(8,128)(2,1)}) custom-call(bf16[512,768]{1,0:T(8,128)(2,1)S(1)} %copy-done.84, bf16[512,768]{1,0:T(8,128)(2,1)S(1)} %copy-done.82, bf16[512,768]{1,0:T(8,128)(2,1)S(1)} %copy-done.84, ...), custom_call_target="tpu_custom_call" | custom-call | flops 5368709120 | bytes 8388608 | tf_op jit(solution)/shard_map/attend_back/pallas_call | solution.py:304
  367.2 7.1 %collective-permute-start.50 = (bf16[256,1024]{1,0:T(8,128)(2,1)S(1)}, bf16[256,1024]{1,0:T(8,128)(2,1)S(1)}, u32[]{:S(2)}, u32[]{:S(2)}) collective-permute-start(bf16[256,1024]{1,0:T(8,128)(2,1)S(1)} %get-tuple-element.332), channel_id=1, source_target_pairs={{0,4},{4,0},{1,5},{5,1},{2,6},{6,2},{3,7},{7,3},{8,12},{12,8},{9,1... | collective-permute-start | bytes 1572872 | tf_op jit(solution)/shard_map/ppermute | solution.py:823
  380.7 6.7 %weight_grad.6 = bf16[8,1024,128]{2,1,0:T(8,128)(2,1)} custom-call(s32[2]{0:T(128)S(1)} %pad_add_fusion.1.where_ref, bf16[512,1024]{1,0:T(8,128)(2,1)} %get-tuple-element.267.refs_0_, bf16[512,1024]{1,0:T(8,128)(2,1)} %get-tuple-element.322.refs_1_, bf16[512,768]{1,0:T(8,128)(2,1)} %copy-done.13, bf16[512,768]{1,0:T(8,128)(2,1)} %copy-done.14, ...), custom_call_target="tpu_custom_call" | custom-call | flops 2147483648 | bytes 12582912 | tf_op jit(solution)/shard_map/weight_grad/pallas_call | solution.py:648
  387.5 4.9 collective-permute-done.52.refs_3_
  403.3 5.6 ffn_back.6
  408.8 4.5 collective-permute-done.54.refs_0_
  416.8 4.2 ffn_back.7
  421.0 8.5 %collective-permute-done.57 = bf16[1024,128]{1,0:T(8,128)(2,1)S(1)} collective-permute-done((bf16[1024,128]{1,0:T(8,128)(2,1)S(1)}, bf16[1024,128]{1,0:T(8,128)(2,1)S(1)}, u32[]{:S(2)}, u32[]{:S(2)}) %collective-permute-start.57) | collective-permute-done | bytes 262176 | tf_op jit(solution)/shard_map/ppermute | solution.py:823
  431.7 3.1 collective-permute-start.59
  434.8 6.0 %weight_grad.7 = (bf16[2,1024,128]{2,1,0:T(8,128)(2,1)}, bf16[2,1024,128]{2,1,0:T(8,128)(2,1)S(1)}, bf16[2,1024,128]{2,1,0:T(8,128)(2,1)}, bf16[2,1024,128]{2,1,0:T(8,128)(2,1)S(1)}) custom-call(s32[2]{0:T(128)S(1)} %pad_add_fusion.1.where_ref, bf16[512,1024]{1,0:T(8,128)(2,1)} %get-tuple-element.352.refs_0_, bf16[512,1024]{1,0:T(8,128)(2,1)} %get-tuple-element.353.refs_1_, ...), custom_call_target="tpu_custom_call" | custom-call | flops 2147483648 | bytes 12582912 | tf_op jit(solution)/shard_map/weight_grad/pallas_call | solution.py:648
  445.4 5.3 weight_grad.8
  460.0 6.5 %collective-permute-done.67 = bf16[2,1024,128]{2,1,0:T(8,128)(2,1)S(1)} collective-permute-done((bf16[2,1024,128]{2,1,0:T(8,128)(2,1)S(1)}, bf16[2,1024,128]{2,1,0:T(8,128)(2,1)S(1)}, u32[]{:S(2)}, u32[]{:S(2)}) %collective-permute-start.67) | collective-permute-done | bytes 524320 | tf_op jit(solution)/shard_map/ppermute | solution.py:827
  466.5 2.9 collective-permute-done.68
  469.6 8.3 %attend_back.6 = (bf16[512,256]{1,0:T(8,128)(2,1)S(1)}, f32[1,256]{1,0:T(1,128)S(1)}, f32[1024,256]{1,0:T(8,128)S(1)}, f32[1024,256]{1,0:T(8,128)S(1)}, bf16[512,1024]{1,0:T(8,128)(2,1)}) custom-call(bf16[512,768]{1,0:T(8,128)(2,1)S(1)} %copy-done.78, bf16[512,768]{1,0:T(8,128)(2,1)S(1)} %copy-done.78, bf16[512,768]{1,0:T(8,128)(2,1)S(1)} %copy-done.80, ...), custom_call_target="tpu_custom_call" | custom-call | flops 5368709120 | bytes 8388608 | tf_op jit(solution)/shard_map/attend_back/pallas_call | solution.py:304
  484.1 8.8 %attend_back.7 = (bf16[512,768]{1,0:T(8,128)(2,1)S(1)}, bf16[512,768]{1,0:T(8,128)(2,1)S(1)}, f32[2,256]{1,0:T(2,128)S(1)}, bf16[512,1024]{1,0:T(8,128)(2,1)}) custom-call(bf16[512,768]{1,0:T(8,128)(2,1)S(1)} %copy-done.80, bf16[512,768]{1,0:T(8,128)(2,1)S(1)} %copy-done.78, bf16[512,768]{1,0:T(8,128)(2,1)S(1)} %copy-done.80, ...), custom_call_target="tpu_custom_call" | custom-call | flops 5368709120 | bytes 8388608 | tf_op jit(solution)/shard_map/attend_back/pallas_call | solution.py:304
  492.9 5.3 collective-permute-done.74.got_ref
  502.7 6.2 %weight_grad.9 = (bf16[2,1024,128]{2,1,0:T(8,128)(2,1)}, bf16[2,1024,128]{2,1,0:T(8,128)(2,1)S(1)}, bf16[2,1024,128]{2,1,0:T(8,128)(2,1)}, bf16[2,1024,128]{2,1,0:T(8,128)(2,1)S(1)}) custom-call(s32[2]{0:T(128)S(1)} %pad_add_fusion.1.where_ref, bf16[512,1024]{1,0:T(8,128)(2,1)} %get-tuple-element.318.refs_0_, bf16[512,1024]{1,0:T(8,128)(2,1)} %get-tuple-element.319.refs_1_, ...), custom_call_target="tpu_custom_call" | custom-call | flops 2147483648 | bytes 12582912 | tf_op jit(solution)/shard_map/weight_grad/pallas_call | solution.py:648
  520.7 3.5 collective-permute-done.76
  525.4 2.5 collective-permute-done.79.got_ref
  531.9 4.3 collective-permute-done.80
  536.7 2.3 add_convert_fusion
  541.7 4.2 collective-permute-done.90
  556.7 2.7 collective-permute-done.93
  565.8 8.1 %collective-permute-done.88.got_ref = bf16[1024,128]{1,0:T(8,128)(2,1)S(1)} collective-permute-done((bf16[1024,128]{1,0:T(8,128)(2,1)S(1)}, bf16[1024,128]{1,0:T(8,128)(2,1)S(1)}, u32[]{:S(2)}, u32[]{:S(2)}) %collective-permute-start.88) | collective-permute-done | bytes 262176 | tf_op jit(solution)/shard_map/ppermute | solution.py:823
  (590 shorter events, 201.4 us)
Async XLA Ops:
  7.2 109.5 %all-gather.5.cloned.1.call-start = ((), (), s32[]{:S(2)}) async-start(), calls=%async_computation.2 | async-start | bytes 2621440 | tf_op jit(solution)/shard_map/all_gather | solution.py:894
  8.2 16.0 %collective-permute-start = (bf16[1024,128]{1,0:T(8,128)(2,1)S(1)}, bf16[1024,128]{1,0:T(8,128)(2,1)S(1)}, u32[]{:S(2)}, u32[]{:S(2)}) collective-permute-start(bf16[1024,128]{1,0:T(8,128)(2,1)S(1)} %pack.2), channel_id=1, source_target_pairs={{0,2},{2,0},{1,3},{3,1},{4,6},{6,4},{5,7},{7,5},{8,10},{10,8},{9,1... | collective-permute-start | bytes 786440 | tf_op jit(solution)/shard_map/ppermute | solution.py:823
  24.2 8.1 %collective-permute-start.1 = (bf16[256,1024]{1,0:T(8,128)(2,1)}, bf16[256,1024]{1,0:T(8,128)(2,1)}, u32[]{:S(2)}, u32[]{:S(2)}) collective-permute-start(bf16[256,1024]{1,0:T(8,128)(2,1)} %param.11), channel_id=1, source_target_pairs={{2,4},{4,2},{3,5},{5,3},{10,12},{12,10},{11,13},{13,11},{18,20},{2... | collective-permute-start | bytes 1572872 | tf_op jit(solution)/shard_map/ppermute | solution.py:831
  32.4 19.2 %collective-permute-start.3 = (bf16[256,1024]{1,0:T(8,128)(2,1)S(1)}, bf16[256,1024]{1,0:T(8,128)(2,1)S(1)}, u32[]{:S(2)}, u32[]{:S(2)}) collective-permute-start(bf16[256,1024]{1,0:T(8,128)(2,1)S(1)} %broadcast_select_fusion.4.refs_0_), channel_id=1, source_target_pairs={{0,1},{1,0},{2,3},{3,2},{4,5},{5,4},{6,7},{7,6},{8,9},{9,8},{10,11... | collective-permute-start | bytes 1572872 | tf_op jit(solution)/shard_map/ppermute | solution.py:823
  37.9 121.9 %all-gather.7.cloned.1.call-start = ((), (), s32[]{:S(2)}) async-start(), calls=%async_computation.3 | async-start | bytes 5242880 | tf_op jit(solution)/shard_map/all_gather | solution.py:894
  38.0 64.5 %collective-permute-start.5 = (bf16[5120,128]{1,0:T(8,128)(2,1)S(1)}, bf16[5120,128]{1,0:T(8,128)(2,1)}, u32[]{:S(2)}, u32[]{:S(2)}) collective-permute-start(bf16[5120,128]{1,0:T(8,128)(2,1)S(1)} %pack.3), channel_id=1, source_target_pairs={{0,2},{2,0},{1,3},{3,1},{4,6},{6,4},{5,7},{7,5},{8,10},{10,8},{9,1... | collective-permute-start | bytes 3932168 | tf_op jit(solution)/shard_map/ppermute | solution.py:823
  44.8 12.5 %collective-permute-start.2 = (bf16[256,1024]{1,0:T(8,128)(2,1)S(1)}, bf16[256,1024]{1,0:T(8,128)(2,1)S(1)}, u32[]{:S(2)}, u32[]{:S(2)}) collective-permute-start(bf16[256,1024]{1,0:T(8,128)(2,1)S(1)} %broadcast_select_fusion.4.refs_0_), channel_id=1, source_target_pairs={{0,4},{4,0},{1,5},{5,1},{2,6},{6,2},{3,7},{7,3},{8,12},{12,8},{9,1... | collective-permute-start | bytes 1572872 | tf_op jit(solution)/shard_map/ppermute | solution.py:823
  51.6 6.4 %collective-permute-start.4 = (bf16[256,1024]{1,0:T(8,128)(2,1)S(1)}, bf16[256,1024]{1,0:T(8,128)(2,1)S(1)}, u32[]{:S(2)}, u32[]{:S(2)}) collective-permute-start(bf16[256,1024]{1,0:T(8,128)(2,1)S(1)} %collective-permute-done.3.refs_2_), channel_id=1, source_target_pairs={{0,4},{4,0},{1,5},{5,1},{2,6},{6,2},{3,7},{7,3},{8,12},{12,8},{9,1... | collective-permute-start | bytes 1572872 | tf_op jit(solution)/shard_map/ppermute | solution.py:823
  65.7 8.5 %collective-permute-start.6 = (f32[1,768]{1,0:T(1,128)S(1)}, f32[1,768]{1,0:T(1,128)S(1)}, u32[]{:S(2)}, u32[]{:S(2)}) collective-permute-start(f32[1,768]{1,0:T(1,128)S(1)} %pad_maximum_fusion.7), channel_id=1, source_target_pairs={{0,1},{1,0},{2,3},{3,2},{4,5},{5,4},{6,7},{7,6},{8,9},{9,8},{10,11... | collective-permute-start | bytes 9224 | tf_op jit(solution)/shard_map/ppermute | solution.py:823
  107.7 96.0 %all-gather.9.cloned.1.call-start = ((), (), s32[]{:S(2)}) async-start(), calls=%async_computation.4 | async-start | bytes 2621440 | tf_op jit(solution)/shard_map/all_gather | solution.py:894
  114.6 16.3 %collective-permute-start.13 = (bf16[256,1024]{1,0:T(8,128)(2,1)}, bf16[256,1024]{1,0:T(8,128)(2,1)}, u32[]{:S(2)}, u32[]{:S(2)}) collective-permute-start(bf16[256,1024]{1,0:T(8,128)(2,1)} %param.12), channel_id=1, source_target_pairs={{2,4},{4,2},{3,5},{5,3},{10,12},{12,10},{11,13},{13,11},{18,20},{2... | collective-permute-start | bytes 1572872 | tf_op jit(solution)/shard_map/ppermute | solution.py:831
  133.2 15.0 %collective-permute-start.15 = (bf16[256,1024]{1,0:T(8,128)(2,1)S(1)}, bf16[256,1024]{1,0:T(8,128)(2,1)S(1)}, u32[]{:S(2)}, u32[]{:S(2)}) collective-permute-start(bf16[256,1024]{1,0:T(8,128)(2,1)S(1)} %add_convert_fusion.8), channel_id=1, source_target_pairs={{0,1},{1,0},{2,3},{3,2},{4,5},{5,4},{6,7},{7,6},{8,9},{9,8},{10,11... | collective-permute-start | bytes 1572872 | tf_op jit(solution)/shard_map/ppermute | solution.py:823
  152.7 10.5 %collective-permute-start.17 = (bf16[256,1024]{1,0:T(8,128)(2,1)}, bf16[256,1024]{1,0:T(8,128)(2,1)}, u32[]{:S(2)}, u32[]{:S(2)}) collective-permute-start(bf16[256,1024]{1,0:T(8,128)(2,1)} %get-tuple-element.252.refs_0_), channel_id=1, source_target_pairs={{0,4},{4,0},{1,5},{5,1},{2,6},{6,2},{3,7},{7,3},{8,12},{12,8},{9,1... | collective-permute-start | bytes 1572872 | tf_op jit(solution)/shard_map/ppermute | solution.py:823
  153.1 19.4 %collective-permute-start.18 = (bf16[256,1024]{1,0:T(8,128)(2,1)}, bf16[256,1024]{1,0:T(8,128)(2,1)S(1)}, u32[]{:S(2)}, u32[]{:S(2)}) collective-permute-start(bf16[256,1024]{1,0:T(8,128)(2,1)} %get-tuple-element.252.refs_0_), channel_id=1, source_target_pairs={{0,1},{1,0},{2,3},{3,2},{4,5},{5,4},{6,7},{7,6},{8,9},{9,8},{10,11... | collective-permute-start | bytes 1572872 | tf_op jit(solution)/shard_map/ppermute | solution.py:823
  155.7 95.8 %all-gather.11.cloned.1.call-start = ((), (), s32[]{:S(2)}) async-start(), calls=%async_computation.5 | async-start | bytes 5242880 | tf_op jit(solution)/shard_map/all_gather | solution.py:894
  186.0 213.1 %reduce-scatter.3.cloned.1.call-start = ((), (), s32[]{:S(2)}) async-start(), calls=%async_computation.6 | async-start | bytes 5242880 | tf_op jit(solution)/shard_map/reduce_scatter | solution.py:911
  186.2 14.2 %collective-permute-start.22 = (bf16[256,1024]{1,0:T(8,128)(2,1)S(1)}, bf16[256,1024]{1,0:T(8,128)(2,1)S(1)}, u32[]{:S(2)}, u32[]{:S(2)}) collective-permute-start(bf16[256,1024]{1,0:T(8,128)(2,1)S(1)} %copy-done.120), channel_id=1, source_target_pairs={{0,1},{1,0},{2,3},{3,2},{4,5},{5,4},{6,7},{7,6},{8,9},{9,8},{10,11... | collective-permute-start | bytes 1572872 | tf_op jit(solution)/shard_map/ppermute | solution.py:823
  202.2 14.5 %collective-permute-start.25 = (bf16[256,1024]{1,0:T(8,128)(2,1)}, bf16[256,1024]{1,0:T(8,128)(2,1)S(1)}, u32[]{:S(2)}, u32[]{:S(2)}) collective-permute-start(bf16[256,1024]{1,0:T(8,128)(2,1)} %get-tuple-element.263.refs_0_), channel_id=1, source_target_pairs={{0,1},{1,0},{2,3},{3,2},{4,5},{5,4},{6,7},{7,6},{8,9},{9,8},{10,11... | collective-permute-start | bytes 1572872 | tf_op jit(solution)/shard_map/ppermute | solution.py:823
  228.2 14.0 %collective-permute-start.28 = (bf16[256,1024]{1,0:T(8,128)(2,1)S(1)}, bf16[256,1024]{1,0:T(8,128)(2,1)S(1)}, u32[]{:S(2)}, u32[]{:S(2)}) collective-permute-start(bf16[256,1024]{1,0:T(8,128)(2,1)S(1)} %add_convert_fusion.6), channel_id=1, source_target_pairs={{0,1},{1,0},{2,3},{3,2},{4,5},{5,4},{6,7},{7,6},{8,9},{9,8},{10,11... | collective-permute-start | bytes 1572872 | tf_op jit(solution)/shard_map/ppermute | solution.py:823
  245.9 9.0 %collective-permute-start.30 = (bf16[256,1024]{1,0:T(8,128)(2,1)}, bf16[256,1024]{1,0:T(8,128)(2,1)S(1)}, u32[]{:S(2)}, u32[]{:S(2)}) collective-permute-start(bf16[256,1024]{1,0:T(8,128)(2,1)} %get-tuple-element.278.refs_0_), channel_id=1, source_target_pairs={{0,4},{4,0},{1,5},{5,1},{2,6},{6,2},{3,7},{7,3},{8,12},{12,8},{9,1... | collective-permute-start | bytes 1572872 | tf_op jit(solution)/shard_map/ppermute | solution.py:823
  246.0 15.9 %collective-permute-start.32 = (bf16[256,1024]{1,0:T(8,128)(2,1)}, bf16[256,1024]{1,0:T(8,128)(2,1)S(1)}, u32[]{:S(2)}, u32[]{:S(2)}) collective-permute-start(bf16[256,1024]{1,0:T(8,128)(2,1)} %get-tuple-element.278.refs_0_), channel_id=1, source_target_pairs={{0,1},{1,0},{2,3},{3,2},{4,5},{5,4},{6,7},{7,6},{8,9},{9,8},{10,11... | collective-permute-start | bytes 1572872 | tf_op jit(solution)/shard_map/ppermute | solution.py:823
  261.9 14.4 %collective-permute-start.38 = (bf16[256,1024]{1,0:T(8,128)(2,1)S(1)}, bf16[256,1024]{1,0:T(8,128)(2,1)S(1)}, u32[]{:S(2)}, u32[]{:S(2)}) collective-permute-start(bf16[256,1024]{1,0:T(8,128)(2,1)S(1)} %broadcast_select_fusion.3), channel_id=1, source_target_pairs={{0,1},{1,0},{2,3},{3,2},{4,5},{5,4},{6,7},{7,6},{8,9},{9,8},{10,11... | collective-permute-start | bytes 1572872 | tf_op jit(solution)/shard_map/ppermute | solution.py:823
  269.2 7.6 %collective-permute-start.35 = (bf16[256,1024]{1,0:T(8,128)(2,1)S(1)}, bf16[256,1024]{1,0:T(8,128)(2,1)S(1)}, u32[]{:S(2)}, u32[]{:S(2)}) collective-permute-start(bf16[256,1024]{1,0:T(8,128)(2,1)S(1)} %get-tuple-element.288), channel_id=1, source_target_pairs={{0,4},{4,0},{1,5},{5,1},{2,6},{6,2},{3,7},{7,3},{8,12},{12,8},{9,1... | collective-permute-start | bytes 1572872 | tf_op jit(solution)/shard_map/ppermute | solution.py:823
  270.1 10.4 %collective-permute-start.37 = (bf16[256,1024]{1,0:T(8,128)(2,1)S(1)}, bf16[256,1024]{1,0:T(8,128)(2,1)S(1)}, u32[]{:S(2)}, u32[]{:S(2)}) collective-permute-start(bf16[256,1024]{1,0:T(8,128)(2,1)S(1)} %broadcast_select_fusion.3), channel_id=1, source_target_pairs={{0,4},{4,0},{1,5},{5,1},{2,6},{6,2},{3,7},{7,3},{8,12},{12,8},{9,1... | collective-permute-start | bytes 1572872 | tf_op jit(solution)/shard_map/ppermute | solution.py:823
  277.0 14.2 %collective-permute-start.36 = (bf16[256,1024]{1,0:T(8,128)(2,1)S(1)}, bf16[256,1024]{1,0:T(8,128)(2,1)S(1)}, u32[]{:S(2)}, u32[]{:S(2)}) collective-permute-start(bf16[256,1024]{1,0:T(8,128)(2,1)S(1)} %add_convert_fusion.5), channel_id=1, source_target_pairs={{0,1},{1,0},{2,3},{3,2},{4,5},{5,4},{6,7},{7,6},{8,9},{9,8},{10,11... | collective-permute-start | bytes 1572872 | tf_op jit(solution)/shard_map/ppermute | solution.py:823
  295.2 14.3 %collective-permute-start.41 = (bf16[256,1024]{1,0:T(8,128)(2,1)S(1)}, bf16[256,1024]{1,0:T(8,128)(2,1)S(1)}, u32[]{:S(2)}, u32[]{:S(2)}) collective-permute-start(bf16[256,1024]{1,0:T(8,128)(2,1)S(1)} %get-tuple-element.295.refs_0_), channel_id=1, source_target_pairs={{0,1},{1,0},{2,3},{3,2},{4,5},{5,4},{6,7},{7,6},{8,9},{9,8},{10,11... | collective-permute-start | bytes 1572872 | tf_op jit(solution)/shard_map/ppermute | solution.py:823
  316.7 13.9 %collective-permute-start.44 = (bf16[256,1024]{1,0:T(8,128)(2,1)}, bf16[256,1024]{1,0:T(8,128)(2,1)S(1)}, u32[]{:S(2)}, u32[]{:S(2)}) collective-permute-start(bf16[256,1024]{1,0:T(8,128)(2,1)} %get-tuple-element.312), channel_id=1, source_target_pairs={{0,4},{4,0},{1,5},{5,1},{2,6},{6,2},{3,7},{7,3},{8,12},{12,8},{9,1... | collective-permute-start | bytes 1572872 | tf_op jit(solution)/shard_map/ppermute | solution.py:823
  319.4 14.2 %collective-permute-start.45 = (bf16[256,1024]{1,0:T(8,128)(2,1)}, bf16[256,1024]{1,0:T(8,128)(2,1)S(1)}, u32[]{:S(2)}, u32[]{:S(2)}) collective-permute-start(bf16[256,1024]{1,0:T(8,128)(2,1)} %add_convert_fusion.4), channel_id=1, source_target_pairs={{0,1},{1,0},{2,3},{3,2},{4,5},{5,4},{6,7},{7,6},{8,9},{9,8},{10,11... | collective-permute-start | bytes 1572872 | tf_op jit(solution)/shard_map/ppermute | solution.py:823
  340.3 102.8 %reduce-scatter.5.cloned.1.call-start = ((), (), s32[]{:S(2)}) async-start(), calls=%async_computation.7 | async-start | bytes 2621440 | tf_op jit(solution)/shard_map/reduce_scatter | solution.py:911
  341.3 14.3 %collective-permute-start.48 = (bf16[256,1024]{1,0:T(8,128)(2,1)S(1)}, bf16[256,1024]{1,0:T(8,128)(2,1)S(1)}, u32[]{:S(2)}, u32[]{:S(2)}) collective-permute-start(bf16[256,1024]{1,0:T(8,128)(2,1)S(1)} %copy-done.74), channel_id=1, source_target_pairs={{0,1},{1,0},{2,3},{3,2},{4,5},{5,4},{6,7},{7,6},{8,9},{9,8},{10,11... | collective-permute-start | bytes 1572872 | tf_op jit(solution)/shard_map/ppermute | solution.py:823
  355.6 10.5 %collective-permute-start.47 = (bf16[256,1024]{1,0:T(8,128)(2,1)S(1)}, bf16[256,1024]{1,0:T(8,128)(2,1)S(1)}, u32[]{:S(2)}, u32[]{:S(2)}) collective-permute-start(bf16[256,1024]{1,0:T(8,128)(2,1)S(1)} %copy-done.26), channel_id=1, source_target_pairs={{2,4},{4,2},{3,5},{5,3},{10,12},{12,10},{11,13},{13,11},{18,20},{2... | collective-permute-start | bytes 1572872 | tf_op jit(solution)/shard_map/ppermute | solution.py:831
  367.2 8.6 %collective-permute-start.50 = (bf16[256,1024]{1,0:T(8,128)(2,1)S(1)}, bf16[256,1024]{1,0:T(8,128)(2,1)S(1)}, u32[]{:S(2)}, u32[]{:S(2)}) collective-permute-start(bf16[256,1024]{1,0:T(8,128)(2,1)S(1)} %get-tuple-element.332), channel_id=1, source_target_pairs={{0,4},{4,0},{1,5},{5,1},{2,6},{6,2},{3,7},{7,3},{8,12},{12,8},{9,1... | collective-permute-start | bytes 1572872 | tf_op jit(solution)/shard_map/ppermute | solution.py:823
  378.4 14.0 %collective-permute-start.52 = (bf16[256,1024]{1,0:T(8,128)(2,1)S(1)}, bf16[256,1024]{1,0:T(8,128)(2,1)S(1)}, u32[]{:S(2)}, u32[]{:S(2)}) collective-permute-start(bf16[256,1024]{1,0:T(8,128)(2,1)S(1)} %add_convert_fusion.3), channel_id=1, source_target_pairs={{0,1},{1,0},{2,3},{3,2},{4,5},{5,4},{6,7},{7,6},{8,9},{9,8},{10,11... | collective-permute-start | bytes 1572872 | tf_op jit(solution)/shard_map/ppermute | solution.py:823
  398.7 14.7 %collective-permute-start.54 = (bf16[256,1024]{1,0:T(8,128)(2,1)}, bf16[256,1024]{1,0:T(8,128)(2,1)}, u32[]{:S(2)}, u32[]{:S(2)}) collective-permute-start(bf16[256,1024]{1,0:T(8,128)(2,1)} %get-tuple-element.346.refs_0_), channel_id=1, source_target_pairs={{0,1},{1,0},{2,3},{3,2},{4,5},{5,4},{6,7},{7,6},{8,9},{9,8},{10,11... | collective-permute-start | bytes 1572872 | tf_op jit(solution)/shard_map/ppermute | solution.py:823
  401.2 12.2 %collective-permute-start.56 = (bf16[2048,128]{1,0:T(8,128)(2,1)S(1)}, bf16[2048,128]{1,0:T(8,128)(2,1)S(1)}, u32[]{:S(2)}, u32[]{:S(2)}) collective-permute-start(bf16[2048,128]{1,0:T(8,128)(2,1)S(1)} %get-tuple-element.359), channel_id=1, source_target_pairs={{0,4},{4,0},{1,5},{5,1},{2,6},{6,2},{3,7},{7,3},{8,12},{12,8},{9,1... | collective-permute-start | bytes 1572872 | tf_op jit(solution)/shard_map/ppermute | solution.py:823
  414.3 15.2 %collective-permute-start.57 = (bf16[1024,128]{1,0:T(8,128)(2,1)S(1)}, bf16[1024,128]{1,0:T(8,128)(2,1)S(1)}, u32[]{:S(2)}, u32[]{:S(2)}) collective-permute-start(bf16[1024,128]{1,0:T(8,128)(2,1)S(1)} %get-tuple-element.360), channel_id=1, source_target_pairs={{0,2},{2,0},{1,3},{3,1},{4,6},{6,4},{5,7},{7,5},{8,10},{10,8},{9,1... | collective-permute-start | bytes 786440 | tf_op jit(solution)/shard_map/ppermute | solution.py:823
  416.6 36.7 %collective-permute-start.60 = (bf16[256,1024]{1,0:T(8,128)(2,1)}, bf16[256,1024]{1,0:T(8,128)(2,1)S(1)}, u32[]{:S(2)}, u32[]{:S(2)}) collective-permute-start(bf16[256,1024]{1,0:T(8,128)(2,1)} %get-tuple-element.370), channel_id=1, source_target_pairs={{0,4},{4,0},{1,5},{5,1},{2,6},{6,2},{3,7},{7,3},{8,12},{12,8},{9,1... | collective-permute-start | bytes 1572872 | tf_op jit(solution)/shard_map/ppermute | solution.py:823
  431.6 22.4 %collective-permute-start.61 = (bf16[256,1024]{1,0:T(8,128)(2,1)S(1)}, bf16[256,1024]{1,0:T(8,128)(2,1)S(1)}, u32[]{:S(2)}, u32[]{:S(2)}) collective-permute-start(bf16[256,1024]{1,0:T(8,128)(2,1)S(1)} %add_convert_fusion.2), channel_id=1, source_target_pairs={{0,1},{1,0},{2,3},{3,2},{4,5},{5,4},{6,7},{7,6},{8,9},{9,8},{10,11... | collective-permute-start | bytes 1572872 | tf_op jit(solution)/shard_map/ppermute | solution.py:823
  431.7 19.1 %collective-permute-start.59 = (bf16[1024,128]{1,0:T(8,128)(2,1)}, bf16[1024,128]{1,0:T(8,128)(2,1)}, u32[]{:S(2)}, u32[]{:S(2)}) collective-permute-start(bf16[1024,128]{1,0:T(8,128)(2,1)} %get-tuple-element.366), channel_id=1, source_target_pairs={{0,2},{2,0},{1,3},{3,1},{4,6},{6,4},{5,7},{7,5},{8,10},{10,8},{9,1... | collective-permute-start | bytes 786440 | tf_op jit(solution)/shard_map/ppermute | solution.py:823
  441.6 17.1 %collective-permute-start.65 = (bf16[2,1024,128]{2,1,0:T(8,128)(2,1)}, bf16[2,1024,128]{2,1,0:T(8,128)(2,1)}, u32[]{:S(2)}, u32[]{:S(2)}) collective-permute-start(bf16[2,1024,128]{2,1,0:T(8,128)(2,1)} %get-tuple-element.363), channel_id=1, source_target_pairs={{0,16},{8,24},{16,0},{24,8},{1,17},{9,25},{17,1},{25,9},{2,18},{10... | collective-permute-start | bytes 1572872 | tf_op jit(solution)/shard_map/ppermute | solution.py:827
  444.8 15.1 %collective-permute-start.66 = (bf16[2,1024,128]{2,1,0:T(8,128)(2,1)}, bf16[2,1024,128]{2,1,0:T(8,128)(2,1)S(1)}, u32[]{:S(2)}, u32[]{:S(2)}) collective-permute-start(bf16[2,1024,128]{2,1,0:T(8,128)(2,1)} %get-tuple-element.377), channel_id=1, source_target_pairs={{0,8},{8,0},{16,24},{24,16},{1,9},{9,1},{17,25},{25,17},{2,10},{10... | collective-permute-start | bytes 1572872 | tf_op jit(solution)/shard_map/ppermute | solution.py:827
  450.8 15.7 %collective-permute-start.67 = (bf16[2,1024,128]{2,1,0:T(8,128)(2,1)S(1)}, bf16[2,1024,128]{2,1,0:T(8,128)(2,1)S(1)}, u32[]{:S(2)}, u32[]{:S(2)}) collective-permute-start(bf16[2,1024,128]{2,1,0:T(8,128)(2,1)S(1)} %get-tuple-element.365), channel_id=1, source_target_pairs={{0,16},{8,24},{16,0},{24,8},{1,17},{9,25},{17,1},{25,9},{2,18},{10... | collective-permute-start | bytes 1572872 | tf_op jit(solution)/shard_map/ppermute | solution.py:827
  453.3 16.1 %collective-permute-start.68 = (bf16[2,1024,128]{2,1,0:T(8,128)(2,1)S(1)}, bf16[2,1024,128]{2,1,0:T(8,128)(2,1)S(1)}, u32[]{:S(2)}, u32[]{:S(2)}) collective-permute-start(bf16[2,1024,128]{2,1,0:T(8,128)(2,1)S(1)} %get-tuple-element.378), channel_id=1, source_target_pairs={{0,8},{8,0},{16,24},{24,16},{1,9},{9,1},{17,25},{25,17},{2,10},{10... | collective-permute-start | bytes 1572872 | tf_op jit(solution)/shard_map/ppermute | solution.py:827
  456.7 21.2 %collective-permute-start.62 = (bf16[256,1024]{1,0:T(8,128)(2,1)S(1)}, bf16[256,1024]{1,0:T(8,128)(2,1)S(1)}, u32[]{:S(2)}, u32[]{:S(2)}) collective-permute-start(bf16[256,1024]{1,0:T(8,128)(2,1)S(1)} %get-tuple-element.373.refs_8_), channel_id=1, source_target_pairs={{0,1},{1,0},{2,3},{3,2},{4,5},{5,4},{6,7},{7,6},{8,9},{9,8},{10,11... | collective-permute-start | bytes 1572872 | tf_op jit(solution)/shard_map/ppermute | solution.py:823
  458.7 10.8 %collective-permute-start.63 = (bf16[256,1024]{1,0:T(8,128)(2,1)S(1)}, bf16[256,1024]{1,0:T(8,128)(2,1)S(1)}, u32[]{:S(2)}, u32[]{:S(2)}) collective-permute-start(bf16[256,1024]{1,0:T(8,128)(2,1)S(1)} %get-tuple-element.373.refs_8_), channel_id=1, source_target_pairs={{0,4},{4,0},{1,5},{5,1},{2,6},{6,2},{3,7},{7,3},{8,12},{12,8},{9,1... | collective-permute-start | bytes 1572872 | tf_op jit(solution)/shard_map/ppermute | solution.py:823
  478.0 14.8 %collective-permute-start.69 = (bf16[1,1024,128]{2,1,0:T(8,128)(2,1)S(1)}, bf16[1,1024,128]{2,1,0:T(8,128)(2,1)S(1)}, u32[]{:S(2)}, u32[]{:S(2)}) collective-permute-start(bf16[1,1024,128]{2,1,0:T(8,128)(2,1)S(1)} %add_convert_fusion.17), channel_id=1, source_target_pairs={{0,8},{8,0},{16,24},{24,16},{1,9},{9,1},{17,25},{25,17},{2,10},{10... | collective-permute-start | bytes 786440 | tf_op jit(solution)/shard_map/ppermute | solution.py:827
  478.7 14.2 %collective-permute-start.70 = (bf16[1,1024,128]{2,1,0:T(8,128)(2,1)S(1)}, bf16[1,1024,128]{2,1,0:T(8,128)(2,1)S(1)}, u32[]{:S(2)}, u32[]{:S(2)}) collective-permute-start(bf16[1,1024,128]{2,1,0:T(8,128)(2,1)S(1)} %add_convert_fusion.16), channel_id=1, source_target_pairs={{0,16},{8,24},{16,0},{24,8},{1,17},{9,25},{17,1},{25,9},{2,18},{10... | collective-permute-start | bytes 786440 | tf_op jit(solution)/shard_map/ppermute | solution.py:827
  480.1 12.8 %collective-permute-start.71 = (bf16[1,1024,128]{2,1,0:T(8,128)(2,1)S(1)}, bf16[1,1024,128]{2,1,0:T(8,128)(2,1)S(1)}, u32[]{:S(2)}, u32[]{:S(2)}) collective-permute-start(bf16[1,1024,128]{2,1,0:T(8,128)(2,1)S(1)} %add_convert_fusion.15), channel_id=1, source_target_pairs={{0,8},{8,0},{16,24},{24,16},{1,9},{9,1},{17,25},{25,17},{2,10},{10... | collective-permute-start | bytes 786440 | tf_op jit(solution)/shard_map/ppermute | solution.py:827
  482.2 10.7 %collective-permute-start.72 = (bf16[1,1024,128]{2,1,0:T(8,128)(2,1)S(1)}, bf16[1,1024,128]{2,1,0:T(8,128)(2,1)S(1)}, u32[]{:S(2)}, u32[]{:S(2)}) collective-permute-start(bf16[1,1024,128]{2,1,0:T(8,128)(2,1)S(1)} %add_convert_fusion.14), channel_id=1, source_target_pairs={{0,16},{8,24},{16,0},{24,8},{1,17},{9,25},{17,1},{25,9},{2,18},{10... | collective-permute-start | bytes 786440 | tf_op jit(solution)/shard_map/ppermute | solution.py:827
  483.7 14.5 %collective-permute-start.74 = (bf16[1024,128]{1,0:T(8,128)(2,1)S(1)}, bf16[1024,128]{1,0:T(8,128)(2,1)S(1)}, u32[]{:S(2)}, u32[]{:S(2)}) collective-permute-start(bf16[1024,128]{1,0:T(8,128)(2,1)S(1)} %broadcast_select_fusion.5), channel_id=1, source_target_pairs={{0,2},{2,0},{1,3},{3,1},{4,6},{6,4},{5,7},{7,5},{8,10},{10,8},{9,1... | collective-permute-start | bytes 786440 | tf_op jit(solution)/shard_map/ppermute | solution.py:823
  501.0 11.4 %collective-permute-start.78 = (bf16[1024,128]{1,0:T(8,128)(2,1)}, bf16[1024,128]{1,0:T(8,128)(2,1)S(1)}, u32[]{:S(2)}, u32[]{:S(2)}) collective-permute-start(bf16[1024,128]{1,0:T(8,128)(2,1)} %fusion.12), channel_id=1, source_target_pairs={{0,4},{4,0},{1,5},{5,1},{2,6},{6,2},{3,7},{7,3},{8,12},{12,8},{9,1... | collective-permute-start | bytes 786440 | tf_op jit(solution)/shard_map/ppermute | solution.py:823
  501.6 28.4 %collective-permute-start.85 = (bf16[1024,128]{1,0:T(8,128)(2,1)}, bf16[1024,128]{1,0:T(8,128)(2,1)}, u32[]{:S(2)}, u32[]{:S(2)}) collective-permute-start(bf16[1024,128]{1,0:T(8,128)(2,1)} %fusion.14), channel_id=1, source_target_pairs={{0,4},{4,0},{1,5},{5,1},{2,6},{6,2},{3,7},{7,3},{8,12},{12,8},{9,1... | collective-permute-start | bytes 786440 | tf_op jit(solution)/shard_map/ppermute | solution.py:823
  509.6 14.6 %collective-permute-start.76 = (bf16[2,1024,128]{2,1,0:T(8,128)(2,1)}, bf16[2,1024,128]{2,1,0:T(8,128)(2,1)}, u32[]{:S(2)}, u32[]{:S(2)}) collective-permute-start(bf16[2,1024,128]{2,1,0:T(8,128)(2,1)} %get-tuple-element.407), channel_id=1, source_target_pairs={{0,16},{8,24},{16,0},{24,8},{1,17},{9,25},{17,1},{25,9},{2,18},{10... | collective-permute-start | bytes 1572872 | tf_op jit(solution)/shard_map/ppermute | solution.py:827
  510.8 14.4 %collective-permute-start.77 = (bf16[2,1024,128]{2,1,0:T(8,128)(2,1)}, bf16[2,1024,128]{2,1,0:T(8,128)(2,1)S(1)}, u32[]{:S(2)}, u32[]{:S(2)}) collective-permute-start(bf16[2,1024,128]{2,1,0:T(8,128)(2,1)} %get-tuple-element.409), channel_id=1, source_target_pairs={{0,8},{8,0},{16,24},{24,16},{1,9},{9,1},{17,25},{25,17},{2,10},{10... | collective-permute-start | bytes 1572872 | tf_op jit(solution)/shard_map/ppermute | solution.py:827
  514.4 13.5 %collective-permute-start.79 = (bf16[1024,128]{1,0:T(8,128)(2,1)S(1)}, bf16[1024,128]{1,0:T(8,128)(2,1)S(1)}, u32[]{:S(2)}, u32[]{:S(2)}) collective-permute-start(bf16[1024,128]{1,0:T(8,128)(2,1)S(1)} %get-tuple-element.461), channel_id=1, source_target_pairs={{0,2},{2,0},{1,3},{3,1},{4,6},{6,4},{5,7},{7,5},{8,10},{10,8},{9,1... | collective-permute-start | bytes 786440 | tf_op jit(solution)/shard_map/ppermute | solution.py:823
  514.4 22.3 %collective-permute-start.83 = (bf16[256,1024]{1,0:T(8,128)(2,1)}, bf16[256,1024]{1,0:T(8,128)(2,1)}, u32[]{:S(2)}, u32[]{:S(2)}) collective-permute-start(bf16[256,1024]{1,0:T(8,128)(2,1)} %add_convert_fusion.1), channel_id=1, source_target_pairs={{0,1},{1,0},{2,3},{3,2},{4,5},{5,4},{6,7},{7,6},{8,9},{9,8},{10,11... | collective-permute-start | bytes 1572872 | tf_op jit(solution)/shard_map/ppermute | solution.py:823
  524.3 12.5 %collective-permute-start.82 = (bf16[256,1024]{1,0:T(8,128)(2,1)}, bf16[256,1024]{1,0:T(8,128)(2,1)}, u32[]{:S(2)}, u32[]{:S(2)}) collective-permute-start(bf16[256,1024]{1,0:T(8,128)(2,1)} %get-tuple-element.417), channel_id=1, source_target_pairs={{0,4},{4,0},{1,5},{5,1},{2,6},{6,2},{3,7},{7,3},{8,12},{12,8},{9,1... | collective-permute-start | bytes 1572872 | tf_op jit(solution)/shard_map/ppermute | solution.py:823
  527.9 8.3 %collective-permute-start.80 = (bf16[1,1024,128]{2,1,0:T(8,128)(2,1)S(1)}, bf16[1,1024,128]{2,1,0:T(8,128)(2,1)}, u32[]{:S(2)}, u32[]{:S(2)}) collective-permute-start(bf16[1,1024,128]{2,1,0:T(8,128)(2,1)S(1)} %add_convert_fusion.13), channel_id=1, source_target_pairs={{0,8},{8,0},{16,24},{24,16},{1,9},{9,1},{17,25},{25,17},{2,10},{10... | collective-permute-start | bytes 786440 | tf_op jit(solution)/shard_map/ppermute | solution.py:827
  528.4 8.0 %collective-permute-start.81 = (bf16[1,1024,128]{2,1,0:T(8,128)(2,1)S(1)}, bf16[1,1024,128]{2,1,0:T(8,128)(2,1)}, u32[]{:S(2)}, u32[]{:S(2)}) collective-permute-start(bf16[1,1024,128]{2,1,0:T(8,128)(2,1)S(1)} %add_convert_fusion.12), channel_id=1, source_target_pairs={{0,16},{8,24},{16,0},{24,8},{1,17},{9,25},{17,1},{25,9},{2,18},{10... | collective-permute-start | bytes 786440 | tf_op jit(solution)/shard_map/ppermute | solution.py:827
  531.9 16.5 %collective-permute-start.86 = (bf16[1024,128]{1,0:T(8,128)(2,1)}, bf16[1024,128]{1,0:T(8,128)(2,1)}, u32[]{:S(2)}, u32[]{:S(2)}) collective-permute-start(bf16[1024,128]{1,0:T(8,128)(2,1)} %get-tuple-element.420), channel_id=1, source_target_pairs={{0,2},{2,0},{1,3},{3,1},{4,6},{6,4},{5,7},{7,5},{8,10},{10,8},{9,1... | collective-permute-start | bytes 786440 | tf_op jit(solution)/shard_map/ppermute | solution.py:823
  539.3 6.6 %collective-permute-start.90 = (f32[4,2,768]{2,1,0:T(2,128)S(1)}, f32[4,2,768]{2,1,0:T(2,128)S(1)}, u32[]{:S(2)}, u32[]{:S(2)}) collective-permute-start(f32[4,2,768]{2,1,0:T(2,128)S(1)} %bitcast.114), channel_id=1, source_target_pairs={{0,1},{1,0},{2,3},{3,2},{4,5},{5,4},{6,7},{7,6},{8,9},{9,8},{10,11... | collective-permute-start | bytes 73736 | tf_op jit(solution)/shard_map/ppermute | solution.py:823
  540.2 24.5 %collective-permute-start.84 = (bf16[256,1024]{1,0:T(8,128)(2,1)}, bf16[256,1024]{1,0:T(8,128)(2,1)}, u32[]{:S(2)}, u32[]{:S(2)}) collective-permute-start(bf16[256,1024]{1,0:T(8,128)(2,1)} %add_convert_fusion), channel_id=1, source_target_pairs={{2,4},{4,2},{3,5},{5,3},{10,12},{12,10},{11,13},{13,11},{18,20},{2... | collective-permute-start | bytes 1572872 | tf_op jit(solution)/shard_map/ppermute | solution.py:831
  548.4 13.0 %collective-permute-start.87 = (bf16[1024,128]{1,0:T(8,128)(2,1)}, bf16[1024,128]{1,0:T(8,128)(2,1)S(1)}, u32[]{:S(2)}, u32[]{:S(2)}) collective-permute-start(bf16[1024,128]{1,0:T(8,128)(2,1)} %fusion.13), channel_id=1, source_target_pairs={{0,4},{4,0},{1,5},{5,1},{2,6},{6,2},{3,7},{7,3},{8,12},{12,8},{9,1... | collective-permute-start | bytes 786440 | tf_op jit(solution)/shard_map/ppermute | solution.py:823
  562.6 11.3 %collective-permute-start.88 = (bf16[1024,128]{1,0:T(8,128)(2,1)S(1)}, bf16[1024,128]{1,0:T(8,128)(2,1)S(1)}, u32[]{:S(2)}, u32[]{:S(2)}) collective-permute-start(bf16[1024,128]{1,0:T(8,128)(2,1)S(1)} %fusion.15), channel_id=1, source_target_pairs={{0,2},{2,0},{1,3},{3,1},{4,6},{6,4},{5,7},{7,5},{8,10},{10,8},{9,1... | collective-permute-start | bytes 786440 | tf_op jit(solution)/shard_map/ppermute | solution.py:823
  (174 other events, 1110.2 us)
Sparse Core Ops, SparseCore 0:
  38.0 39.7 all-gather.4
  107.8 52.0 all-gather.6
  161.7 35.3 all-gather.8
  198.8 52.7 all-gather.10
  340.4 52.3 reduce-scatter.2
  395.9 35.1 reduce-scatter.4

commit v5 on v4

--- a/solution.py
+++ b/solution.py
@@ -1000,14 +1000,15 @@
     tile_a0 = pack((("qkv", 0), ("out", 0)), args)
     a0_crossed = swap(tile_a0, "zh")
     g_a0 = Gather(("qkv", "out"), tile_a0, a0_crossed, widths, pos, where, n_d)
-    rest = [("up", 0), ("down", 0), ("qkv", 1), ("out", 1), ("up", 1), ("down", 1)]
+    rest = [("up", 0), ("down", 0), ("qkv", 1), ("out", 1)]
+    tile_f1 = pack((("up", 1), ("down", 1)), args)
     tile_rest = pack(rest, args)
     small_own = jnp.concatenate([a.reshape(1, -1) for a in (gains, biases, up_bias)], 1)
     src, seg_col, seg_row = maps(
         lengths, order, jnp.stack([d * 2 + zh, slot]).astype(jnp.int32), 4 * rows
     )
     seg_near, seg_far = seg_col[: 2 * rows], seg_col[2 * rows :]
-    g_a0.cores(src, small_own, tile_rest)
+    g_a0.cores(src, small_own, tile_rest, tile_f1)
     g_a0.collect()
     raw_got = to_home(after(tokens, a0_crossed))
     raw = jnp.where(stay, tokens, raw_got)
@@ -1020,7 +1021,7 @@
         part = slice(at, at + lines)
         gathers.append(Gather(fields, tile_rest[part], rest_crossed[part], widths, pos, where, n_d))
         at += lines
-    g_f0, g_a1, g_f1 = gathers
+    g_f0, g_a1 = gathers
     x_near, x_far, hidden = deal_rows(src, [*raw_near, *far_rows(raw_far)])
     small_near = gather_small(after(small_own, x_near[0]), pos, n_d)
     small_far = swap(small_near, "zh")
@@ -1041,6 +1042,8 @@
     g_f0.collect()
     cot_got = to_home(after(cotangent, f0_other, small_far))
     cot_near, cot_sent = send_rows(jnp.where(stay, cotangent, cot_got))
+    f1_crossed = swap(after(tile_f1, cot_got), "zh")
+    g_f1 = Gather(("up", "down"), tile_f1, f1_crossed, widths, pos, where, n_d)
     weights = [g_a0.weights(), {}]
 
     kept = []
@@ -1074,6 +1077,8 @@
             after(proj_near, chip), proj, seg_near, seg_row, w["out"], scale, heads
         )
         terms = chip_sum(mine, theirs, crossed)
+        if first:
+            terms = (terms[0], after(terms[1], f1_crossed))
         terms = (*terms, crossed)
         at = [bias_row(layer, 2), gain_row(layer, 0), bias_row(layer, 3)]
         normed, low, n_one, r_one = norm((hidden, *terms), vectors, *at)

time: 588 us -> 580 us (0.986)
    ppermute x74 -> x75, waiting for transfers between devices: 177 us -> 187 us  [swap(): return lax.ppermute(a, axis, SWAP)]
    all_gather x4, waiting for transfers between devices: 7.75 us -> 0.89 us  [collect(): self.stacks = [lax.all_gather(both, 'd', axis=0, tiled=True)]]
    ppermute x74 -> x75, starting transfers between devices: 66.4 us -> 60.3 us  [swap(): return lax.ppermute(a, axis, SWAP)]
  transfers between devices with their start and end apart: 100 -> 101, of which waited for: 56 -> 57; matrix products, arithmetic and copies ran while one was open for 8% -> 8% of each run, Pallas kernels for 29% -> 30%
where the time goes in v5:
time: 580 us; the launch traced here: 574 us
  waiting for transfers between devices  208 us (36%)
  Pallas kernels  182 us (31%)
  starting transfers between devices  84.9 us (15%)
  local copies, waits for them, and re-layouts  51.4 us (9%)
  other arithmetic  30.3 us (5%)
  between operations  16.2 us (3%)
    ppermute x75, waiting for transfers between devices, swap(): return lax.ppermute(a, axis, SWAP)  187 us
    ppermute x75, starting transfers between devices, swap(): return lax.ppermute(a, axis, SWAP)  60.3 us
    unnamed x279, local copies, waits for them, and re-layouts  39 us
    pallas_call x5, Pallas kernels, weight_grad(): pl.pallas_call(functools.partial(grad_kernel, fields, counts, specs), gri...  33.8 us
    pallas_call x4, Pallas kernels, attend_back(): pl.pallas_call(functools.partial(attend_back_kernel, scale, heads, last),...  33.5 us
    pallas_call x4, Pallas kernels, ffn(): pl.pallas_call(ffn_kernel, grid=(ff // tile,), in_specs=[*blocks_in(x), p...  24.4 us
    pallas_call x4, Pallas kernels, ffn_back(): pl.pallas_call(ffn_back_kernel, grid=(ff // tile,), in_specs=[*blocks_in(...  20 us
    ppermute x16, waiting for transfers between devices, flip_d(): return lax.ppermute(a, 'd', [(i, i ^ 1 << bit) for i in range(n_d)])  20 us
  transfers between devices with their start and end apart: 101, of which 57 were waited for; matrix products, arithmetic and copies ran while one was open for 8% of the time, Pallas kernels for 30%

profile of v5, /device:TPU:0, one launch (start us, length us, event | category | flops | bytes accessed | tf_op | source)
XLA Modules:
  0.0 573.6 jit_solution(13785554116259028489)
XLA Ops:
  8.3 4.1 collective-permute-start
  18.6 5.8 %collective-permute-done = bf16[1024,128]{1,0:T(8,128)(2,1)S(1)} collective-permute-done((bf16[1024,128]{1,0:T(8,128)(2,1)S(1)}, bf16[1024,128]{1,0:T(8,128)(2,1)S(1)}, u32[]{:S(2)}, u32[]{:S(2)}) %collective-permute-start) | collective-permute-done | bytes 262176 | tf_op jit(solution)/shard_map/ppermute | solution.py:823
  29.4 4.4 collective-permute-start.3
  33.8 8.3 %collective-permute-start.2 = (bf16[256,1024]{1,0:T(8,128)(2,1)S(1)}, bf16[256,1024]{1,0:T(8,128)(2,1)S(1)}, u32[]{:S(2)}, u32[]{:S(2)}) collective-permute-start(bf16[256,1024]{1,0:T(8,128)(2,1)S(1)} %broadcast_select_fusion.4.refs_0_), channel_id=1, source_target_pairs={{0,4},{4,0},{1,5},{5,1},{2,6},{6,2},{3,7},{7,3},{8,12},{12,8},{9,1... | collective-permute-start | bytes 1572872 | tf_op jit(solution)/shard_map/ppermute | solution.py:823
  42.1 2.3 collective-permute-done.3.refs_2_
  44.4 5.7 collective-permute-start.4
  51.6 2.4 deal_rows.1
  59.1 9.5 %collective-permute-done.6 = f32[1,768]{1,0:T(1,128)S(1)} collective-permute-done((f32[1,768]{1,0:T(1,128)S(1)}, f32[1,768]{1,0:T(1,128)S(1)}, u32[]{:S(2)}, u32[]{:S(2)}) %collective-permute-start.6) | collective-permute-done | bytes 3104 | tf_op jit(solution)/shard_map/ppermute | solution.py:823
  75.2 12.1 %collective-permute-done.5 = bf16[3072,128]{1,0:T(8,128)(2,1)} collective-permute-done((bf16[3072,128]{1,0:T(8,128)(2,1)S(1)}, bf16[3072,128]{1,0:T(8,128)(2,1)}, u32[]{:S(2)}, u32[]{:S(2)}) %collective-permute-start.5) | collective-permute-done | bytes 786464 | tf_op jit(solution)/shard_map/ppermute | solution.py:823
  92.6 5.6 collective-permute-done.12
  106.3 2.4 project.4
  108.7 2.4 project.5
  111.1 4.8 attend.4
  118.1 2.6 collective-permute-start.15
  121.2 4.8 attend.5
  126.0 17.4 %collective-permute-done.15.refs_3_ = bf16[256,1024]{1,0:T(8,128)(2,1)S(1)} collective-permute-done((bf16[256,1024]{1,0:T(8,128)(2,1)S(1)}, bf16[256,1024]{1,0:T(8,128)(2,1)S(1)}, u32[]{:S(2)}, u32[]{:S(2)}) %collective-permute-start.15) | collective-permute-done | bytes 524320 | tf_op jit(solution)/shard_map/ppermute | solution.py:823
  144.4 2.4 collective-permute-done.17
  152.9 3.3 place.5
  158.6 6.5 %ffn.4 = (bf16[512,1024]{1,0:T(8,128)(2,1)}, f32[512,1024]{1,0:T(8,128)}, f32[256,1024]{1,0:T(8,128)S(1)}, bf16[256,1024]{1,0:T(8,128)(2,1)S(1)}, bf16[512,1024]{1,0:T(8,128)(2,1)}) custom-call(bf16[256,1024]{1,0:T(8,128)(2,1)} %get-tuple-element.256.refs_0_, bf16[256,1024]{1,0:T(8,128)(2,1)S(1)} %copy-done.69, ...), custom_call_target="tpu_custom_call" | custom-call | flops 2147483648 | bytes 9437184 | tf_op jit(solution)/shard_map/ffn/pallas_call | solution.py:354
  168.1 5.5 ffn.5
  181.7 12.6 %collective-permute-done.23.refs_3_ = bf16[256,1024]{1,0:T(8,128)(2,1)S(1)} collective-permute-done((bf16[256,1024]{1,0:T(8,128)(2,1)}, bf16[256,1024]{1,0:T(8,128)(2,1)S(1)}, u32[]{:S(2)}, u32[]{:S(2)}) %collective-permute-start.23) | collective-permute-done | bytes 524320 | tf_op jit(solution)/shard_map/ppermute | solution.py:823
  199.2 3.9 project.6
  203.1 7.5 %collective-permute-done.26.refs_0_ = bf16[256,1024]{1,0:T(8,128)(2,1)S(1)} collective-permute-done((bf16[256,1024]{1,0:T(8,128)(2,1)}, bf16[256,1024]{1,0:T(8,128)(2,1)S(1)}, u32[]{:S(2)}, u32[]{:S(2)}) %collective-permute-start.26) | collective-permute-done | bytes 524320 | tf_op jit(solution)/shard_map/ppermute | solution.py:823
  212.5 2.6 project.7
  215.1 4.8 attend.6
  223.0 4.8 attend.7
  227.8 8.2 %collective-permute-done.29.refs_3_ = bf16[256,1024]{1,0:T(8,128)(2,1)S(1)} collective-permute-done((bf16[256,1024]{1,0:T(8,128)(2,1)S(1)}, bf16[256,1024]{1,0:T(8,128)(2,1)S(1)}, u32[]{:S(2)}, u32[]{:S(2)}) %collective-permute-start.29) | collective-permute-done | bytes 524320 | tf_op jit(solution)/shard_map/ppermute | solution.py:823
  241.6 3.3 place.7
  245.0 7.0 %ffn.6 = (bf16[512,1024]{1,0:T(8,128)(2,1)}, f32[512,1024]{1,0:T(8,128)}, f32[256,1024]{1,0:T(8,128)S(1)}, bf16[256,1024]{1,0:T(8,128)(2,1)S(1)}, bf16[512,1024]{1,0:T(8,128)(2,1)}) custom-call(bf16[256,1024]{1,0:T(8,128)(2,1)} %get-tuple-element.282.refs_0_, bf16[256,1024]{1,0:T(8,128)(2,1)S(1)} %collective-permute-done.31.refs_1_, ...), custom_call_target="tpu_custom_call" | custom-call | flops 2147483648 | bytes 9437184 | tf_op jit(solution)/shard_map/ffn/pallas_call | solution.py:354
  252.0 2.3 collective-permute-done.33.refs_0_
  256.1 5.4 ffn.7
  262.0 6.6 %collective-permute-done.39 = bf16[256,1024]{1,0:T(8,128)(2,1)S(1)} collective-permute-done((bf16[256,1024]{1,0:T(8,128)(2,1)S(1)}, bf16[256,1024]{1,0:T(8,128)(2,1)S(1)}, u32[]{:S(2)}, u32[]{:S(2)}) %collective-permute-start.39) | collective-permute-done | bytes 524320 | tf_op jit(solution)/shard_map/ppermute | solution.py:823
  273.2 10.4 %collective-permute-done.37.refs_3_ = bf16[256,1024]{1,0:T(8,128)(2,1)S(1)} collective-permute-done((bf16[256,1024]{1,0:T(8,128)(2,1)S(1)}, bf16[256,1024]{1,0:T(8,128)(2,1)S(1)}, u32[]{:S(2)}, u32[]{:S(2)}) %collective-permute-start.37) | collective-permute-done | bytes 524320 | tf_op jit(solution)/shard_map/ppermute | solution.py:823
  289.5 5.2 ffn_back.4
  295.6 6.3 %collective-permute-done.42.refs_0_ = bf16[256,1024]{1,0:T(8,128)(2,1)S(1)} collective-permute-done((bf16[256,1024]{1,0:T(8,128)(2,1)S(1)}, bf16[256,1024]{1,0:T(8,128)(2,1)S(1)}, u32[]{:S(2)}, u32[]{:S(2)}) %collective-permute-start.42) | collective-permute-done | bytes 524320 | tf_op jit(solution)/shard_map/ppermute | solution.py:823
  303.8 5.1 ffn_back.5
  312.7 9.6 %weight_grad.5 = bf16[8,2048,128]{2,1,0:T(8,128)(2,1)} custom-call(s32[2]{0:T(128)S(1)} %pad_add_fusion.1.where_ref, bf16[512,1024]{1,0:T(8,128)(2,1)} %get-tuple-element.289.refs_0_, bf16[512,1024]{1,0:T(8,128)(2,1)} %get-tuple-element.298.refs_1_, bf16[512,1024]{1,0:T(8,128)(2,1)} %get-tuple-element.301.refs_2_, ...), custom_call_target="tpu_custom_call" | custom-call | flops 4294967296 | bytes 12582912 | tf_op jit(solution)/shard_map/weight_grad/pallas_call | solution.py:648
  323.2 2.8 collective-permute-done.46.refs_3_
  337.8 7.9 %attend_back.4 = (bf16[512,256]{1,0:T(8,128)(2,1)S(1)}, f32[1,256]{1,0:T(1,128)S(1)}, f32[1024,256]{1,0:T(8,128)S(1)}, f32[1024,256]{1,0:T(8,128)S(1)}, bf16[512,1024]{1,0:T(8,128)(2,1)}) custom-call(bf16[512,768]{1,0:T(8,128)(2,1)S(1)} %copy-done.79, bf16[512,768]{1,0:T(8,128)(2,1)S(1)} %copy-done.79, bf16[512,768]{1,0:T(8,128)(2,1)S(1)} %copy-done.81, ...), custom_call_target="tpu_custom_call" | custom-call | flops 5368709120 | bytes 8388608 | tf_op jit(solution)/shard_map/attend_back/pallas_call | solution.py:304
  349.9 8.6 %attend_back.5 = (bf16[512,768]{1,0:T(8,128)(2,1)S(1)}, bf16[512,768]{1,0:T(8,128)(2,1)S(1)}, f32[2,256]{1,0:T(2,128)S(1)}, bf16[512,1024]{1,0:T(8,128)(2,1)}) custom-call(bf16[512,768]{1,0:T(8,128)(2,1)S(1)} %copy-done.81, bf16[512,768]{1,0:T(8,128)(2,1)S(1)} %copy-done.79, bf16[512,768]{1,0:T(8,128)(2,1)S(1)} %copy-done.81, ...), custom_call_target="tpu_custom_call" | custom-call | flops 5368709120 | bytes 8388608 | tf_op jit(solution)/shard_map/attend_back/pallas_call | solution.py:304
  359.5 7.1 %collective-permute-start.51 = (bf16[256,1024]{1,0:T(8,128)(2,1)S(1)}, bf16[256,1024]{1,0:T(8,128)(2,1)S(1)}, u32[]{:S(2)}, u32[]{:S(2)}) collective-permute-start(bf16[256,1024]{1,0:T(8,128)(2,1)S(1)} %get-tuple-element.336), channel_id=1, source_target_pairs={{0,4},{4,0},{1,5},{5,1},{2,6},{6,2},{3,7},{7,3},{8,12},{12,8},{9,1... | collective-permute-start | bytes 1572872 | tf_op jit(solution)/shard_map/ppermute | solution.py:823
  373.1 6.7 %weight_grad.6 = bf16[8,1024,128]{2,1,0:T(8,128)(2,1)} custom-call(s32[2]{0:T(128)S(1)} %pad_add_fusion.1.where_ref, bf16[512,1024]{1,0:T(8,128)(2,1)} %get-tuple-element.271.refs_0_, bf16[512,1024]{1,0:T(8,128)(2,1)} %get-tuple-element.326.refs_1_, bf16[512,768]{1,0:T(8,128)(2,1)} %copy-done.13, bf16[512,768]{1,0:T(8,128)(2,1)} %copy-done.14, ...), custom_call_target="tpu_custom_call" | custom-call | flops 2147483648 | bytes 12582912 | tf_op jit(solution)/shard_map/weight_grad/pallas_call | solution.py:648
  379.8 4.9 collective-permute-done.53.refs_3_
  395.3 5.6 ffn_back.6
  400.9 4.8 collective-permute-done.55.refs_0_
  407.9 4.2 ffn_back.7
  412.1 9.5 %collective-permute-done.58 = bf16[1024,128]{1,0:T(8,128)(2,1)S(1)} collective-permute-done((bf16[1024,128]{1,0:T(8,128)(2,1)S(1)}, bf16[1024,128]{1,0:T(8,128)(2,1)S(1)}, u32[]{:S(2)}, u32[]{:S(2)}) %collective-permute-start.58) | collective-permute-done | bytes 262176 | tf_op jit(solution)/shard_map/ppermute | solution.py:823
  425.7 6.0 %weight_grad.7 = (bf16[2,1024,128]{2,1,0:T(8,128)(2,1)}, bf16[2,1024,128]{2,1,0:T(8,128)(2,1)S(1)}, bf16[2,1024,128]{2,1,0:T(8,128)(2,1)}, bf16[2,1024,128]{2,1,0:T(8,128)(2,1)S(1)}) custom-call(s32[2]{0:T(128)S(1)} %pad_add_fusion.1.where_ref, bf16[512,1024]{1,0:T(8,128)(2,1)} %get-tuple-element.356.refs_0_, bf16[512,1024]{1,0:T(8,128)(2,1)} %get-tuple-element.357.refs_1_, ...), custom_call_target="tpu_custom_call" | custom-call | flops 2147483648 | bytes 12582912 | tf_op jit(solution)/shard_map/weight_grad/pallas_call | solution.py:648
  437.2 5.3 weight_grad.8
  448.0 2.5 collective-permute-start.63
  451.6 5.7 collective-permute-done.68
  457.4 2.9 collective-permute-done.69
  460.5 8.3 %attend_back.6 = (bf16[512,256]{1,0:T(8,128)(2,1)S(1)}, f32[1,256]{1,0:T(1,128)S(1)}, f32[1024,256]{1,0:T(8,128)S(1)}, f32[1024,256]{1,0:T(8,128)S(1)}, bf16[512,1024]{1,0:T(8,128)(2,1)}) custom-call(bf16[512,768]{1,0:T(8,128)(2,1)S(1)} %copy-done.75, bf16[512,768]{1,0:T(8,128)(2,1)S(1)} %copy-done.75, bf16[512,768]{1,0:T(8,128)(2,1)S(1)} %copy-done.77, ...), custom_call_target="tpu_custom_call" | custom-call | flops 5368709120 | bytes 8388608 | tf_op jit(solution)/shard_map/attend_back/pallas_call | solution.py:304
  476.0 8.8 %attend_back.7 = (bf16[512,768]{1,0:T(8,128)(2,1)S(1)}, bf16[512,768]{1,0:T(8,128)(2,1)S(1)}, f32[2,256]{1,0:T(2,128)S(1)}, bf16[512,1024]{1,0:T(8,128)(2,1)}) custom-call(bf16[512,768]{1,0:T(8,128)(2,1)S(1)} %copy-done.77, bf16[512,768]{1,0:T(8,128)(2,1)S(1)} %copy-done.75, bf16[512,768]{1,0:T(8,128)(2,1)S(1)} %copy-done.77, ...), custom_call_target="tpu_custom_call" | custom-call | flops 5368709120 | bytes 8388608 | tf_op jit(solution)/shard_map/attend_back/pallas_call | solution.py:304
  484.8 4.3 collective-permute-done.75.got_ref
  493.6 6.2 %weight_grad.9 = (bf16[2,1024,128]{2,1,0:T(8,128)(2,1)}, bf16[2,1024,128]{2,1,0:T(8,128)(2,1)S(1)}, bf16[2,1024,128]{2,1,0:T(8,128)(2,1)}, bf16[2,1024,128]{2,1,0:T(8,128)(2,1)S(1)}) custom-call(s32[2]{0:T(128)S(1)} %pad_add_fusion.1.where_ref, bf16[512,1024]{1,0:T(8,128)(2,1)} %get-tuple-element.322.refs_0_, bf16[512,1024]{1,0:T(8,128)(2,1)} %get-tuple-element.323.refs_1_, ...), custom_call_target="tpu_custom_call" | custom-call | flops 2147483648 | bytes 12582912 | tf_op jit(solution)/shard_map/weight_grad/pallas_call | solution.py:648
  505.3 3.0 collective-permute-start.84
  512.6 2.5 collective-permute-done.77
  516.3 3.5 collective-permute-done.80.got_ref
  523.8 4.2 collective-permute-done.81
  528.6 2.3 add_convert_fusion
  533.6 3.9 collective-permute-done.91
  548.6 2.7 collective-permute-done.94
  557.7 8.1 %collective-permute-done.89.got_ref = bf16[1024,128]{1,0:T(8,128)(2,1)S(1)} collective-permute-done((bf16[1024,128]{1,0:T(8,128)(2,1)S(1)}, bf16[1024,128]{1,0:T(8,128)(2,1)S(1)}, u32[]{:S(2)}, u32[]{:S(2)}) %collective-permute-start.89) | collective-permute-done | bytes 262176 | tf_op jit(solution)/shard_map/ppermute | solution.py:823
  (593 shorter events, 197.4 us)
Async XLA Ops:
  7.2 94.5 %all-gather.5.cloned.1.call-start = ((), (), s32[]{:S(2)}) async-start(), calls=%async_computation.2 | async-start | bytes 2621440 | tf_op jit(solution)/shard_map/all_gather | solution.py:894
  8.3 16.0 %collective-permute-start = (bf16[1024,128]{1,0:T(8,128)(2,1)S(1)}, bf16[1024,128]{1,0:T(8,128)(2,1)S(1)}, u32[]{:S(2)}, u32[]{:S(2)}) collective-permute-start(bf16[1024,128]{1,0:T(8,128)(2,1)S(1)} %pack.3), channel_id=1, source_target_pairs={{0,2},{2,0},{1,3},{3,1},{4,6},{6,4},{5,7},{7,5},{8,10},{10,8},{9,1... | collective-permute-start | bytes 786440 | tf_op jit(solution)/shard_map/ppermute | solution.py:823
  29.2 123.7 %all-gather.7.cloned.1.call-start = ((), (), s32[]{:S(2)}) async-start(), calls=%async_computation.3 | async-start | bytes 5242880 | tf_op jit(solution)/shard_map/all_gather | solution.py:894
  29.4 15.0 %collective-permute-start.3 = (bf16[256,1024]{1,0:T(8,128)(2,1)S(1)}, bf16[256,1024]{1,0:T(8,128)(2,1)S(1)}, u32[]{:S(2)}, u32[]{:S(2)}) collective-permute-start(bf16[256,1024]{1,0:T(8,128)(2,1)S(1)} %broadcast_select_fusion.4.refs_0_), channel_id=1, source_target_pairs={{0,1},{1,0},{2,3},{3,2},{4,5},{5,4},{6,7},{7,6},{8,9},{9,8},{10,11... | collective-permute-start | bytes 1572872 | tf_op jit(solution)/shard_map/ppermute | solution.py:823
  33.8 17.3 %collective-permute-start.2 = (bf16[256,1024]{1,0:T(8,128)(2,1)S(1)}, bf16[256,1024]{1,0:T(8,128)(2,1)S(1)}, u32[]{:S(2)}, u32[]{:S(2)}) collective-permute-start(bf16[256,1024]{1,0:T(8,128)(2,1)S(1)} %broadcast_select_fusion.4.refs_0_), channel_id=1, source_target_pairs={{0,4},{4,0},{1,5},{5,1},{2,6},{6,2},{3,7},{7,3},{8,12},{12,8},{9,1... | collective-permute-start | bytes 1572872 | tf_op jit(solution)/shard_map/ppermute | solution.py:823
  44.4 7.2 %collective-permute-start.4 = (bf16[256,1024]{1,0:T(8,128)(2,1)S(1)}, bf16[256,1024]{1,0:T(8,128)(2,1)S(1)}, u32[]{:S(2)}, u32[]{:S(2)}) collective-permute-start(bf16[256,1024]{1,0:T(8,128)(2,1)S(1)} %collective-permute-done.3.refs_2_), channel_id=1, source_target_pairs={{0,4},{4,0},{1,5},{5,1},{2,6},{6,2},{3,7},{7,3},{8,12},{12,8},{9,1... | collective-permute-start | bytes 1572872 | tf_op jit(solution)/shard_map/ppermute | solution.py:823
  50.0 37.3 %collective-permute-start.5 = (bf16[3072,128]{1,0:T(8,128)(2,1)S(1)}, bf16[3072,128]{1,0:T(8,128)(2,1)}, u32[]{:S(2)}, u32[]{:S(2)}) collective-permute-start(bf16[3072,128]{1,0:T(8,128)(2,1)S(1)} %pack.4), channel_id=1, source_target_pairs={{0,2},{2,0},{1,3},{3,1},{4,6},{6,4},{5,7},{7,5},{8,10},{10,8},{9,1... | collective-permute-start | bytes 2359304 | tf_op jit(solution)/shard_map/ppermute | solution.py:823
  57.1 11.5 %collective-permute-start.6 = (f32[1,768]{1,0:T(1,128)S(1)}, f32[1,768]{1,0:T(1,128)S(1)}, u32[]{:S(2)}, u32[]{:S(2)}) collective-permute-start(f32[1,768]{1,0:T(1,128)S(1)} %pad_maximum_fusion.7), channel_id=1, source_target_pairs={{0,1},{1,0},{2,3},{3,2},{4,5},{5,4},{6,7},{7,6},{8,9},{9,8},{10,11... | collective-permute-start | bytes 9224 | tf_op jit(solution)/shard_map/ppermute | solution.py:823
  73.7 14.8 %collective-permute-start.9 = (f32[8,768]{1,0:T(8,128)S(1)}, f32[8,768]{1,0:T(8,128)S(1)}, u32[]{:S(2)}, u32[]{:S(2)}) collective-permute-start(f32[8,768]{1,0:T(8,128)S(1)} %maximum_select_fusion.3), channel_id=1, source_target_pairs={{0,16},{8,24},{16,0},{24,8},{1,17},{9,25},{17,1},{25,9},{2,18},{10... | collective-permute-start | bytes 73736 | tf_op jit(solution)/shard_map/ppermute | solution.py:827
  92.2 104.8 %all-gather.9.cloned.1.call-start = ((), (), s32[]{:S(2)}) async-start(), calls=%async_computation.4 | async-start | bytes 2621440 | tf_op jit(solution)/shard_map/all_gather | solution.py:894
  99.6 16.3 %collective-permute-start.13 = (bf16[256,1024]{1,0:T(8,128)(2,1)}, bf16[256,1024]{1,0:T(8,128)(2,1)}, u32[]{:S(2)}, u32[]{:S(2)}) collective-permute-start(bf16[256,1024]{1,0:T(8,128)(2,1)} %param.12), channel_id=1, source_target_pairs={{2,4},{4,2},{3,5},{5,3},{10,12},{12,10},{11,13},{13,11},{18,20},{2... | collective-permute-start | bytes 1572872 | tf_op jit(solution)/shard_map/ppermute | solution.py:831
  118.1 25.3 %collective-permute-start.15 = (bf16[256,1024]{1,0:T(8,128)(2,1)S(1)}, bf16[256,1024]{1,0:T(8,128)(2,1)S(1)}, u32[]{:S(2)}, u32[]{:S(2)}) collective-permute-start(bf16[256,1024]{1,0:T(8,128)(2,1)S(1)} %add_convert_fusion.8), channel_id=1, source_target_pairs={{0,1},{1,0},{2,3},{3,2},{4,5},{5,4},{6,7},{7,6},{8,9},{9,8},{10,11... | collective-permute-start | bytes 1572872 | tf_op jit(solution)/shard_map/ppermute | solution.py:823
  120.7 26.1 %collective-permute-start.17 = (bf16[2048,128]{1,0:T(8,128)(2,1)S(1)}, bf16[2048,128]{1,0:T(8,128)(2,1)S(1)}, u32[]{:S(2)}, u32[]{:S(2)}) collective-permute-start(bf16[2048,128]{1,0:T(8,128)(2,1)S(1)} %pack.5), channel_id=1, source_target_pairs={{0,2},{2,0},{1,3},{3,1},{4,6},{6,4},{5,7},{7,5},{8,10},{10,8},{9,1... | collective-permute-start | bytes 1572872 | tf_op jit(solution)/shard_map/ppermute | solution.py:823
  150.1 6.2 %collective-permute-start.18 = (bf16[256,1024]{1,0:T(8,128)(2,1)}, bf16[256,1024]{1,0:T(8,128)(2,1)S(1)}, u32[]{:S(2)}, u32[]{:S(2)}) collective-permute-start(bf16[256,1024]{1,0:T(8,128)(2,1)} %get-tuple-element.256.refs_0_), channel_id=1, source_target_pairs={{0,4},{4,0},{1,5},{5,1},{2,6},{6,2},{3,7},{7,3},{8,12},{12,8},{9,1... | collective-permute-start | bytes 1572872 | tf_op jit(solution)/shard_map/ppermute | solution.py:823
  150.6 15.6 %collective-permute-start.19 = (bf16[256,1024]{1,0:T(8,128)(2,1)}, bf16[256,1024]{1,0:T(8,128)(2,1)S(1)}, u32[]{:S(2)}, u32[]{:S(2)}) collective-permute-start(bf16[256,1024]{1,0:T(8,128)(2,1)} %get-tuple-element.256.refs_0_), channel_id=1, source_target_pairs={{0,1},{1,0},{2,3},{3,2},{4,5},{5,4},{6,7},{7,6},{8,9},{9,8},{10,11... | collective-permute-start | bytes 1572872 | tf_op jit(solution)/shard_map/ppermute | solution.py:823
  152.5 89.1 %all-gather.11.cloned.1.call-start = ((), (), s32[]{:S(2)}) async-start(), calls=%async_computation.5 | async-start | bytes 5242880 | tf_op jit(solution)/shard_map/all_gather | solution.py:894
  179.7 211.7 %reduce-scatter.3.cloned.1.call-start = ((), (), s32[]{:S(2)}) async-start(), calls=%async_computation.6 | async-start | bytes 5242880 | tf_op jit(solution)/shard_map/reduce_scatter | solution.py:911
  179.9 14.4 %collective-permute-start.23 = (bf16[256,1024]{1,0:T(8,128)(2,1)}, bf16[256,1024]{1,0:T(8,128)(2,1)S(1)}, u32[]{:S(2)}, u32[]{:S(2)}) collective-permute-start(bf16[256,1024]{1,0:T(8,128)(2,1)} %add_convert_fusion.7), channel_id=1, source_target_pairs={{0,1},{1,0},{2,3},{3,2},{4,5},{5,4},{6,7},{7,6},{8,9},{9,8},{10,11... | collective-permute-start | bytes 1572872 | tf_op jit(solution)/shard_map/ppermute | solution.py:823
  196.0 14.5 %collective-permute-start.26 = (bf16[256,1024]{1,0:T(8,128)(2,1)}, bf16[256,1024]{1,0:T(8,128)(2,1)S(1)}, u32[]{:S(2)}, u32[]{:S(2)}) collective-permute-start(bf16[256,1024]{1,0:T(8,128)(2,1)} %get-tuple-element.267.refs_0_), channel_id=1, source_target_pairs={{0,1},{1,0},{2,3},{3,2},{4,5},{5,4},{6,7},{7,6},{8,9},{9,8},{10,11... | collective-permute-start | bytes 1572872 | tf_op jit(solution)/shard_map/ppermute | solution.py:823
  222.0 14.0 %collective-permute-start.29 = (bf16[256,1024]{1,0:T(8,128)(2,1)S(1)}, bf16[256,1024]{1,0:T(8,128)(2,1)S(1)}, u32[]{:S(2)}, u32[]{:S(2)}) collective-permute-start(bf16[256,1024]{1,0:T(8,128)(2,1)S(1)} %add_convert_fusion.6), channel_id=1, source_target_pairs={{0,1},{1,0},{2,3},{3,2},{4,5},{5,4},{6,7},{7,6},{8,9},{9,8},{10,11... | collective-permute-start | bytes 1572872 | tf_op jit(solution)/shard_map/ppermute | solution.py:823
  239.8 14.4 %collective-permute-start.33 = (bf16[256,1024]{1,0:T(8,128)(2,1)}, bf16[256,1024]{1,0:T(8,128)(2,1)S(1)}, u32[]{:S(2)}, u32[]{:S(2)}) collective-permute-start(bf16[256,1024]{1,0:T(8,128)(2,1)} %get-tuple-element.282.refs_0_), channel_id=1, source_target_pairs={{0,1},{1,0},{2,3},{3,2},{4,5},{5,4},{6,7},{7,6},{8,9},{9,8},{10,11... | collective-permute-start | bytes 1572872 | tf_op jit(solution)/shard_map/ppermute | solution.py:823
  254.3 14.3 %collective-permute-start.39 = (bf16[256,1024]{1,0:T(8,128)(2,1)S(1)}, bf16[256,1024]{1,0:T(8,128)(2,1)S(1)}, u32[]{:S(2)}, u32[]{:S(2)}) collective-permute-start(bf16[256,1024]{1,0:T(8,128)(2,1)S(1)} %broadcast_select_fusion.3), channel_id=1, source_target_pairs={{0,1},{1,0},{2,3},{3,2},{4,5},{5,4},{6,7},{7,6},{8,9},{9,8},{10,11... | collective-permute-start | bytes 1572872 | tf_op jit(solution)/shard_map/ppermute | solution.py:823
  261.5 7.6 %collective-permute-start.36 = (bf16[256,1024]{1,0:T(8,128)(2,1)S(1)}, bf16[256,1024]{1,0:T(8,128)(2,1)S(1)}, u32[]{:S(2)}, u32[]{:S(2)}) collective-permute-start(bf16[256,1024]{1,0:T(8,128)(2,1)S(1)} %get-tuple-element.292), channel_id=1, source_target_pairs={{0,4},{4,0},{1,5},{5,1},{2,6},{6,2},{3,7},{7,3},{8,12},{12,8},{9,1... | collective-permute-start | bytes 1572872 | tf_op jit(solution)/shard_map/ppermute | solution.py:823
  261.9 10.4 %collective-permute-start.38 = (bf16[256,1024]{1,0:T(8,128)(2,1)S(1)}, bf16[256,1024]{1,0:T(8,128)(2,1)S(1)}, u32[]{:S(2)}, u32[]{:S(2)}) collective-permute-start(bf16[256,1024]{1,0:T(8,128)(2,1)S(1)} %broadcast_select_fusion.3), channel_id=1, source_target_pairs={{0,4},{4,0},{1,5},{5,1},{2,6},{6,2},{3,7},{7,3},{8,12},{12,8},{9,1... | collective-permute-start | bytes 1572872 | tf_op jit(solution)/shard_map/ppermute | solution.py:823
  269.3 14.2 %collective-permute-start.37 = (bf16[256,1024]{1,0:T(8,128)(2,1)S(1)}, bf16[256,1024]{1,0:T(8,128)(2,1)S(1)}, u32[]{:S(2)}, u32[]{:S(2)}) collective-permute-start(bf16[256,1024]{1,0:T(8,128)(2,1)S(1)} %add_convert_fusion.5), channel_id=1, source_target_pairs={{0,1},{1,0},{2,3},{3,2},{4,5},{5,4},{6,7},{7,6},{8,9},{9,8},{10,11... | collective-permute-start | bytes 1572872 | tf_op jit(solution)/shard_map/ppermute | solution.py:823
  287.6 14.3 %collective-permute-start.42 = (bf16[256,1024]{1,0:T(8,128)(2,1)S(1)}, bf16[256,1024]{1,0:T(8,128)(2,1)S(1)}, u32[]{:S(2)}, u32[]{:S(2)}) collective-permute-start(bf16[256,1024]{1,0:T(8,128)(2,1)S(1)} %get-tuple-element.299.refs_0_), channel_id=1, source_target_pairs={{0,1},{1,0},{2,3},{3,2},{4,5},{5,4},{6,7},{7,6},{8,9},{9,8},{10,11... | collective-permute-start | bytes 1572872 | tf_op jit(solution)/shard_map/ppermute | solution.py:823
  309.1 13.3 %collective-permute-start.45 = (bf16[256,1024]{1,0:T(8,128)(2,1)}, bf16[256,1024]{1,0:T(8,128)(2,1)S(1)}, u32[]{:S(2)}, u32[]{:S(2)}) collective-permute-start(bf16[256,1024]{1,0:T(8,128)(2,1)} %get-tuple-element.316), channel_id=1, source_target_pairs={{0,4},{4,0},{1,5},{5,1},{2,6},{6,2},{3,7},{7,3},{8,12},{12,8},{9,1... | collective-permute-start | bytes 1572872 | tf_op jit(solution)/shard_map/ppermute | solution.py:823
  311.8 14.2 %collective-permute-start.46 = (bf16[256,1024]{1,0:T(8,128)(2,1)}, bf16[256,1024]{1,0:T(8,128)(2,1)S(1)}, u32[]{:S(2)}, u32[]{:S(2)}) collective-permute-start(bf16[256,1024]{1,0:T(8,128)(2,1)} %add_convert_fusion.4), channel_id=1, source_target_pairs={{0,1},{1,0},{2,3},{3,2},{4,5},{5,4},{6,7},{7,6},{8,9},{9,8},{10,11... | collective-permute-start | bytes 1572872 | tf_op jit(solution)/shard_map/ppermute | solution.py:823
  332.6 101.3 %reduce-scatter.5.cloned.1.call-start = ((), (), s32[]{:S(2)}) async-start(), calls=%async_computation.7 | async-start | bytes 2621440 | tf_op jit(solution)/shard_map/reduce_scatter | solution.py:911
  333.7 14.3 %collective-permute-start.49 = (bf16[256,1024]{1,0:T(8,128)(2,1)S(1)}, bf16[256,1024]{1,0:T(8,128)(2,1)S(1)}, u32[]{:S(2)}, u32[]{:S(2)}) collective-permute-start(bf16[256,1024]{1,0:T(8,128)(2,1)S(1)} %copy-done.71), channel_id=1, source_target_pairs={{0,1},{1,0},{2,3},{3,2},{4,5},{5,4},{6,7},{7,6},{8,9},{9,8},{10,11... | collective-permute-start | bytes 1572872 | tf_op jit(solution)/shard_map/ppermute | solution.py:823
  348.0 10.5 %collective-permute-start.48 = (bf16[256,1024]{1,0:T(8,128)(2,1)S(1)}, bf16[256,1024]{1,0:T(8,128)(2,1)S(1)}, u32[]{:S(2)}, u32[]{:S(2)}) collective-permute-start(bf16[256,1024]{1,0:T(8,128)(2,1)S(1)} %copy-done.26), channel_id=1, source_target_pairs={{2,4},{4,2},{3,5},{5,3},{10,12},{12,10},{11,13},{13,11},{18,20},{2... | collective-permute-start | bytes 1572872 | tf_op jit(solution)/shard_map/ppermute | solution.py:831
  359.5 8.6 %collective-permute-start.51 = (bf16[256,1024]{1,0:T(8,128)(2,1)S(1)}, bf16[256,1024]{1,0:T(8,128)(2,1)S(1)}, u32[]{:S(2)}, u32[]{:S(2)}) collective-permute-start(bf16[256,1024]{1,0:T(8,128)(2,1)S(1)} %get-tuple-element.336), channel_id=1, source_target_pairs={{0,4},{4,0},{1,5},{5,1},{2,6},{6,2},{3,7},{7,3},{8,12},{12,8},{9,1... | collective-permute-start | bytes 1572872 | tf_op jit(solution)/shard_map/ppermute | solution.py:823
  370.7 14.0 %collective-permute-start.53 = (bf16[256,1024]{1,0:T(8,128)(2,1)S(1)}, bf16[256,1024]{1,0:T(8,128)(2,1)S(1)}, u32[]{:S(2)}, u32[]{:S(2)}) collective-permute-start(bf16[256,1024]{1,0:T(8,128)(2,1)S(1)} %add_convert_fusion.3), channel_id=1, source_target_pairs={{0,1},{1,0},{2,3},{3,2},{4,5},{5,4},{6,7},{7,6},{8,9},{9,8},{10,11... | collective-permute-start | bytes 1572872 | tf_op jit(solution)/shard_map/ppermute | solution.py:823
  391.1 14.7 %collective-permute-start.55 = (bf16[256,1024]{1,0:T(8,128)(2,1)}, bf16[256,1024]{1,0:T(8,128)(2,1)}, u32[]{:S(2)}, u32[]{:S(2)}) collective-permute-start(bf16[256,1024]{1,0:T(8,128)(2,1)} %get-tuple-element.350.refs_0_), channel_id=1, source_target_pairs={{0,1},{1,0},{2,3},{3,2},{4,5},{5,4},{6,7},{7,6},{8,9},{9,8},{10,11... | collective-permute-start | bytes 1572872 | tf_op jit(solution)/shard_map/ppermute | solution.py:823
  393.6 12.2 %collective-permute-start.57 = (bf16[2048,128]{1,0:T(8,128)(2,1)S(1)}, bf16[2048,128]{1,0:T(8,128)(2,1)S(1)}, u32[]{:S(2)}, u32[]{:S(2)}) collective-permute-start(bf16[2048,128]{1,0:T(8,128)(2,1)S(1)} %get-tuple-element.363), channel_id=1, source_target_pairs={{0,4},{4,0},{1,5},{5,1},{2,6},{6,2},{3,7},{7,3},{8,12},{12,8},{9,1... | collective-permute-start | bytes 1572872 | tf_op jit(solution)/shard_map/ppermute | solution.py:823
  406.6 14.9 %collective-permute-start.58 = (bf16[1024,128]{1,0:T(8,128)(2,1)S(1)}, bf16[1024,128]{1,0:T(8,128)(2,1)S(1)}, u32[]{:S(2)}, u32[]{:S(2)}) collective-permute-start(bf16[1024,128]{1,0:T(8,128)(2,1)S(1)} %get-tuple-element.364), channel_id=1, source_target_pairs={{0,2},{2,0},{1,3},{3,1},{4,6},{6,4},{5,7},{7,5},{8,10},{10,8},{9,1... | collective-permute-start | bytes 786440 | tf_op jit(solution)/shard_map/ppermute | solution.py:823
  407.4 36.8 %collective-permute-start.61 = (bf16[256,1024]{1,0:T(8,128)(2,1)}, bf16[256,1024]{1,0:T(8,128)(2,1)S(1)}, u32[]{:S(2)}, u32[]{:S(2)}) collective-permute-start(bf16[256,1024]{1,0:T(8,128)(2,1)} %get-tuple-element.374), channel_id=1, source_target_pairs={{0,4},{4,0},{1,5},{5,1},{2,6},{6,2},{3,7},{7,3},{8,12},{12,8},{9,1... | collective-permute-start | bytes 1572872 | tf_op jit(solution)/shard_map/ppermute | solution.py:823
  423.7 21.6 %collective-permute-start.62 = (bf16[256,1024]{1,0:T(8,128)(2,1)S(1)}, bf16[256,1024]{1,0:T(8,128)(2,1)S(1)}, u32[]{:S(2)}, u32[]{:S(2)}) collective-permute-start(bf16[256,1024]{1,0:T(8,128)(2,1)S(1)} %add_convert_fusion.2), channel_id=1, source_target_pairs={{0,1},{1,0},{2,3},{3,2},{4,5},{5,4},{6,7},{7,6},{8,9},{9,8},{10,11... | collective-permute-start | bytes 1572872 | tf_op jit(solution)/shard_map/ppermute | solution.py:823
  423.7 18.8 %collective-permute-start.60 = (bf16[1024,128]{1,0:T(8,128)(2,1)}, bf16[1024,128]{1,0:T(8,128)(2,1)}, u32[]{:S(2)}, u32[]{:S(2)}) collective-permute-start(bf16[1024,128]{1,0:T(8,128)(2,1)} %get-tuple-element.370), channel_id=1, source_target_pairs={{0,2},{2,0},{1,3},{3,1},{4,6},{6,4},{5,7},{7,5},{8,10},{10,8},{9,1... | collective-permute-start | bytes 786440 | tf_op jit(solution)/shard_map/ppermute | solution.py:823
  432.5 18.0 %collective-permute-start.66 = (bf16[2,1024,128]{2,1,0:T(8,128)(2,1)}, bf16[2,1024,128]{2,1,0:T(8,128)(2,1)}, u32[]{:S(2)}, u32[]{:S(2)}) collective-permute-start(bf16[2,1024,128]{2,1,0:T(8,128)(2,1)} %get-tuple-element.367), channel_id=1, source_target_pairs={{0,16},{8,24},{16,0},{24,8},{1,17},{9,25},{17,1},{25,9},{2,18},{10... | collective-permute-start | bytes 1572872 | tf_op jit(solution)/shard_map/ppermute | solution.py:827
  435.7 15.8 %collective-permute-start.67 = (bf16[2,1024,128]{2,1,0:T(8,128)(2,1)}, bf16[2,1024,128]{2,1,0:T(8,128)(2,1)S(1)}, u32[]{:S(2)}, u32[]{:S(2)}) collective-permute-start(bf16[2,1024,128]{2,1,0:T(8,128)(2,1)} %get-tuple-element.381), channel_id=1, source_target_pairs={{0,8},{8,0},{16,24},{24,16},{1,9},{9,1},{17,25},{25,17},{2,10},{10... | collective-permute-start | bytes 1572872 | tf_op jit(solution)/shard_map/ppermute | solution.py:827
  442.6 14.7 %collective-permute-start.68 = (bf16[2,1024,128]{2,1,0:T(8,128)(2,1)S(1)}, bf16[2,1024,128]{2,1,0:T(8,128)(2,1)S(1)}, u32[]{:S(2)}, u32[]{:S(2)}) collective-permute-start(bf16[2,1024,128]{2,1,0:T(8,128)(2,1)S(1)} %get-tuple-element.369), channel_id=1, source_target_pairs={{0,16},{8,24},{16,0},{24,8},{1,17},{9,25},{17,1},{25,9},{2,18},{10... | collective-permute-start | bytes 1572872 | tf_op jit(solution)/shard_map/ppermute | solution.py:827
  444.2 16.1 %collective-permute-start.69 = (bf16[2,1024,128]{2,1,0:T(8,128)(2,1)S(1)}, bf16[2,1024,128]{2,1,0:T(8,128)(2,1)S(1)}, u32[]{:S(2)}, u32[]{:S(2)}) collective-permute-start(bf16[2,1024,128]{2,1,0:T(8,128)(2,1)S(1)} %get-tuple-element.382), channel_id=1, source_target_pairs={{0,8},{8,0},{16,24},{24,16},{1,9},{9,1},{17,25},{25,17},{2,10},{10... | collective-permute-start | bytes 1572872 | tf_op jit(solution)/shard_map/ppermute | solution.py:827
  448.0 20.8 %collective-permute-start.63 = (bf16[256,1024]{1,0:T(8,128)(2,1)S(1)}, bf16[256,1024]{1,0:T(8,128)(2,1)S(1)}, u32[]{:S(2)}, u32[]{:S(2)}) collective-permute-start(bf16[256,1024]{1,0:T(8,128)(2,1)S(1)} %get-tuple-element.377.refs_8_), channel_id=1, source_target_pairs={{0,1},{1,0},{2,3},{3,2},{4,5},{5,4},{6,7},{7,6},{8,9},{9,8},{10,11... | collective-permute-start | bytes 1572872 | tf_op jit(solution)/shard_map/ppermute | solution.py:823
  450.5 9.9 %collective-permute-start.64 = (bf16[256,1024]{1,0:T(8,128)(2,1)S(1)}, bf16[256,1024]{1,0:T(8,128)(2,1)S(1)}, u32[]{:S(2)}, u32[]{:S(2)}) collective-permute-start(bf16[256,1024]{1,0:T(8,128)(2,1)S(1)} %get-tuple-element.377.refs_8_), channel_id=1, source_target_pairs={{0,4},{4,0},{1,5},{5,1},{2,6},{6,2},{3,7},{7,3},{8,12},{12,8},{9,1... | collective-permute-start | bytes 1572872 | tf_op jit(solution)/shard_map/ppermute | solution.py:823
  468.9 15.9 %collective-permute-start.70 = (bf16[1,1024,128]{2,1,0:T(8,128)(2,1)S(1)}, bf16[1,1024,128]{2,1,0:T(8,128)(2,1)S(1)}, u32[]{:S(2)}, u32[]{:S(2)}) collective-permute-start(bf16[1,1024,128]{2,1,0:T(8,128)(2,1)S(1)} %add_convert_fusion.17), channel_id=1, source_target_pairs={{0,8},{8,0},{16,24},{24,16},{1,9},{9,1},{17,25},{25,17},{2,10},{10... | collective-permute-start | bytes 786440 | tf_op jit(solution)/shard_map/ppermute | solution.py:827
  470.5 14.3 %collective-permute-start.71 = (bf16[1,1024,128]{2,1,0:T(8,128)(2,1)S(1)}, bf16[1,1024,128]{2,1,0:T(8,128)(2,1)S(1)}, u32[]{:S(2)}, u32[]{:S(2)}) collective-permute-start(bf16[1,1024,128]{2,1,0:T(8,128)(2,1)S(1)} %add_convert_fusion.16), channel_id=1, source_target_pairs={{0,16},{8,24},{16,0},{24,8},{1,17},{9,25},{17,1},{25,9},{2,18},{10... | collective-permute-start | bytes 786440 | tf_op jit(solution)/shard_map/ppermute | solution.py:827
  471.0 13.8 %collective-permute-start.72 = (bf16[1,1024,128]{2,1,0:T(8,128)(2,1)S(1)}, bf16[1,1024,128]{2,1,0:T(8,128)(2,1)S(1)}, u32[]{:S(2)}, u32[]{:S(2)}) collective-permute-start(bf16[1,1024,128]{2,1,0:T(8,128)(2,1)S(1)} %add_convert_fusion.15), channel_id=1, source_target_pairs={{0,8},{8,0},{16,24},{24,16},{1,9},{9,1},{17,25},{25,17},{2,10},{10... | collective-permute-start | bytes 786440 | tf_op jit(solution)/shard_map/ppermute | solution.py:827
  473.1 11.8 %collective-permute-start.73 = (bf16[1,1024,128]{2,1,0:T(8,128)(2,1)S(1)}, bf16[1,1024,128]{2,1,0:T(8,128)(2,1)S(1)}, u32[]{:S(2)}, u32[]{:S(2)}) collective-permute-start(bf16[1,1024,128]{2,1,0:T(8,128)(2,1)S(1)} %add_convert_fusion.14), channel_id=1, source_target_pairs={{0,16},{8,24},{16,0},{24,8},{1,17},{9,25},{17,1},{25,9},{2,18},{10... | collective-permute-start | bytes 786440 | tf_op jit(solution)/shard_map/ppermute | solution.py:827
  474.6 14.5 %collective-permute-start.75 = (bf16[1024,128]{1,0:T(8,128)(2,1)S(1)}, bf16[1024,128]{1,0:T(8,128)(2,1)S(1)}, u32[]{:S(2)}, u32[]{:S(2)}) collective-permute-start(bf16[1024,128]{1,0:T(8,128)(2,1)S(1)} %broadcast_select_fusion.5), channel_id=1, source_target_pairs={{0,2},{2,0},{1,3},{3,1},{4,6},{6,4},{5,7},{7,5},{8,10},{10,8},{9,1... | collective-permute-start | bytes 786440 | tf_op jit(solution)/shard_map/ppermute | solution.py:823
  491.9 11.4 %collective-permute-start.79 = (bf16[1024,128]{1,0:T(8,128)(2,1)}, bf16[1024,128]{1,0:T(8,128)(2,1)S(1)}, u32[]{:S(2)}, u32[]{:S(2)}) collective-permute-start(bf16[1024,128]{1,0:T(8,128)(2,1)} %fusion.12), channel_id=1, source_target_pairs={{0,4},{4,0},{1,5},{5,1},{2,6},{6,2},{3,7},{7,3},{8,12},{12,8},{9,1... | collective-permute-start | bytes 786440 | tf_op jit(solution)/shard_map/ppermute | solution.py:823
  492.4 29.4 %collective-permute-start.86 = (bf16[1024,128]{1,0:T(8,128)(2,1)}, bf16[1024,128]{1,0:T(8,128)(2,1)}, u32[]{:S(2)}, u32[]{:S(2)}) collective-permute-start(bf16[1024,128]{1,0:T(8,128)(2,1)} %fusion.14), channel_id=1, source_target_pairs={{0,4},{4,0},{1,5},{5,1},{2,6},{6,2},{3,7},{7,3},{8,12},{12,8},{9,1... | collective-permute-start | bytes 786440 | tf_op jit(solution)/shard_map/ppermute | solution.py:823
  500.5 14.6 %collective-permute-start.77 = (bf16[2,1024,128]{2,1,0:T(8,128)(2,1)}, bf16[2,1024,128]{2,1,0:T(8,128)(2,1)}, u32[]{:S(2)}, u32[]{:S(2)}) collective-permute-start(bf16[2,1024,128]{2,1,0:T(8,128)(2,1)} %get-tuple-element.411), channel_id=1, source_target_pairs={{0,16},{8,24},{16,0},{24,8},{1,17},{9,25},{17,1},{25,9},{2,18},{10... | collective-permute-start | bytes 1572872 | tf_op jit(solution)/shard_map/ppermute | solution.py:827
  501.7 14.4 %collective-permute-start.78 = (bf16[2,1024,128]{2,1,0:T(8,128)(2,1)}, bf16[2,1024,128]{2,1,0:T(8,128)(2,1)S(1)}, u32[]{:S(2)}, u32[]{:S(2)}) collective-permute-start(bf16[2,1024,128]{2,1,0:T(8,128)(2,1)} %get-tuple-element.413), channel_id=1, source_target_pairs={{0,8},{8,0},{16,24},{24,16},{1,9},{9,1},{17,25},{25,17},{2,10},{10... | collective-permute-start | bytes 1572872 | tf_op jit(solution)/shard_map/ppermute | solution.py:827
  505.3 14.5 %collective-permute-start.80 = (bf16[1024,128]{1,0:T(8,128)(2,1)S(1)}, bf16[1024,128]{1,0:T(8,128)(2,1)S(1)}, u32[]{:S(2)}, u32[]{:S(2)}) collective-permute-start(bf16[1024,128]{1,0:T(8,128)(2,1)S(1)} %get-tuple-element.465), channel_id=1, source_target_pairs={{0,2},{2,0},{1,3},{3,1},{4,6},{6,4},{5,7},{7,5},{8,10},{10,8},{9,1... | collective-permute-start | bytes 786440 | tf_op jit(solution)/shard_map/ppermute | solution.py:823
  505.3 23.3 %collective-permute-start.84 = (bf16[256,1024]{1,0:T(8,128)(2,1)}, bf16[256,1024]{1,0:T(8,128)(2,1)}, u32[]{:S(2)}, u32[]{:S(2)}) collective-permute-start(bf16[256,1024]{1,0:T(8,128)(2,1)} %add_convert_fusion.1), channel_id=1, source_target_pairs={{0,1},{1,0},{2,3},{3,2},{4,5},{5,4},{6,7},{7,6},{8,9},{9,8},{10,11... | collective-permute-start | bytes 1572872 | tf_op jit(solution)/shard_map/ppermute | solution.py:823
  515.1 13.5 %collective-permute-start.83 = (bf16[256,1024]{1,0:T(8,128)(2,1)}, bf16[256,1024]{1,0:T(8,128)(2,1)}, u32[]{:S(2)}, u32[]{:S(2)}) collective-permute-start(bf16[256,1024]{1,0:T(8,128)(2,1)} %get-tuple-element.421), channel_id=1, source_target_pairs={{0,4},{4,0},{1,5},{5,1},{2,6},{6,2},{3,7},{7,3},{8,12},{12,8},{9,1... | collective-permute-start | bytes 1572872 | tf_op jit(solution)/shard_map/ppermute | solution.py:823
  519.8 8.3 %collective-permute-start.81 = (bf16[1,1024,128]{2,1,0:T(8,128)(2,1)S(1)}, bf16[1,1024,128]{2,1,0:T(8,128)(2,1)}, u32[]{:S(2)}, u32[]{:S(2)}) collective-permute-start(bf16[1,1024,128]{2,1,0:T(8,128)(2,1)S(1)} %add_convert_fusion.13), channel_id=1, source_target_pairs={{0,8},{8,0},{16,24},{24,16},{1,9},{9,1},{17,25},{25,17},{2,10},{10... | collective-permute-start | bytes 786440 | tf_op jit(solution)/shard_map/ppermute | solution.py:827
  520.3 8.0 %collective-permute-start.82 = (bf16[1,1024,128]{2,1,0:T(8,128)(2,1)S(1)}, bf16[1,1024,128]{2,1,0:T(8,128)(2,1)}, u32[]{:S(2)}, u32[]{:S(2)}) collective-permute-start(bf16[1,1024,128]{2,1,0:T(8,128)(2,1)S(1)} %add_convert_fusion.12), channel_id=1, source_target_pairs={{0,16},{8,24},{16,0},{24,8},{1,17},{9,25},{17,1},{25,9},{2,18},{10... | collective-permute-start | bytes 786440 | tf_op jit(solution)/shard_map/ppermute | solution.py:827
  523.8 16.3 %collective-permute-start.87 = (bf16[1024,128]{1,0:T(8,128)(2,1)}, bf16[1024,128]{1,0:T(8,128)(2,1)}, u32[]{:S(2)}, u32[]{:S(2)}) collective-permute-start(bf16[1024,128]{1,0:T(8,128)(2,1)} %get-tuple-element.424), channel_id=1, source_target_pairs={{0,2},{2,0},{1,3},{3,1},{4,6},{6,4},{5,7},{7,5},{8,10},{10,8},{9,1... | collective-permute-start | bytes 786440 | tf_op jit(solution)/shard_map/ppermute | solution.py:823
  531.2 6.3 %collective-permute-start.91 = (f32[4,2,768]{2,1,0:T(2,128)S(1)}, f32[4,2,768]{2,1,0:T(2,128)S(1)}, u32[]{:S(2)}, u32[]{:S(2)}) collective-permute-start(f32[4,2,768]{2,1,0:T(2,128)S(1)} %bitcast.114), channel_id=1, source_target_pairs={{0,1},{1,0},{2,3},{3,2},{4,5},{5,4},{6,7},{7,6},{8,9},{9,8},{10,11... | collective-permute-start | bytes 73736 | tf_op jit(solution)/shard_map/ppermute | solution.py:823
  532.1 24.5 %collective-permute-start.85 = (bf16[256,1024]{1,0:T(8,128)(2,1)}, bf16[256,1024]{1,0:T(8,128)(2,1)}, u32[]{:S(2)}, u32[]{:S(2)}) collective-permute-start(bf16[256,1024]{1,0:T(8,128)(2,1)} %add_convert_fusion), channel_id=1, source_target_pairs={{2,4},{4,2},{3,5},{5,3},{10,12},{12,10},{11,13},{13,11},{18,20},{2... | collective-permute-start | bytes 1572872 | tf_op jit(solution)/shard_map/ppermute | solution.py:831
  540.2 13.1 %collective-permute-start.88 = (bf16[1024,128]{1,0:T(8,128)(2,1)}, bf16[1024,128]{1,0:T(8,128)(2,1)S(1)}, u32[]{:S(2)}, u32[]{:S(2)}) collective-permute-start(bf16[1024,128]{1,0:T(8,128)(2,1)} %fusion.13), channel_id=1, source_target_pairs={{0,4},{4,0},{1,5},{5,1},{2,6},{6,2},{3,7},{7,3},{8,12},{12,8},{9,1... | collective-permute-start | bytes 786440 | tf_op jit(solution)/shard_map/ppermute | solution.py:823
  554.5 11.2 %collective-permute-start.89 = (bf16[1024,128]{1,0:T(8,128)(2,1)S(1)}, bf16[1024,128]{1,0:T(8,128)(2,1)S(1)}, u32[]{:S(2)}, u32[]{:S(2)}) collective-permute-start(bf16[1024,128]{1,0:T(8,128)(2,1)S(1)} %fusion.15), channel_id=1, source_target_pairs={{0,2},{2,0},{1,3},{3,1},{4,6},{6,4},{5,7},{7,5},{8,10},{10,8},{9,1... | collective-permute-start | bytes 786440 | tf_op jit(solution)/shard_map/ppermute | solution.py:823
  (175 other events, 1149.8 us)
Sparse Core Ops, SparseCore 0:
  29.4 37.2 all-gather.4
  92.3 52.7 all-gather.6
  152.6 34.5 all-gather.8
  188.9 52.6 all-gather.10
  332.8 51.5 reduce-scatter.2
  387.4 35.1 reduce-scatter.4

commit v6 on v5

--- a/solution.py
+++ b/solution.py
@@ -103,25 +103,25 @@
 
 def project_kernel(*refs):
     x_refs, (w_ref, add_ref, out_ref, x_ref) = refs[:2], refs[2:]
-
-    @pl.when(pl.program_id(0) == 0)
-    def _():
-        x_ref[...] = stack_rows(x_refs)
-
-    out_ref[...] = (nn(x_ref[...], w_ref[0]) + add_ref[...]).astype(bf16)
+    x = stack_rows(x_refs)
+    x_ref[...] = x
+    width = w_ref.shape[2]
+    for j in range(3):
+        at = slice(j * width, (j + 1) * width)
+        out_ref[:, at] = (nn(x, w_ref[j]) + add_ref[:, at]).astype(bf16)
 
 
 def project(x, w_qkv, add):
     rows = 2 * x[0].shape[0]
     _, d, width = w_qkv.shape
+    outs = [struct((rows, 3 * width), bf16), hbm((rows, d), bf16)]
     return pl.pallas_call(
         project_kernel,
-        grid=(3,),
-        in_specs=blocks_in(x)
-        + [pl.BlockSpec((1, d, width), lambda i: (i, 0, 0)), pl.BlockSpec((1, width), lambda i: (0, i))],
-        out_specs=[pl.BlockSpec((rows, width), lambda i: (0, i)), pl.BlockSpec((rows, d), whole(0, 0))],
-        out_shape=[struct((rows, 3 * width), bf16), hbm((rows, d), bf16)],
-        compiler_params=params(12),
+        grid=(1,),
+        in_specs=blocks_in((*x, w_qkv, add)),
+        out_specs=blocks_in(outs),
+        out_shape=outs,
+        compiler_params=params(16),
         cost_estimate=cost(6 * rows * d * width, 4 * MIB),
         name="project",
     )(*x, w_qkv, add)

time: 580 us -> 577 us (level)
  transfers between devices with their start and end apart: 101 -> 101, of which waited for: 57 -> 57; matrix products, arithmetic and copies ran while one was open for 8% -> 8% of each run, Pallas kernels for 30% -> 29%
where the time goes in v6:
time: 577 us; the launch traced here: 570 us
  waiting for transfers between devices  205 us (36%)
  Pallas kernels  177 us (31%)
  starting transfers between devices  89.8 us (16%)
  local copies, waits for them, and re-layouts  51.1 us (9%)
  other arithmetic  30.3 us (5%)
  between operations  16.1 us (3%)
    ppermute x75, waiting for transfers between devices, swap(): return lax.ppermute(a, axis, SWAP)  183 us
    ppermute x75, starting transfers between devices, swap(): return lax.ppermute(a, axis, SWAP)  64.9 us
    unnamed x279, local copies, waits for them, and re-layouts  38.8 us
    pallas_call x5, Pallas kernels, weight_grad(): pl.pallas_call(functools.partial(grad_kernel, fields, counts, specs), gri...  33.9 us
    pallas_call x4, Pallas kernels, attend_back(): pl.pallas_call(functools.partial(attend_back_kernel, scale, heads, last),...  33.6 us
    pallas_call x4, Pallas kernels, ffn(): pl.pallas_call(ffn_kernel, grid=(ff // tile,), in_specs=[*blocks_in(x), p...  23.9 us
    pallas_call x4, Pallas kernels, ffn_back(): pl.pallas_call(ffn_back_kernel, grid=(ff // tile,), in_specs=[*blocks_in(...  20 us
    ppermute x16, waiting for transfers between devices, flip_d(): return lax.ppermute(a, 'd', [(i, i ^ 1 << bit) for i in range(n_d)])  20 us
  transfers between devices with their start and end apart: 101, of which 57 were waited for; matrix products, arithmetic and copies ran while one was open for 8% of the time, Pallas kernels for 29%

profile of v6, /device:TPU:0, one launch (start us, length us, event | category | flops | bytes accessed | tf_op | source)
XLA Modules:
  0.0 570.2 jit_solution(6536314869110485738)
XLA Ops:
  8.3 4.1 collective-permute-start
  18.6 5.8 %collective-permute-done = bf16[1024,128]{1,0:T(8,128)(2,1)S(1)} collective-permute-done((bf16[1024,128]{1,0:T(8,128)(2,1)S(1)}, bf16[1024,128]{1,0:T(8,128)(2,1)S(1)}, u32[]{:S(2)}, u32[]{:S(2)}) %collective-permute-start) | collective-permute-done | bytes 262176 | tf_op jit(solution)/shard_map/ppermute | solution.py:823
  29.4 4.4 collective-permute-start.3
  33.8 8.3 %collective-permute-start.2 = (bf16[256,1024]{1,0:T(8,128)(2,1)S(1)}, bf16[256,1024]{1,0:T(8,128)(2,1)S(1)}, u32[]{:S(2)}, u32[]{:S(2)}) collective-permute-start(bf16[256,1024]{1,0:T(8,128)(2,1)S(1)} %broadcast_select_fusion.4.refs_0_), channel_id=1, source_target_pairs={{0,4},{4,0},{1,5},{5,1},{2,6},{6,2},{3,7},{7,3},{8,12},{12,8},{9,1... | collective-permute-start | bytes 1572872 | tf_op jit(solution)/shard_map/ppermute | solution.py:823
  42.1 2.3 collective-permute-done.3.refs_2_
  44.4 5.7 collective-permute-start.4
  51.6 2.4 deal_rows.1
  59.1 9.5 %collective-permute-done.6 = f32[1,768]{1,0:T(1,128)S(1)} collective-permute-done((f32[1,768]{1,0:T(1,128)S(1)}, f32[1,768]{1,0:T(1,128)S(1)}, u32[]{:S(2)}, u32[]{:S(2)}) %collective-permute-start.6) | collective-permute-done | bytes 3104 | tf_op jit(solution)/shard_map/ppermute | solution.py:823
  71.4 2.2 collective-permute-done.8
  75.2 12.1 %collective-permute-done.5 = bf16[3072,128]{1,0:T(8,128)(2,1)} collective-permute-done((bf16[3072,128]{1,0:T(8,128)(2,1)S(1)}, bf16[3072,128]{1,0:T(8,128)(2,1)}, u32[]{:S(2)}, u32[]{:S(2)}) %collective-permute-start.5) | collective-permute-done | bytes 786464 | tf_op jit(solution)/shard_map/ppermute | solution.py:823
  92.6 5.6 collective-permute-done.12
  101.7 2.1 place.4
  108.8 4.8 attend.4
  113.6 2.7 collective-permute-start.14
  120.5 4.8 attend.5
  125.3 17.2 %collective-permute-done.15.refs_3_ = bf16[256,1024]{1,0:T(8,128)(2,1)S(1)} collective-permute-done((bf16[256,1024]{1,0:T(8,128)(2,1)S(1)}, bf16[256,1024]{1,0:T(8,128)(2,1)S(1)}, u32[]{:S(2)}, u32[]{:S(2)}) %collective-permute-start.15) | collective-permute-done | bytes 524320 | tf_op jit(solution)/shard_map/ppermute | solution.py:823
  150.5 3.3 place.5
  156.1 6.5 %ffn.4 = (bf16[512,1024]{1,0:T(8,128)(2,1)}, f32[512,1024]{1,0:T(8,128)}, f32[256,1024]{1,0:T(8,128)S(1)}, bf16[256,1024]{1,0:T(8,128)(2,1)S(1)}, bf16[512,1024]{1,0:T(8,128)(2,1)}) custom-call(bf16[256,1024]{1,0:T(8,128)(2,1)} %get-tuple-element.256.refs_0_, bf16[256,1024]{1,0:T(8,128)(2,1)S(1)} %copy-done.69, ...), custom_call_target="tpu_custom_call" | custom-call | flops 2147483648 | bytes 9437184 | tf_op jit(solution)/shard_map/ffn/pallas_call | solution.py:354
  165.6 5.4 ffn.5
  179.4 12.6 %collective-permute-done.23.refs_3_ = bf16[256,1024]{1,0:T(8,128)(2,1)S(1)} collective-permute-done((bf16[256,1024]{1,0:T(8,128)(2,1)}, bf16[256,1024]{1,0:T(8,128)(2,1)S(1)}, u32[]{:S(2)}, u32[]{:S(2)}) %collective-permute-start.23) | collective-permute-done | bytes 524320 | tf_op jit(solution)/shard_map/ppermute | solution.py:823
  194.9 2.3 place.6
  197.2 2.6 project.6
  199.9 8.4 %collective-permute-done.26.refs_0_ = bf16[256,1024]{1,0:T(8,128)(2,1)S(1)} collective-permute-done((bf16[256,1024]{1,0:T(8,128)(2,1)}, bf16[256,1024]{1,0:T(8,128)(2,1)S(1)}, u32[]{:S(2)}, u32[]{:S(2)}) %collective-permute-start.26) | collective-permute-done | bytes 524320 | tf_op jit(solution)/shard_map/ppermute | solution.py:823
  211.4 4.8 attend.6
  219.5 4.8 attend.7
  224.3 8.0 %collective-permute-done.29.refs_3_ = bf16[256,1024]{1,0:T(8,128)(2,1)S(1)} collective-permute-done((bf16[256,1024]{1,0:T(8,128)(2,1)S(1)}, bf16[256,1024]{1,0:T(8,128)(2,1)S(1)}, u32[]{:S(2)}, u32[]{:S(2)}) %collective-permute-start.29) | collective-permute-done | bytes 524320 | tf_op jit(solution)/shard_map/ppermute | solution.py:823
  239.3 3.3 place.7
  242.7 6.5 %ffn.6 = (bf16[512,1024]{1,0:T(8,128)(2,1)}, f32[512,1024]{1,0:T(8,128)}, f32[256,1024]{1,0:T(8,128)S(1)}, bf16[256,1024]{1,0:T(8,128)(2,1)S(1)}, bf16[512,1024]{1,0:T(8,128)(2,1)}) custom-call(bf16[256,1024]{1,0:T(8,128)(2,1)} %get-tuple-element.282.refs_0_, bf16[256,1024]{1,0:T(8,128)(2,1)S(1)} %collective-permute-done.31.refs_1_, ...), custom_call_target="tpu_custom_call" | custom-call | flops 2147483648 | bytes 9437184 | tf_op jit(solution)/shard_map/ffn/pallas_call | solution.py:354
  252.9 5.4 ffn.7
  258.9 6.4 %collective-permute-done.39 = bf16[256,1024]{1,0:T(8,128)(2,1)S(1)} collective-permute-done((bf16[256,1024]{1,0:T(8,128)(2,1)S(1)}, bf16[256,1024]{1,0:T(8,128)(2,1)S(1)}, u32[]{:S(2)}, u32[]{:S(2)}) %collective-permute-start.39) | collective-permute-done | bytes 524320 | tf_op jit(solution)/shard_map/ppermute | solution.py:823
  270.1 10.1 %collective-permute-done.37.refs_3_ = bf16[256,1024]{1,0:T(8,128)(2,1)S(1)} collective-permute-done((bf16[256,1024]{1,0:T(8,128)(2,1)S(1)}, bf16[256,1024]{1,0:T(8,128)(2,1)S(1)}, u32[]{:S(2)}, u32[]{:S(2)}) %collective-permute-start.37) | collective-permute-done | bytes 524320 | tf_op jit(solution)/shard_map/ppermute | solution.py:823
  286.2 5.4 ffn_back.4
  292.6 6.1 %collective-permute-done.42.refs_0_ = bf16[256,1024]{1,0:T(8,128)(2,1)S(1)} collective-permute-done((bf16[256,1024]{1,0:T(8,128)(2,1)S(1)}, bf16[256,1024]{1,0:T(8,128)(2,1)S(1)}, u32[]{:S(2)}, u32[]{:S(2)}) %collective-permute-start.42) | collective-permute-done | bytes 524320 | tf_op jit(solution)/shard_map/ppermute | solution.py:823
  300.6 4.9 ffn_back.5
  309.5 9.6 %weight_grad.5 = bf16[8,2048,128]{2,1,0:T(8,128)(2,1)} custom-call(s32[2]{0:T(128)S(1)} %pad_add_fusion.1.where_ref, bf16[512,1024]{1,0:T(8,128)(2,1)} %get-tuple-element.289.refs_0_, bf16[512,1024]{1,0:T(8,128)(2,1)} %get-tuple-element.298.refs_1_, bf16[512,1024]{1,0:T(8,128)(2,1)} %get-tuple-element.301.refs_2_, ...), custom_call_target="tpu_custom_call" | custom-call | flops 4294967296 | bytes 12582912 | tf_op jit(solution)/shard_map/weight_grad/pallas_call | solution.py:648
  320.0 2.5 collective-permute-done.46.refs_3_
  334.4 7.9 %attend_back.4 = (bf16[512,256]{1,0:T(8,128)(2,1)S(1)}, f32[1,256]{1,0:T(1,128)S(1)}, f32[1024,256]{1,0:T(8,128)S(1)}, f32[1024,256]{1,0:T(8,128)S(1)}, bf16[512,1024]{1,0:T(8,128)(2,1)}) custom-call(bf16[512,768]{1,0:T(8,128)(2,1)S(1)} %copy-done.79, bf16[512,768]{1,0:T(8,128)(2,1)S(1)} %copy-done.79, bf16[512,768]{1,0:T(8,128)(2,1)S(1)} %copy-done.81, ...), custom_call_target="tpu_custom_call" | custom-call | flops 5368709120 | bytes 8388608 | tf_op jit(solution)/shard_map/attend_back/pallas_call | solution.py:304
  342.3 2.2 collective-permute-done.49.refs_8_
  346.5 8.6 %attend_back.5 = (bf16[512,768]{1,0:T(8,128)(2,1)S(1)}, bf16[512,768]{1,0:T(8,128)(2,1)S(1)}, f32[2,256]{1,0:T(2,128)S(1)}, bf16[512,1024]{1,0:T(8,128)(2,1)}) custom-call(bf16[512,768]{1,0:T(8,128)(2,1)S(1)} %copy-done.81, bf16[512,768]{1,0:T(8,128)(2,1)S(1)} %copy-done.79, bf16[512,768]{1,0:T(8,128)(2,1)S(1)} %copy-done.81, ...), custom_call_target="tpu_custom_call" | custom-call | flops 5368709120 | bytes 8388608 | tf_op jit(solution)/shard_map/attend_back/pallas_call | solution.py:304
  356.1 7.1 %collective-permute-start.51 = (bf16[256,1024]{1,0:T(8,128)(2,1)S(1)}, bf16[256,1024]{1,0:T(8,128)(2,1)S(1)}, u32[]{:S(2)}, u32[]{:S(2)}) collective-permute-start(bf16[256,1024]{1,0:T(8,128)(2,1)S(1)} %get-tuple-element.336), channel_id=1, source_target_pairs={{0,4},{4,0},{1,5},{5,1},{2,6},{6,2},{3,7},{7,3},{8,12},{12,8},{9,1... | collective-permute-start | bytes 1572872 | tf_op jit(solution)/shard_map/ppermute | solution.py:823
  369.6 6.8 %weight_grad.6 = bf16[8,1024,128]{2,1,0:T(8,128)(2,1)} custom-call(s32[2]{0:T(128)S(1)} %pad_add_fusion.1.where_ref, bf16[512,1024]{1,0:T(8,128)(2,1)} %get-tuple-element.271.refs_0_, bf16[512,1024]{1,0:T(8,128)(2,1)} %get-tuple-element.326.refs_1_, bf16[512,768]{1,0:T(8,128)(2,1)} %copy-done.13, bf16[512,768]{1,0:T(8,128)(2,1)} %copy-done.14, ...), custom_call_target="tpu_custom_call" | custom-call | flops 2147483648 | bytes 12582912 | tf_op jit(solution)/shard_map/weight_grad/pallas_call | solution.py:648
  376.4 4.9 collective-permute-done.53.refs_3_
  387.9 2.2 slice_bitcast_fusion
  391.9 5.6 ffn_back.6
  397.5 4.8 collective-permute-done.55.refs_0_
  404.4 4.2 ffn_back.7
  408.6 9.5 %collective-permute-done.58 = bf16[1024,128]{1,0:T(8,128)(2,1)S(1)} collective-permute-done((bf16[1024,128]{1,0:T(8,128)(2,1)S(1)}, bf16[1024,128]{1,0:T(8,128)(2,1)S(1)}, u32[]{:S(2)}, u32[]{:S(2)}) %collective-permute-start.58) | collective-permute-done | bytes 262176 | tf_op jit(solution)/shard_map/ppermute | solution.py:823
  422.3 6.0 %weight_grad.7 = (bf16[2,1024,128]{2,1,0:T(8,128)(2,1)}, bf16[2,1024,128]{2,1,0:T(8,128)(2,1)S(1)}, bf16[2,1024,128]{2,1,0:T(8,128)(2,1)}, bf16[2,1024,128]{2,1,0:T(8,128)(2,1)S(1)}) custom-call(s32[2]{0:T(128)S(1)} %pad_add_fusion.1.where_ref, bf16[512,1024]{1,0:T(8,128)(2,1)} %get-tuple-element.356.refs_0_, bf16[512,1024]{1,0:T(8,128)(2,1)} %get-tuple-element.357.refs_1_, ...), custom_call_target="tpu_custom_call" | custom-call | flops 2147483648 | bytes 12582912 | tf_op jit(solution)/shard_map/weight_grad/pallas_call | solution.py:648
  433.8 5.3 weight_grad.8
  444.6 2.5 collective-permute-start.63
  448.2 5.7 %collective-permute-done.68 = bf16[2,1024,128]{2,1,0:T(8,128)(2,1)S(1)} collective-permute-done((bf16[2,1024,128]{2,1,0:T(8,128)(2,1)S(1)}, bf16[2,1024,128]{2,1,0:T(8,128)(2,1)S(1)}, u32[]{:S(2)}, u32[]{:S(2)}) %collective-permute-start.68) | collective-permute-done | bytes 524320 | tf_op jit(solution)/shard_map/ppermute | solution.py:827
  454.0 2.9 collective-permute-done.69
  457.1 8.3 %attend_back.6 = (bf16[512,256]{1,0:T(8,128)(2,1)S(1)}, f32[1,256]{1,0:T(1,128)S(1)}, f32[1024,256]{1,0:T(8,128)S(1)}, f32[1024,256]{1,0:T(8,128)S(1)}, bf16[512,1024]{1,0:T(8,128)(2,1)}) custom-call(bf16[512,768]{1,0:T(8,128)(2,1)S(1)} %copy-done.75, bf16[512,768]{1,0:T(8,128)(2,1)S(1)} %copy-done.75, bf16[512,768]{1,0:T(8,128)(2,1)S(1)} %copy-done.77, ...), custom_call_target="tpu_custom_call" | custom-call | flops 5368709120 | bytes 8388608 | tf_op jit(solution)/shard_map/attend_back/pallas_call | solution.py:304
  472.6 8.8 %attend_back.7 = (bf16[512,768]{1,0:T(8,128)(2,1)S(1)}, bf16[512,768]{1,0:T(8,128)(2,1)S(1)}, f32[2,256]{1,0:T(2,128)S(1)}, bf16[512,1024]{1,0:T(8,128)(2,1)}) custom-call(bf16[512,768]{1,0:T(8,128)(2,1)S(1)} %copy-done.77, bf16[512,768]{1,0:T(8,128)(2,1)S(1)} %copy-done.75, bf16[512,768]{1,0:T(8,128)(2,1)S(1)} %copy-done.77, ...), custom_call_target="tpu_custom_call" | custom-call | flops 5368709120 | bytes 8388608 | tf_op jit(solution)/shard_map/attend_back/pallas_call | solution.py:304
  481.4 4.3 collective-permute-done.75.got_ref
  490.2 6.2 %weight_grad.9 = (bf16[2,1024,128]{2,1,0:T(8,128)(2,1)}, bf16[2,1024,128]{2,1,0:T(8,128)(2,1)S(1)}, bf16[2,1024,128]{2,1,0:T(8,128)(2,1)}, bf16[2,1024,128]{2,1,0:T(8,128)(2,1)S(1)}) custom-call(s32[2]{0:T(128)S(1)} %pad_add_fusion.1.where_ref, bf16[512,1024]{1,0:T(8,128)(2,1)} %get-tuple-element.322.refs_0_, bf16[512,1024]{1,0:T(8,128)(2,1)} %get-tuple-element.323.refs_1_, ...), custom_call_target="tpu_custom_call" | custom-call | flops 2147483648 | bytes 12582912 | tf_op jit(solution)/shard_map/weight_grad/pallas_call | solution.py:648
  501.9 2.9 collective-permute-start.84
  509.2 2.6 collective-permute-done.77
  512.9 3.5 collective-permute-done.80.got_ref
  520.4 4.2 collective-permute-done.81
  525.2 2.3 add_convert_fusion
  530.1 3.9 collective-permute-done.91
  545.2 2.7 collective-permute-done.94
  554.2 8.1 %collective-permute-done.89.got_ref = bf16[1024,128]{1,0:T(8,128)(2,1)S(1)} collective-permute-done((bf16[1024,128]{1,0:T(8,128)(2,1)S(1)}, bf16[1024,128]{1,0:T(8,128)(2,1)S(1)}, u32[]{:S(2)}, u32[]{:S(2)}) %collective-permute-start.89) | collective-permute-done | bytes 262176 | tf_op jit(solution)/shard_map/ppermute | solution.py:823
  (593 shorter events, 197.1 us)
Async XLA Ops:
  7.2 94.5 %all-gather.5.cloned.1.call-start = ((), (), s32[]{:S(2)}) async-start(), calls=%async_computation.2 | async-start | bytes 2621440 | tf_op jit(solution)/shard_map/all_gather | solution.py:894
  8.3 16.0 %collective-permute-start = (bf16[1024,128]{1,0:T(8,128)(2,1)S(1)}, bf16[1024,128]{1,0:T(8,128)(2,1)S(1)}, u32[]{:S(2)}, u32[]{:S(2)}) collective-permute-start(bf16[1024,128]{1,0:T(8,128)(2,1)S(1)} %pack.3), channel_id=1, source_target_pairs={{0,2},{2,0},{1,3},{3,1},{4,6},{6,4},{5,7},{7,5},{8,10},{10,8},{9,1... | collective-permute-start | bytes 786440 | tf_op jit(solution)/shard_map/ppermute | solution.py:823
  29.2 121.2 %all-gather.7.cloned.1.call-start = ((), (), s32[]{:S(2)}) async-start(), calls=%async_computation.3 | async-start | bytes 5242880 | tf_op jit(solution)/shard_map/all_gather | solution.py:894
  29.4 15.0 %collective-permute-start.3 = (bf16[256,1024]{1,0:T(8,128)(2,1)S(1)}, bf16[256,1024]{1,0:T(8,128)(2,1)S(1)}, u32[]{:S(2)}, u32[]{:S(2)}) collective-permute-start(bf16[256,1024]{1,0:T(8,128)(2,1)S(1)} %broadcast_select_fusion.4.refs_0_), channel_id=1, source_target_pairs={{0,1},{1,0},{2,3},{3,2},{4,5},{5,4},{6,7},{7,6},{8,9},{9,8},{10,11... | collective-permute-start | bytes 1572872 | tf_op jit(solution)/shard_map/ppermute | solution.py:823
  33.8 17.3 %collective-permute-start.2 = (bf16[256,1024]{1,0:T(8,128)(2,1)S(1)}, bf16[256,1024]{1,0:T(8,128)(2,1)S(1)}, u32[]{:S(2)}, u32[]{:S(2)}) collective-permute-start(bf16[256,1024]{1,0:T(8,128)(2,1)S(1)} %broadcast_select_fusion.4.refs_0_), channel_id=1, source_target_pairs={{0,4},{4,0},{1,5},{5,1},{2,6},{6,2},{3,7},{7,3},{8,12},{12,8},{9,1... | collective-permute-start | bytes 1572872 | tf_op jit(solution)/shard_map/ppermute | solution.py:823
  44.4 7.2 %collective-permute-start.4 = (bf16[256,1024]{1,0:T(8,128)(2,1)S(1)}, bf16[256,1024]{1,0:T(8,128)(2,1)S(1)}, u32[]{:S(2)}, u32[]{:S(2)}) collective-permute-start(bf16[256,1024]{1,0:T(8,128)(2,1)S(1)} %collective-permute-done.3.refs_2_), channel_id=1, source_target_pairs={{0,4},{4,0},{1,5},{5,1},{2,6},{6,2},{3,7},{7,3},{8,12},{12,8},{9,1... | collective-permute-start | bytes 1572872 | tf_op jit(solution)/shard_map/ppermute | solution.py:823
  50.0 37.3 %collective-permute-start.5 = (bf16[3072,128]{1,0:T(8,128)(2,1)S(1)}, bf16[3072,128]{1,0:T(8,128)(2,1)}, u32[]{:S(2)}, u32[]{:S(2)}) collective-permute-start(bf16[3072,128]{1,0:T(8,128)(2,1)S(1)} %pack.4), channel_id=1, source_target_pairs={{0,2},{2,0},{1,3},{3,1},{4,6},{6,4},{5,7},{7,5},{8,10},{10,8},{9,1... | collective-permute-start | bytes 2359304 | tf_op jit(solution)/shard_map/ppermute | solution.py:823
  57.1 11.5 %collective-permute-start.6 = (f32[1,768]{1,0:T(1,128)S(1)}, f32[1,768]{1,0:T(1,128)S(1)}, u32[]{:S(2)}, u32[]{:S(2)}) collective-permute-start(f32[1,768]{1,0:T(1,128)S(1)} %pad_maximum_fusion.7), channel_id=1, source_target_pairs={{0,1},{1,0},{2,3},{3,2},{4,5},{5,4},{6,7},{7,6},{8,9},{9,8},{10,11... | collective-permute-start | bytes 9224 | tf_op jit(solution)/shard_map/ppermute | solution.py:823
  73.7 14.8 %collective-permute-start.9 = (f32[8,768]{1,0:T(8,128)S(1)}, f32[8,768]{1,0:T(8,128)S(1)}, u32[]{:S(2)}, u32[]{:S(2)}) collective-permute-start(f32[8,768]{1,0:T(8,128)S(1)} %maximum_select_fusion.3), channel_id=1, source_target_pairs={{0,16},{8,24},{16,0},{24,8},{1,17},{9,25},{17,1},{25,9},{2,18},{10... | collective-permute-start | bytes 73736 | tf_op jit(solution)/shard_map/ppermute | solution.py:827
  92.2 102.7 %all-gather.9.cloned.1.call-start = ((), (), s32[]{:S(2)}) async-start(), calls=%async_computation.4 | async-start | bytes 2621440 | tf_op jit(solution)/shard_map/all_gather | solution.py:894
  99.6 14.0 %collective-permute-start.13 = (bf16[256,1024]{1,0:T(8,128)(2,1)}, bf16[256,1024]{1,0:T(8,128)(2,1)}, u32[]{:S(2)}, u32[]{:S(2)}) collective-permute-start(bf16[256,1024]{1,0:T(8,128)(2,1)} %param.12), channel_id=1, source_target_pairs={{2,4},{4,2},{3,5},{5,3},{10,12},{12,10},{11,13},{13,11},{18,20},{2... | collective-permute-start | bytes 1572872 | tf_op jit(solution)/shard_map/ppermute | solution.py:831
  118.0 24.4 %collective-permute-start.15 = (bf16[256,1024]{1,0:T(8,128)(2,1)S(1)}, bf16[256,1024]{1,0:T(8,128)(2,1)S(1)}, u32[]{:S(2)}, u32[]{:S(2)}) collective-permute-start(bf16[256,1024]{1,0:T(8,128)(2,1)S(1)} %add_convert_fusion.8), channel_id=1, source_target_pairs={{0,1},{1,0},{2,3},{3,2},{4,5},{5,4},{6,7},{7,6},{8,9},{9,8},{10,11... | collective-permute-start | bytes 1572872 | tf_op jit(solution)/shard_map/ppermute | solution.py:823
  118.4 26.1 %collective-permute-start.17 = (bf16[2048,128]{1,0:T(8,128)(2,1)S(1)}, bf16[2048,128]{1,0:T(8,128)(2,1)S(1)}, u32[]{:S(2)}, u32[]{:S(2)}) collective-permute-start(bf16[2048,128]{1,0:T(8,128)(2,1)S(1)} %pack.5), channel_id=1, source_target_pairs={{0,2},{2,0},{1,3},{3,1},{4,6},{6,4},{5,7},{7,5},{8,10},{10,8},{9,1... | collective-permute-start | bytes 1572872 | tf_op jit(solution)/shard_map/ppermute | solution.py:823
  148.5 15.2 %collective-permute-start.19 = (bf16[256,1024]{1,0:T(8,128)(2,1)}, bf16[256,1024]{1,0:T(8,128)(2,1)S(1)}, u32[]{:S(2)}, u32[]{:S(2)}) collective-permute-start(bf16[256,1024]{1,0:T(8,128)(2,1)} %get-tuple-element.256.refs_0_), channel_id=1, source_target_pairs={{0,1},{1,0},{2,3},{3,2},{4,5},{5,4},{6,7},{7,6},{8,9},{9,8},{10,11... | collective-permute-start | bytes 1572872 | tf_op jit(solution)/shard_map/ppermute | solution.py:823
  150.2 89.1 %all-gather.11.cloned.1.call-start = ((), (), s32[]{:S(2)}) async-start(), calls=%async_computation.5 | async-start | bytes 5242880 | tf_op jit(solution)/shard_map/all_gather | solution.py:894
  177.1 210.8 %reduce-scatter.3.cloned.1.call-start = ((), (), s32[]{:S(2)}) async-start(), calls=%async_computation.6 | async-start | bytes 5242880 | tf_op jit(solution)/shard_map/reduce_scatter | solution.py:911
  177.6 14.4 %collective-permute-start.23 = (bf16[256,1024]{1,0:T(8,128)(2,1)}, bf16[256,1024]{1,0:T(8,128)(2,1)S(1)}, u32[]{:S(2)}, u32[]{:S(2)}) collective-permute-start(bf16[256,1024]{1,0:T(8,128)(2,1)} %add_convert_fusion.7), channel_id=1, source_target_pairs={{0,1},{1,0},{2,3},{3,2},{4,5},{5,4},{6,7},{7,6},{8,9},{9,8},{10,11... | collective-permute-start | bytes 1572872 | tf_op jit(solution)/shard_map/ppermute | solution.py:823
  193.7 14.5 %collective-permute-start.26 = (bf16[256,1024]{1,0:T(8,128)(2,1)}, bf16[256,1024]{1,0:T(8,128)(2,1)S(1)}, u32[]{:S(2)}, u32[]{:S(2)}) collective-permute-start(bf16[256,1024]{1,0:T(8,128)(2,1)} %get-tuple-element.267.refs_0_), channel_id=1, source_target_pairs={{0,1},{1,0},{2,3},{3,2},{4,5},{5,4},{6,7},{7,6},{8,9},{9,8},{10,11... | collective-permute-start | bytes 1572872 | tf_op jit(solution)/shard_map/ppermute | solution.py:823
  218.3 14.0 %collective-permute-start.29 = (bf16[256,1024]{1,0:T(8,128)(2,1)S(1)}, bf16[256,1024]{1,0:T(8,128)(2,1)S(1)}, u32[]{:S(2)}, u32[]{:S(2)}) collective-permute-start(bf16[256,1024]{1,0:T(8,128)(2,1)S(1)} %add_convert_fusion.6), channel_id=1, source_target_pairs={{0,1},{1,0},{2,3},{3,2},{4,5},{5,4},{6,7},{7,6},{8,9},{9,8},{10,11... | collective-permute-start | bytes 1572872 | tf_op jit(solution)/shard_map/ppermute | solution.py:823
  236.4 6.2 %collective-permute-start.31 = (bf16[256,1024]{1,0:T(8,128)(2,1)}, bf16[256,1024]{1,0:T(8,128)(2,1)S(1)}, u32[]{:S(2)}, u32[]{:S(2)}) collective-permute-start(bf16[256,1024]{1,0:T(8,128)(2,1)} %get-tuple-element.282.refs_0_), channel_id=1, source_target_pairs={{0,4},{4,0},{1,5},{5,1},{2,6},{6,2},{3,7},{7,3},{8,12},{12,8},{9,1... | collective-permute-start | bytes 1572872 | tf_op jit(solution)/shard_map/ppermute | solution.py:823
  236.5 14.4 %collective-permute-start.33 = (bf16[256,1024]{1,0:T(8,128)(2,1)}, bf16[256,1024]{1,0:T(8,128)(2,1)S(1)}, u32[]{:S(2)}, u32[]{:S(2)}) collective-permute-start(bf16[256,1024]{1,0:T(8,128)(2,1)} %get-tuple-element.282.refs_0_), channel_id=1, source_target_pairs={{0,1},{1,0},{2,3},{3,2},{4,5},{5,4},{6,7},{7,6},{8,9},{9,8},{10,11... | collective-permute-start | bytes 1572872 | tf_op jit(solution)/shard_map/ppermute | solution.py:823
  251.0 14.3 %collective-permute-start.39 = (bf16[256,1024]{1,0:T(8,128)(2,1)S(1)}, bf16[256,1024]{1,0:T(8,128)(2,1)S(1)}, u32[]{:S(2)}, u32[]{:S(2)}) collective-permute-start(bf16[256,1024]{1,0:T(8,128)(2,1)S(1)} %broadcast_select_fusion.3), channel_id=1, source_target_pairs={{0,1},{1,0},{2,3},{3,2},{4,5},{5,4},{6,7},{7,6},{8,9},{9,8},{10,11... | collective-permute-start | bytes 1572872 | tf_op jit(solution)/shard_map/ppermute | solution.py:823
  258.3 7.6 %collective-permute-start.36 = (bf16[256,1024]{1,0:T(8,128)(2,1)S(1)}, bf16[256,1024]{1,0:T(8,128)(2,1)S(1)}, u32[]{:S(2)}, u32[]{:S(2)}) collective-permute-start(bf16[256,1024]{1,0:T(8,128)(2,1)S(1)} %get-tuple-element.292), channel_id=1, source_target_pairs={{0,4},{4,0},{1,5},{5,1},{2,6},{6,2},{3,7},{7,3},{8,12},{12,8},{9,1... | collective-permute-start | bytes 1572872 | tf_op jit(solution)/shard_map/ppermute | solution.py:823
  258.9 10.4 %collective-permute-start.38 = (bf16[256,1024]{1,0:T(8,128)(2,1)S(1)}, bf16[256,1024]{1,0:T(8,128)(2,1)S(1)}, u32[]{:S(2)}, u32[]{:S(2)}) collective-permute-start(bf16[256,1024]{1,0:T(8,128)(2,1)S(1)} %broadcast_select_fusion.3), channel_id=1, source_target_pairs={{0,4},{4,0},{1,5},{5,1},{2,6},{6,2},{3,7},{7,3},{8,12},{12,8},{9,1... | collective-permute-start | bytes 1572872 | tf_op jit(solution)/shard_map/ppermute | solution.py:823
  266.1 14.2 %collective-permute-start.37 = (bf16[256,1024]{1,0:T(8,128)(2,1)S(1)}, bf16[256,1024]{1,0:T(8,128)(2,1)S(1)}, u32[]{:S(2)}, u32[]{:S(2)}) collective-permute-start(bf16[256,1024]{1,0:T(8,128)(2,1)S(1)} %add_convert_fusion.5), channel_id=1, source_target_pairs={{0,1},{1,0},{2,3},{3,2},{4,5},{5,4},{6,7},{7,6},{8,9},{9,8},{10,11... | collective-permute-start | bytes 1572872 | tf_op jit(solution)/shard_map/ppermute | solution.py:823
  284.3 14.3 %collective-permute-start.42 = (bf16[256,1024]{1,0:T(8,128)(2,1)S(1)}, bf16[256,1024]{1,0:T(8,128)(2,1)S(1)}, u32[]{:S(2)}, u32[]{:S(2)}) collective-permute-start(bf16[256,1024]{1,0:T(8,128)(2,1)S(1)} %get-tuple-element.299.refs_0_), channel_id=1, source_target_pairs={{0,1},{1,0},{2,3},{3,2},{4,5},{5,4},{6,7},{7,6},{8,9},{9,8},{10,11... | collective-permute-start | bytes 1572872 | tf_op jit(solution)/shard_map/ppermute | solution.py:823
  305.6 13.6 %collective-permute-start.45 = (bf16[256,1024]{1,0:T(8,128)(2,1)}, bf16[256,1024]{1,0:T(8,128)(2,1)S(1)}, u32[]{:S(2)}, u32[]{:S(2)}) collective-permute-start(bf16[256,1024]{1,0:T(8,128)(2,1)} %get-tuple-element.316), channel_id=1, source_target_pairs={{0,4},{4,0},{1,5},{5,1},{2,6},{6,2},{3,7},{7,3},{8,12},{12,8},{9,1... | collective-permute-start | bytes 1572872 | tf_op jit(solution)/shard_map/ppermute | solution.py:823
  308.3 14.2 %collective-permute-start.46 = (bf16[256,1024]{1,0:T(8,128)(2,1)}, bf16[256,1024]{1,0:T(8,128)(2,1)S(1)}, u32[]{:S(2)}, u32[]{:S(2)}) collective-permute-start(bf16[256,1024]{1,0:T(8,128)(2,1)} %add_convert_fusion.4), channel_id=1, source_target_pairs={{0,1},{1,0},{2,3},{3,2},{4,5},{5,4},{6,7},{7,6},{8,9},{9,8},{10,11... | collective-permute-start | bytes 1572872 | tf_op jit(solution)/shard_map/ppermute | solution.py:823
  329.2 101.4 %reduce-scatter.5.cloned.1.call-start = ((), (), s32[]{:S(2)}) async-start(), calls=%async_computation.7 | async-start | bytes 2621440 | tf_op jit(solution)/shard_map/reduce_scatter | solution.py:911
  330.2 14.3 %collective-permute-start.49 = (bf16[256,1024]{1,0:T(8,128)(2,1)S(1)}, bf16[256,1024]{1,0:T(8,128)(2,1)S(1)}, u32[]{:S(2)}, u32[]{:S(2)}) collective-permute-start(bf16[256,1024]{1,0:T(8,128)(2,1)S(1)} %copy-done.71), channel_id=1, source_target_pairs={{0,1},{1,0},{2,3},{3,2},{4,5},{5,4},{6,7},{7,6},{8,9},{9,8},{10,11... | collective-permute-start | bytes 1572872 | tf_op jit(solution)/shard_map/ppermute | solution.py:823
  344.6 10.5 %collective-permute-start.48 = (bf16[256,1024]{1,0:T(8,128)(2,1)S(1)}, bf16[256,1024]{1,0:T(8,128)(2,1)S(1)}, u32[]{:S(2)}, u32[]{:S(2)}) collective-permute-start(bf16[256,1024]{1,0:T(8,128)(2,1)S(1)} %copy-done.26), channel_id=1, source_target_pairs={{2,4},{4,2},{3,5},{5,3},{10,12},{12,10},{11,13},{13,11},{18,20},{2... | collective-permute-start | bytes 1572872 | tf_op jit(solution)/shard_map/ppermute | solution.py:831
  356.1 8.6 %collective-permute-start.51 = (bf16[256,1024]{1,0:T(8,128)(2,1)S(1)}, bf16[256,1024]{1,0:T(8,128)(2,1)S(1)}, u32[]{:S(2)}, u32[]{:S(2)}) collective-permute-start(bf16[256,1024]{1,0:T(8,128)(2,1)S(1)} %get-tuple-element.336), channel_id=1, source_target_pairs={{0,4},{4,0},{1,5},{5,1},{2,6},{6,2},{3,7},{7,3},{8,12},{12,8},{9,1... | collective-permute-start | bytes 1572872 | tf_op jit(solution)/shard_map/ppermute | solution.py:823
  367.3 14.0 %collective-permute-start.53 = (bf16[256,1024]{1,0:T(8,128)(2,1)S(1)}, bf16[256,1024]{1,0:T(8,128)(2,1)S(1)}, u32[]{:S(2)}, u32[]{:S(2)}) collective-permute-start(bf16[256,1024]{1,0:T(8,128)(2,1)S(1)} %add_convert_fusion.3), channel_id=1, source_target_pairs={{0,1},{1,0},{2,3},{3,2},{4,5},{5,4},{6,7},{7,6},{8,9},{9,8},{10,11... | collective-permute-start | bytes 1572872 | tf_op jit(solution)/shard_map/ppermute | solution.py:823
  387.6 14.7 %collective-permute-start.55 = (bf16[256,1024]{1,0:T(8,128)(2,1)}, bf16[256,1024]{1,0:T(8,128)(2,1)}, u32[]{:S(2)}, u32[]{:S(2)}) collective-permute-start(bf16[256,1024]{1,0:T(8,128)(2,1)} %get-tuple-element.350.refs_0_), channel_id=1, source_target_pairs={{0,1},{1,0},{2,3},{3,2},{4,5},{5,4},{6,7},{7,6},{8,9},{9,8},{10,11... | collective-permute-start | bytes 1572872 | tf_op jit(solution)/shard_map/ppermute | solution.py:823
  390.1 12.2 %collective-permute-start.57 = (bf16[2048,128]{1,0:T(8,128)(2,1)S(1)}, bf16[2048,128]{1,0:T(8,128)(2,1)S(1)}, u32[]{:S(2)}, u32[]{:S(2)}) collective-permute-start(bf16[2048,128]{1,0:T(8,128)(2,1)S(1)} %get-tuple-element.363), channel_id=1, source_target_pairs={{0,4},{4,0},{1,5},{5,1},{2,6},{6,2},{3,7},{7,3},{8,12},{12,8},{9,1... | collective-permute-start | bytes 1572872 | tf_op jit(solution)/shard_map/ppermute | solution.py:823
  403.2 14.9 %collective-permute-start.58 = (bf16[1024,128]{1,0:T(8,128)(2,1)S(1)}, bf16[1024,128]{1,0:T(8,128)(2,1)S(1)}, u32[]{:S(2)}, u32[]{:S(2)}) collective-permute-start(bf16[1024,128]{1,0:T(8,128)(2,1)S(1)} %get-tuple-element.364), channel_id=1, source_target_pairs={{0,2},{2,0},{1,3},{3,1},{4,6},{6,4},{5,7},{7,5},{8,10},{10,8},{9,1... | collective-permute-start | bytes 786440 | tf_op jit(solution)/shard_map/ppermute | solution.py:823
  403.9 36.8 %collective-permute-start.61 = (bf16[256,1024]{1,0:T(8,128)(2,1)}, bf16[256,1024]{1,0:T(8,128)(2,1)S(1)}, u32[]{:S(2)}, u32[]{:S(2)}) collective-permute-start(bf16[256,1024]{1,0:T(8,128)(2,1)} %get-tuple-element.374), channel_id=1, source_target_pairs={{0,4},{4,0},{1,5},{5,1},{2,6},{6,2},{3,7},{7,3},{8,12},{12,8},{9,1... | collective-permute-start | bytes 1572872 | tf_op jit(solution)/shard_map/ppermute | solution.py:823
  420.2 21.6 %collective-permute-start.62 = (bf16[256,1024]{1,0:T(8,128)(2,1)S(1)}, bf16[256,1024]{1,0:T(8,128)(2,1)S(1)}, u32[]{:S(2)}, u32[]{:S(2)}) collective-permute-start(bf16[256,1024]{1,0:T(8,128)(2,1)S(1)} %add_convert_fusion.2), channel_id=1, source_target_pairs={{0,1},{1,0},{2,3},{3,2},{4,5},{5,4},{6,7},{7,6},{8,9},{9,8},{10,11... | collective-permute-start | bytes 1572872 | tf_op jit(solution)/shard_map/ppermute | solution.py:823
  420.3 18.8 %collective-permute-start.60 = (bf16[1024,128]{1,0:T(8,128)(2,1)}, bf16[1024,128]{1,0:T(8,128)(2,1)}, u32[]{:S(2)}, u32[]{:S(2)}) collective-permute-start(bf16[1024,128]{1,0:T(8,128)(2,1)} %get-tuple-element.370), channel_id=1, source_target_pairs={{0,2},{2,0},{1,3},{3,1},{4,6},{6,4},{5,7},{7,5},{8,10},{10,8},{9,1... | collective-permute-start | bytes 786440 | tf_op jit(solution)/shard_map/ppermute | solution.py:823
  429.1 18.0 %collective-permute-start.66 = (bf16[2,1024,128]{2,1,0:T(8,128)(2,1)}, bf16[2,1024,128]{2,1,0:T(8,128)(2,1)}, u32[]{:S(2)}, u32[]{:S(2)}) collective-permute-start(bf16[2,1024,128]{2,1,0:T(8,128)(2,1)} %get-tuple-element.367), channel_id=1, source_target_pairs={{0,16},{8,24},{16,0},{24,8},{1,17},{9,25},{17,1},{25,9},{2,18},{10... | collective-permute-start | bytes 1572872 | tf_op jit(solution)/shard_map/ppermute | solution.py:827
  432.3 15.8 %collective-permute-start.67 = (bf16[2,1024,128]{2,1,0:T(8,128)(2,1)}, bf16[2,1024,128]{2,1,0:T(8,128)(2,1)S(1)}, u32[]{:S(2)}, u32[]{:S(2)}) collective-permute-start(bf16[2,1024,128]{2,1,0:T(8,128)(2,1)} %get-tuple-element.381), channel_id=1, source_target_pairs={{0,8},{8,0},{16,24},{24,16},{1,9},{9,1},{17,25},{25,17},{2,10},{10... | collective-permute-start | bytes 1572872 | tf_op jit(solution)/shard_map/ppermute | solution.py:827
  439.2 14.8 %collective-permute-start.68 = (bf16[2,1024,128]{2,1,0:T(8,128)(2,1)S(1)}, bf16[2,1024,128]{2,1,0:T(8,128)(2,1)S(1)}, u32[]{:S(2)}, u32[]{:S(2)}) collective-permute-start(bf16[2,1024,128]{2,1,0:T(8,128)(2,1)S(1)} %get-tuple-element.369), channel_id=1, source_target_pairs={{0,16},{8,24},{16,0},{24,8},{1,17},{9,25},{17,1},{25,9},{2,18},{10... | collective-permute-start | bytes 1572872 | tf_op jit(solution)/shard_map/ppermute | solution.py:827
  440.8 16.1 %collective-permute-start.69 = (bf16[2,1024,128]{2,1,0:T(8,128)(2,1)S(1)}, bf16[2,1024,128]{2,1,0:T(8,128)(2,1)S(1)}, u32[]{:S(2)}, u32[]{:S(2)}) collective-permute-start(bf16[2,1024,128]{2,1,0:T(8,128)(2,1)S(1)} %get-tuple-element.382), channel_id=1, source_target_pairs={{0,8},{8,0},{16,24},{24,16},{1,9},{9,1},{17,25},{25,17},{2,10},{10... | collective-permute-start | bytes 1572872 | tf_op jit(solution)/shard_map/ppermute | solution.py:827
  444.6 20.8 %collective-permute-start.63 = (bf16[256,1024]{1,0:T(8,128)(2,1)S(1)}, bf16[256,1024]{1,0:T(8,128)(2,1)S(1)}, u32[]{:S(2)}, u32[]{:S(2)}) collective-permute-start(bf16[256,1024]{1,0:T(8,128)(2,1)S(1)} %get-tuple-element.377.refs_8_), channel_id=1, source_target_pairs={{0,1},{1,0},{2,3},{3,2},{4,5},{5,4},{6,7},{7,6},{8,9},{9,8},{10,11... | collective-permute-start | bytes 1572872 | tf_op jit(solution)/shard_map/ppermute | solution.py:823
  447.1 9.9 %collective-permute-start.64 = (bf16[256,1024]{1,0:T(8,128)(2,1)S(1)}, bf16[256,1024]{1,0:T(8,128)(2,1)S(1)}, u32[]{:S(2)}, u32[]{:S(2)}) collective-permute-start(bf16[256,1024]{1,0:T(8,128)(2,1)S(1)} %get-tuple-element.377.refs_8_), channel_id=1, source_target_pairs={{0,4},{4,0},{1,5},{5,1},{2,6},{6,2},{3,7},{7,3},{8,12},{12,8},{9,1... | collective-permute-start | bytes 1572872 | tf_op jit(solution)/shard_map/ppermute | solution.py:823
  465.5 15.9 %collective-permute-start.70 = (bf16[1,1024,128]{2,1,0:T(8,128)(2,1)S(1)}, bf16[1,1024,128]{2,1,0:T(8,128)(2,1)S(1)}, u32[]{:S(2)}, u32[]{:S(2)}) collective-permute-start(bf16[1,1024,128]{2,1,0:T(8,128)(2,1)S(1)} %add_convert_fusion.17), channel_id=1, source_target_pairs={{0,8},{8,0},{16,24},{24,16},{1,9},{9,1},{17,25},{25,17},{2,10},{10... | collective-permute-start | bytes 786440 | tf_op jit(solution)/shard_map/ppermute | solution.py:827
  467.0 14.3 %collective-permute-start.71 = (bf16[1,1024,128]{2,1,0:T(8,128)(2,1)S(1)}, bf16[1,1024,128]{2,1,0:T(8,128)(2,1)S(1)}, u32[]{:S(2)}, u32[]{:S(2)}) collective-permute-start(bf16[1,1024,128]{2,1,0:T(8,128)(2,1)S(1)} %add_convert_fusion.16), channel_id=1, source_target_pairs={{0,16},{8,24},{16,0},{24,8},{1,17},{9,25},{17,1},{25,9},{2,18},{10... | collective-permute-start | bytes 786440 | tf_op jit(solution)/shard_map/ppermute | solution.py:827
  467.6 13.8 %collective-permute-start.72 = (bf16[1,1024,128]{2,1,0:T(8,128)(2,1)S(1)}, bf16[1,1024,128]{2,1,0:T(8,128)(2,1)S(1)}, u32[]{:S(2)}, u32[]{:S(2)}) collective-permute-start(bf16[1,1024,128]{2,1,0:T(8,128)(2,1)S(1)} %add_convert_fusion.15), channel_id=1, source_target_pairs={{0,8},{8,0},{16,24},{24,16},{1,9},{9,1},{17,25},{25,17},{2,10},{10... | collective-permute-start | bytes 786440 | tf_op jit(solution)/shard_map/ppermute | solution.py:827
  469.7 11.7 %collective-permute-start.73 = (bf16[1,1024,128]{2,1,0:T(8,128)(2,1)S(1)}, bf16[1,1024,128]{2,1,0:T(8,128)(2,1)S(1)}, u32[]{:S(2)}, u32[]{:S(2)}) collective-permute-start(bf16[1,1024,128]{2,1,0:T(8,128)(2,1)S(1)} %add_convert_fusion.14), channel_id=1, source_target_pairs={{0,16},{8,24},{16,0},{24,8},{1,17},{9,25},{17,1},{25,9},{2,18},{10... | collective-permute-start | bytes 786440 | tf_op jit(solution)/shard_map/ppermute | solution.py:827
  471.2 14.5 %collective-permute-start.75 = (bf16[1024,128]{1,0:T(8,128)(2,1)S(1)}, bf16[1024,128]{1,0:T(8,128)(2,1)S(1)}, u32[]{:S(2)}, u32[]{:S(2)}) collective-permute-start(bf16[1024,128]{1,0:T(8,128)(2,1)S(1)} %broadcast_select_fusion.5), channel_id=1, source_target_pairs={{0,2},{2,0},{1,3},{3,1},{4,6},{6,4},{5,7},{7,5},{8,10},{10,8},{9,1... | collective-permute-start | bytes 786440 | tf_op jit(solution)/shard_map/ppermute | solution.py:823
  488.5 11.4 %collective-permute-start.79 = (bf16[1024,128]{1,0:T(8,128)(2,1)}, bf16[1024,128]{1,0:T(8,128)(2,1)S(1)}, u32[]{:S(2)}, u32[]{:S(2)}) collective-permute-start(bf16[1024,128]{1,0:T(8,128)(2,1)} %fusion.12), channel_id=1, source_target_pairs={{0,4},{4,0},{1,5},{5,1},{2,6},{6,2},{3,7},{7,3},{8,12},{12,8},{9,1... | collective-permute-start | bytes 786440 | tf_op jit(solution)/shard_map/ppermute | solution.py:823
  489.0 29.4 %collective-permute-start.86 = (bf16[1024,128]{1,0:T(8,128)(2,1)}, bf16[1024,128]{1,0:T(8,128)(2,1)}, u32[]{:S(2)}, u32[]{:S(2)}) collective-permute-start(bf16[1024,128]{1,0:T(8,128)(2,1)} %fusion.14), channel_id=1, source_target_pairs={{0,4},{4,0},{1,5},{5,1},{2,6},{6,2},{3,7},{7,3},{8,12},{12,8},{9,1... | collective-permute-start | bytes 786440 | tf_op jit(solution)/shard_map/ppermute | solution.py:823
  497.1 14.6 %collective-permute-start.77 = (bf16[2,1024,128]{2,1,0:T(8,128)(2,1)}, bf16[2,1024,128]{2,1,0:T(8,128)(2,1)}, u32[]{:S(2)}, u32[]{:S(2)}) collective-permute-start(bf16[2,1024,128]{2,1,0:T(8,128)(2,1)} %get-tuple-element.411), channel_id=1, source_target_pairs={{0,16},{8,24},{16,0},{24,8},{1,17},{9,25},{17,1},{25,9},{2,18},{10... | collective-permute-start | bytes 1572872 | tf_op jit(solution)/shard_map/ppermute | solution.py:827
  498.3 14.5 %collective-permute-start.78 = (bf16[2,1024,128]{2,1,0:T(8,128)(2,1)}, bf16[2,1024,128]{2,1,0:T(8,128)(2,1)S(1)}, u32[]{:S(2)}, u32[]{:S(2)}) collective-permute-start(bf16[2,1024,128]{2,1,0:T(8,128)(2,1)} %get-tuple-element.413), channel_id=1, source_target_pairs={{0,8},{8,0},{16,24},{24,16},{1,9},{9,1},{17,25},{25,17},{2,10},{10... | collective-permute-start | bytes 1572872 | tf_op jit(solution)/shard_map/ppermute | solution.py:827
  501.9 14.5 %collective-permute-start.80 = (bf16[1024,128]{1,0:T(8,128)(2,1)S(1)}, bf16[1024,128]{1,0:T(8,128)(2,1)S(1)}, u32[]{:S(2)}, u32[]{:S(2)}) collective-permute-start(bf16[1024,128]{1,0:T(8,128)(2,1)S(1)} %get-tuple-element.465), channel_id=1, source_target_pairs={{0,2},{2,0},{1,3},{3,1},{4,6},{6,4},{5,7},{7,5},{8,10},{10,8},{9,1... | collective-permute-start | bytes 786440 | tf_op jit(solution)/shard_map/ppermute | solution.py:823
  501.9 23.3 %collective-permute-start.84 = (bf16[256,1024]{1,0:T(8,128)(2,1)}, bf16[256,1024]{1,0:T(8,128)(2,1)}, u32[]{:S(2)}, u32[]{:S(2)}) collective-permute-start(bf16[256,1024]{1,0:T(8,128)(2,1)} %add_convert_fusion.1), channel_id=1, source_target_pairs={{0,1},{1,0},{2,3},{3,2},{4,5},{5,4},{6,7},{7,6},{8,9},{9,8},{10,11... | collective-permute-start | bytes 1572872 | tf_op jit(solution)/shard_map/ppermute | solution.py:823
  511.7 13.4 %collective-permute-start.83 = (bf16[256,1024]{1,0:T(8,128)(2,1)}, bf16[256,1024]{1,0:T(8,128)(2,1)}, u32[]{:S(2)}, u32[]{:S(2)}) collective-permute-start(bf16[256,1024]{1,0:T(8,128)(2,1)} %get-tuple-element.421), channel_id=1, source_target_pairs={{0,4},{4,0},{1,5},{5,1},{2,6},{6,2},{3,7},{7,3},{8,12},{12,8},{9,1... | collective-permute-start | bytes 1572872 | tf_op jit(solution)/shard_map/ppermute | solution.py:823
  516.3 8.3 %collective-permute-start.81 = (bf16[1,1024,128]{2,1,0:T(8,128)(2,1)S(1)}, bf16[1,1024,128]{2,1,0:T(8,128)(2,1)}, u32[]{:S(2)}, u32[]{:S(2)}) collective-permute-start(bf16[1,1024,128]{2,1,0:T(8,128)(2,1)S(1)} %add_convert_fusion.13), channel_id=1, source_target_pairs={{0,8},{8,0},{16,24},{24,16},{1,9},{9,1},{17,25},{25,17},{2,10},{10... | collective-permute-start | bytes 786440 | tf_op jit(solution)/shard_map/ppermute | solution.py:827
  516.9 8.0 %collective-permute-start.82 = (bf16[1,1024,128]{2,1,0:T(8,128)(2,1)S(1)}, bf16[1,1024,128]{2,1,0:T(8,128)(2,1)}, u32[]{:S(2)}, u32[]{:S(2)}) collective-permute-start(bf16[1,1024,128]{2,1,0:T(8,128)(2,1)S(1)} %add_convert_fusion.12), channel_id=1, source_target_pairs={{0,16},{8,24},{16,0},{24,8},{1,17},{9,25},{17,1},{25,9},{2,18},{10... | collective-permute-start | bytes 786440 | tf_op jit(solution)/shard_map/ppermute | solution.py:827
  520.4 16.3 %collective-permute-start.87 = (bf16[1024,128]{1,0:T(8,128)(2,1)}, bf16[1024,128]{1,0:T(8,128)(2,1)}, u32[]{:S(2)}, u32[]{:S(2)}) collective-permute-start(bf16[1024,128]{1,0:T(8,128)(2,1)} %get-tuple-element.424), channel_id=1, source_target_pairs={{0,2},{2,0},{1,3},{3,1},{4,6},{6,4},{5,7},{7,5},{8,10},{10,8},{9,1... | collective-permute-start | bytes 786440 | tf_op jit(solution)/shard_map/ppermute | solution.py:823
  527.7 6.3 %collective-permute-start.91 = (f32[4,2,768]{2,1,0:T(2,128)S(1)}, f32[4,2,768]{2,1,0:T(2,128)S(1)}, u32[]{:S(2)}, u32[]{:S(2)}) collective-permute-start(f32[4,2,768]{2,1,0:T(2,128)S(1)} %bitcast.114), channel_id=1, source_target_pairs={{0,1},{1,0},{2,3},{3,2},{4,5},{5,4},{6,7},{7,6},{8,9},{9,8},{10,11... | collective-permute-start | bytes 73736 | tf_op jit(solution)/shard_map/ppermute | solution.py:823
  528.7 24.5 %collective-permute-start.85 = (bf16[256,1024]{1,0:T(8,128)(2,1)}, bf16[256,1024]{1,0:T(8,128)(2,1)}, u32[]{:S(2)}, u32[]{:S(2)}) collective-permute-start(bf16[256,1024]{1,0:T(8,128)(2,1)} %add_convert_fusion), channel_id=1, source_target_pairs={{2,4},{4,2},{3,5},{5,3},{10,12},{12,10},{11,13},{13,11},{18,20},{2... | collective-permute-start | bytes 1572872 | tf_op jit(solution)/shard_map/ppermute | solution.py:831
  536.7 13.1 %collective-permute-start.88 = (bf16[1024,128]{1,0:T(8,128)(2,1)}, bf16[1024,128]{1,0:T(8,128)(2,1)S(1)}, u32[]{:S(2)}, u32[]{:S(2)}) collective-permute-start(bf16[1024,128]{1,0:T(8,128)(2,1)} %fusion.13), channel_id=1, source_target_pairs={{0,4},{4,0},{1,5},{5,1},{2,6},{6,2},{3,7},{7,3},{8,12},{12,8},{9,1... | collective-permute-start | bytes 786440 | tf_op jit(solution)/shard_map/ppermute | solution.py:823
  551.0 11.3 %collective-permute-start.89 = (bf16[1024,128]{1,0:T(8,128)(2,1)S(1)}, bf16[1024,128]{1,0:T(8,128)(2,1)S(1)}, u32[]{:S(2)}, u32[]{:S(2)}) collective-permute-start(bf16[1024,128]{1,0:T(8,128)(2,1)S(1)} %fusion.15), channel_id=1, source_target_pairs={{0,2},{2,0},{1,3},{3,1},{4,6},{6,4},{5,7},{7,5},{8,10},{10,8},{9,1... | collective-permute-start | bytes 786440 | tf_op jit(solution)/shard_map/ppermute | solution.py:823
  (175 other events, 1141.6 us)
Sparse Core Ops, SparseCore 0:
  29.4 37.2 all-gather.4
  92.3 52.7 all-gather.6
  150.3 34.5 all-gather.8
  186.6 52.6 all-gather.10
  329.3 51.5 reduce-scatter.2
  384.0 35.1 reduce-scatter.4
